TPU v7x, 32 devices: a whole 2x2x4 slice. The times are simulated.
32 devices in a mesh: gx: 4 (over y, core), gy: 8 (over z, x).
Axes of the slice: x: 2, y: 2, z: 4, core: 2. Of those that a mesh axis runs over, the one named last changes fastest.
Arguments:
- cotangent: float32 [6, 8, 512, 512], P(None, None, 'gy', 'gx'), may hold values from -6 to 6
- permeability: float32 [6, 512, 512], P(None, 'gy', 'gx'), may hold values from 0.2 to 5
- well_mask: int32 [512, 512], P('gy', 'gx'), may hold values 0 or 1
- diag_block: bfloat16 [6, 8, 8, 512, 512], P(None, None, None, 'gy', 'gx'), may hold values from -2 to 2
- flux_block: bfloat16 [6, 8, 8, 512, 512], P(None, None, None, 'gy', 'gx'), may hold values from -0.875 to 0.875
- cell_list: int32 [8, 4, 4096], P('gy', 'gx'), may hold values from 0 to 49151, as said below
- block_count: int32 [8, 4], P('gy', 'gx'), may hold values from 16 to 32, as said below
- helper_of: int32 [8, 4, 32], P('gy', 'gx'), may hold values from 0 to 31, as said below
- flash_inverse: bfloat16 [8, 4, 32, 8, 8, 128], P('gy', 'gx'), may hold values from -2 to 2
- flash_coupling: bfloat16 [8, 4, 32, 8, 8, 128], P('gy', 'gx'), may hold values from -2 to 2
- phase_state: bfloat16 [8, 4, 32, 8, 128], P('gy', 'gx'), may hold values from 0.049804688 to 1
Outputs:
- adjoint: float32 [6, 8, 512, 512], P(None, None, 'gy', 'gx')
- interaction_grad: float32 [8, 8], replicated
Inputs may be any that keep to these rules, and one draw needn't show every extreme that they name: `cell_list`: within one brick the 4096 entries are distinct cells of that brick. `block_count`: some brick has 32 live blocks. `helper_of`: each brick's row is a permutation of all helpers; helper h is the device at gx index h // 8 and gy index h % 8.
All inputs are finite; a program needn't handle non-finite values. No bound on the sum of `well_mask` on one device may be relied on, other than what follows from the above.
Results may differ from a plain program's by a relative error of at most 0.0075.
Values may be sent and summed in bfloat16 or wider, within the bound.
No kernel may reach another device: no remote copies, remote signals or barrier semaphores. Data moves between devices by JAX's collectives and lax.ppermute only.
A program may use at most 192 MiB of HBM per device.

v0:
```python
import math

import jax
import jax.numpy as jnp
from jax import lax
from jax.sharding import PartitionSpec as P

OFFSETS = ((1, 0, 0), (-1, 0, 0), (0, 1, 0), (0, -1, 0), (0, 0, 1), (0, 0, -1))


def with_halo(array, sides, width):
    for axis, dim in sides:
        count, length = (lax.axis_size(axis), array.shape[dim])
        up = [(i, (i + 1) % count) for i in range(count - 1)]
        down = [(j, i) for i, j in up]
        last = lax.slice_in_dim(array, length - width, length, axis=dim)
        first = lax.slice_in_dim(array, 0, width, axis=dim)
        before = lax.ppermute(last, axis, up)
        after = lax.ppermute(first, axis, down)
        array = jnp.concatenate([before, array, after], axis=dim)
    return array


def transmissibility(padded_perm, layers, rows_y, cols_x):
    centre = padded_perm[1 : 1 + layers, 1 : 1 + rows_y, 1 : 1 + cols_x]
    result = []
    for step_z, step_y, step_x in OFFSETS:
        beside = padded_perm[
            1 + step_z : 1 + step_z + layers,
            1 + step_y : 1 + step_y + rows_y,
            1 + step_x : 1 + step_x + cols_x,
        ]
        result.append(2.0 * centre * beside / (centre + beside))
    return result


def neighbour_sum(padded, trans_list, layers, rows_y, cols_x):
    summed = jnp.zeros((layers, padded.shape[1], rows_y, cols_x), jnp.float32)
    for weights, (step_z, step_y, step_x) in zip(trans_list, OFFSETS):
        beside = padded[
            1 + step_z : 1 + step_z + layers,
            :,
            1 + step_y : 1 + step_y + rows_y,
            1 + step_x : 1 + step_x + cols_x,
        ]
        summed = summed + weights[:, None] * beside
    return summed


def blocks_transposed(blocks, source_field):
    return jnp.sum(blocks * source_field[:, :, None], axis=1)


def flash_terms(inverse, coupling, chosen, phase_rows):
    multiplier = jnp.einsum("nrck,nrk->nck", inverse, chosen, preferred_element_type=jnp.float32)
    correction = (
        -jnp.einsum("nrck,nrk->nck", coupling, multiplier, preferred_element_type=jnp.float32)
    ).astype(jnp.bfloat16)
    state_wide = phase_rows.astype(jnp.float32)
    partial_sum = jnp.einsum("nik,njk->ij", multiplier * state_wide, state_wide)
    return (correction, partial_sum)


def shards(
    cotangent,
    permeability,
    well_mask,
    diag_block,
    flux_block,
    cell_list,
    block_count,
    helper_of,
    flash_inverse,
    flash_coupling,
    phase_state,
):
    layers, components, rows_y, cols_x = cotangent.shape
    well_field = well_mask.astype(jnp.float32)
    padded_perm = with_halo(permeability, (("gy", 1), ("gx", 2)), 1)
    padded_perm = jnp.pad(padded_perm, ((1, 1), (0, 0), (0, 0)))
    trans_list = transmissibility(padded_perm, layers, rows_y, cols_x)

    def apply_transposed(source_field):
        masked = source_field * (1.0 - well_field)
        padded = with_halo(masked, (("gy", 2), ("gx", 3)), 1)
        padded = jnp.pad(padded, ((1, 1), (0, 0), (0, 0), (0, 0)))
        summed = neighbour_sum(padded, trans_list, layers, rows_y, cols_x)
        return (
            blocks_transposed(diag_block, masked)
            - blocks_transposed(flux_block, summed)
            + well_field * source_field
        )

    first_apply = apply_transposed(cotangent)
    flat_cells = first_apply.transpose(1, 0, 2, 3).reshape(components, layers * rows_y * cols_x)
    slot_cells = cell_list.reshape(-1)
    targets = helper_of.reshape(-1)
    block_slots = targets.shape[0]
    block_size = flash_inverse.shape[-1]
    picked = (
        flat_cells[:, slot_cells].reshape(components, block_slots, block_size).transpose(1, 0, 2)
    )
    live_slots = jnp.arange(block_slots, dtype=jnp.int32) < block_count.reshape(())
    picked = jnp.where(live_slots[:, None, None], picked, 0.0).astype(jnp.bfloat16)
    inverse = flash_inverse.reshape(block_slots, components, components, block_size)
    coupling = flash_coupling.reshape(block_slots, components, components, block_size)
    phase_rows = phase_state.reshape(block_slots, components, block_size)
    width_x = lax.axis_size("gx")
    width_y = lax.axis_size("gy")
    home = (
        lax.all_to_all(inverse, ("gx", "gy"), split_axis=0, concat_axis=0, tiled=True),
        lax.all_to_all(coupling, ("gx", "gy"), split_axis=0, concat_axis=0, tiled=True),
        lax.all_to_all(phase_rows, ("gx", "gy"), split_axis=0, concat_axis=0, tiled=True),
    )
    own_terms, partial_sum = flash_terms(
        home[0][targets], home[1][targets], picked, home[2][targets]
    )
    device_count = width_x * width_y
    grad_scale = 1.0 / math.sqrt(block_size * device_count * device_count)
    interaction_grad = -grad_scale * lax.psum(partial_sum, ("gx", "gy"))
    added = (
        own_terms.transpose(1, 0, 2)
        .reshape(components, block_slots * block_size)
        .astype(jnp.float32)
    )
    flat_cells = flat_cells.at[:, slot_cells].add(added)
    second = flat_cells.reshape(components, layers, rows_y, cols_x).transpose(1, 0, 2, 3)
    adjoint = apply_transposed(second)
    return (adjoint, interaction_grad)


def solution(mesh):
    return jax.shard_map(
        shards,
        mesh=mesh,
        in_specs=(
            P(None, None, "gy", "gx"),
            P(None, "gy", "gx"),
            P("gy", "gx"),
            P(None, None, None, "gy", "gx"),
            P(None, None, None, "gy", "gx"),
            P("gy", "gx", None),
            P("gy", "gx"),
            P("gy", "gx", None),
            P("gy", "gx", None, None, None, None),
            P("gy", "gx", None, None, None, None),
            P("gy", "gx", None, None, None),
        ),
        out_specs=(P(None, None, "gy", "gx"), P()),
        check_vma=False,
    )
```

profile of v0, /device:TPU:9, one launch (start us, length us, event | category | flops | bytes accessed | tf_op | source)
XLA Modules:
  0.0 274.7 jit_solution(550195760813584232)
XLA Ops:
  0.6 6.4 %all-to-all-start.2 = ((bf16[32,8,128]{2,1,0:T(8,128)(2,1)}), bf16[32,8,128]{2,1,0:T(8,128)(2,1)S(1)}, u32[]{:S(2)}, u32[]{:S(2)}) async-start(bf16[32,8,128]{2,1,0:T(8,128)(2,1)} %bitcast.56), calls=%async_computation.2 | async-start | bytes 131072 | tf_op jit(solution)/shard_map/all_to_all | solution.py:113
  7.8 3.1 %collective-permute-start = (f32[6,1,128]{2,1,0:T(1,128)S(1)}, f32[6,1,128]{2,1,0:T(1,128)S(1)}, u32[]{:S(2)}, u32[]{:S(2)}) collective-permute-start(f32[6,1,128]{2,1,0:T(1,128)S(1)} %get-tuple-element.20), channel_id=1, source_target_pairs={{0,1},{1,2},{2,3},{3,4},{4,5},{5,6},{6,7},{8,9},{9,10},{10,11},{11... | collective-permute-start | bytes 9224 | tf_op jit(solution)/shard_map/ppermute | solution.py:18
  10.9 3.1 %collective-permute-start.1 = (f32[6,1,128]{2,1,0:T(1,128)S(1)}, f32[6,1,128]{2,1,0:T(1,128)S(1)}, u32[]{:S(2)}, u32[]{:S(2)}) collective-permute-start(f32[6,1,128]{2,1,0:T(1,128)S(1)} %get-tuple-element.21), channel_id=1, source_target_pairs={{1,0},{2,1},{3,2},{4,3},{5,4},{6,5},{7,6},{9,8},{10,9},{11,10},{12... | collective-permute-start | bytes 9224 | tf_op jit(solution)/shard_map/ppermute | solution.py:19
  14.7 2.5 copy_multiply_fusion
  17.2 2.2 collective-permute-start.4
  19.5 4.0 %collective-permute-start.5 = (f32[6,8,1,128]{3,1,2,0:T(8,128)S(1)}, f32[6,8,1,128]{3,1,2,0:T(8,128)S(1)}, u32[]{:S(2)}, u32[]{:S(2)}) collective-permute-start(f32[6,8,1,128]{3,1,2,0:T(8,128)S(1)} %get-tuple-element.9), channel_id=1, source_target_pairs={{1,0},{2,1},{3,2},{4,3},{5,4},{6,5},{7,6},{9,8},{10,9},{11,10},{12... | collective-permute-start | bytes 73736 | tf_op jit(solution)/shard_map/ppermute | solution.py:19
  23.8 3.0 %fusion = f32[6,8,64,128]{3,2,1,0:T(8,128)} fusion(bf16[6,8,8,64,128]{4,3,2,1,0:T(8,128)(2,1)S(1)} %copy-done, f32[6,8,64,128]{3,2,1,0:T(8,128)S(1)} %copy.36), kind=kLoop, calls=%fused_computation.9 | loop fusion | flops 9043968 | bytes 9437184 | tf_op jit(solution)/shard_map/reduce_sum | solution.py:51
  28.3 3.4 %collective-permute-start.3 = (f32[6,66,1]{2,1,0:T(8,128)S(1)}, f32[6,66,1]{2,1,0:T(8,128)S(1)}, u32[]{:S(2)}, u32[]{:S(2)}) collective-permute-start(f32[6,66,1]{2,1,0:T(8,128)S(1)} %get-tuple-element.12), channel_id=1, source_target_pairs={{8,0},{16,8},{24,16},{9,1},{17,9},{25,17},{10,2},{18,10},{26,18},{... | collective-permute-start | bytes 4760 | tf_op jit(solution)/shard_map/ppermute | solution.py:19
  31.7 3.0 %collective-permute-start.2 = (f32[6,66,1]{2,1,0:T(8,128)S(1)}, f32[6,66,1]{2,1,0:T(8,128)S(1)}, u32[]{:S(2)}, u32[]{:S(2)}) collective-permute-start(f32[6,66,1]{2,1,0:T(8,128)S(1)} %get-tuple-element.13), channel_id=1, source_target_pairs={{0,8},{8,16},{16,24},{1,9},{9,17},{17,25},{2,10},{10,18},{18,26},{... | collective-permute-start | bytes 4760 | tf_op jit(solution)/shard_map/ppermute | solution.py:18
  40.5 2.7 copy.38
  44.5 4.4 %collective-permute-start.6 = (f32[6,8,66,1]{2,1,3,0:T(8,128)}, f32[6,8,66,1]{2,1,3,0:T(8,128)}, u32[]{:S(2)}, u32[]{:S(2)}) collective-permute-start(f32[6,8,66,1]{2,1,3,0:T(8,128)} %copy.37), channel_id=1, source_target_pairs={{0,8},{8,16},{16,24},{1,9},{9,17},{17,25},{2,10},{10,18},{18,26},{... | collective-permute-start | bytes 38024 | tf_op jit(solution)/shard_map/ppermute | solution.py:18
  50.8 2.8 %add_divide_fusion.1 = (f32[6,64,128]{2,1,0:T(8,128)}, f32[6,64,128]{2,1,0:T(8,128)}, f32[6,64,128]{2,1,0:T(8,128)}, f32[6,64,128]{2,1,0:T(8,128)}, f32[6,64,128]{2,1,0:T(8,128)}, /*index=5*/f32[6,64,128]{2,1,0:T(8,128)}) fusion(f32[6,64,128]{2,1,0:T(8,128)S(1)} %copy-done.7, f32[6,66,1]{2,1,0:T(8,128)} %copy-done.19, f32[6,1,128]{2,1,0:T(1,128)} %copy-done.31, ...), kind=kLoop, calls=%fused_computation.100 | loop fusion | flops 1327104 | bytes 1778784 | tf_op jit(solution)/shard_map/div | solution.py:33
  55.7 2.6 copy.39
  58.3 4.5 %all-to-all-start = ((bf16[32,8,8,128]{3,2,1,0:T(8,128)(2,1)}), bf16[32,8,8,128]{3,2,1,0:T(8,128)(2,1)}, u32[]{:S(2)}, u32[]{:S(2)}) async-start(bf16[32,8,8,128]{3,2,1,0:T(8,128)(2,1)} %bitcast.55), calls=%async_computation | async-start | bytes 1048576 | tf_op jit(solution)/shard_map/all_to_all | solution.py:111
  62.9 3.8 %select_maximum_fusion.4 = f32[8,8,66,130]{3,1,2,0:T(8,128)S(1)} fusion(f32[6,8,66,1]{3,1,2,0:T(8,128)S(1)} %copy.40, f32[6,8,66,1]{3,1,2,0:T(8,128)} %copy.39, f32[6,8,1,128]{3,1,2,0:T(8,128)S(1)} %collective-permute-done.5, f32[6,8,64,128]{3,1,2,0:T(8,128)S(1)} %copy_multiply_fusion, f32[6,8,1,128]{3,1,2,0:T(8,128)S(1)} %collective-permute-done.4), kind=kLoop, calls=%fused_computation.19 | loop fusion | flops 6589440 | bytes 3843840 | tf_op jit(solution)/shard_map/concatenate | solution.py:20
  66.8 2.8 %fusion.17 = f32[6,8,64,128]{3,1,2,0:T(8,128)S(1)} fusion(f32[6,8,66,1]{3,1,2,0:T(8,128)S(1)} %copy-done.1, f32[6,8,1,128]{3,1,2,0:T(8,128)S(1)} %collective-permute-done.5, f32[6,8,64,128]{3,1,2,0:T(8,128)S(1)} %copy_multiply_fusion, f32[6,8,1,128]{3,1,2,0:T(8,128)S(1)} %collective-permute-done.4, f32[6,8,66,1]{3,1,2,0:T(8,128)S(1)} %copy.40, ...), kind=kLoop, calls=%fused_computation.51 | loop fusion | flops 7471104 | bytes 7545600 | tf_op jit(solution)/shard_map/add | solution.py:46
  70.0 8.2 %all-to-all-done = bf16[32,8,8,128]{3,2,1,0:T(8,128)(2,1)} async-done(((bf16[32,8,8,128]{3,2,1,0:T(8,128)(2,1)}), bf16[32,8,8,128]{3,2,1,0:T(8,128)(2,1)}, u32[]{:S(2)}, u32[]{:S(2)}) %all-to-all-start) | async-done | bytes 524320 | tf_op jit(solution)/shard_map/all_to_all | solution.py:111
  78.1 3.6 %all-to-all-start.1 = ((bf16[32,8,8,128]{3,2,1,0:T(8,128)(2,1)}), bf16[32,8,8,128]{3,2,1,0:T(8,128)(2,1)S(1)}, u32[]{:S(2)}, u32[]{:S(2)}) async-start(bf16[32,8,8,128]{3,2,1,0:T(8,128)(2,1)} %bitcast.18), calls=%async_computation.1 | async-start | bytes 1048576 | tf_op jit(solution)/shard_map/all_to_all | solution.py:112
  81.8 5.0 %fusion.2 = f32[6,8,64,128]{3,2,1,0:T(8,128)S(1)} fusion(bf16[6,8,8,64,128]{4,3,2,1,0:T(8,128)(2,1)} %param.15, f32[6,8,64,128]{3,2,1,0:T(8,128)S(1)} %copy.43), kind=kLoop, calls=%fused_computation.11 | loop fusion | flops 9043968 | bytes 9437184 | tf_op jit(solution)/shard_map/reduce_sum | solution.py:51
  87.4 12.6 %copy.44 = f32[8,6,64,128]{0,3,2,1:T(8,128)} copy(f32[8,6,64,128]{3,2,0,1:T(8,128)S(1)} %add_bitcast_fusion) | data formatting | bytes 3145728 | tf_op jit(solution)/shard_map/transpose | solution.py:95
  100.0 22.5 %gather_fusion = bf16[4096,8]{1,0:T(8,128)(2,1)} fusion(f32[8,49152]{0,1:T(8,128)} %bitcast.47, s32[4096]{0:T(1024)S(1)} %broadcast_clamp_fusion), kind=kCustom, calls=%fused_computation | custom fusion | bytes 147456 | tf_op jit(solution)/shard_map/gather | solution.py:101
  129.5 36.7 %scatter_custom_fusion = f32[8,49152]{0,1:T(8,128)} fusion(f32[8,49152]{0,1:T(8,128)} %bitcast.48, s32[4096]{0:T(1024)} %bitcast.58, bf16[4096,8]{1,0:T(8,128)(2,1)S(1)} %bitcast.53), kind=kCustom, calls=%fused_computation.24 | custom fusion | flops 65536 | bytes 1638400 | tf_op jit(solution)/shard_map/scatter-add | solution.py:126
  166.3 13.4 %copy.45 = f32[8,6,64,128]{3,0,2,1:T(8,128)S(1)} copy(f32[8,6,64,128]{0,3,2,1:T(8,128)} %bitcast.49) | data formatting | bytes 3145728 | tf_op jit(solution)/shard_map/reshape | solution.py:127
  180.1 3.1 %collective-permute-start.8 = (f32[6,8,1,128]{3,1,2,0:T(8,128)S(1)}, f32[6,8,1,128]{3,1,2,0:T(8,128)S(1)}, u32[]{:S(2)}, u32[]{:S(2)}) collective-permute-start(f32[6,8,1,128]{3,1,2,0:T(8,128)S(1)} %get-tuple-element.6), channel_id=1, source_target_pairs={{0,1},{1,2},{2,3},{3,4},{4,5},{5,6},{6,7},{8,9},{9,10},{10,11},{11... | collective-permute-start | bytes 73736 | tf_op jit(solution)/shard_map/ppermute | solution.py:18
  183.2 3.2 %collective-permute-start.9 = (f32[6,8,1,128]{3,1,2,0:T(8,128)S(1)}, f32[6,8,1,128]{3,1,2,0:T(8,128)S(1)}, u32[]{:S(2)}, u32[]{:S(2)}) collective-permute-start(f32[6,8,1,128]{3,1,2,0:T(8,128)S(1)} %get-tuple-element.7), channel_id=1, source_target_pairs={{1,0},{2,1},{3,2},{4,3},{5,4},{6,5},{7,6},{9,8},{10,9},{11,10},{12... | collective-permute-start | bytes 73736 | tf_op jit(solution)/shard_map/ppermute | solution.py:19
  186.5 6.0 %fusion.1 = f32[6,8,64,128]{3,2,1,0:T(8,128)} fusion(bf16[6,8,8,64,128]{4,3,2,1,0:T(8,128)(2,1)} %param.14, f32[6,8,64,128]{3,2,1,0:T(8,128)S(1)} %copy.46), kind=kLoop, calls=%fused_computation.10 | loop fusion | flops 9043968 | bytes 9437184 | tf_op jit(solution)/shard_map/reduce_sum | solution.py:51
  192.6 39.1 %psum.7 = f32[8,8]{1,0:T(8,128)S(1)} all-reduce(f32[8,8]{1,0:T(8,128)S(1)} %convolution_bitcast_fusion), channel_id=1, replica_groups=mesh['gx'=4,'gy'=8] {'gx','gy'}, use_global_device_ids=true, to_apply=%region_5.6 | all-reduce | flops 64 | bytes 512 | tf_op jit(solution)/shard_map/psum | solution.py:120
  234.7 2.0 copy.48
  237.4 5.3 %collective-permute-start.10 = (f32[6,8,66,1]{2,1,3,0:T(8,128)S(1)}, f32[6,8,66,1]{2,1,3,0:T(8,128)S(1)}, u32[]{:S(2)}, u32[]{:S(2)}) collective-permute-start(f32[6,8,66,1]{2,1,3,0:T(8,128)S(1)} %copy.47), channel_id=1, source_target_pairs={{0,8},{8,16},{16,24},{1,9},{9,17},{17,25},{2,10},{10,18},{18,26},{... | collective-permute-start | bytes 38024 | tf_op jit(solution)/shard_map/ppermute | solution.py:18
  245.2 15.3 %copy.54 = f32[8,6,64,128]{3,2,0,1:T(8,128)} copy(f32[8,6,64,128]{0,3,2,1:T(8,128)} %bitcast.50) | data formatting | bytes 3145728 | tf_op jit(solution)/shard_map/reshape | solution.py:127
  264.0 3.8 %select_maximum_fusion = f32[8,8,66,130]{3,1,2,0:T(8,128)S(1)} fusion(f32[6,8,66,1]{3,1,2,0:T(8,128)S(1)} %copy.50, f32[6,8,66,1]{3,1,2,0:T(8,128)} %copy.49, f32[6,8,1,128]{3,1,2,0:T(8,128)S(1)} %copy-done.27, f32[6,8,64,128]{3,1,2,0:T(8,128)S(1)} %multiply_bitcast_fusion, f32[6,8,1,128]{3,1,2,0:T(8,128)S(1)} %copy-done.25), kind=kLoop, calls=%fused_computation.15 | loop fusion | flops 6589440 | bytes 3843840 | tf_op jit(solution)/shard_map/concatenate | solution.py:20
  267.9 2.8 %fusion.8 = f32[6,8,64,128]{3,1,2,0:T(8,128)S(1)} fusion(f32[6,8,66,1]{3,1,2,0:T(8,128)S(1)} %copy-done.2, f32[6,8,1,128]{3,1,2,0:T(8,128)S(1)} %copy-done.27, f32[6,8,64,128]{3,1,2,0:T(8,128)S(1)} %multiply_bitcast_fusion, f32[6,8,1,128]{3,1,2,0:T(8,128)S(1)} %copy-done.25, f32[6,8,66,1]{3,1,2,0:T(8,128)S(1)} %copy.50, ...), kind=kLoop, calls=%fused_computation.32 | loop fusion | flops 7471104 | bytes 7545600 | tf_op jit(solution)/shard_map/add | solution.py:46
  (132 shorter events, 35.5 us)
Async XLA Ops:
  0.6 57.7 %all-to-all-start.2 = ((bf16[32,8,128]{2,1,0:T(8,128)(2,1)}), bf16[32,8,128]{2,1,0:T(8,128)(2,1)S(1)}, u32[]{:S(2)}, u32[]{:S(2)}) async-start(bf16[32,8,128]{2,1,0:T(8,128)(2,1)} %bitcast.56), calls=%async_computation.2 | async-start | bytes 131072 | tf_op jit(solution)/shard_map/all_to_all | solution.py:113
  7.8 20.4 %collective-permute-start = (f32[6,1,128]{2,1,0:T(1,128)S(1)}, f32[6,1,128]{2,1,0:T(1,128)S(1)}, u32[]{:S(2)}, u32[]{:S(2)}) collective-permute-start(f32[6,1,128]{2,1,0:T(1,128)S(1)} %get-tuple-element.20), channel_id=1, source_target_pairs={{0,1},{1,2},{2,3},{3,4},{4,5},{5,6},{6,7},{8,9},{9,10},{10,11},{11... | collective-permute-start | bytes 9224 | tf_op jit(solution)/shard_map/ppermute | solution.py:18
  10.9 17.3 %collective-permute-start.1 = (f32[6,1,128]{2,1,0:T(1,128)S(1)}, f32[6,1,128]{2,1,0:T(1,128)S(1)}, u32[]{:S(2)}, u32[]{:S(2)}) collective-permute-start(f32[6,1,128]{2,1,0:T(1,128)S(1)} %get-tuple-element.21), channel_id=1, source_target_pairs={{1,0},{2,1},{3,2},{4,3},{5,4},{6,5},{7,6},{9,8},{10,9},{11,10},{12... | collective-permute-start | bytes 9224 | tf_op jit(solution)/shard_map/ppermute | solution.py:19
  14.7 9.1 %copy-start = (bf16[6,8,8,64,128]{4,3,2,1,0:T(8,128)(2,1)S(1)}, bf16[6,8,8,64,128]{4,3,2,1,0:T(8,128)(2,1)}, u32[]{:S(2)}) copy-start(bf16[6,8,8,64,128]{4,3,2,1,0:T(8,128)(2,1)} %param.14) | copy-start | bytes 18874372
  17.2 21.5 %collective-permute-start.4 = (f32[6,8,1,128]{3,1,2,0:T(8,128)S(1)}, f32[6,8,1,128]{3,1,2,0:T(8,128)S(1)}, u32[]{:S(2)}, u32[]{:S(2)}) collective-permute-start(f32[6,8,1,128]{3,1,2,0:T(8,128)S(1)} %get-tuple-element.8), channel_id=1, source_target_pairs={{0,1},{1,2},{2,3},{3,4},{4,5},{5,6},{6,7},{8,9},{9,10},{10,11},{11... | collective-permute-start | bytes 73736 | tf_op jit(solution)/shard_map/ppermute | solution.py:18
  19.4 4.3 %copy-start.34 = (s32[1,1,32]{2,1,0:T(1,128)S(1)}, s32[1,1,32]{2,1,0:T(1,128)}, u32[]{:S(2)}) copy-start(s32[1,1,32]{2,1,0:T(1,128)} %param.18) | copy-start | bytes 388
  19.4 4.3 %copy-start.32 = (s32[1,1,4096]{2,1,0:T(1,128)S(1)}, s32[1,1,4096]{2,1,0:T(1,128)}, u32[]{:S(2)}) copy-start(s32[1,1,4096]{2,1,0:T(1,128)} %param.16) | copy-start | bytes 49156
  19.5 19.2 %collective-permute-start.5 = (f32[6,8,1,128]{3,1,2,0:T(8,128)S(1)}, f32[6,8,1,128]{3,1,2,0:T(8,128)S(1)}, u32[]{:S(2)}, u32[]{:S(2)}) collective-permute-start(f32[6,8,1,128]{3,1,2,0:T(8,128)S(1)} %get-tuple-element.9), channel_id=1, source_target_pairs={{1,0},{2,1},{3,2},{4,3},{5,4},{6,5},{7,6},{9,8},{10,9},{11,10},{12... | collective-permute-start | bytes 73736 | tf_op jit(solution)/shard_map/ppermute | solution.py:19
  23.8 4.3 %copy-start.7 = (f32[6,64,128]{2,1,0:T(8,128)S(1)}, f32[6,64,128]{2,1,0:T(8,128)}, u32[]{:S(2)}) copy-start(f32[6,64,128]{2,1,0:T(8,128)} %param.12) | copy-start | bytes 589828
  23.8 11.5 %copy-start.28 = (s32[64,128]{1,0:T(8,128)S(1)}, s32[64,128]{1,0:T(8,128)}, u32[]{:S(2)}) copy-start(s32[64,128]{1,0:T(8,128)} %param.13) | copy-start | bytes 98308
  28.1 10.6 %copy-start.30 = (f32[6,1,128]{2,1,0:T(1,128)}, f32[6,1,128]{2,1,0:T(1,128)S(1)}, u32[]{:S(2)}) copy-start(f32[6,1,128]{2,1,0:T(1,128)S(1)} %collective-permute-done) | copy-start | bytes 9220
  28.2 10.5 %copy-start.31 = (f32[6,1,128]{2,1,0:T(1,128)}, f32[6,1,128]{2,1,0:T(1,128)S(1)}, u32[]{:S(2)}) copy-start(f32[6,1,128]{2,1,0:T(1,128)S(1)} %collective-permute-done.1) | copy-start | bytes 9220
  28.3 8.1 %collective-permute-start.3 = (f32[6,66,1]{2,1,0:T(8,128)S(1)}, f32[6,66,1]{2,1,0:T(8,128)S(1)}, u32[]{:S(2)}, u32[]{:S(2)}) collective-permute-start(f32[6,66,1]{2,1,0:T(8,128)S(1)} %get-tuple-element.12), channel_id=1, source_target_pairs={{8,0},{16,8},{24,16},{9,1},{17,9},{25,17},{10,2},{18,10},{26,18},{... | collective-permute-start | bytes 4760 | tf_op jit(solution)/shard_map/ppermute | solution.py:19
  31.7 5.9 %collective-permute-start.2 = (f32[6,66,1]{2,1,0:T(8,128)S(1)}, f32[6,66,1]{2,1,0:T(8,128)S(1)}, u32[]{:S(2)}, u32[]{:S(2)}) collective-permute-start(f32[6,66,1]{2,1,0:T(8,128)S(1)} %get-tuple-element.13), channel_id=1, source_target_pairs={{0,8},{8,16},{16,24},{1,9},{9,17},{17,25},{2,10},{10,18},{18,26},{... | collective-permute-start | bytes 4760 | tf_op jit(solution)/shard_map/ppermute | solution.py:18
  44.5 11.3 %collective-permute-start.6 = (f32[6,8,66,1]{2,1,3,0:T(8,128)}, f32[6,8,66,1]{2,1,3,0:T(8,128)}, u32[]{:S(2)}, u32[]{:S(2)}) collective-permute-start(f32[6,8,66,1]{2,1,3,0:T(8,128)} %copy.37), channel_id=1, source_target_pairs={{0,8},{8,16},{16,24},{1,9},{9,17},{17,25},{2,10},{10,18},{18,26},{... | collective-permute-start | bytes 38024 | tf_op jit(solution)/shard_map/ppermute | solution.py:18
  48.8 5.5 %collective-permute-start.7 = (f32[6,8,66,1]{2,1,3,0:T(8,128)}, f32[6,8,66,1]{2,1,3,0:T(8,128)}, u32[]{:S(2)}, u32[]{:S(2)}) collective-permute-start(f32[6,8,66,1]{2,1,3,0:T(8,128)} %copy.38), channel_id=1, source_target_pairs={{8,0},{16,8},{24,16},{9,1},{17,9},{25,17},{10,2},{18,10},{26,18},{... | collective-permute-start | bytes 38024 | tf_op jit(solution)/shard_map/ppermute | solution.py:19
  58.3 19.8 %all-to-all-start = ((bf16[32,8,8,128]{3,2,1,0:T(8,128)(2,1)}), bf16[32,8,8,128]{3,2,1,0:T(8,128)(2,1)}, u32[]{:S(2)}, u32[]{:S(2)}) async-start(bf16[32,8,8,128]{3,2,1,0:T(8,128)(2,1)} %bitcast.55), calls=%async_computation | async-start | bytes 1048576 | tf_op jit(solution)/shard_map/all_to_all | solution.py:111
  78.1 49.6 %all-to-all-start.1 = ((bf16[32,8,8,128]{3,2,1,0:T(8,128)(2,1)}), bf16[32,8,8,128]{3,2,1,0:T(8,128)(2,1)S(1)}, u32[]{:S(2)}, u32[]{:S(2)}) async-start(bf16[32,8,8,128]{3,2,1,0:T(8,128)(2,1)} %bitcast.18), calls=%async_computation.1 | async-start | bytes 1048576 | tf_op jit(solution)/shard_map/all_to_all | solution.py:112
  81.8 5.0 %copy-start.3 = (f32[6,8,64,128]{3,2,1,0:T(8,128)S(1)}, f32[6,8,64,128]{3,2,1,0:T(8,128)}, u32[]{:S(2)}) copy-start(f32[6,8,64,128]{3,2,1,0:T(8,128)} %fusion) | copy-start | bytes 4718596
  81.8 5.0 %copy-start.6 = (f32[6,8,64,128]{3,2,1,0:T(8,128)S(1)}, f32[6,8,64,128]{3,2,1,0:T(8,128)}, u32[]{:S(2)}) copy-start(f32[6,8,64,128]{3,2,1,0:T(8,128)} %param.11) | copy-start | bytes 4718596
  87.4 35.1 %copy-start.33 = (pred[32]{0:T(512)(128)(4,1)S(1)}, pred[32]{0:T(512)(128)(4,1)}, u32[]{:S(2)}) copy-start(pred[32]{0:T(512)(128)(4,1)} %iota_compare_fusion.4) | copy-start | bytes 100
  166.3 13.4 %copy-start.23 = (f32[64,128]{1,0:T(8,128)S(1)}, f32[64,128]{1,0:T(8,128)}, u32[]{:S(2)}) copy-start(f32[64,128]{1,0:T(8,128)} %copy-done.22) | copy-start | bytes 98308
  180.1 51.6 %collective-permute-start.8 = (f32[6,8,1,128]{3,1,2,0:T(8,128)S(1)}, f32[6,8,1,128]{3,1,2,0:T(8,128)S(1)}, u32[]{:S(2)}, u32[]{:S(2)}) collective-permute-start(f32[6,8,1,128]{3,1,2,0:T(8,128)S(1)} %get-tuple-element.6), channel_id=1, source_target_pairs={{0,1},{1,2},{2,3},{3,4},{4,5},{5,6},{6,7},{8,9},{9,10},{10,11},{11... | collective-permute-start | bytes 73736 | tf_op jit(solution)/shard_map/ppermute | solution.py:18
  183.2 9.3 %copy-start.21 = (bf16[32,8,128]{2,1,0:T(8,128)(2,1)S(1)}, bf16[32,8,128]{2,1,0:T(8,128)(2,1)}, u32[]{:S(2)}) copy-start(bf16[32,8,128]{2,1,0:T(8,128)(2,1)} %gather_fusion.3) | copy-start | bytes 196612
  183.2 48.5 %collective-permute-start.9 = (f32[6,8,1,128]{3,1,2,0:T(8,128)S(1)}, f32[6,8,1,128]{3,1,2,0:T(8,128)S(1)}, u32[]{:S(2)}, u32[]{:S(2)}) collective-permute-start(f32[6,8,1,128]{3,1,2,0:T(8,128)S(1)} %get-tuple-element.7), channel_id=1, source_target_pairs={{1,0},{2,1},{3,2},{4,3},{5,4},{6,5},{7,6},{9,8},{10,9},{11,10},{12... | collective-permute-start | bytes 73736 | tf_op jit(solution)/shard_map/ppermute | solution.py:19
  237.4 24.6 %collective-permute-start.10 = (f32[6,8,66,1]{2,1,3,0:T(8,128)S(1)}, f32[6,8,66,1]{2,1,3,0:T(8,128)S(1)}, u32[]{:S(2)}, u32[]{:S(2)}) collective-permute-start(f32[6,8,66,1]{2,1,3,0:T(8,128)S(1)} %copy.47), channel_id=1, source_target_pairs={{0,8},{8,16},{16,24},{1,9},{9,17},{17,25},{2,10},{10,18},{18,26},{... | collective-permute-start | bytes 38024 | tf_op jit(solution)/shard_map/ppermute | solution.py:18
  242.7 17.9 %collective-permute-start.11 = (f32[6,8,66,1]{2,1,3,0:T(8,128)S(1)}, f32[6,8,66,1]{2,1,3,0:T(8,128)}, u32[]{:S(2)}, u32[]{:S(2)}) collective-permute-start(f32[6,8,66,1]{2,1,3,0:T(8,128)S(1)} %copy.48), channel_id=1, source_target_pairs={{8,0},{16,8},{24,16},{9,1},{17,9},{25,17},{10,2},{18,10},{26,18},{... | collective-permute-start | bytes 38024 | tf_op jit(solution)/shard_map/ppermute | solution.py:19
  263.9 3.9 %copy-start.12 = (f32[6,64,128]{2,1,0:T(8,128)S(1)}, f32[6,64,128]{2,1,0:T(8,128)}, u32[]{:S(2)}) copy-start(f32[6,64,128]{2,1,0:T(8,128)} %get-tuple-element.16) | copy-start | bytes 589828
  263.9 3.9 %copy-start.14 = (f32[6,64,128]{2,1,0:T(8,128)S(1)}, f32[6,64,128]{2,1,0:T(8,128)}, u32[]{:S(2)}) copy-start(f32[6,64,128]{2,1,0:T(8,128)} %get-tuple-element.17) | copy-start | bytes 589828
  263.9 3.9 %copy-start.16 = (f32[6,64,128]{2,1,0:T(8,128)S(1)}, f32[6,64,128]{2,1,0:T(8,128)}, u32[]{:S(2)}) copy-start(f32[6,64,128]{2,1,0:T(8,128)} %get-tuple-element.18) | copy-start | bytes 589828
  263.9 3.9 %copy-start.18 = (f32[6,64,128]{2,1,0:T(8,128)S(1)}, f32[6,64,128]{2,1,0:T(8,128)}, u32[]{:S(2)}) copy-start(f32[6,64,128]{2,1,0:T(8,128)} %get-tuple-element.19) | copy-start | bytes 589828
  263.9 7.1 %slice-start = ((s8[6291456]{0:T(1024)(128)(4,1)}), s8[4194304]{0:T(1024)(128)(4,1)S(1)}, s32[]{:S(2)}) async-start(s8[6291456]{0:T(1024)(128)(4,1)} %bitcast.51), calls=%async_computation.3 | async-start | bytes 8388608
  (20 other events, 59.1 us)
where the time goes:
time: 277 us; the launch traced here: 275 us
  local copies, waits for them, and re-layouts  89.6 us (32%)
  other arithmetic  79.4 us (29%)
  starting transfers between devices  53.1 us (19%)
  blocking collectives  39.1 us (14%)
  waiting for transfers between devices  11.2 us (4%)
    psum x1, blocking collectives, shards(): interaction_grad = -grad_scale * lax.psum(partial_sum, ('gx', 'gy'))  39.1 us
    scatter-add x1, other arithmetic, shards(): flat_cells = flat_cells.at[:, slot_cells].add(added)  36.7 us
    reshape x2, local copies, waits for them, and re-layouts, shards(): flat_cells.reshape(components, layers, rows_y, cols_x).transpose(1, 0, 2, 3)  28.7 us
    gather x1, local copies, waits for them, and re-layouts, shards(): flat_cells[:, slot_cells].reshape(components, block_slots, block_size)  22.5 us
    ppermute x6, starting transfers between devices, with_halo(): before = lax.ppermute(last, axis, up)  21 us
    ppermute x6, starting transfers between devices, with_halo(): after = lax.ppermute(first, axis, down)  17.5 us
    reduce_sum x4, other arithmetic, blocks_transposed(): return jnp.sum(blocks * source_field[:, :, None], axis=1)  16 us
    transpose x1, local copies, waits for them, and re-layouts, shards(): first_apply.transpose(1, 0, 2, 3)  12.6 us
  transfers between devices with their start and end apart: 15, of which 4 were waited for; matrix products, arithmetic and copies ran while one was open for 36% of the time, Pallas kernels for 0%

commit v1 on v0

v1 whole, which is shorter than its diff:
```python
import functools
import math

import jax
import jax.numpy as jnp
from jax import lax
from jax.experimental import pallas as pl
from jax.experimental.pallas import tpu as pltpu
from jax.sharding import PartitionSpec as P

F32 = jnp.float32
BF16 = jnp.bfloat16
AXES = ("gx", "gy")
MIB = 1024 * 1024
CHUNK = 512


def params(mib):
    return pltpu.CompilerParams(vmem_limit_bytes=mib * MIB)


def cost(flops, moved):
    return pl.CostEstimate(flops=int(flops), bytes_accessed=int(moved), transcendentals=0)


def product_kernel(inverse_ref, coupling_ref, out_ref):
    blocks, comps = inverse_ref.shape[:2]

    def one(b, carry):
        inverse = inverse_ref[b].astype(F32)
        coupling = coupling_ref[b].astype(F32)
        for r in range(comps):
            row = inverse[r, 0:1] * coupling[0]
            for m in range(1, comps):
                row += inverse[r, m : m + 1] * coupling[m]
            out_ref[b, r] = row.astype(BF16)
        return carry

    lax.fori_loop(0, blocks, one, 0)


def flash_product(inverse, coupling):
    return pl.pallas_call(
        product_kernel,
        out_shape=jax.ShapeDtypeStruct(inverse.shape, BF16),
        compiler_params=params(24),
        cost_estimate=cost(16 * inverse.size, 6 * inverse.size),
    )(inverse, coupling)


def write_edges(field, clear, perm_ref, low_y, high_y, low_x, high_x):
    layers, rows, cols = perm_ref.shape
    comps = low_y.shape[0] // layers - 1
    lane = lax.broadcasted_iota(jnp.int32, (rows, cols), 1)
    left = jnp.zeros((rows, cols), F32)
    right = jnp.zeros((rows, cols), F32)
    for k in range(layers):
        for c in range(comps + 1):
            if c < comps:
                value, at = field(k, c) * clear, k * comps + c
            else:
                value, at = perm_ref[k], layers * comps + k
            low_y[at : at + 1, :] = value[0:1]
            high_y[at : at + 1, :] = value[rows - 1 : rows]
            left = jnp.where(lane == at, value[:, 0:1], left)
            right = jnp.where(lane == at, value[:, cols - 1 : cols], right)
    low_x[...] = left
    high_x[...] = right


def edges_kernel(field_ref, mask_ref, perm_ref, low_y, high_y, low_x, high_x):
    clear = 1.0 - mask_ref[...].astype(F32)
    write_edges(lambda k, c: field_ref[k, c], clear, perm_ref, low_y, high_y, low_x, high_x)


def edge_shapes(layers, comps, rows, cols):
    along_y = jax.ShapeDtypeStruct((layers * (comps + 1), cols), F32)
    along_x = jax.ShapeDtypeStruct((rows, cols), F32)
    return [along_y, along_y, along_x, along_x]


def edges(field, mask, perm):
    return pl.pallas_call(
        edges_kernel,
        out_shape=edge_shapes(*field.shape),
        compiler_params=params(24),
        cost_estimate=cost(4 * field.size, 4 * field.size),
    )(field, mask, perm)


def exchange(sides):
    low_y, high_y, low_x, high_x = sides

    def both(low, high, axis):
        count = lax.axis_size(axis)
        up = [(i, i + 1) for i in range(count - 1)]
        down = [(j, i) for i, j in up]
        return lax.ppermute(high, axis, up), lax.ppermute(low, axis, down)

    return (*both(low_y, high_y, "gy"), *both(low_x, high_x, "gx"))


TILE = 16


def diag_kernel(field_ref, mask_ref, block_ref, out_ref):
    comps, rows = field_ref.shape[1:3]
    for y in range(0, rows, TILE):
        here = slice(y, y + TILE)
        well = mask_ref[here].astype(F32)
        values = [field_ref[0, c, here] for c in range(comps)]
        total = [well * value for value in values]
        for r in range(comps):
            source = values[r] * (1.0 - well)
            for c in range(comps):
                total[c] += block_ref[0, r, c, here].astype(F32) * source
        for c in range(comps):
            out_ref[0, c, here] = total[c]


def diag_part(field, mask, block):
    layers, comps, rows, cols = field.shape
    layer = pl.BlockSpec((1, comps, rows, cols), lambda k: (k, 0, 0, 0))
    return pl.pallas_call(
        diag_kernel,
        grid=(layers,),
        in_specs=[
            layer,
            pl.BlockSpec((rows, cols), lambda k: (0, 0)),
            pl.BlockSpec((1, comps, comps, rows, cols), lambda k: (k, 0, 0, 0, 0)),
        ],
        out_specs=layer,
        out_shape=jax.ShapeDtypeStruct(field.shape, F32),
        compiler_params=params(24),
        cost_estimate=cost(2 * block.size, 2 * block.size + 8 * field.size),
    )(field, mask, block)


def flux_kernel(want_rounded, before_ref, field_ref, mask_ref, perm_ref, low_y, high_y, low_x, high_x, block_ref, *rest):
    if want_rounded:
        out_ref, rounded_ref, padded, padded_perm = rest
    else:
        out_ref, padded, padded_perm = rest
    layers, comps, rows, cols = field_ref.shape
    top = 8
    k = pl.program_id(0)
    above = jnp.minimum(k + 1, layers - 1)
    below = jnp.maximum(k - 1, 0)
    clear = 1.0 - mask_ref[...].astype(F32)
    for c in range(comps):
        padded[c, top : top + rows] = field_ref[k, c] * clear
        padded[c, top - 1 : top] = low_y[pl.ds(k * comps + c, 1)]
        padded[c, top + rows : top + rows + 1] = high_y[pl.ds(k * comps + c, 1)]
    padded_perm[top : top + rows] = perm_ref[k]
    padded_perm[top - 1 : top] = low_y[pl.ds(layers * comps + k, 1)]
    padded_perm[top + rows : top + rows + 1] = high_y[pl.ds(layers * comps + k, 1)]
    lane = lax.broadcasted_iota(jnp.int32, (TILE, cols), 1)
    is_first, is_last = lane == 0, lane == cols - 1
    turn_field = lax.rem(cols - k * comps, cols)
    turn_perm = lax.rem(cols - (layers * comps + k), cols)

    def weight(centre, beside):
        return 2.0 * centre * beside / (centre + beside)

    for y in range(0, rows, TILE):
        here = slice(y, y + TILE)
        at = top + y
        free = 1.0 - mask_ref[here].astype(F32)
        low_field, high_field = (pltpu.roll(ref[here], turn_field, 1) for ref in (low_x, high_x))
        low_perm, high_perm = (pltpu.roll(ref[here], turn_perm, 1) for ref in (low_x, high_x))

        def beside_x(value, low, high):
            return (
                jnp.where(is_first, low, pltpu.roll(value, 1, 1)),
                jnp.where(is_last, high, pltpu.roll(value, cols - 1, 1)),
            )

        centre = perm_ref[k, here]
        perm_left, perm_right = beside_x(centre, low_perm[:, 0:1], high_perm[:, 0:1])
        weights = [
            jnp.where(k < layers - 1, weight(centre, perm_ref[above, here]), 0.0) * free,
            jnp.where(k > 0, weight(centre, perm_ref[below, here]), 0.0) * free,
            weight(centre, padded_perm[at + 1 : at + 1 + TILE]),
            weight(centre, padded_perm[at - 1 : at - 1 + TILE]),
            weight(centre, perm_right),
            weight(centre, perm_left),
        ]
        total = [None] * comps
        for r in range(comps):
            own = padded[r, at : at + TILE]
            left, right = beside_x(own, low_field[:, r : r + 1], high_field[:, r : r + 1])
            summed = (
                weights[0] * field_ref[above, r, here]
                + weights[1] * field_ref[below, r, here]
                + weights[2] * padded[r, at + 1 : at + 1 + TILE]
                + weights[3] * padded[r, at - 1 : at - 1 + TILE]
                + weights[4] * right
                + weights[5] * left
            )
            for c in range(comps):
                term = block_ref[0, r, c, here].astype(F32) * summed
                total[c] = term if r == 0 else total[c] + term
        for c in range(comps):
            value = before_ref[0, c, here] - total[c]
            out_ref[0, c, here] = value
            if want_rounded:
                rounded_ref[c * rows + y : c * rows + y + TILE, :] = value.astype(BF16)


def flux_part(before, field, mask, perm, halos, block, want_rounded):
    layers, comps, rows, cols = field.shape
    layer = pl.BlockSpec((1, comps, rows, cols), lambda k: (k, 0, 0, 0))

    def whole(array):
        return pl.BlockSpec(array.shape, lambda k: (0,) * array.ndim)

    out_specs = [layer]
    out_shape = [jax.ShapeDtypeStruct(field.shape, F32)]
    if want_rounded:
        out_specs.append(pl.BlockSpec((comps * rows, cols), lambda k: (0, k)))
        out_shape.append(jax.ShapeDtypeStruct((comps * rows, layers * cols), BF16))
    return pl.pallas_call(
        functools.partial(flux_kernel, want_rounded),
        grid=(layers,),
        in_specs=[
            layer,
            whole(field),
            whole(mask),
            whole(perm),
            *(whole(halo) for halo in halos),
            pl.BlockSpec((1, comps, comps, rows, cols), lambda k: (k, 0, 0, 0, 0)),
        ],
        out_specs=out_specs,
        out_shape=out_shape,
        scratch_shapes=[
            pltpu.VMEM((comps, rows + 16, cols), F32),
            pltpu.VMEM((rows + 16, cols), F32),
        ],
        compiler_params=params(24),
        cost_estimate=cost(4 * block.size, 2 * block.size + 12 * field.size),
    )(before, field, mask, perm, *halos, block)


def split_cells(cells, rows, cols):
    layer = cells // (rows * cols)
    y = (cells // cols) % rows
    return layer * cols + cells % cols, y


def one_hot(column, count, slots):
    number = lax.broadcasted_iota(jnp.int32, (count, slots), 0)
    return jnp.where(number == column, 1.0, 0.0).astype(BF16)


def gather_kernel(rows, cols, helper_ref, count_ref, cells_ref, rounded_ref, picked_ref, sent_ref):
    chunks, _, slots = cells_ref.shape
    width = picked_ref.shape[-1]
    comps = picked_ref.shape[1]
    per_chunk = slots // width
    row_number = lax.broadcasted_iota(jnp.int32, (rows, slots), 0)

    def one(i, carry):
        column, y = split_cells(cells_ref[i], rows, cols)
        chosen = one_hot(column, rounded_ref.shape[1], slots)
        found = jnp.dot(rounded_ref[...], chosen, preferred_element_type=F32)
        at_row = row_number == y
        values = [
            jnp.sum(jnp.where(at_row, found[c * rows : (c + 1) * rows], 0.0), axis=0, keepdims=True)
            for c in range(comps)
        ]
        values = jnp.concatenate(values, axis=0)
        for j in range(per_chunk):
            b = i * per_chunk + j
            live = jnp.where(b < count_ref[0, 0], 1.0, 0.0)
            value = (values[:, j * width : (j + 1) * width] * live).astype(BF16)
            picked_ref[b] = value
            sent_ref[helper_ref[0, 0, b]] = value
        return carry

    lax.fori_loop(0, chunks, one, 0)


def gather(rounded, cells, helper, count, comps, rows, cols, width):
    blocks = helper.shape[-1]
    shape = jax.ShapeDtypeStruct((blocks, comps, width), BF16)
    smem = pl.BlockSpec(memory_space=pltpu.SMEM)
    vmem = pl.BlockSpec(memory_space=pltpu.VMEM)
    return pl.pallas_call(
        functools.partial(gather_kernel, rows, cols),
        in_specs=[smem, smem, vmem, vmem],
        out_specs=[vmem, vmem],
        out_shape=[shape, shape],
        compiler_params=params(32),
        cost_estimate=cost(2 * rounded.size * cells.size, 2 * rounded.size),
    )(helper, count, cells, rounded)


def scatter_kernel(
    helper_ref, cells_ref, picked_ref, home_ref, first_ref, mask_ref, perm_ref, second_ref, low_y, high_y, low_x, high_x, added
):
    layers, comps, rows, cols = first_ref.shape
    chunks, _, slots = cells_ref.shape
    width = picked_ref.shape[-1]
    per_chunk = slots // width
    row_number = lax.broadcasted_iota(jnp.int32, (rows, slots), 0)
    added[...] = jnp.zeros_like(added)

    def one(i, carry):
        column, y = split_cells(cells_ref[i], rows, cols)
        chosen = one_hot(column, added.shape[1], slots)
        parts = []
        for j in range(per_chunk):
            b = i * per_chunk + j
            home = home_ref[helper_ref[0, 0, b]].astype(F32)
            value = picked_ref[b].astype(F32)
            part = home[0] * value[0:1]
            for r in range(1, comps):
                part += home[r] * value[r : r + 1]
            parts.append((-part).astype(BF16).astype(F32))
        correction = jnp.concatenate(parts, axis=1)
        at_row = row_number == y
        spread = jnp.concatenate(
            [jnp.where(at_row, correction[c : c + 1], 0.0).astype(BF16) for c in range(comps)], axis=0
        )
        added[...] += lax.dot_general(spread, chosen, (((1,), (1,)), ((), ())), preferred_element_type=F32)
        return carry

    lax.fori_loop(0, chunks, one, 0)
    for k in range(layers):
        for c in range(comps):
            second_ref[k, c] = first_ref[k, c] + added[c * rows : (c + 1) * rows, k * cols : (k + 1) * cols]
    clear = 1.0 - mask_ref[...].astype(F32)
    write_edges(lambda k, c: second_ref[k, c], clear, perm_ref, low_y, high_y, low_x, high_x)


def scatter(first, picked, home, helper, cells, mask, perm):
    layers, comps, rows, cols = first.shape
    smem = pl.BlockSpec(memory_space=pltpu.SMEM)
    vmem = pl.BlockSpec(memory_space=pltpu.VMEM)
    return pl.pallas_call(
        scatter_kernel,
        in_specs=[smem] + [vmem] * 6,
        out_specs=[vmem] * 5,
        out_shape=[jax.ShapeDtypeStruct(first.shape, F32), *edge_shapes(*first.shape)],
        scratch_shapes=[pltpu.VMEM((comps * rows, layers * cols), F32)],
        compiler_params=params(40),
        cost_estimate=cost(2 * first.size * cells.size, 8 * first.size),
    )(helper, cells, picked, home, first, mask, perm)


def grad_kernel(inverse_ref, state_ref, picked_ref, out_ref):
    blocks, comps = inverse_ref.shape[:2]
    width = inverse_ref.shape[-1]

    def one(b, totals):
        inverse = inverse_ref[b].astype(F32)
        value = picked_ref[b].astype(F32)
        state = state_ref[b].astype(F32)
        part = inverse[0] * value[0:1]
        for r in range(1, comps):
            part += inverse[r] * value[r : r + 1]
        part *= state
        return tuple(totals[j] + part * state[j : j + 1] for j in range(comps))

    totals = lax.fori_loop(0, blocks, one, (jnp.zeros((comps, width), F32),) * comps)
    lane = lax.broadcasted_iota(jnp.int32, (comps, width), 1)
    result = jnp.zeros((comps, width), F32)
    for j in range(comps):
        result = jnp.where(lane == j, jnp.sum(totals[j], axis=1, keepdims=True), result)
    out_ref[...] = result


def grad_part(inverse, state, picked):
    return pl.pallas_call(
        grad_kernel,
        out_shape=jax.ShapeDtypeStruct((inverse.shape[1], inverse.shape[-1]), F32),
        compiler_params=params(24),
        cost_estimate=cost(4 * inverse.size, 2 * inverse.size),
    )(inverse, state, picked)


def shards(
    cotangent,
    permeability,
    well_mask,
    diag_block,
    flux_block,
    cell_list,
    block_count,
    helper_of,
    flash_inverse,
    flash_coupling,
    phase_state,
):
    layers, comps, rows, cols = cotangent.shape
    blocks, width = helper_of.shape[-1], flash_inverse.shape[-1]
    inverse = flash_inverse.reshape(blocks, comps, comps, width)
    coupling = flash_coupling.reshape(blocks, comps, comps, width)
    state = phase_state.reshape(blocks, comps, width)
    cells = cell_list.reshape(-1, 1, min(CHUNK, cell_list.shape[-1]))

    def to_partners(array):
        return lax.all_to_all(array, AXES, split_axis=0, concat_axis=0, tiled=True)

    home = to_partners(flash_product(inverse, coupling))
    halos = exchange(edges(cotangent, well_mask, permeability))
    before = diag_part(cotangent, well_mask, diag_block)
    first, rounded = flux_part(before, cotangent, well_mask, permeability, halos, flux_block, True)
    picked, sent = gather(rounded, cells, helper_of, block_count, comps, rows, cols, width)
    second, *sides = scatter(first, picked, home, helper_of, cells, well_mask, permeability)
    halos = exchange(sides)
    before = diag_part(second, well_mask, diag_block)
    (adjoint,) = flux_part(before, second, well_mask, permeability, halos, flux_block, False)

    partial_sum = grad_part(inverse, state, to_partners(sent))
    devices = lax.axis_size("gx") * lax.axis_size("gy")
    grad_scale = 1.0 / math.sqrt(width * devices * devices)
    gathered = lax.all_gather(partial_sum, AXES)
    interaction_grad = -grad_scale * jnp.sum(gathered, axis=0)[:, :comps]
    return (adjoint, interaction_grad)


def solution(mesh):
    return jax.shard_map(
        shards,
        mesh=mesh,
        in_specs=(
            P(None, None, "gy", "gx"),
            P(None, "gy", "gx"),
            P("gy", "gx"),
            P(None, None, None, "gy", "gx"),
            P(None, None, None, "gy", "gx"),
            P("gy", "gx", None),
            P("gy", "gx"),
            P("gy", "gx", None),
            P("gy", "gx", None, None, None, None),
            P("gy", "gx", None, None, None, None),
            P("gy", "gx", None, None, None),
        ),
        out_specs=(P(None, None, "gy", "gx"), P()),
        check_vma=False,
    )
```

time: 277 us -> 153 us (0.55)
  local copies, waits for them, and re-layouts: 89.6 us -> 10.4 us
  other arithmetic: 79.4 us -> 0.63 us
  Pallas kernels: 0 us -> 31.8 us
  blocking collectives: 39.1 us -> 60.9 us
  starting transfers between devices: 53.1 us -> 41.6 us
  waiting for transfers between devices: 11.2 us -> 5.16 us
    all_gather x0 -> x1, blocking collectives: none -> 60.9 us  [shards(): gathered = lax.all_gather(partial_sum, AXES)]
    psum x1 -> x0, blocking collectives: 39.1 us -> none  [shards(): interaction_grad = -grad_scale * lax.psum(partial_sum, ('gx', 'gy'))]
    scatter-add x1 -> x0, other arithmetic: 36.7 us -> none  [shards(): flat_cells = flat_cells.at[:, slot_cells].add(added)]
    pallas_call x0 -> x9, Pallas kernels: none -> 31.8 us  [the longest x2 12.2 us: flux_part(): pl.pallas_call(functools.partial(flux_kernel, want_rounded), grid=(layers...]
    reshape x2 -> x0, local copies, waits for them, and re-layouts: 28.7 us -> none  [shards(): flat_cells.reshape(components, layers, rows_y, cols_x).transpose(1, 0, 2, 3)]
    gather x4 -> x0, local copies, waits for them, and re-layouts: 26.4 us -> none  [the longest x1 22.5 us: shards(): flat_cells[:, slot_cells].reshape(components, block_slots, block_size)]
    reduce_sum x4 -> x1, other arithmetic: 16 us -> 0.03 us  [shards(): interaction_grad = -grad_scale * jnp.sum(gathered, axis=0)[:, :comps]]
    transpose x1 -> x0, local copies, waits for them, and re-layouts: 12.6 us -> none  [shards(): first_apply.transpose(1, 0, 2, 3)]
  transfers between devices with their start and end apart: 15 -> 10, of which waited for: 4 -> 2; matrix products, arithmetic and copies ran while one was open for 36% -> 0% of each run, Pallas kernels for 0% -> 4%
where the time goes in v1:
time: 153 us; the launch traced here: 152 us
  blocking collectives  60.9 us (40%)
  starting transfers between devices  41.6 us (27%)
  Pallas kernels  31.8 us (21%)
  local copies, waits for them, and re-layouts  10.4 us (7%)
  waiting for transfers between devices  5.16 us (3%)
  between operations  1.6 us (1%)
    all_gather x1, blocking collectives, shards(): gathered = lax.all_gather(partial_sum, AXES)  60.9 us
    ppermute x8, starting transfers between devices, both(): return (lax.ppermute(high, axis, up), lax.ppermute(low, axis, down))  31.8 us
    pallas_call x2, Pallas kernels, flux_part(): pl.pallas_call(functools.partial(flux_kernel, want_rounded), grid=(layers...  12.2 us
    unnamed x40, local copies, waits for them, and re-layouts  10.4 us
    all_to_all x2, starting transfers between devices, to_partners(): return lax.all_to_all(array, AXES, split_axis=0, concat_axis=0, tiled=True)  9.84 us
    pallas_call x1, Pallas kernels, scatter(): pl.pallas_call(scatter_kernel, in_specs=[smem] + [vmem] * 6, out_specs=[v...  6.89 us
    pallas_call x1, Pallas kernels, gather(): pl.pallas_call(functools.partial(gather_kernel, rows, cols), in_specs=[sm...  5.98 us
    all_to_all x2, waiting for transfers between devices, to_partners(): return lax.all_to_all(array, AXES, split_axis=0, concat_axis=0, tiled=True)  3.94 us
  transfers between devices with their start and end apart: 10, of which 2 were waited for; matrix products, arithmetic and copies ran while one was open for 0% of the time, Pallas kernels for 4%

profile of v1, /device:TPU:9, one launch (start us, length us, event | category | flops | bytes accessed | tf_op | source)
XLA Modules:
  0.0 152.1 jit_solution(7815825723682888279)
XLA Ops:
  0.6 1.4 copy-done.2
  2.0 0.9 copy-done.4
  3.0 0.8 copy-done.6
  3.7 1.2 shard_map.123
  5.0 3.7 %collective-permute-start.2 = (f32[64,128]{1,0:T(8,128)S(1)}, f32[64,128]{1,0:T(8,128)S(1)}, u32[]{:S(2)}, u32[]{:S(2)}) collective-permute-start(f32[64,128]{1,0:T(8,128)S(1)} %get-tuple-element.17), channel_id=1, source_target_pairs={{0,8},{8,16},{16,24},{1,9},{9,17},{17,25},{2,10},{10,18},{18,26},{... | collective-permute-start | bytes 98312 | tf_op jit(solution)/shard_map/ppermute | solution.py:98
  8.7 1.9 %collective-permute-start.3 = (f32[64,128]{1,0:T(8,128)S(1)}, f32[64,128]{1,0:T(8,128)S(1)}, u32[]{:S(2)}, u32[]{:S(2)}) collective-permute-start(f32[64,128]{1,0:T(8,128)S(1)} %get-tuple-element.18), channel_id=1, source_target_pairs={{8,0},{16,8},{24,16},{9,1},{17,9},{25,17},{10,2},{18,10},{26,18},{... | collective-permute-start | bytes 98312 | tf_op jit(solution)/shard_map/ppermute | solution.py:98
  10.6 3.1 %collective-permute-start = (f32[54,128]{1,0:T(8,128)S(1)}, f32[54,128]{1,0:T(8,128)S(1)}, u32[]{:S(2)}, u32[]{:S(2)}) collective-permute-start(f32[54,128]{1,0:T(8,128)S(1)} %get-tuple-element.15), channel_id=1, source_target_pairs={{0,1},{1,2},{2,3},{3,4},{4,5},{5,6},{6,7},{8,9},{9,10},{10,11},{11... | collective-permute-start | bytes 82952 | tf_op jit(solution)/shard_map/ppermute | solution.py:98
  13.7 3.1 %collective-permute-start.1 = (f32[54,128]{1,0:T(8,128)S(1)}, f32[54,128]{1,0:T(8,128)S(1)}, u32[]{:S(2)}, u32[]{:S(2)}) collective-permute-start(f32[54,128]{1,0:T(8,128)S(1)} %get-tuple-element.16), channel_id=1, source_target_pairs={{1,0},{2,1},{3,2},{4,3},{5,4},{6,5},{7,6},{9,8},{10,9},{11,10},{12... | collective-permute-start | bytes 82952 | tf_op jit(solution)/shard_map/ppermute | solution.py:98
  17.5 2.8 %copy-done = bf16[6,8,8,64,128]{4,3,2,1,0:T(8,128)(2,1)S(1)} copy-done((bf16[6,8,8,64,128]{4,3,2,1,0:T(8,128)(2,1)S(1)}, bf16[6,8,8,64,128]{4,3,2,1,0:T(8,128)(2,1)}, u32[]{:S(2)}) %copy-start) | copy-done | bytes 6291480
  20.2 1.4 shard_map.122.before_ref
  21.8 1.3 copy-done.1
  23.0 0.0 copy-done.5
  23.1 5.9 %shard_map.124 = (f32[6,8,64,128]{3,2,1,0:T(8,128)S(1)}, bf16[512,768]{1,0:T(8,128)(2,1)S(1)}) custom-call(f32[6,8,64,128]{3,2,1,0:T(8,128)S(1)} %shard_map.122.before_ref, f32[6,8,64,128]{3,2,1,0:T(8,128)S(1)} %copy-done.2, s32[64,128]{1,0:T(8,128)S(1)} %copy-done.6, f32[6,64,128]{2,1,0:T(8,128)S(1)} %copy-done.5, ...), custom_call_target="tpu_custom_call" | custom-call | flops 12582912 | bytes 11010048 | tf_op jit(solution)/shard_map/pallas_call | solution.py:222
  29.0 6.0 %shard_map.125 = (bf16[32,8,128]{2,1,0:T(8,128)(2,1)S(1)}, bf16[32,8,128]{2,1,0:T(8,128)(2,1)}) custom-call(s32[1,1,32]{2,1,0:T(1,128)S(1)} %copy-done.13, s32[1,1]{1,0:T(1,128)S(6)} %copy.13.count_ref, s32[8,1,512]{2,1,0:T(1,128)S(1)} %bitcast.14, bf16[512,768]{1,0:T(8,128)(2,1)S(1)} %get-tuple-element.19.rounded_ref), custom_call_target="tpu_custom_call" | custom-call | flops 3221225472 | bytes 786432 | tf_op jit(solution)/shard_map/pallas_call | solution.py:288
  35.0 0.6 copy-done.14
  35.6 5.9 %all-to-all-start.1 = ((bf16[32,8,128]{2,1,0:T(8,128)(2,1)}), bf16[32,8,128]{2,1,0:T(8,128)(2,1)S(1)}, u32[]{:S(2)}, u32[]{:S(2)}) async-start(bf16[32,8,128]{2,1,0:T(8,128)(2,1)} %get-tuple-element.27), calls=%async_computation.1 | async-start | bytes 131072 | tf_op jit(solution)/shard_map/all_to_all | solution.py:403
  41.6 1.9 %shard_map.126 = bf16[32,8,8,128]{3,2,1,0:T(8,128)(2,1)} custom-call(bf16[32,8,8,128]{3,2,1,0:T(8,128)(2,1)S(1)} %bitcast.10, bf16[32,8,8,128]{3,2,1,0:T(8,128)(2,1)S(1)} %bitcast.12), custom_call_target="tpu_custom_call" | custom-call | flops 4194304 | bytes 1572864 | tf_op jit(solution)/shard_map/pallas_call | solution.py:43
  43.5 3.9 %all-to-all-done.1.picked_ref = bf16[32,8,128]{2,1,0:T(8,128)(2,1)S(1)} async-done(((bf16[32,8,128]{2,1,0:T(8,128)(2,1)}), bf16[32,8,128]{2,1,0:T(8,128)(2,1)S(1)}, u32[]{:S(2)}, u32[]{:S(2)}) %all-to-all-start.1) | async-done | bytes 65568 | tf_op jit(solution)/shard_map/all_to_all | solution.py:403
  47.5 3.9 %all-to-all-start = ((bf16[32,8,8,128]{3,2,1,0:T(8,128)(2,1)}), bf16[32,8,8,128]{3,2,1,0:T(8,128)(2,1)S(1)}, u32[]{:S(2)}, u32[]{:S(2)}) async-start(bf16[32,8,8,128]{3,2,1,0:T(8,128)(2,1)} %shard_map.126), calls=%async_computation | async-start | bytes 1048576 | tf_op jit(solution)/shard_map/all_to_all | solution.py:403
  51.4 0.6 shard_map.130
  52.0 60.9 %all-gather = f32[256,128]{1,0:T(8,128)S(1)} all-gather(f32[8,128]{1,0:T(8,128)S(1)} %shard_map.130), channel_id=2, replica_groups=mesh['gx'=4,'gy'=8] {'gx','gy'}, dimensions={0}, use_global_device_ids=true | all-gather | bytes 135168 | tf_op jit(solution)/shard_map/all_gather | solution.py:418
  113.0 1.5 %copy-done.11 = f32[6,8,64,128]{3,2,1,0:T(8,128)S(1)} copy-done((f32[6,8,64,128]{3,2,1,0:T(8,128)S(1)}, f32[6,8,64,128]{3,2,1,0:T(8,128)}, u32[]{:S(2)}) %copy-start.11) | copy-done | bytes 1572888
  114.5 1.0 copy-done.15
  115.5 6.9 %shard_map.127 = (f32[6,8,64,128]{3,2,1,0:T(8,128)S(1)}, f32[54,128]{1,0:T(8,128)S(1)}, f32[54,128]{1,0:T(8,128)S(1)}, f32[64,128]{1,0:T(8,128)S(1)}, f32[64,128]{1,0:T(8,128)S(1)}) custom-call(s32[1,1,32]{2,1,0:T(1,128)S(1)} %copy-done.13, s32[8,1,512]{2,1,0:T(1,128)S(1)} %bitcast.15, bf16[32,8,128]{2,1,0:T(8,128)(2,1)S(1)} %copy-done.15, ...), custom_call_target="tpu_custom_call" | custom-call | flops 3221225472 | bytes 3145728 | tf_op jit(solution)/shard_map/pallas_call | solution.py:340
  122.4 2.3 %collective-permute-start.4 = (f32[54,128]{1,0:T(8,128)S(1)}, f32[54,128]{1,0:T(8,128)S(1)}, u32[]{:S(2)}, u32[]{:S(2)}) collective-permute-start(f32[54,128]{1,0:T(8,128)S(1)} %get-tuple-element.23), channel_id=1, source_target_pairs={{0,1},{1,2},{2,3},{3,4},{4,5},{5,6},{6,7},{8,9},{9,10},{10,11},{11... | collective-permute-start | bytes 82952 | tf_op jit(solution)/shard_map/ppermute | solution.py:98
  124.7 5.5 %collective-permute-start.5 = (f32[54,128]{1,0:T(8,128)S(1)}, f32[54,128]{1,0:T(8,128)S(1)}, u32[]{:S(2)}, u32[]{:S(2)}) collective-permute-start(f32[54,128]{1,0:T(8,128)S(1)} %get-tuple-element.24), channel_id=1, source_target_pairs={{1,0},{2,1},{3,2},{4,3},{5,4},{6,5},{7,6},{9,8},{10,9},{11,10},{12... | collective-permute-start | bytes 82952 | tf_op jit(solution)/shard_map/ppermute | solution.py:98
  130.2 10.3 %collective-permute-start.6 = (f32[64,128]{1,0:T(8,128)S(1)}, f32[64,128]{1,0:T(8,128)S(1)}, u32[]{:S(2)}, u32[]{:S(2)}) collective-permute-start(f32[64,128]{1,0:T(8,128)S(1)} %get-tuple-element.25), channel_id=1, source_target_pairs={{0,8},{8,16},{16,24},{1,9},{9,17},{17,25},{2,10},{10,18},{18,26},{... | collective-permute-start | bytes 98312 | tf_op jit(solution)/shard_map/ppermute | solution.py:98
  140.5 1.9 %collective-permute-start.7 = (f32[64,128]{1,0:T(8,128)S(1)}, f32[64,128]{1,0:T(8,128)S(1)}, u32[]{:S(2)}, u32[]{:S(2)}) collective-permute-start(f32[64,128]{1,0:T(8,128)S(1)} %get-tuple-element.26), channel_id=1, source_target_pairs={{8,0},{16,8},{24,16},{9,1},{17,9},{25,17},{10,2},{18,10},{26,18},{... | collective-permute-start | bytes 98312 | tf_op jit(solution)/shard_map/ppermute | solution.py:98
  142.5 0.6 slice_multiply_fusion
  143.1 1.5 shard_map.128.before_ref
  144.6 1.2 collective-permute-done.7.high_x
  145.8 6.4 %shard_map.129 = f32[6,8,64,128]{3,2,1,0:T(8,128)} custom-call(f32[6,8,64,128]{3,2,1,0:T(8,128)S(1)} %shard_map.128.before_ref, f32[6,8,64,128]{3,2,1,0:T(8,128)S(1)} %get-tuple-element.22.field_ref, s32[64,128]{1,0:T(8,128)S(1)} %copy-done.7, f32[6,64,128]{2,1,0:T(8,128)S(1)} %copy-done.5, f32[54,128]{1,0:T(8,128)S(1)} %collective-permute-done.4.low_y, ...), custom_call_target="tpu_custom_call" | custom-call | flops 12582912 | bytes 11010048 | tf_op jit(solution)/shard_map/pallas_call | solution.py:222
  (42 shorter events, 0.1 us)
Async XLA Ops:
  0.6 1.4 copy-start.2
  2.0 0.9 copy-start.4
  3.0 0.8 copy-start.6
  5.0 16.8 %collective-permute-start.2 = (f32[64,128]{1,0:T(8,128)S(1)}, f32[64,128]{1,0:T(8,128)S(1)}, u32[]{:S(2)}, u32[]{:S(2)}) collective-permute-start(f32[64,128]{1,0:T(8,128)S(1)} %get-tuple-element.17), channel_id=1, source_target_pairs={{0,8},{8,16},{16,24},{1,9},{9,17},{17,25},{2,10},{10,18},{18,26},{... | collective-permute-start | bytes 98312 | tf_op jit(solution)/shard_map/ppermute | solution.py:98
  8.7 13.1 %collective-permute-start.3 = (f32[64,128]{1,0:T(8,128)S(1)}, f32[64,128]{1,0:T(8,128)S(1)}, u32[]{:S(2)}, u32[]{:S(2)}) collective-permute-start(f32[64,128]{1,0:T(8,128)S(1)} %get-tuple-element.18), channel_id=1, source_target_pairs={{8,0},{16,8},{24,16},{9,1},{17,9},{25,17},{10,2},{18,10},{26,18},{... | collective-permute-start | bytes 98312 | tf_op jit(solution)/shard_map/ppermute | solution.py:98
  10.6 11.1 %collective-permute-start = (f32[54,128]{1,0:T(8,128)S(1)}, f32[54,128]{1,0:T(8,128)S(1)}, u32[]{:S(2)}, u32[]{:S(2)}) collective-permute-start(f32[54,128]{1,0:T(8,128)S(1)} %get-tuple-element.15), channel_id=1, source_target_pairs={{0,1},{1,2},{2,3},{3,4},{4,5},{5,6},{6,7},{8,9},{9,10},{10,11},{11... | collective-permute-start | bytes 82952 | tf_op jit(solution)/shard_map/ppermute | solution.py:98
  13.7 8.0 %collective-permute-start.1 = (f32[54,128]{1,0:T(8,128)S(1)}, f32[54,128]{1,0:T(8,128)S(1)}, u32[]{:S(2)}, u32[]{:S(2)}) collective-permute-start(f32[54,128]{1,0:T(8,128)S(1)} %get-tuple-element.16), channel_id=1, source_target_pairs={{1,0},{2,1},{3,2},{4,3},{5,4},{6,5},{7,6},{9,8},{10,9},{11,10},{12... | collective-permute-start | bytes 82952 | tf_op jit(solution)/shard_map/ppermute | solution.py:98
  17.4 2.8 %copy-start = (bf16[6,8,8,64,128]{4,3,2,1,0:T(8,128)(2,1)S(1)}, bf16[6,8,8,64,128]{4,3,2,1,0:T(8,128)(2,1)}, u32[]{:S(2)}) copy-start(bf16[6,8,8,64,128]{4,3,2,1,0:T(8,128)(2,1)} %block_ref.6) | copy-start | bytes 18874372
  20.2 2.8 %copy-start.1 = (bf16[6,8,8,64,128]{4,3,2,1,0:T(8,128)(2,1)S(1)}, bf16[6,8,8,64,128]{4,3,2,1,0:T(8,128)(2,1)}, u32[]{:S(2)}) copy-start(bf16[6,8,8,64,128]{4,3,2,1,0:T(8,128)(2,1)} %block_ref.7) | copy-start | bytes 18874372
  20.2 2.8 %copy-start.5 = (f32[6,64,128]{2,1,0:T(8,128)S(1)}, f32[6,64,128]{2,1,0:T(8,128)}, u32[]{:S(2)}) copy-start(f32[6,64,128]{2,1,0:T(8,128)} %perm_ref.7) | copy-start | bytes 589828
  21.7 7.3 %copy-start.12 = (s32[1,1,4096]{2,1,0:T(1,128)S(1)}, s32[1,1,4096]{2,1,0:T(1,128)}, u32[]{:S(2)}) copy-start(s32[1,1,4096]{2,1,0:T(1,128)} %param.16) | copy-start | bytes 49156
  21.7 7.3 %copy-start.13 = (s32[1,1,32]{2,1,0:T(1,128)S(1)}, s32[1,1,32]{2,1,0:T(1,128)}, u32[]{:S(2)}) copy-start(s32[1,1,32]{2,1,0:T(1,128)} %helper_ref.3) | copy-start | bytes 388
  28.9 6.0 %copy-start.10 = (f32[6,8,64,128]{3,2,1,0:T(8,128)}, f32[6,8,64,128]{3,2,1,0:T(8,128)S(1)}, u32[]{:S(2)}) copy-start(f32[6,8,64,128]{3,2,1,0:T(8,128)S(1)} %get-tuple-element.21.first_ref) | copy-start | bytes 4718596
  29.0 12.6 %copy-start.3 = (bf16[1,1,32,8,8,128]{5,4,3,2,1,0:T(8,128)(2,1)S(1)}, bf16[1,1,32,8,8,128]{5,4,3,2,1,0:T(8,128)(2,1)}, u32[]{:S(2)}) copy-start(bf16[1,1,32,8,8,128]{5,4,3,2,1,0:T(8,128)(2,1)} %param.19) | copy-start | bytes 1572868
  29.0 12.6 %copy-start.8 = (bf16[1,1,32,8,8,128]{5,4,3,2,1,0:T(8,128)(2,1)S(1)}, bf16[1,1,32,8,8,128]{5,4,3,2,1,0:T(8,128)(2,1)}, u32[]{:S(2)}) copy-start(bf16[1,1,32,8,8,128]{5,4,3,2,1,0:T(8,128)(2,1)} %param.20) | copy-start | bytes 1572868
  35.0 0.6 copy-start.14
  35.6 15.8 %copy-start.9 = (bf16[1,1,32,8,128]{4,3,2,1,0:T(8,128)(2,1)S(1)}, bf16[1,1,32,8,128]{4,3,2,1,0:T(8,128)(2,1)}, u32[]{:S(2)}) copy-start(bf16[1,1,32,8,128]{4,3,2,1,0:T(8,128)(2,1)} %param.21) | copy-start | bytes 196612
  35.6 11.9 %all-to-all-start.1 = ((bf16[32,8,128]{2,1,0:T(8,128)(2,1)}), bf16[32,8,128]{2,1,0:T(8,128)(2,1)S(1)}, u32[]{:S(2)}, u32[]{:S(2)}) async-start(bf16[32,8,128]{2,1,0:T(8,128)(2,1)} %get-tuple-element.27), calls=%async_computation.1 | async-start | bytes 131072 | tf_op jit(solution)/shard_map/all_to_all | solution.py:403
  41.6 71.4 %copy-start.7 = (s32[64,128]{1,0:T(8,128)S(1)}, s32[64,128]{1,0:T(8,128)}, u32[]{:S(2)}) copy-start(s32[64,128]{1,0:T(8,128)} %mask_ref.11) | copy-start | bytes 98308
  47.5 65.5 %all-to-all-start = ((bf16[32,8,8,128]{3,2,1,0:T(8,128)(2,1)}), bf16[32,8,8,128]{3,2,1,0:T(8,128)(2,1)S(1)}, u32[]{:S(2)}, u32[]{:S(2)}) async-start(bf16[32,8,8,128]{3,2,1,0:T(8,128)(2,1)} %shard_map.126), calls=%async_computation | async-start | bytes 1048576 | tf_op jit(solution)/shard_map/all_to_all | solution.py:403
  51.4 94.4 %slice-start.2 = ((s8[6291456]{0:T(1024)(128)(4,1)}), s8[2097152]{0:T(1024)(128)(4,1)S(1)}, s32[]{:S(2)}) async-start(s8[6291456]{0:T(1024)(128)(4,1)} %bitcast.8), calls=%async_computation.4 | async-start | bytes 4194304
  113.0 30.1 %slice-start = ((s8[6291456]{0:T(1024)(128)(4,1)}), s8[4194304]{0:T(1024)(128)(4,1)S(1)}, s32[]{:S(2)}) async-start(s8[6291456]{0:T(1024)(128)(4,1)} %bitcast.6), calls=%async_computation.2 | async-start | bytes 8388608
  113.0 1.6 %copy-start.11 = (f32[6,8,64,128]{3,2,1,0:T(8,128)S(1)}, f32[6,8,64,128]{3,2,1,0:T(8,128)}, u32[]{:S(2)}) copy-start(f32[6,8,64,128]{3,2,1,0:T(8,128)} %copy-done.10) | copy-start | bytes 4718596
  114.5 1.0 copy-start.15
  115.5 27.5 %slice-start.1 = ((s8[6291456]{0:T(1024)(128)(4,1)}), s8[2097152]{0:T(1024)(128)(4,1)S(1)}, s32[]{:S(2)}) async-start(s8[6291456]{0:T(1024)(128)(4,1)} %bitcast.6), calls=%async_computation.3 | async-start | bytes 4194304
  115.5 30.2 %slice-start.3 = ((s8[6291456]{0:T(1024)(128)(4,1)}), s8[4194304]{0:T(1024)(128)(4,1)S(1)}, s32[]{:S(2)}) async-start(s8[6291456]{0:T(1024)(128)(4,1)} %bitcast.8), calls=%async_computation.5 | async-start | bytes 8388608
  122.4 22.1 %collective-permute-start.4 = (f32[54,128]{1,0:T(8,128)S(1)}, f32[54,128]{1,0:T(8,128)S(1)}, u32[]{:S(2)}, u32[]{:S(2)}) collective-permute-start(f32[54,128]{1,0:T(8,128)S(1)} %get-tuple-element.23), channel_id=1, source_target_pairs={{0,1},{1,2},{2,3},{3,4},{4,5},{5,6},{6,7},{8,9},{9,10},{10,11},{11... | collective-permute-start | bytes 82952 | tf_op jit(solution)/shard_map/ppermute | solution.py:98
  124.7 19.8 %collective-permute-start.5 = (f32[54,128]{1,0:T(8,128)S(1)}, f32[54,128]{1,0:T(8,128)S(1)}, u32[]{:S(2)}, u32[]{:S(2)}) collective-permute-start(f32[54,128]{1,0:T(8,128)S(1)} %get-tuple-element.24), channel_id=1, source_target_pairs={{1,0},{2,1},{3,2},{4,3},{5,4},{6,5},{7,6},{9,8},{10,9},{11,10},{12... | collective-permute-start | bytes 82952 | tf_op jit(solution)/shard_map/ppermute | solution.py:98
  130.2 14.4 %collective-permute-start.6 = (f32[64,128]{1,0:T(8,128)S(1)}, f32[64,128]{1,0:T(8,128)S(1)}, u32[]{:S(2)}, u32[]{:S(2)}) collective-permute-start(f32[64,128]{1,0:T(8,128)S(1)} %get-tuple-element.25), channel_id=1, source_target_pairs={{0,8},{8,16},{16,24},{1,9},{9,17},{17,25},{2,10},{10,18},{18,26},{... | collective-permute-start | bytes 98312 | tf_op jit(solution)/shard_map/ppermute | solution.py:98
  140.5 5.2 %collective-permute-start.7 = (f32[64,128]{1,0:T(8,128)S(1)}, f32[64,128]{1,0:T(8,128)S(1)}, u32[]{:S(2)}, u32[]{:S(2)}) collective-permute-start(f32[64,128]{1,0:T(8,128)S(1)} %get-tuple-element.26), channel_id=1, source_target_pairs={{8,0},{16,8},{24,16},{9,1},{17,9},{25,17},{10,2},{18,10},{26,18},{... | collective-permute-start | bytes 98312 | tf_op jit(solution)/shard_map/ppermute | solution.py:98

commit v2 on v1

--- a/solution.py
+++ b/solution.py
@@ -48,56 +48,72 @@
     )(inverse, coupling)
 
 
-def write_edges(field, clear, perm_ref, low_y, high_y, low_x, high_x):
+def round_up(number, step):
+    return -(-number // step) * step
+
+
+def write_edges(field, comps, clear, perm_ref, side_y, send_y, send_x):
     layers, rows, cols = perm_ref.shape
-    comps = low_y.shape[0] // layers - 1
     lane = lax.broadcasted_iota(jnp.int32, (rows, cols), 1)
-    left = jnp.zeros((rows, cols), F32)
-    right = jnp.zeros((rows, cols), F32)
+    pair = lane // 2
+    along_x = jnp.zeros((rows, cols), F32)
+    side_y[...] = jnp.zeros_like(side_y)
     for k in range(layers):
         for c in range(comps + 1):
             if c < comps:
                 value, at = field(k, c) * clear, k * comps + c
             else:
                 value, at = perm_ref[k], layers * comps + k
-            low_y[at : at + 1, :] = value[0:1]
-            high_y[at : at + 1, :] = value[rows - 1 : rows]
-            left = jnp.where(lane == at, value[:, 0:1], left)
-            right = jnp.where(lane == at, value[:, cols - 1 : cols], right)
-    low_x[...] = left
-    high_x[...] = right
-
-
-def edges_kernel(field_ref, mask_ref, perm_ref, low_y, high_y, low_x, high_x):
+            side_y[0, at : at + 1, :] = value[0:1]
+            side_y[1, at : at + 1, :] = value[rows - 1 : rows]
+            along_x = jnp.where(pair == at, pltpu.roll(value, (2 * at + 1) % cols, 1), along_x)
+    count_y, count_x = send_y.shape[0], send_x.shape[0]
+    me_y = lax.axis_index("gy")
+    along_x = along_x.astype(BF16)
+    for i in range(count_x):
+        send_x[i] = along_x
+    low, high = side_y[0].astype(BF16), side_y[1].astype(BF16)
+    for i in range(count_y):
+        send_y[i] = jnp.where(i < me_y, low, high)
+
+
+def edges_kernel(field_ref, mask_ref, perm_ref, send_y, send_x, side_y):
     clear = 1.0 - mask_ref[...].astype(F32)
-    write_edges(lambda k, c: field_ref[k, c], clear, perm_ref, low_y, high_y, low_x, high_x)
+    write_edges(lambda k, c: field_ref[k, c], field_ref.shape[1], clear, perm_ref, side_y, send_y, send_x)
+
+
+def edge_rows(layers, comps):
+    return round_up(layers * (comps + 1), 16)
 
 
 def edge_shapes(layers, comps, rows, cols):
-    along_y = jax.ShapeDtypeStruct((layers * (comps + 1), cols), F32)
-    along_x = jax.ShapeDtypeStruct((rows, cols), F32)
-    return [along_y, along_y, along_x, along_x]
+    along_y = (lax.axis_size("gy"), edge_rows(layers, comps), cols)
+    along_x = (lax.axis_size("gx"), rows, cols)
+    return [jax.ShapeDtypeStruct(shape, BF16) for shape in (along_y, along_x)]
+
+
+def edge_scratch(layers, comps, cols):
+    return pltpu.VMEM((2, edge_rows(layers, comps), cols), F32)
 
 
 def edges(field, mask, perm):
+    layers, comps, rows, cols = field.shape
     return pl.pallas_call(
         edges_kernel,
         out_shape=edge_shapes(*field.shape),
+        scratch_shapes=[edge_scratch(layers, comps, cols)],
         compiler_params=params(24),
         cost_estimate=cost(4 * field.size, 4 * field.size),
     )(field, mask, perm)
 
 
 def exchange(sides):
-    low_y, high_y, low_x, high_x = sides
-
-    def both(low, high, axis):
-        count = lax.axis_size(axis)
-        up = [(i, i + 1) for i in range(count - 1)]
-        down = [(j, i) for i, j in up]
-        return lax.ppermute(high, axis, up), lax.ppermute(low, axis, down)
-
-    return (*both(low_y, high_y, "gy"), *both(low_x, high_x, "gx"))
+    send_y, send_x = sides
+
+    def swap(array, axis):
+        return lax.all_to_all(array, axis, split_axis=0, concat_axis=0, tiled=True)
+
+    return swap(send_y, "gy"), swap(send_x, "gx")
 
 
 TILE = 16
@@ -118,7 +134,7 @@
             out_ref[0, c, here] = total[c]
 
 
-def diag_part(field, mask, block):
+def diag_part(field, mask, block, mib):
     layers, comps, rows, cols = field.shape
     layer = pl.BlockSpec((1, comps, rows, cols), lambda k: (k, 0, 0, 0))
     return pl.pallas_call(
@@ -131,71 +147,105 @@
         ],
         out_specs=layer,
         out_shape=jax.ShapeDtypeStruct(field.shape, F32),
-        compiler_params=params(24),
+        compiler_params=params(mib),
         cost_estimate=cost(2 * block.size, 2 * block.size + 8 * field.size),
     )(field, mask, block)
 
 
-def flux_kernel(want_rounded, before_ref, field_ref, mask_ref, perm_ref, low_y, high_y, low_x, high_x, block_ref, *rest):
-    if want_rounded:
-        out_ref, rounded_ref, padded, padded_perm = rest
-    else:
-        out_ref, padded, padded_perm = rest
+def reciprocal(value):
+    guess = pl.reciprocal(value, approx=True)
+    return guess * (2.0 - value * guess)
+
+
+def flux_kernel(want_rounded, before_ref, field_ref, mask_ref, perm_ref, from_y, from_x, block_ref, *rest):
+    out_ref = rest[0]
+    rounded_ref = rest[1] if want_rounded else None
+    padded, padded_perm, edge_x, place, beside_edge, perm_edge = rest[-6:]
     layers, comps, rows, cols = field_ref.shape
     top = 8
     k = pl.program_id(0)
     above = jnp.minimum(k + 1, layers - 1)
     below = jnp.maximum(k - 1, 0)
+    me_x, me_y = lax.axis_index("gx"), lax.axis_index("gy")
+    count_x, count_y = from_x.shape[0], from_y.shape[0]
+    lane = lax.broadcasted_iota(jnp.int32, (rows, cols), 1)
+
+    @pl.when(k == 0)
+    def _():
+        low = from_x[jnp.maximum(me_x - 1, 0)].astype(F32)
+        high = from_x[jnp.minimum(me_x + 1, count_x - 1)].astype(F32)
+        low = jnp.where(me_x > 0, low, 0.0)
+        high = jnp.where(me_x < count_x - 1, high, 0.0)
+        edge_x[...] = jnp.where(lane % 2 == 0, low, high)
+        number = lax.broadcasted_iota(jnp.int32, (cols, cols), 0)
+        spot = lax.broadcasted_iota(jnp.int32, (cols, cols), 1)
+        for r in range(comps):
+            taken = ((number == 2 * r) & (spot == 0)) | ((number == 2 * r + 1) & (spot == cols - 1))
+            place[:, r * cols : (r + 1) * cols] = jnp.where(taken, 1.0, 0.0).astype(BF16)
+
+    turned = pltpu.roll(edge_x[...], lax.rem(cols - 2 * comps * k, cols), 1).astype(BF16)
+    beside_edge[...] = jnp.dot(turned, place[...], preferred_element_type=F32)
+    at_low = 2 * (layers * comps + k)
+    perm_low = pltpu.roll(edge_x[...], lax.rem(cols - at_low, cols), 1)
+    perm_high = pltpu.roll(edge_x[...], lax.rem(2 * cols - at_low - 2, cols), 1)
+    perm_edge[...] = jnp.where(lane == 0, perm_low, perm_high)
+
     clear = 1.0 - mask_ref[...].astype(F32)
+    low_y = from_y[jnp.maximum(me_y - 1, 0), pl.ds(pl.multiple_of(16 * (k // 2), 16), 16)].astype(F32)
+    high_y = from_y[jnp.minimum(me_y + 1, count_y - 1), pl.ds(pl.multiple_of(16 * (k // 2), 16), 16)].astype(F32)
+    has_low, has_high = me_y > 0, me_y < count_y - 1
+    odd = k % 2 == 1
+    low_y = jnp.where(has_low, jnp.where(odd, low_y[comps:], low_y[:comps]), 0.0)
+    high_y = jnp.where(has_high, jnp.where(odd, high_y[comps:], high_y[:comps]), 0.0)
+    perm_rows = slice(layers * comps, layers * comps + 16)
+    perm_y_low = from_y[jnp.maximum(me_y - 1, 0), perm_rows].astype(F32)
+    perm_y_high = from_y[jnp.minimum(me_y + 1, count_y - 1), perm_rows].astype(F32)
+    mine = lax.broadcasted_iota(jnp.int32, (16, cols), 0) == k
+    perm_y_low = jnp.sum(jnp.where(mine & has_low, perm_y_low, 0.0), axis=0, keepdims=True)
+    perm_y_high = jnp.sum(jnp.where(mine & has_high, perm_y_high, 0.0), axis=0, keepdims=True)
     for c in range(comps):
         padded[c, top : top + rows] = field_ref[k, c] * clear
-        padded[c, top - 1 : top] = low_y[pl.ds(k * comps + c, 1)]
-        padded[c, top + rows : top + rows + 1] = high_y[pl.ds(k * comps + c, 1)]
+        padded[c, top - 1 : top] = low_y[c : c + 1]
+        padded[c, top + rows : top + rows + 1] = high_y[c : c + 1]
     padded_perm[top : top + rows] = perm_ref[k]
-    padded_perm[top - 1 : top] = low_y[pl.ds(layers * comps + k, 1)]
-    padded_perm[top + rows : top + rows + 1] = high_y[pl.ds(layers * comps + k, 1)]
+    padded_perm[top - 1 : top] = perm_y_low
+    padded_perm[top + rows : top + rows + 1] = perm_y_high
     lane = lax.broadcasted_iota(jnp.int32, (TILE, cols), 1)
     is_first, is_last = lane == 0, lane == cols - 1
-    turn_field = lax.rem(cols - k * comps, cols)
-    turn_perm = lax.rem(cols - (layers * comps + k), cols)
+    inner = jnp.where(is_first | is_last, 0.0, 1.0)
 
     def weight(centre, beside):
-        return 2.0 * centre * beside / (centre + beside)
+        return 2.0 * centre * beside * reciprocal(centre + beside)
 
     for y in range(0, rows, TILE):
         here = slice(y, y + TILE)
         at = top + y
         free = 1.0 - mask_ref[here].astype(F32)
-        low_field, high_field = (pltpu.roll(ref[here], turn_field, 1) for ref in (low_x, high_x))
-        low_perm, high_perm = (pltpu.roll(ref[here], turn_perm, 1) for ref in (low_x, high_x))
-
-        def beside_x(value, low, high):
-            return (
-                jnp.where(is_first, low, pltpu.roll(value, 1, 1)),
-                jnp.where(is_last, high, pltpu.roll(value, cols - 1, 1)),
-            )
-
         centre = perm_ref[k, here]
-        perm_left, perm_right = beside_x(centre, low_perm[:, 0:1], high_perm[:, 0:1])
+        perm_beside = perm_edge[here]
+        perm_left = jnp.where(is_first, perm_beside, pltpu.roll(centre, 1, 1))
+        perm_right = jnp.where(is_last, perm_beside, pltpu.roll(centre, cols - 1, 1))
+        to_left, to_right = weight(centre, perm_left), weight(centre, perm_right)
         weights = [
             jnp.where(k < layers - 1, weight(centre, perm_ref[above, here]), 0.0) * free,
             jnp.where(k > 0, weight(centre, perm_ref[below, here]), 0.0) * free,
             weight(centre, padded_perm[at + 1 : at + 1 + TILE]),
             weight(centre, padded_perm[at - 1 : at - 1 + TILE]),
-            weight(centre, perm_right),
-            weight(centre, perm_left),
+            jnp.where(is_last, 0.0, to_right),
+            jnp.where(is_first, 0.0, to_left),
+            jnp.where(is_first, to_left, to_right) * (1.0 - inner),
         ]
         total = [None] * comps
         for r in range(comps):
             own = padded[r, at : at + TILE]
-            left, right = beside_x(own, low_field[:, r : r + 1], high_field[:, r : r + 1])
             summed = (
                 weights[0] * field_ref[above, r, here]
                 + weights[1] * field_ref[below, r, here]
                 + weights[2] * padded[r, at + 1 : at + 1 + TILE]
                 + weights[3] * padded[r, at - 1 : at - 1 + TILE]
-                + weights[4] * right
-                + weights[5] * left
+                + weights[4] * pltpu.roll(own, cols - 1, 1)
+                + weights[5] * pltpu.roll(own, 1, 1)
+                + weights[6] * beside_edge[here, r * cols : (r + 1) * cols]
             )
             for c in range(comps):
                 term = block_ref[0, r, c, here].astype(F32) * summed
@@ -207,7 +257,7 @@
                 rounded_ref[c * rows + y : c * rows + y + TILE, :] = value.astype(BF16)
 
 
-def flux_part(before, field, mask, perm, halos, block, want_rounded):
+def flux_part(before, field, mask, perm, halos, block, want_rounded, mib):
     layers, comps, rows, cols = field.shape
     layer = pl.BlockSpec((1, comps, rows, cols), lambda k: (k, 0, 0, 0))
 
@@ -235,8 +285,12 @@
         scratch_shapes=[
             pltpu.VMEM((comps, rows + 16, cols), F32),
             pltpu.VMEM((rows + 16, cols), F32),
+            pltpu.VMEM((rows, cols), F32),
+            pltpu.VMEM((cols, comps * cols), BF16),
+            pltpu.VMEM((rows, comps * cols), F32),
+            pltpu.VMEM((rows, cols), F32),
         ],
-        compiler_params=params(24),
+        compiler_params=params(mib),
         cost_estimate=cost(4 * block.size, 2 * block.size + 12 * field.size),
     )(before, field, mask, perm, *halos, block)
 
@@ -296,7 +350,7 @@
 
 
 def scatter_kernel(
-    helper_ref, cells_ref, picked_ref, home_ref, first_ref, mask_ref, perm_ref, second_ref, low_y, high_y, low_x, high_x, added
+    helper_ref, cells_ref, picked_ref, home_ref, first_ref, mask_ref, perm_ref, second_ref, send_y, send_x, added, side_y
 ):
     layers, comps, rows, cols = first_ref.shape
     chunks, _, slots = cells_ref.shape
@@ -330,7 +384,7 @@
         for c in range(comps):
             second_ref[k, c] = first_ref[k, c] + added[c * rows : (c + 1) * rows, k * cols : (k + 1) * cols]
     clear = 1.0 - mask_ref[...].astype(F32)
-    write_edges(lambda k, c: second_ref[k, c], clear, perm_ref, low_y, high_y, low_x, high_x)
+    write_edges(lambda k, c: second_ref[k, c], comps, clear, perm_ref, side_y, send_y, send_x)
 
 
 def scatter(first, picked, home, helper, cells, mask, perm):
@@ -340,9 +394,9 @@
     return pl.pallas_call(
         scatter_kernel,
         in_specs=[smem] + [vmem] * 6,
-        out_specs=[vmem] * 5,
+        out_specs=[vmem] * 3,
         out_shape=[jax.ShapeDtypeStruct(first.shape, F32), *edge_shapes(*first.shape)],
-        scratch_shapes=[pltpu.VMEM((comps * rows, layers * cols), F32)],
+        scratch_shapes=[pltpu.VMEM((comps * rows, layers * cols), F32), edge_scratch(layers, comps, cols)],
         compiler_params=params(40),
         cost_estimate=cost(2 * first.size * cells.size, 8 * first.size),
     )(helper, cells, picked, home, first, mask, perm)
@@ -404,19 +458,21 @@
 
     home = to_partners(flash_product(inverse, coupling))
     halos = exchange(edges(cotangent, well_mask, permeability))
-    before = diag_part(cotangent, well_mask, diag_block)
-    first, rounded = flux_part(before, cotangent, well_mask, permeability, halos, flux_block, True)
+    before = diag_part(cotangent, well_mask, diag_block, 56)
+    first, rounded = flux_part(before, cotangent, well_mask, permeability, halos, flux_block, True, 56)
     picked, sent = gather(rounded, cells, helper_of, block_count, comps, rows, cols, width)
     second, *sides = scatter(first, picked, home, helper_of, cells, well_mask, permeability)
     halos = exchange(sides)
-    before = diag_part(second, well_mask, diag_block)
-    (adjoint,) = flux_part(before, second, well_mask, permeability, halos, flux_block, False)
+    before = diag_part(second, well_mask, diag_block, 24)
+    (adjoint,) = flux_part(before, second, well_mask, permeability, halos, flux_block, False, 24)
 
     partial_sum = grad_part(inverse, state, to_partners(sent))
     devices = lax.axis_size("gx") * lax.axis_size("gy")
     grad_scale = 1.0 / math.sqrt(width * devices * devices)
-    gathered = lax.all_gather(partial_sum, AXES)
-    interaction_grad = -grad_scale * jnp.sum(gathered, axis=0)[:, :comps]
+    for axis in ("gy", "gx"):
+        copies = jnp.broadcast_to(partial_sum[None], (lax.axis_size(axis), *partial_sum.shape))
+        partial_sum = jnp.sum(lax.all_to_all(copies, axis, split_axis=0, concat_axis=0), axis=0)
+    interaction_grad = -grad_scale * partial_sum[:, :comps]
     return (adjoint, interaction_grad)
 
 

time: 153 us -> 122 us (0.80)
  the two profiles are of different devices: /device:TPU:9 before, /device:TPU:0 now
where the time goes in v2:
time: 122 us; the launch traced here: 121 us
  Pallas kernels  35.6 us (29%)
  blocking collectives  27.4 us (22%)
  waiting for transfers between devices  23.8 us (20%)
  starting transfers between devices  18.7 us (15%)
  local copies, waits for them, and re-layouts  13.9 us (11%)
  between operations  1.42 us (1%)
    all_to_all x1, waiting for transfers between devices, to_partners(): return lax.all_to_all(array, AXES, split_axis=0, concat_axis=0, tiled=True)  16.3 us
    all_to_all x2, blocking collectives, swap(): return lax.all_to_all(array, axis, split_axis=0, concat_axis=0, tiled=True)  15.5 us
    unnamed x32, local copies, waits for them, and re-layouts  12.7 us
    pallas_call x2, Pallas kernels, flux_part(): pl.pallas_call(functools.partial(flux_kernel, want_rounded), grid=(layers...  12.4 us
    all_to_all x1, blocking collectives, to_partners(): return lax.all_to_all(array, AXES, split_axis=0, concat_axis=0, tiled=True)  11.9 us
    all_to_all x2, starting transfers between devices, swap(): return lax.all_to_all(array, axis, split_axis=0, concat_axis=0, tiled=True)  9.52 us
    pallas_call x2, Pallas kernels, diag_part(): pl.pallas_call(diag_kernel, grid=(layers,), in_specs=[layer, pl.BlockSpec...  7.81 us
    pallas_call x1, Pallas kernels, scatter(): pl.pallas_call(scatter_kernel, in_specs=[smem] + [vmem] * 6, out_specs=[v...  6.6 us
  transfers between devices with their start and end apart: 5, of which 4 were waited for; matrix products, arithmetic and copies ran while one was open for 1% of the time, Pallas kernels for 13%

profile of v2, /device:TPU:0, one launch (start us, length us, event | category | flops | bytes accessed | tf_op | source)
XLA Modules:
  0.0 121.3 jit_solution(2152846840870136273)
XLA Ops:
  0.6 1.4 %copy-done.2 = f32[6,8,64,128]{3,2,1,0:T(8,128)S(1)} copy-done((f32[6,8,64,128]{3,2,1,0:T(8,128)S(1)}, f32[6,8,64,128]{3,2,1,0:T(8,128)}, u32[]{:S(2)}) %copy-start.2) | copy-done | bytes 1572888
  2.0 0.9 copy-done.4
  3.0 0.8 copy-done.6
  3.7 0.9 shard_map.123
  4.6 8.3 %all_to_all.40.from_x = bf16[4,64,128]{2,1,0:T(8,128)(2,1)} all-to-all(bf16[4,64,128]{2,1,0:T(8,128)(2,1)S(1)} %get-tuple-element.12), channel_id=1, replica_groups=mesh['gx'=4,'gy'=8] {'gx'}, dimensions={0} | all-to-all | bytes 131072 | tf_op jit(solution)/shard_map/all_to_all | solution.py:114
  12.9 6.1 %all-to-all-start = ((bf16[8,64,128]{2,1,0:T(8,128)(2,1)}), bf16[8,64,128]{2,1,0:T(8,128)(2,1)S(1)}, u32[]{:S(2)}, u32[]{:S(2)}) async-start(bf16[8,64,128]{2,1,0:T(8,128)(2,1)} %get-tuple-element.11), calls=%async_computation | async-start | bytes 262144 | tf_op jit(solution)/shard_map/all_to_all | solution.py:114
  19.7 6.4 %shard_map.122.before_ref = f32[6,8,64,128]{3,2,1,0:T(8,128)} custom-call(f32[6,8,64,128]{3,2,1,0:T(8,128)} %field_ref.5, s32[64,128]{1,0:T(8,128)} %mask_ref.11, bf16[6,8,8,64,128]{4,3,2,1,0:T(8,128)(2,1)} %block_ref.6), custom_call_target="tpu_custom_call" | custom-call | flops 6291456 | bytes 9437184 | tf_op jit(solution)/shard_map/pallas_call | solution.py:140
  26.4 0.6 copy-done.15
  27.0 8.1 %shard_map.124 = (f32[6,8,64,128]{3,2,1,0:T(8,128)}, bf16[512,768]{1,0:T(8,128)(2,1)}) custom-call(f32[6,8,64,128]{3,2,1,0:T(8,128)} %shard_map.122.before_ref, f32[6,8,64,128]{3,2,1,0:T(8,128)} %field_ref.5, s32[64,128]{1,0:T(8,128)} %mask_ref.11, f32[6,64,128]{2,1,0:T(8,128)} %perm_ref.7, bf16[8,64,128]{2,1,0:T(8,128)(2,1)} %copy-done.15, ...), custom_call_target="tpu_custom_call" | custom-call | flops 12582912 | bytes 11010048 | tf_op jit(solution)/shard_map/pallas_call | solution.py:272
  35.1 1.1 copy-done.12
  36.3 5.4 %shard_map.125 = (bf16[32,8,128]{2,1,0:T(8,128)(2,1)S(1)}, bf16[32,8,128]{2,1,0:T(8,128)(2,1)S(1)}) custom-call(s32[1,1,32]{2,1,0:T(1,128)S(1)} %copy-done.14, s32[1,1]{1,0:T(1,128)S(6)} %copy.13.count_ref, s32[8,1,512]{2,1,0:T(1,128)S(1)} %bitcast.8, bf16[512,768]{1,0:T(8,128)(2,1)S(1)} %copy-done.12), custom_call_target="tpu_custom_call" | custom-call | flops 3221225472 | bytes 786432 | tf_op jit(solution)/shard_map/pallas_call | solution.py:342
  41.6 11.9 %all_to_all.41.picked_ref = bf16[32,8,128]{2,1,0:T(8,128)(2,1)S(1)} all-to-all(bf16[32,8,128]{2,1,0:T(8,128)(2,1)S(1)} %get-tuple-element.19), channel_id=1, replica_groups=mesh['gx'=4,'gy'=8] {'gx','gy'}, dimensions={0} | all-to-all | bytes 131072 | tf_op jit(solution)/shard_map/all_to_all | solution.py:457
  53.5 0.6 shard_map.130
  54.1 0.6 broadcast_in_dim.4
  54.7 3.3 %all-to-all-start.6 = ((f32[8,8,128]{2,1,0:T(8,128)}), f32[8,8,128]{2,1,0:T(8,128)S(1)}, u32[]{:S(2)}, u32[]{:S(2)}) async-start(f32[8,8,128]{2,1,0:T(8,128)} %broadcast_in_dim.4), calls=%async_computation.6 | async-start | bytes 65536 | tf_op jit(solution)/shard_map/all_to_all | solution.py:474
  58.1 1.9 %shard_map.126 = bf16[32,8,8,128]{3,2,1,0:T(8,128)(2,1)} custom-call(bf16[32,8,8,128]{3,2,1,0:T(8,128)(2,1)S(1)} %bitcast.5, bf16[32,8,8,128]{3,2,1,0:T(8,128)(2,1)S(1)} %bitcast.6), custom_call_target="tpu_custom_call" | custom-call | flops 4194304 | bytes 1572864 | tf_op jit(solution)/shard_map/pallas_call | solution.py:43
  60.0 4.7 %all-to-all-done.6 = f32[8,8,128]{2,1,0:T(8,128)S(1)} async-done(((f32[8,8,128]{2,1,0:T(8,128)}), f32[8,8,128]{2,1,0:T(8,128)S(1)}, u32[]{:S(2)}, u32[]{:S(2)}) %all-to-all-start.6) | async-done | bytes 32800 | tf_op jit(solution)/shard_map/all_to_all | solution.py:474
  64.7 2.6 %all-to-all-start.2 = ((bf16[32,8,8,128]{3,2,1,0:T(8,128)(2,1)}), bf16[32,8,8,128]{3,2,1,0:T(8,128)(2,1)S(1)}, u32[]{:S(2)}, u32[]{:S(2)}) async-start(bf16[32,8,8,128]{3,2,1,0:T(8,128)(2,1)} %shard_map.126), calls=%async_computation.2 | async-start | bytes 1048576 | tf_op jit(solution)/shard_map/all_to_all | solution.py:457
  67.3 16.3 %all-to-all-done.2.home_ref = bf16[32,8,8,128]{3,2,1,0:T(8,128)(2,1)S(1)} async-done(((bf16[32,8,8,128]{3,2,1,0:T(8,128)(2,1)}), bf16[32,8,8,128]{3,2,1,0:T(8,128)(2,1)S(1)}, u32[]{:S(2)}, u32[]{:S(2)}) %all-to-all-start.2) | async-done | bytes 524320 | tf_op jit(solution)/shard_map/all_to_all | solution.py:457
  83.7 0.6 broadcast_in_dim.5
  84.3 3.2 %all-to-all-start.7 = ((f32[4,8,128]{2,1,0:T(8,128)}), f32[4,8,128]{2,1,0:T(8,128)S(1)}, u32[]{:S(2)}, u32[]{:S(2)}) async-start(f32[4,8,128]{2,1,0:T(8,128)} %broadcast_in_dim.5), calls=%async_computation.7 | async-start | bytes 32768 | tf_op jit(solution)/shard_map/all_to_all | solution.py:474
  87.5 1.4 %copy-done.11 = f32[6,8,64,128]{3,2,1,0:T(8,128)S(1)} copy-done((f32[6,8,64,128]{3,2,1,0:T(8,128)S(1)}, f32[6,8,64,128]{3,2,1,0:T(8,128)}, u32[]{:S(2)}) %copy-start.11) | copy-done | bytes 1572888
  88.9 6.6 %shard_map.127 = (f32[6,8,64,128]{3,2,1,0:T(8,128)S(1)}, bf16[8,64,128]{2,1,0:T(8,128)(2,1)}, bf16[4,64,128]{2,1,0:T(8,128)(2,1)S(1)}) custom-call(s32[1,1,32]{2,1,0:T(1,128)S(1)} %copy-done.14, s32[8,1,512]{2,1,0:T(1,128)S(1)} %bitcast.9, bf16[32,8,128]{2,1,0:T(8,128)(2,1)S(1)} %get-tuple-element.14.picked_ref, ...), custom_call_target="tpu_custom_call" | custom-call | flops 3221225472 | bytes 3145728 | tf_op jit(solution)/shard_map/pallas_call | solution.py:394
  95.5 7.3 %all_to_all.42.from_x = bf16[4,64,128]{2,1,0:T(8,128)(2,1)} all-to-all(bf16[4,64,128]{2,1,0:T(8,128)(2,1)S(1)} %get-tuple-element.18), channel_id=1, replica_groups=mesh['gx'=4,'gy'=8] {'gx'}, dimensions={0} | all-to-all | bytes 131072 | tf_op jit(solution)/shard_map/all_to_all | solution.py:114
  102.8 3.4 %all-to-all-start.3 = ((bf16[8,64,128]{2,1,0:T(8,128)(2,1)}), bf16[8,64,128]{2,1,0:T(8,128)(2,1)S(1)}, u32[]{:S(2)}, u32[]{:S(2)}) async-start(bf16[8,64,128]{2,1,0:T(8,128)(2,1)} %get-tuple-element.17), calls=%async_computation.3 | async-start | bytes 262144 | tf_op jit(solution)/shard_map/all_to_all | solution.py:114
  106.2 0.6 slice_multiply_fusion
  106.8 2.8 %copy-done = bf16[6,8,8,64,128]{4,3,2,1,0:T(8,128)(2,1)S(1)} copy-done((bf16[6,8,8,64,128]{4,3,2,1,0:T(8,128)(2,1)S(1)}, bf16[6,8,8,64,128]{4,3,2,1,0:T(8,128)(2,1)}, u32[]{:S(2)}) %copy-start) | copy-done | bytes 6291480
  109.6 1.4 %shard_map.128.before_ref = f32[6,8,64,128]{3,2,1,0:T(8,128)S(1)} custom-call(f32[6,8,64,128]{3,2,1,0:T(8,128)S(1)} %get-tuple-element.16.field_ref, s32[64,128]{1,0:T(8,128)S(1)} %copy-done.7, bf16[6,8,8,64,128]{4,3,2,1,0:T(8,128)(2,1)S(1)} %copy-done), custom_call_target="tpu_custom_call" | custom-call | flops 6291456 | bytes 9437184 | tf_op jit(solution)/shard_map/pallas_call | solution.py:140
  111.0 2.4 %all-to-all-done.3.from_y = bf16[8,64,128]{2,1,0:T(8,128)(2,1)S(1)} async-done(((bf16[8,64,128]{2,1,0:T(8,128)(2,1)}), bf16[8,64,128]{2,1,0:T(8,128)(2,1)S(1)}, u32[]{:S(2)}, u32[]{:S(2)}) %all-to-all-start.3) | async-done | bytes 131104 | tf_op jit(solution)/shard_map/all_to_all | solution.py:114
  113.5 2.8 %copy-done.1 = bf16[6,8,8,64,128]{4,3,2,1,0:T(8,128)(2,1)S(1)} copy-done((bf16[6,8,8,64,128]{4,3,2,1,0:T(8,128)(2,1)S(1)}, bf16[6,8,8,64,128]{4,3,2,1,0:T(8,128)(2,1)}, u32[]{:S(2)}) %copy-start.1) | copy-done | bytes 6291480
  116.2 0.8 copy-done.9
  117.1 4.3 %shard_map.129 = f32[6,8,64,128]{3,2,1,0:T(8,128)} custom-call(f32[6,8,64,128]{3,2,1,0:T(8,128)S(1)} %shard_map.128.before_ref, f32[6,8,64,128]{3,2,1,0:T(8,128)S(1)} %get-tuple-element.16.field_ref, s32[64,128]{1,0:T(8,128)S(1)} %copy-done.7, f32[6,64,128]{2,1,0:T(8,128)S(1)} %copy-done.5, bf16[8,64,128]{2,1,0:T(8,128)(2,1)S(1)} %all-to-all-done.3.from_y, ...), custom_call_target="tpu_custom_call" | custom-call | flops 12582912 | bytes 11010048 | tf_op jit(solution)/shard_map/pallas_call | solution.py:272
  (27 shorter events, 0.4 us)
Async XLA Ops:
  0.6 1.4 %copy-start.2 = (f32[6,8,64,128]{3,2,1,0:T(8,128)S(1)}, f32[6,8,64,128]{3,2,1,0:T(8,128)}, u32[]{:S(2)}) copy-start(f32[6,8,64,128]{3,2,1,0:T(8,128)} %field_ref.5) | copy-start | bytes 4718596
  2.0 0.9 copy-start.4
  3.0 0.8 copy-start.6
  12.9 13.5 %all-to-all-start = ((bf16[8,64,128]{2,1,0:T(8,128)(2,1)}), bf16[8,64,128]{2,1,0:T(8,128)(2,1)S(1)}, u32[]{:S(2)}, u32[]{:S(2)}) async-start(bf16[8,64,128]{2,1,0:T(8,128)(2,1)} %get-tuple-element.11), calls=%async_computation | async-start | bytes 262144 | tf_op jit(solution)/shard_map/all_to_all | solution.py:114
  26.0 9.1 %copy-start.13 = (s32[1,1,4096]{2,1,0:T(1,128)S(1)}, s32[1,1,4096]{2,1,0:T(1,128)}, u32[]{:S(2)}) copy-start(s32[1,1,4096]{2,1,0:T(1,128)} %param.16) | copy-start | bytes 49156
  26.0 9.1 %copy-start.14 = (s32[1,1,32]{2,1,0:T(1,128)S(1)}, s32[1,1,32]{2,1,0:T(1,128)}, u32[]{:S(2)}) copy-start(s32[1,1,32]{2,1,0:T(1,128)} %helper_ref.3) | copy-start | bytes 388
  26.4 0.6 copy-start.15
  35.1 1.1 copy-start.12
  36.3 17.2 %copy-start.3 = (bf16[1,1,32,8,8,128]{5,4,3,2,1,0:T(8,128)(2,1)S(1)}, bf16[1,1,32,8,8,128]{5,4,3,2,1,0:T(8,128)(2,1)}, u32[]{:S(2)}) copy-start(bf16[1,1,32,8,8,128]{5,4,3,2,1,0:T(8,128)(2,1)} %param.19) | copy-start | bytes 1572868
  36.3 17.2 %copy-start.10 = (bf16[1,1,32,8,128]{4,3,2,1,0:T(8,128)(2,1)S(1)}, bf16[1,1,32,8,128]{4,3,2,1,0:T(8,128)(2,1)}, u32[]{:S(2)}) copy-start(bf16[1,1,32,8,128]{4,3,2,1,0:T(8,128)(2,1)} %param.21) | copy-start | bytes 196612
  36.3 21.8 %copy-start.8 = (bf16[1,1,32,8,8,128]{5,4,3,2,1,0:T(8,128)(2,1)S(1)}, bf16[1,1,32,8,8,128]{5,4,3,2,1,0:T(8,128)(2,1)}, u32[]{:S(2)}) copy-start(bf16[1,1,32,8,8,128]{5,4,3,2,1,0:T(8,128)(2,1)} %param.20) | copy-start | bytes 1572868
  54.1 33.4 %copy-start.5 = (f32[6,64,128]{2,1,0:T(8,128)S(1)}, f32[6,64,128]{2,1,0:T(8,128)}, u32[]{:S(2)}) copy-start(f32[6,64,128]{2,1,0:T(8,128)} %perm_ref.7) | copy-start | bytes 589828
  54.1 33.4 %copy-start.7 = (s32[64,128]{1,0:T(8,128)S(1)}, s32[64,128]{1,0:T(8,128)}, u32[]{:S(2)}) copy-start(s32[64,128]{1,0:T(8,128)} %mask_ref.11) | copy-start | bytes 98308
  54.7 10.0 %all-to-all-start.6 = ((f32[8,8,128]{2,1,0:T(8,128)}), f32[8,8,128]{2,1,0:T(8,128)S(1)}, u32[]{:S(2)}, u32[]{:S(2)}) async-start(f32[8,8,128]{2,1,0:T(8,128)} %broadcast_in_dim.4), calls=%async_computation.6 | async-start | bytes 65536 | tf_op jit(solution)/shard_map/all_to_all | solution.py:474
  64.7 19.0 %all-to-all-start.2 = ((bf16[32,8,8,128]{3,2,1,0:T(8,128)(2,1)}), bf16[32,8,8,128]{3,2,1,0:T(8,128)(2,1)S(1)}, u32[]{:S(2)}, u32[]{:S(2)}) async-start(bf16[32,8,8,128]{3,2,1,0:T(8,128)(2,1)} %shard_map.126), calls=%async_computation.2 | async-start | bytes 1048576 | tf_op jit(solution)/shard_map/all_to_all | solution.py:457
  84.3 11.3 %all-to-all-start.7 = ((f32[4,8,128]{2,1,0:T(8,128)}), f32[4,8,128]{2,1,0:T(8,128)S(1)}, u32[]{:S(2)}, u32[]{:S(2)}) async-start(f32[4,8,128]{2,1,0:T(8,128)} %broadcast_in_dim.5), calls=%async_computation.7 | async-start | bytes 32768 | tf_op jit(solution)/shard_map/all_to_all | solution.py:474
  87.5 1.4 %copy-start.11 = (f32[6,8,64,128]{3,2,1,0:T(8,128)S(1)}, f32[6,8,64,128]{3,2,1,0:T(8,128)}, u32[]{:S(2)}) copy-start(f32[6,8,64,128]{3,2,1,0:T(8,128)} %get-tuple-element.15.first_ref) | copy-start | bytes 4718596
  102.8 10.7 %all-to-all-start.3 = ((bf16[8,64,128]{2,1,0:T(8,128)(2,1)}), bf16[8,64,128]{2,1,0:T(8,128)(2,1)S(1)}, u32[]{:S(2)}, u32[]{:S(2)}) async-start(bf16[8,64,128]{2,1,0:T(8,128)(2,1)} %get-tuple-element.17), calls=%async_computation.3 | async-start | bytes 262144 | tf_op jit(solution)/shard_map/all_to_all | solution.py:114
  106.8 2.8 %copy-start = (bf16[6,8,8,64,128]{4,3,2,1,0:T(8,128)(2,1)S(1)}, bf16[6,8,8,64,128]{4,3,2,1,0:T(8,128)(2,1)}, u32[]{:S(2)}) copy-start(bf16[6,8,8,64,128]{4,3,2,1,0:T(8,128)(2,1)} %block_ref.6) | copy-start | bytes 18874372
  113.5 2.8 %copy-start.1 = (bf16[6,8,8,64,128]{4,3,2,1,0:T(8,128)(2,1)S(1)}, bf16[6,8,8,64,128]{4,3,2,1,0:T(8,128)(2,1)}, u32[]{:S(2)}) copy-start(bf16[6,8,8,64,128]{4,3,2,1,0:T(8,128)(2,1)} %block_ref.7) | copy-start | bytes 18874372
  116.2 0.8 copy-start.9

commit v3 on v1

v3 whole, which is shorter than its diff:
```python
import functools
import math

import jax
import jax.numpy as jnp
from jax import lax
from jax.experimental import pallas as pl
from jax.experimental.pallas import tpu as pltpu
from jax.sharding import PartitionSpec as P

F32 = jnp.float32
BF16 = jnp.bfloat16
AXES = ("gx", "gy")
MIB = 1024 * 1024
CHUNK = 512


def params(mib):
    return pltpu.CompilerParams(vmem_limit_bytes=mib * MIB)


def cost(flops, moved):
    return pl.CostEstimate(flops=int(flops), bytes_accessed=int(moved), transcendentals=0)


def round_up(number, step):
    return -(-number // step) * step


def write_edges(field, comps, clear, perm_ref, side_y, sends):
    send_y_0, send_y_1, send_x = sends
    layers, rows, cols = perm_ref.shape
    lane = lax.broadcasted_iota(jnp.int32, (rows, cols), 1)
    pair = lane // 2
    along_x = jnp.zeros((rows, cols), F32)
    side_y[...] = jnp.zeros_like(side_y)
    for k in range(layers):
        for c in range(comps + 1):
            if c < comps:
                value, at = field(k, c) * clear, k * comps + c
            else:
                value, at = perm_ref[k], layers * comps + k
            side_y[0, at : at + 1, :] = value[0:1]
            side_y[1, at : at + 1, :] = value[rows - 1 : rows]
            along_x = jnp.where(pair == at, pltpu.roll(value, (2 * at + 1) % cols, 1), along_x)
    even = lax.axis_index("gy") % 2 == 0
    send_x[...] = along_x.astype(BF16)
    low, high = side_y[0].astype(BF16), side_y[1].astype(BF16)
    send_y_0[...] = jnp.where(even, high, low)
    send_y_1[...] = jnp.where(even, low, high)


def fetch(copies):
    for copy in copies:
        copy.start()
    for copy in copies:
        copy.wait()


def opening_kernel(
    inverse_hbm, coupling_hbm, field_hbm, mask_hbm, perm_hbm,
    product_ref, send_y_0, send_y_1, send_x,
    inverse_ref, coupling_ref, field_ref, mask_ref, perm_ref, side_y, sems,
):
    sources = (inverse_hbm, coupling_hbm, field_hbm, mask_hbm, perm_hbm)
    targets = (inverse_ref, coupling_ref, field_ref, mask_ref, perm_ref)
    copies = [pltpu.make_async_copy(a, b, sems.at[i]) for i, (a, b) in enumerate(zip(sources, targets))]
    for copy in copies:
        copy.start()
    blocks, comps = inverse_ref.shape[:2]
    copies[0].wait()
    copies[1].wait()

    def one(b, carry):
        inverse = inverse_ref[b].astype(F32)
        coupling = coupling_ref[b].astype(F32)
        for r in range(comps):
            row = inverse[r, 0:1] * coupling[0]
            for m in range(1, comps):
                row += inverse[r, m : m + 1] * coupling[m]
            product_ref[b, r] = row.astype(BF16)
        return carry

    lax.fori_loop(0, blocks, one, 0)
    for copy in copies[2:]:
        copy.wait()
    clear = 1.0 - mask_ref[...].astype(F32)
    sends = (send_y_0, send_y_1, send_x)
    write_edges(lambda k, c: field_ref[k, c], comps, clear, perm_ref, side_y, sends)


def edge_rows(layers, comps):
    return round_up(layers * (comps + 1), 16)


def edge_shapes(layers, comps, rows, cols):
    along_y = (edge_rows(layers, comps), cols)
    return [jax.ShapeDtypeStruct(shape, BF16) for shape in (along_y, along_y, (rows, cols))]


def edge_scratch(layers, comps, cols):
    return pltpu.VMEM((2, edge_rows(layers, comps), cols), F32)


def opening(inverse, coupling, field, mask, perm):
    layers, comps, rows, cols = field.shape
    hbm = pl.BlockSpec(memory_space=pltpu.HBM)
    vmem = pl.BlockSpec(memory_space=pltpu.VMEM)
    arrays = (inverse, coupling, field, mask, perm)
    return pl.pallas_call(
        opening_kernel,
        in_specs=[hbm] * 5,
        out_specs=[vmem] * 4,
        out_shape=[jax.ShapeDtypeStruct(inverse.shape, BF16), *edge_shapes(*field.shape)],
        scratch_shapes=[
            *(pltpu.VMEM(array.shape, array.dtype) for array in arrays),
            edge_scratch(layers, comps, cols),
            pltpu.SemaphoreType.DMA((5,)),
        ],
        compiler_params=params(56),
        cost_estimate=cost(16 * inverse.size + 4 * field.size, 6 * inverse.size + 4 * field.size),
    )(*arrays)


def exchange(send_y_0, send_y_1, send_x):
    def swaps(axis, first, second):
        count = lax.axis_size(axis)
        results = []
        for start, array in ((0, first), (1, second)):
            pairs = [(i, i + 1) for i in range(start, count - 1, 2)]
            results.append(lax.ppermute(array, axis, pairs + [(j, i) for i, j in pairs]))
        return results

    return (*swaps("gy", send_y_0, send_y_1), *swaps("gx", send_x, send_x))


TILE = 16
AHEAD = 3


def reciprocal(value):
    guess = pl.reciprocal(value, approx=True)
    return guess * (2.0 - value * guess)


def weight(centre, beside):
    return 2.0 * centre * beside * reciprocal(centre + beside)


def apply_kernel(want_rounded, field_hbm, mask_hbm, perm_hbm, y_0, y_1, x_0, x_1, diag_hbm, flux_hbm, *rest):
    if want_rounded:
        out_hbm, rounded_hbm, *rest, rounded_ref, rounded_sems = rest
    else:
        out_hbm, *rest = rest
    *rest, out_ref, out_sems = rest
    (field_ref, mask_ref, perm_ref, diag_ref, flux_ref, padded, padded_perm, edge_x, place, beside_edge, perm_edge, sems) = rest
    layers, comps, rows, cols = field_ref.shape
    top = 8

    def blocks(k):
        return (
            pltpu.make_async_copy(diag_hbm.at[k], diag_ref.at[k], sems.at[3 + k]),
            pltpu.make_async_copy(flux_hbm.at[k], flux_ref.at[k], sems.at[3 + layers + k]),
        )

    def out_copies(k):
        copies = [pltpu.make_async_copy(out_ref.at[k], out_hbm.at[k], out_sems.at[k])]
        if want_rounded:
            columns = pl.ds(pl.multiple_of(k * cols, cols), cols)
            source, target = rounded_ref.at[:, columns], rounded_hbm.at[:, columns]
            copies.append(pltpu.make_async_copy(source, target, rounded_sems.at[k]))
        return copies

    smalls = [
        pltpu.make_async_copy(field_hbm, field_ref, sems.at[0]),
        pltpu.make_async_copy(mask_hbm, mask_ref, sems.at[1]),
        pltpu.make_async_copy(perm_hbm, perm_ref, sems.at[2]),
    ]
    for copy in smalls:
        copy.start()
    for k in range(min(AHEAD, layers)):
        for copy in blocks(k):
            copy.start()

    lane = lax.broadcasted_iota(jnp.int32, (rows, cols), 1)
    number = lax.broadcasted_iota(jnp.int32, (cols, cols), 0)
    spot = lax.broadcasted_iota(jnp.int32, (cols, cols), 1)
    for r in range(comps):
        taken = ((number == 2 * r) & (spot == 0)) | ((number == 2 * r + 1) & (spot == cols - 1))
        place[:, r * cols : (r + 1) * cols] = jnp.where(taken, 1.0, 0.0).astype(BF16)
    even_x = lax.axis_index("gx") % 2 == 0
    even_y = lax.axis_index("gy") % 2 == 0
    side_0, side_1 = x_0[...].astype(F32), x_1[...].astype(F32)
    edge_x[...] = jnp.where((lane % 2 == 0) == even_x, side_1, side_0)
    for copy in smalls:
        copy.wait()
    clear = 1.0 - mask_ref[...].astype(F32)

    def layer(k, carry):
        above = jnp.minimum(k + 1, layers - 1)
        below = jnp.maximum(k - 1, 0)

        @pl.when(k + AHEAD < layers)
        def _():
            for copy in blocks(k + AHEAD):
                copy.start()

        turned = pltpu.roll(edge_x[...], lax.rem(cols - 2 * comps * k, cols), 1).astype(BF16)
        beside_edge[...] = jnp.dot(turned, place[...], preferred_element_type=F32)
        at_low = 2 * (layers * comps + k)
        perm_low = pltpu.roll(edge_x[...], lax.rem(cols - at_low, cols), 1)
        perm_high = pltpu.roll(edge_x[...], lax.rem(2 * cols - at_low - 2, cols), 1)
        perm_edge[...] = jnp.where(lane == 0, perm_low, perm_high)

        odd = k % 2 == 1
        here = pl.ds(pl.multiple_of(16 * (k // 2), 16), 16)
        side_0, side_1 = y_0[here].astype(F32), y_1[here].astype(F32)
        side_0 = jnp.where(odd, side_0[comps:], side_0[:comps])
        side_1 = jnp.where(odd, side_1[comps:], side_1[:comps])
        low_y, high_y = jnp.where(even_y, side_1, side_0), jnp.where(even_y, side_0, side_1)
        here = slice(layers * comps, layers * comps + 16)
        mine = lax.broadcasted_iota(jnp.int32, (16, cols), 0) == k
        perm_0 = jnp.sum(jnp.where(mine, y_0[here].astype(F32), 0.0), axis=0, keepdims=True)
        perm_1 = jnp.sum(jnp.where(mine, y_1[here].astype(F32), 0.0), axis=0, keepdims=True)
        for c in range(comps):
            padded[c, top : top + rows] = field_ref[k, c] * clear
            padded[c, top - 1 : top] = low_y[c : c + 1]
            padded[c, top + rows : top + rows + 1] = high_y[c : c + 1]
        padded_perm[top : top + rows] = perm_ref[k]
        padded_perm[top - 1 : top] = jnp.where(even_y, perm_1, perm_0)
        padded_perm[top + rows : top + rows + 1] = jnp.where(even_y, perm_0, perm_1)
        for copy in blocks(k):
            copy.wait()

        narrow = lax.broadcasted_iota(jnp.int32, (TILE, cols), 1)
        is_first, is_last = narrow == 0, narrow == cols - 1
        for y in range(0, rows, TILE):
            here = slice(y, y + TILE)
            at = top + y
            well = mask_ref[here].astype(F32)
            free = 1.0 - well
            centre = perm_ref[k, here]
            perm_beside = perm_edge[here]
            perm_left = jnp.where(is_first, perm_beside, pltpu.roll(centre, 1, 1))
            perm_right = jnp.where(is_last, perm_beside, pltpu.roll(centre, cols - 1, 1))
            to_left, to_right = weight(centre, perm_left), weight(centre, perm_right)
            weights = [
                jnp.where(k < layers - 1, weight(centre, perm_ref[above, here]), 0.0) * free,
                jnp.where(k > 0, weight(centre, perm_ref[below, here]), 0.0) * free,
                weight(centre, padded_perm[at + 1 : at + 1 + TILE]),
                weight(centre, padded_perm[at - 1 : at - 1 + TILE]),
                jnp.where(is_last, 0.0, to_right),
                jnp.where(is_first, 0.0, to_left),
                jnp.where(is_first, to_left, jnp.where(is_last, to_right, 0.0)),
            ]
            total = [None] * comps
            for r in range(comps):
                own = padded[r, at : at + TILE]
                summed = (
                    weights[0] * field_ref[above, r, here]
                    + weights[1] * field_ref[below, r, here]
                    + weights[2] * padded[r, at + 1 : at + 1 + TILE]
                    + weights[3] * padded[r, at - 1 : at - 1 + TILE]
                    + weights[4] * pltpu.roll(own, cols - 1, 1)
                    + weights[5] * pltpu.roll(own, 1, 1)
                    + weights[6] * beside_edge[here, r * cols : (r + 1) * cols]
                )
                for c in range(comps):
                    term = diag_ref[k, r, c, here].astype(F32) * own - flux_ref[k, r, c, here].astype(F32) * summed
                    total[c] = term if r == 0 else total[c] + term
            for c in range(comps):
                value = total[c] + well * field_ref[k, c, here]
                out_ref[k, c, here] = value
                if want_rounded:
                    columns = pl.ds(pl.multiple_of(k * cols, cols), cols)
                    rounded_ref[c * rows + y : c * rows + y + TILE, columns] = value.astype(BF16)
        for copy in out_copies(k):
            copy.start()
        return carry

    lax.fori_loop(0, layers, layer, 0)
    for k in range(layers):
        for copy in out_copies(k):
            copy.wait()


def apply_transposed(field, mask, perm, halos, diag, flux, want_rounded, mib):
    layers, comps, rows, cols = field.shape
    hbm = pl.BlockSpec(memory_space=pltpu.HBM)
    vmem = pl.BlockSpec(memory_space=pltpu.VMEM)
    out_shape = [jax.ShapeDtypeStruct(field.shape, F32)]
    extra = []
    if want_rounded:
        out_shape.append(jax.ShapeDtypeStruct((comps * rows, layers * cols), BF16))
        extra = [pltpu.VMEM(out_shape[1].shape, BF16), pltpu.SemaphoreType.DMA((layers,))]
    return pl.pallas_call(
        functools.partial(apply_kernel, want_rounded),
        in_specs=[pl.BlockSpec(memory_space=pl.ANY), hbm, hbm, *[vmem] * 4, hbm, hbm],
        out_specs=[hbm] * len(out_shape),
        out_shape=out_shape,
        scratch_shapes=[
            pltpu.VMEM(field.shape, F32),
            pltpu.VMEM(mask.shape, mask.dtype),
            pltpu.VMEM(perm.shape, F32),
            pltpu.VMEM(diag.shape, BF16),
            pltpu.VMEM(flux.shape, BF16),
            pltpu.VMEM((comps, rows + 16, cols), F32),
            pltpu.VMEM((rows + 16, cols), F32),
            pltpu.VMEM((rows, cols), F32),
            pltpu.VMEM((cols, comps * cols), BF16),
            pltpu.VMEM((rows, comps * cols), F32),
            pltpu.VMEM((rows, cols), F32),
            pltpu.SemaphoreType.DMA((3 + 2 * layers,)),
            pltpu.VMEM(field.shape, F32),
            pltpu.SemaphoreType.DMA((layers,)),
            *extra,
        ],
        compiler_params=params(mib),
        cost_estimate=cost(8 * diag.size, 4 * diag.size + 8 * field.size),
    )(field, mask, perm, *halos, diag, flux)


def split_cells(cells, rows, cols):
    layer = cells // (rows * cols)
    y = (cells // cols) % rows
    return layer * cols + cells % cols, y


def one_hot(column, count, slots):
    number = lax.broadcasted_iota(jnp.int32, (count, slots), 0)
    return jnp.where(number == column, 1.0, 0.0).astype(BF16)


def gather_kernel(rows, cols, helper_ref, count_ref, cells_ref, rounded_ref, picked_ref, sent_ref):
    chunks, _, slots = cells_ref.shape
    width = picked_ref.shape[-1]
    comps = picked_ref.shape[1]
    per_chunk = slots // width
    row_number = lax.broadcasted_iota(jnp.int32, (rows, slots), 0)

    def one(i, carry):
        column, y = split_cells(cells_ref[i], rows, cols)
        chosen = one_hot(column, rounded_ref.shape[1], slots)
        found = jnp.dot(rounded_ref[...], chosen, preferred_element_type=F32)
        at_row = row_number == y
        values = [
            jnp.sum(jnp.where(at_row, found[c * rows : (c + 1) * rows], 0.0), axis=0, keepdims=True)
            for c in range(comps)
        ]
        values = jnp.concatenate(values, axis=0)
        for j in range(per_chunk):
            b = i * per_chunk + j
            live = jnp.where(b < count_ref[0, 0], 1.0, 0.0)
            value = (values[:, j * width : (j + 1) * width] * live).astype(BF16)
            picked_ref[b] = value
            sent_ref[helper_ref[0, 0, b]] = value
        return carry

    lax.fori_loop(0, chunks, one, 0)


def gather(rounded, cells, helper, count, comps, rows, cols, width):
    blocks = helper.shape[-1]
    shape = jax.ShapeDtypeStruct((blocks, comps, width), BF16)
    smem = pl.BlockSpec(memory_space=pltpu.SMEM)
    vmem = pl.BlockSpec(memory_space=pltpu.VMEM)
    return pl.pallas_call(
        functools.partial(gather_kernel, rows, cols),
        in_specs=[smem, smem, vmem, vmem],
        out_specs=[vmem, vmem],
        out_shape=[shape, shape],
        compiler_params=params(32),
        cost_estimate=cost(2 * rounded.size * cells.size, 2 * rounded.size),
    )(helper, count, cells, rounded)


def scatter_kernel(
    helper_ref, cells_ref, picked_ref, home_ref, first_ref, mask_ref, perm_ref,
    second_ref, send_y_0, send_y_1, send_x, added, side_y,
):
    layers, comps, rows, cols = first_ref.shape
    chunks, _, slots = cells_ref.shape
    width = picked_ref.shape[-1]
    per_chunk = slots // width
    row_number = lax.broadcasted_iota(jnp.int32, (rows, slots), 0)
    added[...] = jnp.zeros_like(added)

    def one(i, carry):
        column, y = split_cells(cells_ref[i], rows, cols)
        chosen = one_hot(column, added.shape[1], slots)
        parts = []
        for j in range(per_chunk):
            b = i * per_chunk + j
            home = home_ref[helper_ref[0, 0, b]].astype(F32)
            value = picked_ref[b].astype(F32)
            part = home[0] * value[0:1]
            for r in range(1, comps):
                part += home[r] * value[r : r + 1]
            parts.append((-part).astype(BF16).astype(F32))
        correction = jnp.concatenate(parts, axis=1)
        at_row = row_number == y
        spread = jnp.concatenate(
            [jnp.where(at_row, correction[c : c + 1], 0.0).astype(BF16) for c in range(comps)], axis=0
        )
        added[...] += lax.dot_general(spread, chosen, (((1,), (1,)), ((), ())), preferred_element_type=F32)
        return carry

    lax.fori_loop(0, chunks, one, 0)
    for k in range(layers):
        for c in range(comps):
            second_ref[k, c] = first_ref[k, c] + added[c * rows : (c + 1) * rows, k * cols : (k + 1) * cols]
    clear = 1.0 - mask_ref[...].astype(F32)
    sends = (send_y_0, send_y_1, send_x)
    write_edges(lambda k, c: second_ref[k, c], comps, clear, perm_ref, side_y, sends)


def scatter(first, picked, home, helper, cells, mask, perm):
    layers, comps, rows, cols = first.shape
    smem = pl.BlockSpec(memory_space=pltpu.SMEM)
    vmem = pl.BlockSpec(memory_space=pltpu.VMEM)
    return pl.pallas_call(
        scatter_kernel,
        in_specs=[smem] + [vmem] * 6,
        out_specs=[vmem] * 4,
        out_shape=[jax.ShapeDtypeStruct(first.shape, F32), *edge_shapes(*first.shape)],
        scratch_shapes=[pltpu.VMEM((comps * rows, layers * cols), F32), edge_scratch(layers, comps, cols)],
        compiler_params=params(40),
        cost_estimate=cost(2 * first.size * cells.size, 8 * first.size),
    )(helper, cells, picked, home, first, mask, perm)


GROUPS = 4


def grad_kernel(inverse_ref, state_ref, picked_ref, out_ref):
    blocks, comps = inverse_ref.shape[:2]
    width = inverse_ref.shape[-1]

    def one(b, totals):
        inverse = inverse_ref[b].astype(F32)
        value = picked_ref[b].astype(F32)
        state = state_ref[b].astype(F32)
        part = inverse[0] * value[0:1]
        for r in range(1, comps):
            part += inverse[r] * value[r : r + 1]
        part *= state
        return tuple(totals[j] + part * state[j : j + 1] for j in range(comps))

    share = blocks // GROUPS
    for g in range(GROUPS):
        totals = lax.fori_loop(g * share, (g + 1) * share, one, (jnp.zeros((comps, width), F32),) * comps)
        for j in range(comps):
            out_ref[g, j] = totals[j]


def grad_part(inverse, state, picked):
    comps, width = inverse.shape[1], inverse.shape[-1]
    return pl.pallas_call(
        grad_kernel,
        out_shape=jax.ShapeDtypeStruct((GROUPS, comps, comps, width), F32),
        compiler_params=params(24),
        cost_estimate=cost(4 * inverse.size, 2 * inverse.size),
    )(inverse, state, picked)


def shards(
    cotangent,
    permeability,
    well_mask,
    diag_block,
    flux_block,
    cell_list,
    block_count,
    helper_of,
    flash_inverse,
    flash_coupling,
    phase_state,
):
    layers, comps, rows, cols = cotangent.shape
    blocks, width = helper_of.shape[-1], flash_inverse.shape[-1]
    inverse = flash_inverse.reshape(blocks, comps, comps, width)
    coupling = flash_coupling.reshape(blocks, comps, comps, width)
    state = phase_state.reshape(blocks, comps, width)
    cells = cell_list.reshape(-1, 1, min(CHUNK, cell_list.shape[-1]))

    def to_partners(array):
        return lax.all_to_all(array, AXES, split_axis=0, concat_axis=0, tiled=True)

    product, *sides = opening(inverse, coupling, cotangent, well_mask, permeability)
    home = to_partners(product)
    halos = exchange(*sides)
    first, rounded = apply_transposed(cotangent, well_mask, permeability, halos, diag_block, flux_block, True, 56)
    rounded, home = lax.optimization_barrier((rounded, home))
    picked, sent = gather(rounded, cells, helper_of, block_count, comps, rows, cols, width)
    at_helper = to_partners(sent)
    second, *sides = scatter(first, picked, home, helper_of, cells, well_mask, permeability)
    halos = exchange(*sides)
    (adjoint,) = apply_transposed(second, well_mask, permeability, halos, diag_block, flux_block, False, 32)

    totals = lax.psum(grad_part(inverse, state, at_helper), AXES)
    devices = lax.axis_size("gx") * lax.axis_size("gy")
    grad_scale = 1.0 / math.sqrt(width * devices * devices)
    interaction_grad = -grad_scale * jnp.sum(totals, axis=(0, 3)).T
    return (adjoint, interaction_grad)


def solution(mesh):
    return jax.shard_map(
        shards,
        mesh=mesh,
        in_specs=(
            P(None, None, "gy", "gx"),
            P(None, "gy", "gx"),
            P("gy", "gx"),
            P(None, None, None, "gy", "gx"),
            P(None, None, None, "gy", "gx"),
            P("gy", "gx", None),
            P("gy", "gx"),
            P("gy", "gx", None),
            P("gy", "gx", None, None, None, None),
            P("gy", "gx", None, None, None, None),
            P("gy", "gx", None, None, None),
        ),
        out_specs=(P(None, None, "gy", "gx"), P()),
        check_vma=False,
    )
```

time: 153 us -> 190 us (1.24)
  the two profiles are of different devices: /device:TPU:9 before, /device:TPU:0 now
where the time goes in v3:
time: 190 us; the launch traced here: 189 us
  waiting for transfers between devices  99 us (52%)
  Pallas kernels  32.9 us (17%)
  blocking collectives  18.4 us (10%)
  starting transfers between devices  17.6 us (9%)
  between operations  14.9 us (8%)
  local copies, waits for them, and re-layouts  5.52 us (3%)
    psum x1, waiting for transfers between devices, shards(): totals = lax.psum(grad_part(inverse, state, at_helper), AXES)  97.8 us
    all_to_all x1, blocking collectives, to_partners(): return lax.all_to_all(array, AXES, split_axis=0, concat_axis=0, tiled=True)  18.4 us
    pallas_call x2, Pallas kernels, apply_transposed(): pl.pallas_call(functools.partial(apply_kernel, want_rounded), in_specs=[p...  17 us
    ppermute x8, starting transfers between devices, swaps(): lax.ppermute(array, axis, pairs + [(j, i) for i, j in pairs])  10.3 us
    all_to_all x1, starting transfers between devices, to_partners(): return lax.all_to_all(array, AXES, split_axis=0, concat_axis=0, tiled=True)  7.3 us
    pallas_call x1, Pallas kernels, scatter(): pl.pallas_call(scatter_kernel, in_specs=[smem] + [vmem] * 6, out_specs=[v...  6.05 us
    unnamed x31, local copies, waits for them, and re-layouts  5.52 us
    pallas_call x1, Pallas kernels, gather(): pl.pallas_call(functools.partial(gather_kernel, rows, cols), in_specs=[sm...  5.36 us
  transfers between devices with their start and end apart: 10, of which 3 were waited for; matrix products, arithmetic and copies ran while one was open for 0% of the time, Pallas kernels for 12%

profile of v3, /device:TPU:0, one launch (start us, length us, event | category | flops | bytes accessed | tf_op | source)
XLA Modules:
  0.0 189.3 jit_solution(7921099879644801343)
XLA Ops:
  7.2 3.4 %shard_map.122 = (bf16[32,8,8,128]{3,2,1,0:T(8,128)(2,1)}, bf16[64,128]{1,0:T(8,128)(2,1)}, bf16[64,128]{1,0:T(8,128)(2,1)}, bf16[64,128]{1,0:T(8,128)(2,1)}) custom-call(bf16[32,8,8,128]{3,2,1,0:T(8,128)(2,1)} %bitcast.8, bf16[32,8,8,128]{3,2,1,0:T(8,128)(2,1)} %bitcast.13, f32[6,8,64,128]{3,2,1,0:T(8,128)} %field_hbm.3, s32[64,128]{1,0:T(8,128)} %mask_hbm.5, ...), custom_call_target="tpu_custom_call" | custom-call | flops 5767168 | bytes 3145728 | tf_op jit(solution)/shard_map/pallas_call | solution.py:110
  10.6 7.3 %all-to-all-start = ((bf16[32,8,8,128]{3,2,1,0:T(8,128)(2,1)}), bf16[32,8,8,128]{3,2,1,0:T(8,128)(2,1)S(1)}, u32[]{:S(2)}, u32[]{:S(2)}) async-start(bf16[32,8,8,128]{3,2,1,0:T(8,128)(2,1)} %get-tuple-element.20), calls=%async_computation | async-start | bytes 1048576 | tf_op jit(solution)/shard_map/all_to_all | solution.py:487
  17.9 0.0 all-reduce.2.cloned.1.call-start
  17.9 1.8 collective-permute-start
  19.8 0.7 collective-permute-start.1
  20.4 0.7 collective-permute-start.3
  21.1 2.9 %collective-permute-start.2 = (bf16[64,128]{1,0:T(8,128)(2,1)}, bf16[64,128]{1,0:T(8,128)(2,1)S(1)}, u32[]{:S(2)}, u32[]{:S(2)}) collective-permute-start(bf16[64,128]{1,0:T(8,128)(2,1)} %get-tuple-element.18), channel_id=1, source_target_pairs={{0,8},{16,24},{8,0},{24,16},{1,9},{17,25},{9,1},{25,17},{2,10},{18... | collective-permute-start | bytes 49160 | tf_op jit(solution)/shard_map/ppermute | solution.py:131
  24.6 0.0 copy-start.7
  24.6 0.0 copy-start.8
  24.7 0.3 collective-permute-done.2.x_0
  25.0 0.2 copy-done.9
  25.3 0.0 copy-done.10
  25.3 0.0 copy-done.11
  25.3 0.6 copy-done.12
  25.9 9.3 %shard_map.123 = (f32[6,8,64,128]{3,2,1,0:T(8,128)}, bf16[512,768]{1,0:T(8,128)(2,1)}) custom-call(f32[6,8,64,128]{3,2,1,0:T(8,128)} %field_hbm.3, s32[64,128]{1,0:T(8,128)} %mask_hbm.5, f32[6,64,128]{2,1,0:T(8,128)} %perm_hbm.5, bf16[64,128]{1,0:T(8,128)(2,1)} %copy-done.9, bf16[64,128]{1,0:T(8,128)(2,1)} %copy-done.10, bf16[64,128]{1,0:T(8,128)(2,1)} %copy-done.12, ...), custom_call_target="tpu_custom_call" | custom-call | flops 25165824 | bytes 15728640 | tf_op jit(solution)/shard_map/pallas_call | solution.py:296
  35.2 1.1 copy-done.6
  36.4 5.4 %shard_map.124 = (bf16[32,8,128]{2,1,0:T(8,128)(2,1)S(1)}, bf16[32,8,128]{2,1,0:T(8,128)(2,1)S(1)}) custom-call(s32[1,1,32]{2,1,0:T(1,128)S(1)} %copy-done.8, s32[1,1]{1,0:T(1,128)S(6)} %copy.15.count_ref, s32[8,1,512]{2,1,0:T(1,128)S(1)} %bitcast.11, bf16[512,768]{1,0:T(8,128)(2,1)S(1)} %copy-done.6), custom_call_target="tpu_custom_call" | custom-call | flops 3221225472 | bytes 786432 | tf_op jit(solution)/shard_map/pallas_call | solution.py:367
  41.7 18.4 %all_to_all.10.picked_ref = bf16[32,8,128]{2,1,0:T(8,128)(2,1)S(1)} all-to-all(bf16[32,8,128]{2,1,0:T(8,128)(2,1)S(1)} %get-tuple-element.29), channel_id=1, replica_groups=mesh['gx'=4,'gy'=8] {'gx','gy'}, dimensions={0} | all-to-all | bytes 131072 | tf_op jit(solution)/shard_map/all_to_all | solution.py:487
  60.1 1.2 shard_map.127
  61.3 0.0 all-reduce.2.cloned.1.call-update
  61.3 0.0 slice-start
  61.3 6.0 %shard_map.125 = (f32[6,8,64,128]{3,2,1,0:T(8,128)S(1)}, bf16[64,128]{1,0:T(8,128)(2,1)S(1)}, bf16[64,128]{1,0:T(8,128)(2,1)S(1)}, bf16[64,128]{1,0:T(8,128)(2,1)S(1)}) custom-call(s32[1,1,32]{2,1,0:T(1,128)S(1)} %copy-done.8, s32[8,1,512]{2,1,0:T(1,128)S(1)} %bitcast.12, bf16[32,8,128]{2,1,0:T(8,128)(2,1)S(1)} %get-tuple-element.22.picked_ref, ...), custom_call_target="tpu_custom_call" | custom-call | flops 3221225472 | bytes 3145728 | tf_op jit(solution)/shard_map/pallas_call | solution.py:421
  67.4 0.8 collective-permute-start.4
  68.2 0.7 collective-permute-start.5
  68.9 0.7 collective-permute-start.7
  69.6 2.1 %collective-permute-start.6 = (bf16[64,128]{1,0:T(8,128)(2,1)S(1)}, bf16[64,128]{1,0:T(8,128)(2,1)S(1)}, u32[]{:S(2)}, u32[]{:S(2)}) collective-permute-start(bf16[64,128]{1,0:T(8,128)(2,1)S(1)} %get-tuple-element.28), channel_id=1, source_target_pairs={{0,8},{16,24},{8,0},{24,16},{1,9},{17,25},{9,1},{25,17},{2,10},{18... | collective-permute-start | bytes 49160 | tf_op jit(solution)/shard_map/ppermute | solution.py:131
  71.7 0.8 collective-permute-done.6.x_0
  72.5 2.8 %copy-done = bf16[6,8,8,64,128]{4,3,2,1,0:T(8,128)(2,1)S(1)} copy-done((bf16[6,8,8,64,128]{4,3,2,1,0:T(8,128)(2,1)S(1)}, bf16[6,8,8,64,128]{4,3,2,1,0:T(8,128)(2,1)}, u32[]{:S(2)}) %copy-start) | copy-done | bytes 6291480
  75.3 7.7 %shard_map.126 = f32[6,8,64,128]{3,2,1,0:T(8,128)} custom-call(f32[6,8,64,128]{3,2,1,0:T(8,128)S(1)} %get-tuple-element.25.field_hbm, s32[64,128]{1,0:T(8,128)S(1)} %copy-done.3, f32[6,64,128]{2,1,0:T(8,128)S(1)} %copy-done.2, bf16[64,128]{1,0:T(8,128)(2,1)S(1)} %collective-permute-done.4.y_0, bf16[64,128]{1,0:T(8,128)(2,1)S(1)} %collective-permute-done.5.y_1, ...), custom_call_target="tpu_custom_call" | custom-call | flops 25165824 | bytes 15728640 | tf_op jit(solution)/shard_map/pallas_call | solution.py:296
  83.0 97.8 %all-reduce.2.cloned.1.call-done = f32[4,8,8,128]{3,2,1,0:T(8,128)} async-done(((f32[4,8,8,128]{3,2,1,0:T(8,128)}), f32[4,8,8,128]{3,2,1,0:T(8,128)}) %all-reduce.2.cloned.1.call-update) | async-done | bytes 131088 | tf_op jit(solution)/shard_map/psum | solution.py:500
  180.8 1.0 reduce_sum.9
  181.8 0.7 copy.13
  (30 shorter events, 0.1 us)
Async XLA Ops:
  10.6 24.6 %all-to-all-start = ((bf16[32,8,8,128]{3,2,1,0:T(8,128)(2,1)}), bf16[32,8,8,128]{3,2,1,0:T(8,128)(2,1)S(1)}, u32[]{:S(2)}, u32[]{:S(2)}) async-start(bf16[32,8,8,128]{3,2,1,0:T(8,128)(2,1)} %get-tuple-element.20), calls=%async_computation | async-start | bytes 1048576 | tf_op jit(solution)/shard_map/all_to_all | solution.py:487
  17.9 162.9 %all-reduce.2.cloned.1.call-start = ((), (), s32[]{:S(2)}) async-start(), calls=%async_computation.2 | async-start | bytes 262144 | tf_op jit(solution)/shard_map/psum | solution.py:500
  17.9 6.7 %collective-permute-start = (bf16[64,128]{1,0:T(8,128)(2,1)}, bf16[64,128]{1,0:T(8,128)(2,1)S(1)}, u32[]{:S(2)}, u32[]{:S(2)}) collective-permute-start(bf16[64,128]{1,0:T(8,128)(2,1)} %get-tuple-element.16), channel_id=1, source_target_pairs={{0,1},{2,3},{4,5},{6,7},{1,0},{3,2},{5,4},{7,6},{8,9},{10,11},{12,... | collective-permute-start | bytes 49160 | tf_op jit(solution)/shard_map/ppermute | solution.py:131
  19.8 4.9 %collective-permute-start.1 = (bf16[64,128]{1,0:T(8,128)(2,1)}, bf16[64,128]{1,0:T(8,128)(2,1)S(1)}, u32[]{:S(2)}, u32[]{:S(2)}) collective-permute-start(bf16[64,128]{1,0:T(8,128)(2,1)} %get-tuple-element.17), channel_id=1, source_target_pairs={{1,2},{3,4},{5,6},{2,1},{4,3},{6,5},{9,10},{11,12},{13,14},{10,9},... | collective-permute-start | bytes 49160 | tf_op jit(solution)/shard_map/ppermute | solution.py:131
  20.4 4.3 %collective-permute-start.3 = (bf16[64,128]{1,0:T(8,128)(2,1)}, bf16[64,128]{1,0:T(8,128)(2,1)S(1)}, u32[]{:S(2)}, u32[]{:S(2)}) collective-permute-start(bf16[64,128]{1,0:T(8,128)(2,1)} %get-tuple-element.18), channel_id=1, source_target_pairs={{8,16},{16,8},{9,17},{17,9},{10,18},{18,10},{11,19},{19,11},{12,20... | collective-permute-start | bytes 49160 | tf_op jit(solution)/shard_map/ppermute | solution.py:131
  21.1 3.9 %collective-permute-start.2 = (bf16[64,128]{1,0:T(8,128)(2,1)}, bf16[64,128]{1,0:T(8,128)(2,1)S(1)}, u32[]{:S(2)}, u32[]{:S(2)}) collective-permute-start(bf16[64,128]{1,0:T(8,128)(2,1)} %get-tuple-element.18), channel_id=1, source_target_pairs={{0,8},{16,24},{8,0},{24,16},{1,9},{17,25},{9,1},{25,17},{2,10},{18... | collective-permute-start | bytes 49160 | tf_op jit(solution)/shard_map/ppermute | solution.py:131
  24.6 10.5 %copy-start.7 = (s32[1,1,4096]{2,1,0:T(1,128)S(1)}, s32[1,1,4096]{2,1,0:T(1,128)}, u32[]{:S(2)}) copy-start(s32[1,1,4096]{2,1,0:T(1,128)} %param.16) | copy-start | bytes 49156
  24.6 10.5 %copy-start.8 = (s32[1,1,32]{2,1,0:T(1,128)S(1)}, s32[1,1,32]{2,1,0:T(1,128)}, u32[]{:S(2)}) copy-start(s32[1,1,32]{2,1,0:T(1,128)} %helper_ref.3) | copy-start | bytes 388
  24.7 0.6 copy-start.9
  24.7 0.6 copy-start.10
  24.7 0.6 copy-start.11
  25.3 0.6 copy-start.12
  35.2 1.1 copy-start.6
  36.3 23.7 %copy-start.1 = (bf16[1,1,32,8,8,128]{5,4,3,2,1,0:T(8,128)(2,1)S(1)}, bf16[1,1,32,8,8,128]{5,4,3,2,1,0:T(8,128)(2,1)}, u32[]{:S(2)}) copy-start(bf16[1,1,32,8,8,128]{5,4,3,2,1,0:T(8,128)(2,1)} %param.19) | copy-start | bytes 1572868
  36.3 23.7 %copy-start.4 = (bf16[1,1,32,8,128]{4,3,2,1,0:T(8,128)(2,1)S(1)}, bf16[1,1,32,8,128]{4,3,2,1,0:T(8,128)(2,1)}, u32[]{:S(2)}) copy-start(bf16[1,1,32,8,128]{4,3,2,1,0:T(8,128)(2,1)} %param.21) | copy-start | bytes 196612
  36.3 24.9 %copy-start.2 = (f32[6,64,128]{2,1,0:T(8,128)S(1)}, f32[6,64,128]{2,1,0:T(8,128)}, u32[]{:S(2)}) copy-start(f32[6,64,128]{2,1,0:T(8,128)} %perm_hbm.5) | copy-start | bytes 589828
  36.3 25.0 %copy-start.3 = (s32[64,128]{1,0:T(8,128)S(1)}, s32[64,128]{1,0:T(8,128)}, u32[]{:S(2)}) copy-start(s32[64,128]{1,0:T(8,128)} %mask_hbm.5) | copy-start | bytes 98308
  36.3 25.0 %copy-start.5 = (f32[6,8,64,128]{3,2,1,0:T(8,128)S(1)}, f32[6,8,64,128]{3,2,1,0:T(8,128)}, u32[]{:S(2)}) copy-start(f32[6,8,64,128]{3,2,1,0:T(8,128)} %get-tuple-element.24.first_ref) | copy-start | bytes 4718596
  61.3 11.2 %slice-start = ((s8[6291456]{0:T(1024)(128)(4,1)}), s8[4194304]{0:T(1024)(128)(4,1)S(1)}, s32[]{:S(2)}) async-start(s8[6291456]{0:T(1024)(128)(4,1)} %bitcast.6), calls=%async_computation.3 | async-start | bytes 8388608
  61.3 11.2 %slice-start.1 = ((s8[6291456]{0:T(1024)(128)(4,1)}), s8[2097152]{0:T(1024)(128)(4,1)S(1)}, s32[]{:S(2)}) async-start(s8[6291456]{0:T(1024)(128)(4,1)} %bitcast.6), calls=%async_computation.4 | async-start | bytes 4194304
  67.4 4.3 %collective-permute-start.4 = (bf16[64,128]{1,0:T(8,128)(2,1)S(1)}, bf16[64,128]{1,0:T(8,128)(2,1)S(1)}, u32[]{:S(2)}, u32[]{:S(2)}) collective-permute-start(bf16[64,128]{1,0:T(8,128)(2,1)S(1)} %get-tuple-element.26), channel_id=1, source_target_pairs={{0,1},{2,3},{4,5},{6,7},{1,0},{3,2},{5,4},{7,6},{8,9},{10,11},{12,... | collective-permute-start | bytes 49160 | tf_op jit(solution)/shard_map/ppermute | solution.py:131
  68.2 3.4 %collective-permute-start.5 = (bf16[64,128]{1,0:T(8,128)(2,1)S(1)}, bf16[64,128]{1,0:T(8,128)(2,1)S(1)}, u32[]{:S(2)}, u32[]{:S(2)}) collective-permute-start(bf16[64,128]{1,0:T(8,128)(2,1)S(1)} %get-tuple-element.27), channel_id=1, source_target_pairs={{1,2},{3,4},{5,6},{2,1},{4,3},{6,5},{9,10},{11,12},{13,14},{10,9},... | collective-permute-start | bytes 49160 | tf_op jit(solution)/shard_map/ppermute | solution.py:131
  68.9 2.8 %collective-permute-start.7 = (bf16[64,128]{1,0:T(8,128)(2,1)S(1)}, bf16[64,128]{1,0:T(8,128)(2,1)S(1)}, u32[]{:S(2)}, u32[]{:S(2)}) collective-permute-start(bf16[64,128]{1,0:T(8,128)(2,1)S(1)} %get-tuple-element.28), channel_id=1, source_target_pairs={{8,16},{16,8},{9,17},{17,9},{10,18},{18,10},{11,19},{19,11},{12,20... | collective-permute-start | bytes 49160 | tf_op jit(solution)/shard_map/ppermute | solution.py:131
  69.6 2.9 %collective-permute-start.6 = (bf16[64,128]{1,0:T(8,128)(2,1)S(1)}, bf16[64,128]{1,0:T(8,128)(2,1)S(1)}, u32[]{:S(2)}, u32[]{:S(2)}) collective-permute-start(bf16[64,128]{1,0:T(8,128)(2,1)S(1)} %get-tuple-element.28), channel_id=1, source_target_pairs={{0,8},{16,24},{8,0},{24,16},{1,9},{17,25},{9,1},{25,17},{2,10},{18... | collective-permute-start | bytes 49160 | tf_op jit(solution)/shard_map/ppermute | solution.py:131
  72.5 2.8 %copy-start = (bf16[6,8,8,64,128]{4,3,2,1,0:T(8,128)(2,1)S(1)}, bf16[6,8,8,64,128]{4,3,2,1,0:T(8,128)(2,1)}, u32[]{:S(2)}) copy-start(bf16[6,8,8,64,128]{4,3,2,1,0:T(8,128)(2,1)} %flux_hbm.3) | copy-start | bytes 18874372
Sparse Core Ops, SparseCore 0:
  61.4 119.3 all-reduce.1

commit v4 on v3

--- a/solution.py
+++ b/solution.py
@@ -117,9 +117,9 @@
             edge_scratch(layers, comps, cols),
             pltpu.SemaphoreType.DMA((5,)),
         ],
-        compiler_params=params(56),
-        cost_estimate=cost(16 * inverse.size + 4 * field.size, 6 * inverse.size + 4 * field.size),
-    )(*arrays)
+        compiler_params=params(24),
+        cost_estimate=cost(16 * inverse.size + 4 * field.size, 160 * field.size),
+    )(*(pltpu.with_memory_space_constraint(array, pltpu.HBM) for array in arrays))
 
 
 def exchange(send_y_0, send_y_1, send_x):
@@ -135,7 +135,6 @@
 
 
 TILE = 16
-AHEAD = 3
 
 
 def reciprocal(value):
@@ -147,40 +146,17 @@
     return 2.0 * centre * beside * reciprocal(centre + beside)
 
 
-def apply_kernel(want_rounded, field_hbm, mask_hbm, perm_hbm, y_0, y_1, x_0, x_1, diag_hbm, flux_hbm, *rest):
+def apply_kernel(want_rounded, field_ref, mask_ref, perm_ref, y_0, y_1, x_0, x_1, diag_ref, flux_ref, *rest):
     if want_rounded:
-        out_hbm, rounded_hbm, *rest, rounded_ref, rounded_sems = rest
+        out_ref, rounded_ref, *rest = rest
     else:
-        out_hbm, *rest = rest
-    *rest, out_ref, out_sems = rest
-    (field_ref, mask_ref, perm_ref, diag_ref, flux_ref, padded, padded_perm, edge_x, place, beside_edge, perm_edge, sems) = rest
+        out_hbm, *rest, out_ref, out_sems = rest
+    padded, padded_perm, edge_x, place, beside_edge, perm_edge = rest
     layers, comps, rows, cols = field_ref.shape
     top = 8
 
-    def blocks(k):
-        return (
-            pltpu.make_async_copy(diag_hbm.at[k], diag_ref.at[k], sems.at[3 + k]),
-            pltpu.make_async_copy(flux_hbm.at[k], flux_ref.at[k], sems.at[3 + layers + k]),
-        )
-
-    def out_copies(k):
-        copies = [pltpu.make_async_copy(out_ref.at[k], out_hbm.at[k], out_sems.at[k])]
-        if want_rounded:
-            columns = pl.ds(pl.multiple_of(k * cols, cols), cols)
-            source, target = rounded_ref.at[:, columns], rounded_hbm.at[:, columns]
-            copies.append(pltpu.make_async_copy(source, target, rounded_sems.at[k]))
-        return copies
-
-    smalls = [
-        pltpu.make_async_copy(field_hbm, field_ref, sems.at[0]),
-        pltpu.make_async_copy(mask_hbm, mask_ref, sems.at[1]),
-        pltpu.make_async_copy(perm_hbm, perm_ref, sems.at[2]),
-    ]
-    for copy in smalls:
-        copy.start()
-    for k in range(min(AHEAD, layers)):
-        for copy in blocks(k):
-            copy.start()
+    def out_copy(k):
+        return pltpu.make_async_copy(out_ref.at[k], out_hbm.at[k], out_sems.at[k])
 
     lane = lax.broadcasted_iota(jnp.int32, (rows, cols), 1)
     number = lax.broadcasted_iota(jnp.int32, (cols, cols), 0)
@@ -192,18 +168,11 @@
     even_y = lax.axis_index("gy") % 2 == 0
     side_0, side_1 = x_0[...].astype(F32), x_1[...].astype(F32)
     edge_x[...] = jnp.where((lane % 2 == 0) == even_x, side_1, side_0)
-    for copy in smalls:
-        copy.wait()
     clear = 1.0 - mask_ref[...].astype(F32)
 
     def layer(k, carry):
         above = jnp.minimum(k + 1, layers - 1)
         below = jnp.maximum(k - 1, 0)
-
-        @pl.when(k + AHEAD < layers)
-        def _():
-            for copy in blocks(k + AHEAD):
-                copy.start()
 
         turned = pltpu.roll(edge_x[...], lax.rem(cols - 2 * comps * k, cols), 1).astype(BF16)
         beside_edge[...] = jnp.dot(turned, place[...], preferred_element_type=F32)
@@ -229,9 +198,6 @@
         padded_perm[top : top + rows] = perm_ref[k]
         padded_perm[top - 1 : top] = jnp.where(even_y, perm_1, perm_0)
         padded_perm[top + rows : top + rows + 1] = jnp.where(even_y, perm_0, perm_1)
-        for copy in blocks(k):
-            copy.wait()
-
         narrow = lax.broadcasted_iota(jnp.int32, (TILE, cols), 1)
         is_first, is_last = narrow == 0, narrow == cols - 1
         for y in range(0, rows, TILE):
@@ -274,48 +240,41 @@
                 if want_rounded:
                     columns = pl.ds(pl.multiple_of(k * cols, cols), cols)
                     rounded_ref[c * rows + y : c * rows + y + TILE, columns] = value.astype(BF16)
-        for copy in out_copies(k):
-            copy.start()
+        if not want_rounded:
+            out_copy(k).start()
         return carry
 
     lax.fori_loop(0, layers, layer, 0)
-    for k in range(layers):
-        for copy in out_copies(k):
-            copy.wait()
-
-
-def apply_transposed(field, mask, perm, halos, diag, flux, want_rounded, mib):
+    if not want_rounded:
+        for k in range(layers):
+            out_copy(k).wait()
+
+
+def apply_transposed(field, mask, perm, halos, diag, flux, want_rounded):
     layers, comps, rows, cols = field.shape
-    hbm = pl.BlockSpec(memory_space=pltpu.HBM)
     vmem = pl.BlockSpec(memory_space=pltpu.VMEM)
     out_shape = [jax.ShapeDtypeStruct(field.shape, F32)]
-    extra = []
     if want_rounded:
+        out_specs, tail = [vmem, vmem], []
         out_shape.append(jax.ShapeDtypeStruct((comps * rows, layers * cols), BF16))
-        extra = [pltpu.VMEM(out_shape[1].shape, BF16), pltpu.SemaphoreType.DMA((layers,))]
+    else:
+        out_specs = [pl.BlockSpec(memory_space=pltpu.HBM)]
+        tail = [pltpu.VMEM(field.shape, F32), pltpu.SemaphoreType.DMA((layers,))]
     return pl.pallas_call(
         functools.partial(apply_kernel, want_rounded),
-        in_specs=[pl.BlockSpec(memory_space=pl.ANY), hbm, hbm, *[vmem] * 4, hbm, hbm],
-        out_specs=[hbm] * len(out_shape),
+        in_specs=[vmem] * 9,
+        out_specs=out_specs,
         out_shape=out_shape,
         scratch_shapes=[
-            pltpu.VMEM(field.shape, F32),
-            pltpu.VMEM(mask.shape, mask.dtype),
-            pltpu.VMEM(perm.shape, F32),
-            pltpu.VMEM(diag.shape, BF16),
-            pltpu.VMEM(flux.shape, BF16),
             pltpu.VMEM((comps, rows + 16, cols), F32),
             pltpu.VMEM((rows + 16, cols), F32),
             pltpu.VMEM((rows, cols), F32),
             pltpu.VMEM((cols, comps * cols), BF16),
             pltpu.VMEM((rows, comps * cols), F32),
             pltpu.VMEM((rows, cols), F32),
-            pltpu.SemaphoreType.DMA((3 + 2 * layers,)),
-            pltpu.VMEM(field.shape, F32),
-            pltpu.SemaphoreType.DMA((layers,)),
-            *extra,
+            *tail,
         ],
-        compiler_params=params(mib),
+        compiler_params=params(24),
         cost_estimate=cost(8 * diag.size, 4 * diag.size + 8 * field.size),
     )(field, mask, perm, *halos, diag, flux)
 
@@ -424,12 +383,9 @@
         out_specs=[vmem] * 4,
         out_shape=[jax.ShapeDtypeStruct(first.shape, F32), *edge_shapes(*first.shape)],
         scratch_shapes=[pltpu.VMEM((comps * rows, layers * cols), F32), edge_scratch(layers, comps, cols)],
-        compiler_params=params(40),
-        cost_estimate=cost(2 * first.size * cells.size, 8 * first.size),
+        compiler_params=params(24),
+        cost_estimate=cost(2 * first.size * cells.size, 160 * first.size),
     )(helper, cells, picked, home, first, mask, perm)
-
-
-GROUPS = 4
 
 
 def grad_kernel(inverse_ref, state_ref, picked_ref, out_ref):
@@ -446,21 +402,38 @@
         part *= state
         return tuple(totals[j] + part * state[j : j + 1] for j in range(comps))
 
-    share = blocks // GROUPS
-    for g in range(GROUPS):
-        totals = lax.fori_loop(g * share, (g + 1) * share, one, (jnp.zeros((comps, width), F32),) * comps)
-        for j in range(comps):
-            out_ref[g, j] = totals[j]
-
-
-def grad_part(inverse, state, picked):
+    totals = lax.fori_loop(0, blocks, one, (jnp.zeros((comps, width), F32),) * comps)
+    lane = lax.broadcasted_iota(jnp.int32, (comps, width), 1)
+    result = jnp.zeros((comps, width), F32)
+    for j in range(comps):
+        result = jnp.where(lane == j, jnp.sum(totals[j], axis=1, keepdims=True), result)
+    for i in range(out_ref.shape[0]):
+        out_ref[i] = result
+
+
+def grad_part(inverse, state, picked, copies):
     comps, width = inverse.shape[1], inverse.shape[-1]
     return pl.pallas_call(
         grad_kernel,
-        out_shape=jax.ShapeDtypeStruct((GROUPS, comps, comps, width), F32),
+        out_shape=jax.ShapeDtypeStruct((copies, comps, width), F32),
         compiler_params=params(24),
         cost_estimate=cost(4 * inverse.size, 2 * inverse.size),
     )(inverse, state, picked)
+
+
+def total_kernel(scale, parts_ref, out_ref):
+    total = parts_ref[0]
+    for i in range(1, parts_ref.shape[0]):
+        total += parts_ref[i]
+    out_ref[...] = (total * scale)[:, : out_ref.shape[1]]
+
+
+def grad_total(parts, scale):
+    return pl.pallas_call(
+        functools.partial(total_kernel, scale),
+        out_shape=jax.ShapeDtypeStruct((parts.shape[1],) * 2, F32),
+        cost_estimate=cost(parts.size, 4 * parts.size),
+    )(parts)
 
 
 def shards(
@@ -489,18 +462,17 @@
     product, *sides = opening(inverse, coupling, cotangent, well_mask, permeability)
     home = to_partners(product)
     halos = exchange(*sides)
-    first, rounded = apply_transposed(cotangent, well_mask, permeability, halos, diag_block, flux_block, True, 56)
+    first, rounded = apply_transposed(cotangent, well_mask, permeability, halos, diag_block, flux_block, True)
     rounded, home = lax.optimization_barrier((rounded, home))
     picked, sent = gather(rounded, cells, helper_of, block_count, comps, rows, cols, width)
     at_helper = to_partners(sent)
     second, *sides = scatter(first, picked, home, helper_of, cells, well_mask, permeability)
     halos = exchange(*sides)
-    (adjoint,) = apply_transposed(second, well_mask, permeability, halos, diag_block, flux_block, False, 32)
-
-    totals = lax.psum(grad_part(inverse, state, at_helper), AXES)
+    at_helper, *halos = lax.optimization_barrier((at_helper, *halos))
     devices = lax.axis_size("gx") * lax.axis_size("gy")
-    grad_scale = 1.0 / math.sqrt(width * devices * devices)
-    interaction_grad = -grad_scale * jnp.sum(totals, axis=(0, 3)).T
+    parts = to_partners(grad_part(inverse, state, at_helper, devices))
+    (adjoint,) = apply_transposed(second, well_mask, permeability, halos, diag_block, flux_block, False)
+    interaction_grad = grad_total(parts, -1.0 / math.sqrt(width * devices * devices))
     return (adjoint, interaction_grad)
 
 

time: 190 us -> 85.3 us (0.45)
  the two profiles are of different devices: /device:TPU:0 before, /device:TPU:9 now
where the time goes in v4:
time: 85.3 us; the launch traced here: 83.8 us
  starting transfers between devices  34.9 us (41%)
  Pallas kernels  28.2 us (33%)
  local copies, waits for them, and re-layouts  15.4 us (18%)
  waiting for transfers between devices  3.76 us (4%)
  between operations  1.54 us (2%)
    all_to_all x3, starting transfers between devices, to_partners(): return lax.all_to_all(array, AXES, split_axis=0, concat_axis=0, tiled=True)  20.1 us
    unnamed x32, local copies, waits for them, and re-layouts  15.4 us
    ppermute x8, starting transfers between devices, swaps(): lax.ppermute(array, axis, pairs + [(j, i) for i, j in pairs])  14.8 us
    pallas_call x2, Pallas kernels, apply_transposed(): pl.pallas_call(functools.partial(apply_kernel, want_rounded), in_specs=[v...  10.1 us
    pallas_call x1, Pallas kernels, scatter(): pl.pallas_call(scatter_kernel, in_specs=[smem] + [vmem] * 6, out_specs=[v...  6 us
    pallas_call x1, Pallas kernels, gather(): pl.pallas_call(functools.partial(gather_kernel, rows, cols), in_specs=[sm...  5.99 us
    ppermute x8, waiting for transfers between devices, swaps(): lax.ppermute(array, axis, pairs + [(j, i) for i, j in pairs])  3.75 us
    pallas_call x1, Pallas kernels, opening(): pl.pallas_call(opening_kernel, in_specs=[hbm] * 5, out_specs=[vmem] * 4,...  3.32 us
  transfers between devices with their start and end apart: 11, of which 2 were waited for; matrix products, arithmetic and copies ran while one was open for 0% of the time, Pallas kernels for 19%

profile of v4, /device:TPU:9, one launch (start us, length us, event | category | flops | bytes accessed | tf_op | source)
XLA Modules:
  0.0 83.8 jit_solution(10523706888216472314)
XLA Ops:
  0.7 3.3 %shard_map.122 = (bf16[32,8,8,128]{3,2,1,0:T(8,128)(2,1)}, bf16[64,128]{1,0:T(8,128)(2,1)S(1)}, bf16[64,128]{1,0:T(8,128)(2,1)S(1)}, bf16[64,128]{1,0:T(8,128)(2,1)S(1)}) custom-call(bf16[32,8,8,128]{3,2,1,0:T(8,128)(2,1)} %bitcast.4, bf16[32,8,8,128]{3,2,1,0:T(8,128)(2,1)} %bitcast.9, f32[6,8,64,128]{3,2,1,0:T(8,128)} %field_ref.1, s32[64,128]{1,0:T(8,128)} %mask_ref.5, ...), custom_call_target="tpu_custom_call" | custom-call | flops 5767168 | bytes 62914560 | tf_op jit(solution)/shard_map/pallas_call | solution.py:110
  4.0 6.4 %all-to-all-start = ((bf16[32,8,8,128]{3,2,1,0:T(8,128)(2,1)}), bf16[32,8,8,128]{3,2,1,0:T(8,128)(2,1)S(1)}, u32[]{:S(2)}, u32[]{:S(2)}) async-start(bf16[32,8,8,128]{3,2,1,0:T(8,128)(2,1)} %get-tuple-element.25), calls=%async_computation | async-start | bytes 1048576 | tf_op jit(solution)/shard_map/all_to_all | solution.py:460
  10.4 1.2 %collective-permute-start = (bf16[64,128]{1,0:T(8,128)(2,1)S(1)}, bf16[64,128]{1,0:T(8,128)(2,1)S(1)}, u32[]{:S(2)}, u32[]{:S(2)}) collective-permute-start(bf16[64,128]{1,0:T(8,128)(2,1)S(1)} %get-tuple-element.21), channel_id=1, source_target_pairs={{0,1},{2,3},{4,5},{6,7},{1,0},{3,2},{5,4},{7,6},{8,9},{10,11},{12,... | collective-permute-start | bytes 49160 | tf_op jit(solution)/shard_map/ppermute | solution.py:131
  11.6 2.0 %collective-permute-start.1 = (bf16[64,128]{1,0:T(8,128)(2,1)S(1)}, bf16[64,128]{1,0:T(8,128)(2,1)S(1)}, u32[]{:S(2)}, u32[]{:S(2)}) collective-permute-start(bf16[64,128]{1,0:T(8,128)(2,1)S(1)} %get-tuple-element.22), channel_id=1, source_target_pairs={{1,2},{3,4},{5,6},{2,1},{4,3},{6,5},{9,10},{11,12},{13,14},{10,9},... | collective-permute-start | bytes 49160 | tf_op jit(solution)/shard_map/ppermute | solution.py:131
  13.6 4.1 %collective-permute-start.3 = (bf16[64,128]{1,0:T(8,128)(2,1)S(1)}, bf16[64,128]{1,0:T(8,128)(2,1)S(1)}, u32[]{:S(2)}, u32[]{:S(2)}) collective-permute-start(bf16[64,128]{1,0:T(8,128)(2,1)S(1)} %get-tuple-element.23), channel_id=1, source_target_pairs={{8,16},{16,8},{9,17},{17,9},{10,18},{18,10},{11,19},{19,11},{12,20... | collective-permute-start | bytes 49160 | tf_op jit(solution)/shard_map/ppermute | solution.py:131
  17.7 0.1 collective-permute-start.2
  17.8 0.0 copy-start.14
  18.5 2.4 %collective-permute-done.1.y_1 = bf16[64,128]{1,0:T(8,128)(2,1)S(1)} collective-permute-done((bf16[64,128]{1,0:T(8,128)(2,1)S(1)}, bf16[64,128]{1,0:T(8,128)(2,1)S(1)}, u32[]{:S(2)}, u32[]{:S(2)}) %collective-permute-start.1) | collective-permute-done | bytes 16416 | tf_op jit(solution)/shard_map/ppermute | solution.py:131
  20.9 0.0 copy-start
  20.9 2.8 %copy-done = bf16[6,8,8,64,128]{4,3,2,1,0:T(8,128)(2,1)S(1)} copy-done((bf16[6,8,8,64,128]{4,3,2,1,0:T(8,128)(2,1)S(1)}, bf16[6,8,8,64,128]{4,3,2,1,0:T(8,128)(2,1)}, u32[]{:S(2)}) %copy-start) | copy-done | bytes 6291480
  23.7 2.8 %copy-done.2 = bf16[6,8,8,64,128]{4,3,2,1,0:T(8,128)(2,1)S(1)} copy-done((bf16[6,8,8,64,128]{4,3,2,1,0:T(8,128)(2,1)S(1)}, bf16[6,8,8,64,128]{4,3,2,1,0:T(8,128)(2,1)}, u32[]{:S(2)}) %copy-start.2) | copy-done | bytes 6291480
  26.5 4.7 %shard_map.123 = (f32[6,8,64,128]{3,2,1,0:T(8,128)S(1)}, bf16[512,768]{1,0:T(8,128)(2,1)S(1)}) custom-call(f32[6,8,64,128]{3,2,1,0:T(8,128)S(1)} %copy-done.4, s32[64,128]{1,0:T(8,128)S(1)} %copy-done.9, f32[6,64,128]{2,1,0:T(8,128)S(1)} %copy-done.6, bf16[64,128]{1,0:T(8,128)(2,1)S(1)} %collective-permute-done.y_0, ...), custom_call_target="tpu_custom_call" | custom-call | flops 25165824 | bytes 15728640 | tf_op jit(solution)/shard_map/pallas_call | solution.py:263
  31.2 0.0 copy-start.11
  31.2 1.1 %copy-done.11 = f32[6,8,64,128]{3,2,1,0:T(8,128)} copy-done((f32[6,8,64,128]{3,2,1,0:T(8,128)}, f32[6,8,64,128]{3,2,1,0:T(8,128)S(1)}, u32[]{:S(2)}) %copy-start.11) | copy-done | bytes 1572888
  32.4 6.0 %shard_map.124 = (bf16[32,8,128]{2,1,0:T(8,128)(2,1)S(1)}, bf16[32,8,128]{2,1,0:T(8,128)(2,1)}) custom-call(s32[1,1,32]{2,1,0:T(1,128)S(1)} %copy-done.14, s32[1,1]{1,0:T(1,128)S(6)} %copy.13.count_ref, s32[8,1,512]{2,1,0:T(1,128)S(1)} %bitcast.7, bf16[512,768]{1,0:T(8,128)(2,1)S(1)} %get-tuple-element.26.rounded_ref), custom_call_target="tpu_custom_call" | custom-call | flops 3221225472 | bytes 786432 | tf_op jit(solution)/shard_map/pallas_call | solution.py:326
  38.4 7.6 %all-to-all-start.1 = ((bf16[32,8,128]{2,1,0:T(8,128)(2,1)}), bf16[32,8,128]{2,1,0:T(8,128)(2,1)S(1)}, u32[]{:S(2)}, u32[]{:S(2)}) async-start(bf16[32,8,128]{2,1,0:T(8,128)(2,1)} %get-tuple-element.31), calls=%async_computation.1 | async-start | bytes 131072 | tf_op jit(solution)/shard_map/all_to_all | solution.py:460
  45.9 1.0 %copy-done.8 = bf16[32,8,8,128]{3,2,1,0:T(8,128)(2,1)S(1)} copy-done((bf16[32,8,8,128]{3,2,1,0:T(8,128)(2,1)S(1)}, bf16[32,8,8,128]{3,2,1,0:T(8,128)(2,1)}, u32[]{:S(2)}) %copy-start.8) | copy-done | bytes 524312
  47.0 1.4 %copy-done.12 = f32[6,8,64,128]{3,2,1,0:T(8,128)S(1)} copy-done((f32[6,8,64,128]{3,2,1,0:T(8,128)S(1)}, f32[6,8,64,128]{3,2,1,0:T(8,128)}, u32[]{:S(2)}) %copy-start.12) | copy-done | bytes 1572888
  48.4 6.0 %shard_map.125 = (f32[6,8,64,128]{3,2,1,0:T(8,128)S(1)}, bf16[64,128]{1,0:T(8,128)(2,1)S(1)}, bf16[64,128]{1,0:T(8,128)(2,1)S(1)}, bf16[64,128]{1,0:T(8,128)(2,1)S(1)}) custom-call(s32[1,1,32]{2,1,0:T(1,128)S(1)} %copy-done.14, s32[8,1,512]{2,1,0:T(1,128)S(1)} %bitcast.8, bf16[32,8,128]{2,1,0:T(8,128)(2,1)S(1)} %get-tuple-element.27.picked_ref, ...), custom_call_target="tpu_custom_call" | custom-call | flops 3221225472 | bytes 62914560 | tf_op jit(solution)/shard_map/pallas_call | solution.py:380
  54.4 1.2 %collective-permute-start.4 = (bf16[64,128]{1,0:T(8,128)(2,1)S(1)}, bf16[64,128]{1,0:T(8,128)(2,1)S(1)}, u32[]{:S(2)}, u32[]{:S(2)}) collective-permute-start(bf16[64,128]{1,0:T(8,128)(2,1)S(1)} %get-tuple-element.32), channel_id=1, source_target_pairs={{0,1},{2,3},{4,5},{6,7},{1,0},{3,2},{5,4},{7,6},{8,9},{10,11},{12,... | collective-permute-start | bytes 49160 | tf_op jit(solution)/shard_map/ppermute | solution.py:131
  55.6 2.0 %collective-permute-start.5 = (bf16[64,128]{1,0:T(8,128)(2,1)S(1)}, bf16[64,128]{1,0:T(8,128)(2,1)S(1)}, u32[]{:S(2)}, u32[]{:S(2)}) collective-permute-start(bf16[64,128]{1,0:T(8,128)(2,1)S(1)} %get-tuple-element.33), channel_id=1, source_target_pairs={{1,2},{3,4},{5,6},{2,1},{4,3},{6,5},{9,10},{11,12},{13,14},{10,9},... | collective-permute-start | bytes 49160 | tf_op jit(solution)/shard_map/ppermute | solution.py:131
  57.6 4.1 %collective-permute-start.7 = (bf16[64,128]{1,0:T(8,128)(2,1)S(1)}, bf16[64,128]{1,0:T(8,128)(2,1)S(1)}, u32[]{:S(2)}, u32[]{:S(2)}) collective-permute-start(bf16[64,128]{1,0:T(8,128)(2,1)S(1)} %get-tuple-element.34), channel_id=1, source_target_pairs={{8,16},{16,8},{9,17},{17,9},{10,18},{18,10},{11,19},{19,11},{12,20... | collective-permute-start | bytes 49160 | tf_op jit(solution)/shard_map/ppermute | solution.py:131
  61.7 0.1 collective-permute-start.6
  61.8 1.3 %collective-permute-done.7.x_1 = bf16[64,128]{1,0:T(8,128)(2,1)S(1)} collective-permute-done((bf16[64,128]{1,0:T(8,128)(2,1)S(1)}, bf16[64,128]{1,0:T(8,128)(2,1)S(1)}, u32[]{:S(2)}, u32[]{:S(2)}) %collective-permute-start.7) | collective-permute-done | bytes 16416 | tf_op jit(solution)/shard_map/ppermute | solution.py:131
  63.2 1.3 %shard_map.127 = f32[32,8,128]{2,1,0:T(8,128)} custom-call(bf16[32,8,8,128]{3,2,1,0:T(8,128)(2,1)S(1)} %bitcast.5, bf16[32,8,128]{2,1,0:T(8,128)(2,1)S(1)} %bitcast.6, bf16[32,8,128]{2,1,0:T(8,128)(2,1)S(1)} %all-to-all-done.1.picked_ref), custom_call_target="tpu_custom_call" | custom-call | flops 1048576 | bytes 524288 | tf_op jit(solution)/shard_map/pallas_call | solution.py:416
  64.4 6.1 %all-to-all-start.2 = ((f32[32,8,128]{2,1,0:T(8,128)}), f32[32,8,128]{2,1,0:T(8,128)S(1)}, u32[]{:S(2)}, u32[]{:S(2)}) async-start(f32[32,8,128]{2,1,0:T(8,128)} %shard_map.127), calls=%async_computation.2 | async-start | bytes 262144 | tf_op jit(solution)/shard_map/all_to_all | solution.py:460
  70.6 0.0 copy-start.1
  70.6 2.8 %copy-done.1 = bf16[6,8,8,64,128]{4,3,2,1,0:T(8,128)(2,1)S(1)} copy-done((bf16[6,8,8,64,128]{4,3,2,1,0:T(8,128)(2,1)S(1)}, bf16[6,8,8,64,128]{4,3,2,1,0:T(8,128)(2,1)}, u32[]{:S(2)}) %copy-start.1) | copy-done | bytes 6291480
  73.4 2.8 %copy-done.3 = bf16[6,8,8,64,128]{4,3,2,1,0:T(8,128)(2,1)S(1)} copy-done((bf16[6,8,8,64,128]{4,3,2,1,0:T(8,128)(2,1)S(1)}, bf16[6,8,8,64,128]{4,3,2,1,0:T(8,128)(2,1)}, u32[]{:S(2)}) %copy-start.3) | copy-done | bytes 6291480
  76.1 5.4 %shard_map.126 = f32[6,8,64,128]{3,2,1,0:T(8,128)} custom-call(f32[6,8,64,128]{3,2,1,0:T(8,128)S(1)} %get-tuple-element.30.field_ref, s32[64,128]{1,0:T(8,128)S(1)} %copy-done.9, f32[6,64,128]{2,1,0:T(8,128)S(1)} %copy-done.6, bf16[64,128]{1,0:T(8,128)(2,1)S(1)} %collective-permute-done.4.y_0, bf16[64,128]{1,0:T(8,128)(2,1)S(1)} %collective-permute-done.5.y_1, ...), custom_call_target="tpu_custom_call" | custom-call | flops 25165824 | bytes 15728640 | tf_op jit(solution)/shard_map/pallas_call | solution.py:263
  81.6 0.6 copy-done.15
  82.3 1.5 %shard_map.128 = f32[8,8]{1,0:T(8,128)} custom-call(f32[32,8,128]{2,1,0:T(8,128)} %copy-done.15), custom_call_target="tpu_custom_call" | custom-call | flops 32768 | bytes 131072 | tf_op jit(solution)/shard_map/pallas_call | solution.py:432
  (29 shorter events, 0.1 us)
Async XLA Ops:
  0.6 20.3 %copy-start.4 = (f32[6,8,64,128]{3,2,1,0:T(8,128)S(1)}, f32[6,8,64,128]{3,2,1,0:T(8,128)}, u32[]{:S(2)}) copy-start(f32[6,8,64,128]{3,2,1,0:T(8,128)} %field_ref.1) | copy-start | bytes 4718596
  0.6 20.3 %copy-start.6 = (f32[6,64,128]{2,1,0:T(8,128)S(1)}, f32[6,64,128]{2,1,0:T(8,128)}, u32[]{:S(2)}) copy-start(f32[6,64,128]{2,1,0:T(8,128)} %perm_ref.5) | copy-start | bytes 589828
  0.7 20.3 %copy-start.9 = (s32[64,128]{1,0:T(8,128)S(1)}, s32[64,128]{1,0:T(8,128)}, u32[]{:S(2)}) copy-start(s32[64,128]{1,0:T(8,128)} %mask_ref.5) | copy-start | bytes 98308
  4.0 28.4 %all-to-all-start = ((bf16[32,8,8,128]{3,2,1,0:T(8,128)(2,1)}), bf16[32,8,8,128]{3,2,1,0:T(8,128)(2,1)S(1)}, u32[]{:S(2)}, u32[]{:S(2)}) async-start(bf16[32,8,8,128]{3,2,1,0:T(8,128)(2,1)} %get-tuple-element.25), calls=%async_computation | async-start | bytes 1048576 | tf_op jit(solution)/shard_map/all_to_all | solution.py:460
  10.4 8.1 %collective-permute-start = (bf16[64,128]{1,0:T(8,128)(2,1)S(1)}, bf16[64,128]{1,0:T(8,128)(2,1)S(1)}, u32[]{:S(2)}, u32[]{:S(2)}) collective-permute-start(bf16[64,128]{1,0:T(8,128)(2,1)S(1)} %get-tuple-element.21), channel_id=1, source_target_pairs={{0,1},{2,3},{4,5},{6,7},{1,0},{3,2},{5,4},{7,6},{8,9},{10,11},{12,... | collective-permute-start | bytes 49160 | tf_op jit(solution)/shard_map/ppermute | solution.py:131
  11.6 9.3 %collective-permute-start.1 = (bf16[64,128]{1,0:T(8,128)(2,1)S(1)}, bf16[64,128]{1,0:T(8,128)(2,1)S(1)}, u32[]{:S(2)}, u32[]{:S(2)}) collective-permute-start(bf16[64,128]{1,0:T(8,128)(2,1)S(1)} %get-tuple-element.22), channel_id=1, source_target_pairs={{1,2},{3,4},{5,6},{2,1},{4,3},{6,5},{9,10},{11,12},{13,14},{10,9},... | collective-permute-start | bytes 49160 | tf_op jit(solution)/shard_map/ppermute | solution.py:131
  13.6 7.3 %collective-permute-start.3 = (bf16[64,128]{1,0:T(8,128)(2,1)S(1)}, bf16[64,128]{1,0:T(8,128)(2,1)S(1)}, u32[]{:S(2)}, u32[]{:S(2)}) collective-permute-start(bf16[64,128]{1,0:T(8,128)(2,1)S(1)} %get-tuple-element.23), channel_id=1, source_target_pairs={{8,16},{16,8},{9,17},{17,9},{10,18},{18,10},{11,19},{19,11},{12,20... | collective-permute-start | bytes 49160 | tf_op jit(solution)/shard_map/ppermute | solution.py:131
  17.7 3.2 %collective-permute-start.2 = (bf16[64,128]{1,0:T(8,128)(2,1)S(1)}, bf16[64,128]{1,0:T(8,128)(2,1)S(1)}, u32[]{:S(2)}, u32[]{:S(2)}) collective-permute-start(bf16[64,128]{1,0:T(8,128)(2,1)S(1)} %get-tuple-element.23), channel_id=1, source_target_pairs={{0,8},{16,24},{8,0},{24,16},{1,9},{17,25},{9,1},{25,17},{2,10},{18... | collective-permute-start | bytes 49160 | tf_op jit(solution)/shard_map/ppermute | solution.py:131
  17.8 14.6 %copy-start.14 = (s32[1,1,32]{2,1,0:T(1,128)S(1)}, s32[1,1,32]{2,1,0:T(1,128)}, u32[]{:S(2)}) copy-start(s32[1,1,32]{2,1,0:T(1,128)} %helper_ref.3) | copy-start | bytes 388
  20.9 2.8 %copy-start = (bf16[6,8,8,64,128]{4,3,2,1,0:T(8,128)(2,1)S(1)}, bf16[6,8,8,64,128]{4,3,2,1,0:T(8,128)(2,1)}, u32[]{:S(2)}) copy-start(bf16[6,8,8,64,128]{4,3,2,1,0:T(8,128)(2,1)} %diag_ref.3) | copy-start | bytes 18874372
  23.7 2.8 %copy-start.2 = (bf16[6,8,8,64,128]{4,3,2,1,0:T(8,128)(2,1)S(1)}, bf16[6,8,8,64,128]{4,3,2,1,0:T(8,128)(2,1)}, u32[]{:S(2)}) copy-start(bf16[6,8,8,64,128]{4,3,2,1,0:T(8,128)(2,1)} %flux_ref.3) | copy-start | bytes 18874372
  26.5 5.9 %copy-start.13 = (s32[1,1,4096]{2,1,0:T(1,128)S(1)}, s32[1,1,4096]{2,1,0:T(1,128)}, u32[]{:S(2)}) copy-start(s32[1,1,4096]{2,1,0:T(1,128)} %param.16) | copy-start | bytes 49156
  31.2 1.1 %copy-start.11 = (f32[6,8,64,128]{3,2,1,0:T(8,128)}, f32[6,8,64,128]{3,2,1,0:T(8,128)S(1)}, u32[]{:S(2)}) copy-start(f32[6,8,64,128]{3,2,1,0:T(8,128)S(1)} %get-tuple-element.29.first_ref) | copy-start | bytes 4718596
  32.4 6.0 %copy-start.7 = (bf16[32,8,8,128]{3,2,1,0:T(8,128)(2,1)}, bf16[32,8,8,128]{3,2,1,0:T(8,128)(2,1)S(1)}, u32[]{:S(2)}) copy-start(bf16[32,8,8,128]{3,2,1,0:T(8,128)(2,1)S(1)} %all-to-all-done.home_ref) | copy-start | bytes 1572868
  38.4 24.8 %all-to-all-start.1 = ((bf16[32,8,128]{2,1,0:T(8,128)(2,1)}), bf16[32,8,128]{2,1,0:T(8,128)(2,1)S(1)}, u32[]{:S(2)}, u32[]{:S(2)}) async-start(bf16[32,8,128]{2,1,0:T(8,128)(2,1)} %get-tuple-element.31), calls=%async_computation.1 | async-start | bytes 131072 | tf_op jit(solution)/shard_map/all_to_all | solution.py:460
  45.9 1.0 %copy-start.8 = (bf16[32,8,8,128]{3,2,1,0:T(8,128)(2,1)S(1)}, bf16[32,8,8,128]{3,2,1,0:T(8,128)(2,1)}, u32[]{:S(2)}) copy-start(bf16[32,8,8,128]{3,2,1,0:T(8,128)(2,1)} %copy-done.7) | copy-start | bytes 1572868
  47.0 1.4 %copy-start.12 = (f32[6,8,64,128]{3,2,1,0:T(8,128)S(1)}, f32[6,8,64,128]{3,2,1,0:T(8,128)}, u32[]{:S(2)}) copy-start(f32[6,8,64,128]{3,2,1,0:T(8,128)} %copy-done.11) | copy-start | bytes 4718596
  48.4 14.8 %copy-start.5 = (bf16[1,1,32,8,8,128]{5,4,3,2,1,0:T(8,128)(2,1)S(1)}, bf16[1,1,32,8,8,128]{5,4,3,2,1,0:T(8,128)(2,1)}, u32[]{:S(2)}) copy-start(bf16[1,1,32,8,8,128]{5,4,3,2,1,0:T(8,128)(2,1)} %param.19) | copy-start | bytes 1572868
  48.4 14.8 %copy-start.10 = (bf16[1,1,32,8,128]{4,3,2,1,0:T(8,128)(2,1)S(1)}, bf16[1,1,32,8,128]{4,3,2,1,0:T(8,128)(2,1)}, u32[]{:S(2)}) copy-start(bf16[1,1,32,8,128]{4,3,2,1,0:T(8,128)(2,1)} %param.21) | copy-start | bytes 196612
  54.4 7.4 %collective-permute-start.4 = (bf16[64,128]{1,0:T(8,128)(2,1)S(1)}, bf16[64,128]{1,0:T(8,128)(2,1)S(1)}, u32[]{:S(2)}, u32[]{:S(2)}) collective-permute-start(bf16[64,128]{1,0:T(8,128)(2,1)S(1)} %get-tuple-element.32), channel_id=1, source_target_pairs={{0,1},{2,3},{4,5},{6,7},{1,0},{3,2},{5,4},{7,6},{8,9},{10,11},{12,... | collective-permute-start | bytes 49160 | tf_op jit(solution)/shard_map/ppermute | solution.py:131
  55.6 6.2 %collective-permute-start.5 = (bf16[64,128]{1,0:T(8,128)(2,1)S(1)}, bf16[64,128]{1,0:T(8,128)(2,1)S(1)}, u32[]{:S(2)}, u32[]{:S(2)}) collective-permute-start(bf16[64,128]{1,0:T(8,128)(2,1)S(1)} %get-tuple-element.33), channel_id=1, source_target_pairs={{1,2},{3,4},{5,6},{2,1},{4,3},{6,5},{9,10},{11,12},{13,14},{10,9},... | collective-permute-start | bytes 49160 | tf_op jit(solution)/shard_map/ppermute | solution.py:131
  57.6 5.5 %collective-permute-start.7 = (bf16[64,128]{1,0:T(8,128)(2,1)S(1)}, bf16[64,128]{1,0:T(8,128)(2,1)S(1)}, u32[]{:S(2)}, u32[]{:S(2)}) collective-permute-start(bf16[64,128]{1,0:T(8,128)(2,1)S(1)} %get-tuple-element.34), channel_id=1, source_target_pairs={{8,16},{16,8},{9,17},{17,9},{10,18},{18,10},{11,19},{19,11},{12,20... | collective-permute-start | bytes 49160 | tf_op jit(solution)/shard_map/ppermute | solution.py:131
  61.7 1.4 %collective-permute-start.6 = (bf16[64,128]{1,0:T(8,128)(2,1)S(1)}, bf16[64,128]{1,0:T(8,128)(2,1)S(1)}, u32[]{:S(2)}, u32[]{:S(2)}) collective-permute-start(bf16[64,128]{1,0:T(8,128)(2,1)S(1)} %get-tuple-element.34), channel_id=1, source_target_pairs={{0,8},{16,24},{8,0},{24,16},{1,9},{17,25},{9,1},{25,17},{2,10},{18... | collective-permute-start | bytes 49160 | tf_op jit(solution)/shard_map/ppermute | solution.py:131
  64.4 17.2 %all-to-all-start.2 = ((f32[32,8,128]{2,1,0:T(8,128)}), f32[32,8,128]{2,1,0:T(8,128)S(1)}, u32[]{:S(2)}, u32[]{:S(2)}) async-start(f32[32,8,128]{2,1,0:T(8,128)} %shard_map.127), calls=%async_computation.2 | async-start | bytes 262144 | tf_op jit(solution)/shard_map/all_to_all | solution.py:460
  70.6 2.8 %copy-start.1 = (bf16[6,8,8,64,128]{4,3,2,1,0:T(8,128)(2,1)S(1)}, bf16[6,8,8,64,128]{4,3,2,1,0:T(8,128)(2,1)}, u32[]{:S(2)}) copy-start(bf16[6,8,8,64,128]{4,3,2,1,0:T(8,128)(2,1)} %diag_ref.3) | copy-start | bytes 18874372
  73.4 2.8 %copy-start.3 = (bf16[6,8,8,64,128]{4,3,2,1,0:T(8,128)(2,1)S(1)}, bf16[6,8,8,64,128]{4,3,2,1,0:T(8,128)(2,1)}, u32[]{:S(2)}) copy-start(bf16[6,8,8,64,128]{4,3,2,1,0:T(8,128)(2,1)} %flux_ref.3) | copy-start | bytes 18874372
  81.6 0.7 copy-start.15

commit v5 on v4

--- a/solution.py
+++ b/solution.py
@@ -50,43 +50,20 @@
     send_y_1[...] = jnp.where(even, low, high)
 
 
-def fetch(copies):
+def opening_kernel(
+    field_hbm, mask_hbm, perm_hbm,
+    send_y_0, send_y_1, send_x, field_ref, mask_ref, perm_ref,
+    side_y, sems,
+):
+    sources, targets = (field_hbm, mask_hbm, perm_hbm), (field_ref, mask_ref, perm_ref)
+    copies = [pltpu.make_async_copy(a, b, sems.at[i]) for i, (a, b) in enumerate(zip(sources, targets))]
     for copy in copies:
         copy.start()
     for copy in copies:
         copy.wait()
-
-
-def opening_kernel(
-    inverse_hbm, coupling_hbm, field_hbm, mask_hbm, perm_hbm,
-    product_ref, send_y_0, send_y_1, send_x,
-    inverse_ref, coupling_ref, field_ref, mask_ref, perm_ref, side_y, sems,
-):
-    sources = (inverse_hbm, coupling_hbm, field_hbm, mask_hbm, perm_hbm)
-    targets = (inverse_ref, coupling_ref, field_ref, mask_ref, perm_ref)
-    copies = [pltpu.make_async_copy(a, b, sems.at[i]) for i, (a, b) in enumerate(zip(sources, targets))]
-    for copy in copies:
-        copy.start()
-    blocks, comps = inverse_ref.shape[:2]
-    copies[0].wait()
-    copies[1].wait()
-
-    def one(b, carry):
-        inverse = inverse_ref[b].astype(F32)
-        coupling = coupling_ref[b].astype(F32)
-        for r in range(comps):
-            row = inverse[r, 0:1] * coupling[0]
-            for m in range(1, comps):
-                row += inverse[r, m : m + 1] * coupling[m]
-            product_ref[b, r] = row.astype(BF16)
-        return carry
-
-    lax.fori_loop(0, blocks, one, 0)
-    for copy in copies[2:]:
-        copy.wait()
     clear = 1.0 - mask_ref[...].astype(F32)
     sends = (send_y_0, send_y_1, send_x)
-    write_edges(lambda k, c: field_ref[k, c], comps, clear, perm_ref, side_y, sends)
+    write_edges(lambda k, c: field_ref[k, c], field_ref.shape[1], clear, perm_ref, side_y, sends)
 
 
 def edge_rows(layers, comps):
@@ -102,23 +79,22 @@
     return pltpu.VMEM((2, edge_rows(layers, comps), cols), F32)
 
 
-def opening(inverse, coupling, field, mask, perm):
+def opening(field, mask, perm):
     layers, comps, rows, cols = field.shape
     hbm = pl.BlockSpec(memory_space=pltpu.HBM)
     vmem = pl.BlockSpec(memory_space=pltpu.VMEM)
-    arrays = (inverse, coupling, field, mask, perm)
+    arrays = (field, mask, perm)
     return pl.pallas_call(
         opening_kernel,
-        in_specs=[hbm] * 5,
-        out_specs=[vmem] * 4,
-        out_shape=[jax.ShapeDtypeStruct(inverse.shape, BF16), *edge_shapes(*field.shape)],
+        in_specs=[hbm] * 3,
+        out_specs=[vmem] * 6,
+        out_shape=[*edge_shapes(*field.shape), *(pltpu.VMEM(array.shape, array.dtype) for array in arrays)],
         scratch_shapes=[
-            *(pltpu.VMEM(array.shape, array.dtype) for array in arrays),
             edge_scratch(layers, comps, cols),
-            pltpu.SemaphoreType.DMA((5,)),
+            pltpu.SemaphoreType.DMA((3,)),
         ],
-        compiler_params=params(24),
-        cost_estimate=cost(16 * inverse.size + 4 * field.size, 160 * field.size),
+        compiler_params=params(16),
+        cost_estimate=cost(4 * field.size, 8 * field.size),
     )(*(pltpu.with_memory_space_constraint(array, pltpu.HBM) for array in arrays))
 
 
@@ -146,17 +122,29 @@
     return 2.0 * centre * beside * reciprocal(centre + beside)
 
 
-def apply_kernel(want_rounded, field_ref, mask_ref, perm_ref, y_0, y_1, x_0, x_1, diag_ref, flux_ref, *rest):
-    if want_rounded:
-        out_ref, rounded_ref, *rest = rest
+def apply_kernel(is_first_apply, field_ref, mask_ref, perm_ref, y_0, y_1, x_0, x_1, diag_in, flux_in, *rest):
+    if is_first_apply:
+        out_ref, rounded_ref, diag_ref, flux_ref, *rest, sems = rest
     else:
         out_hbm, *rest, out_ref, out_sems = rest
+        diag_ref, flux_ref = diag_in, flux_in
     padded, padded_perm, edge_x, place, beside_edge, perm_edge = rest
     layers, comps, rows, cols = field_ref.shape
     top = 8
 
     def out_copy(k):
         return pltpu.make_async_copy(out_ref.at[k], out_hbm.at[k], out_sems.at[k])
+
+    def blocks(k):
+        return (
+            pltpu.make_async_copy(diag_in.at[k], diag_ref.at[k], sems.at[0, k]),
+            pltpu.make_async_copy(flux_in.at[k], flux_ref.at[k], sems.at[1, k]),
+        )
+
+    if is_first_apply:
+        for k in range(layers):
+            for copy in blocks(k):
+                copy.start()
 
     lane = lax.broadcasted_iota(jnp.int32, (rows, cols), 1)
     number = lax.broadcasted_iota(jnp.int32, (cols, cols), 0)
@@ -198,6 +186,9 @@
         padded_perm[top : top + rows] = perm_ref[k]
         padded_perm[top - 1 : top] = jnp.where(even_y, perm_1, perm_0)
         padded_perm[top + rows : top + rows + 1] = jnp.where(even_y, perm_0, perm_1)
+        if is_first_apply:
+            for copy in blocks(k):
+                copy.wait()
         narrow = lax.broadcasted_iota(jnp.int32, (TILE, cols), 1)
         is_first, is_last = narrow == 0, narrow == cols - 1
         for y in range(0, rows, TILE):
@@ -237,32 +228,36 @@
             for c in range(comps):
                 value = total[c] + well * field_ref[k, c, here]
                 out_ref[k, c, here] = value
-                if want_rounded:
+                if is_first_apply:
                     columns = pl.ds(pl.multiple_of(k * cols, cols), cols)
                     rounded_ref[c * rows + y : c * rows + y + TILE, columns] = value.astype(BF16)
-        if not want_rounded:
+        if not is_first_apply:
             out_copy(k).start()
         return carry
 
     lax.fori_loop(0, layers, layer, 0)
-    if not want_rounded:
+    if not is_first_apply:
         for k in range(layers):
             out_copy(k).wait()
 
 
-def apply_transposed(field, mask, perm, halos, diag, flux, want_rounded):
+def apply_transposed(field, mask, perm, halos, diag, flux, is_first_apply):
     layers, comps, rows, cols = field.shape
     vmem = pl.BlockSpec(memory_space=pltpu.VMEM)
+    hbm = pl.BlockSpec(memory_space=pltpu.HBM)
     out_shape = [jax.ShapeDtypeStruct(field.shape, F32)]
-    if want_rounded:
-        out_specs, tail = [vmem, vmem], []
+    if is_first_apply:
+        block_spec, out_specs = hbm, [vmem] * 4
         out_shape.append(jax.ShapeDtypeStruct((comps * rows, layers * cols), BF16))
+        out_shape += [pltpu.VMEM(diag.shape, BF16), pltpu.VMEM(flux.shape, BF16)]
+        tail = [pltpu.SemaphoreType.DMA((2, layers))]
+        diag, flux = (pltpu.with_memory_space_constraint(block, pltpu.HBM) for block in (diag, flux))
     else:
-        out_specs = [pl.BlockSpec(memory_space=pltpu.HBM)]
+        block_spec, out_specs = vmem, [hbm]
         tail = [pltpu.VMEM(field.shape, F32), pltpu.SemaphoreType.DMA((layers,))]
     return pl.pallas_call(
-        functools.partial(apply_kernel, want_rounded),
-        in_specs=[vmem] * 9,
+        functools.partial(apply_kernel, is_first_apply),
+        in_specs=[vmem] * 7 + [block_spec] * 2,
         out_specs=out_specs,
         out_shape=out_shape,
         scratch_shapes=[
@@ -290,10 +285,9 @@
     return jnp.where(number == column, 1.0, 0.0).astype(BF16)
 
 
-def gather_kernel(rows, cols, helper_ref, count_ref, cells_ref, rounded_ref, picked_ref, sent_ref):
+def gather_kernel(rows, cols, helper_ref, count_ref, cells_ref, rounded_ref, sent_ref):
     chunks, _, slots = cells_ref.shape
-    width = picked_ref.shape[-1]
-    comps = picked_ref.shape[1]
+    comps, width = sent_ref.shape[1:]
     per_chunk = slots // width
     row_number = lax.broadcasted_iota(jnp.int32, (rows, slots), 0)
 
@@ -310,9 +304,7 @@
         for j in range(per_chunk):
             b = i * per_chunk + j
             live = jnp.where(b < count_ref[0, 0], 1.0, 0.0)
-            value = (values[:, j * width : (j + 1) * width] * live).astype(BF16)
-            picked_ref[b] = value
-            sent_ref[helper_ref[0, 0, b]] = value
+            sent_ref[helper_ref[0, 0, b]] = (values[:, j * width : (j + 1) * width] * live).astype(BF16)
         return carry
 
     lax.fori_loop(0, chunks, one, 0)
@@ -326,20 +318,69 @@
     return pl.pallas_call(
         functools.partial(gather_kernel, rows, cols),
         in_specs=[smem, smem, vmem, vmem],
-        out_specs=[vmem, vmem],
-        out_shape=[shape, shape],
-        compiler_params=params(32),
+        out_specs=vmem,
+        out_shape=shape,
+        compiler_params=params(16),
         cost_estimate=cost(2 * rounded.size * cells.size, 2 * rounded.size),
     )(helper, count, cells, rounded)
 
 
+PARTS = 3
+
+
+def helper_kernel(inverse_ref, coupling_ref, state_ref, picked_ref, reply_ref):
+    blocks, comps = inverse_ref.shape[:2]
+    width = inverse_ref.shape[-1]
+
+    def transposed(block_ref, b, value):
+        block = block_ref[b].astype(F32)
+        total = block[0] * value[0:1]
+        for r in range(1, comps):
+            total += block[r] * value[r : r + 1]
+        return total
+
+    def one(b, totals):
+        multiplier = transposed(inverse_ref, b, picked_ref[b].astype(F32))
+        state = state_ref[b].astype(F32)
+        part = multiplier * state
+        correction = -transposed(coupling_ref, b, multiplier)
+        reply_ref[b, 0:comps] = correction.astype(BF16)
+        return tuple(totals[j] + part * state[j : j + 1] for j in range(comps))
+
+    totals = lax.fori_loop(0, blocks, one, (jnp.zeros((comps, width), F32),) * comps)
+    lane = lax.broadcasted_iota(jnp.int32, (comps, width), 1)
+    rest = jnp.zeros((comps, width), F32)
+    for j in range(comps):
+        column = jnp.sum(totals[j], axis=1, keepdims=True)
+        rest = jnp.where(lane % comps == j, column, rest)
+    packed = jnp.zeros((comps, width), F32)
+    for part in range(PARTS):
+        rounded = rest.astype(BF16).astype(F32)
+        packed = jnp.where(lane // comps == part, rounded, packed)
+        rest = rest - rounded
+    packed = packed.astype(BF16)
+    for b in range(blocks):
+        reply_ref[b, comps : 2 * comps] = packed
+
+
+def at_helper(inverse, coupling, state, picked):
+    blocks, comps, _, width = inverse.shape
+    return pl.pallas_call(
+        helper_kernel,
+        out_shape=jax.ShapeDtypeStruct((blocks, 2 * comps, width), BF16),
+        compiler_params=params(16),
+        cost_estimate=cost(4 * inverse.size, 4 * inverse.size),
+    )(inverse, coupling, state, picked)
+
+
 def scatter_kernel(
-    helper_ref, cells_ref, picked_ref, home_ref, first_ref, mask_ref, perm_ref,
-    second_ref, send_y_0, send_y_1, send_x, added, side_y,
+    scale, helper_ref, cells_ref, back_ref, first_ref, mask_ref, perm_ref,
+    second_ref, send_y_0, send_y_1, send_x, grad_ref,
+    added, side_y,
 ):
     layers, comps, rows, cols = first_ref.shape
     chunks, _, slots = cells_ref.shape
-    width = picked_ref.shape[-1]
+    width = back_ref.shape[-1]
     per_chunk = slots // width
     row_number = lax.broadcasted_iota(jnp.int32, (rows, slots), 0)
     added[...] = jnp.zeros_like(added)
@@ -347,15 +388,7 @@
     def one(i, carry):
         column, y = split_cells(cells_ref[i], rows, cols)
         chosen = one_hot(column, added.shape[1], slots)
-        parts = []
-        for j in range(per_chunk):
-            b = i * per_chunk + j
-            home = home_ref[helper_ref[0, 0, b]].astype(F32)
-            value = picked_ref[b].astype(F32)
-            part = home[0] * value[0:1]
-            for r in range(1, comps):
-                part += home[r] * value[r : r + 1]
-            parts.append((-part).astype(BF16).astype(F32))
+        parts = [back_ref[helper_ref[0, 0, i * per_chunk + j]].astype(F32)[:comps] for j in range(per_chunk)]
         correction = jnp.concatenate(parts, axis=1)
         at_row = row_number == y
         spread = jnp.concatenate(
@@ -372,68 +405,33 @@
     sends = (send_y_0, send_y_1, send_x)
     write_edges(lambda k, c: second_ref[k, c], comps, clear, perm_ref, side_y, sends)
 
-
-def scatter(first, picked, home, helper, cells, mask, perm):
+    def add_part(b, total):
+        return total + back_ref[b].astype(F32)[comps:]
+
+    total = lax.fori_loop(0, back_ref.shape[0], add_part, jnp.zeros((comps, width), F32))
+    whole = total
+    for part in range(1, PARTS):
+        whole += pltpu.roll(total, width - part * comps, 1)
+    grad_ref[...] = (whole * scale)[:, :comps]
+
+
+def scatter(first, back, helper, cells, mask, perm, scale):
     layers, comps, rows, cols = first.shape
     smem = pl.BlockSpec(memory_space=pltpu.SMEM)
     vmem = pl.BlockSpec(memory_space=pltpu.VMEM)
     return pl.pallas_call(
-        scatter_kernel,
-        in_specs=[smem] + [vmem] * 6,
-        out_specs=[vmem] * 4,
-        out_shape=[jax.ShapeDtypeStruct(first.shape, F32), *edge_shapes(*first.shape)],
+        functools.partial(scatter_kernel, scale),
+        in_specs=[smem] + [vmem] * 5,
+        out_specs=[vmem] * 5,
+        out_shape=[
+            jax.ShapeDtypeStruct(first.shape, F32),
+            *edge_shapes(*first.shape),
+            jax.ShapeDtypeStruct((comps, comps), F32),
+        ],
         scratch_shapes=[pltpu.VMEM((comps * rows, layers * cols), F32), edge_scratch(layers, comps, cols)],
         compiler_params=params(24),
-        cost_estimate=cost(2 * first.size * cells.size, 160 * first.size),
-    )(helper, cells, picked, home, first, mask, perm)
-
-
-def grad_kernel(inverse_ref, state_ref, picked_ref, out_ref):
-    blocks, comps = inverse_ref.shape[:2]
-    width = inverse_ref.shape[-1]
-
-    def one(b, totals):
-        inverse = inverse_ref[b].astype(F32)
-        value = picked_ref[b].astype(F32)
-        state = state_ref[b].astype(F32)
-        part = inverse[0] * value[0:1]
-        for r in range(1, comps):
-            part += inverse[r] * value[r : r + 1]
-        part *= state
-        return tuple(totals[j] + part * state[j : j + 1] for j in range(comps))
-
-    totals = lax.fori_loop(0, blocks, one, (jnp.zeros((comps, width), F32),) * comps)
-    lane = lax.broadcasted_iota(jnp.int32, (comps, width), 1)
-    result = jnp.zeros((comps, width), F32)
-    for j in range(comps):
-        result = jnp.where(lane == j, jnp.sum(totals[j], axis=1, keepdims=True), result)
-    for i in range(out_ref.shape[0]):
-        out_ref[i] = result
-
-
-def grad_part(inverse, state, picked, copies):
-    comps, width = inverse.shape[1], inverse.shape[-1]
-    return pl.pallas_call(
-        grad_kernel,
-        out_shape=jax.ShapeDtypeStruct((copies, comps, width), F32),
-        compiler_params=params(24),
-        cost_estimate=cost(4 * inverse.size, 2 * inverse.size),
-    )(inverse, state, picked)
-
-
-def total_kernel(scale, parts_ref, out_ref):
-    total = parts_ref[0]
-    for i in range(1, parts_ref.shape[0]):
-        total += parts_ref[i]
-    out_ref[...] = (total * scale)[:, : out_ref.shape[1]]
-
-
-def grad_total(parts, scale):
-    return pl.pallas_call(
-        functools.partial(total_kernel, scale),
-        out_shape=jax.ShapeDtypeStruct((parts.shape[1],) * 2, F32),
-        cost_estimate=cost(parts.size, 4 * parts.size),
-    )(parts)
+        cost_estimate=cost(2 * first.size * cells.size, 8 * first.size),
+    )(helper, cells, back, first, mask, perm)
 
 
 def shards(
@@ -459,20 +457,18 @@
     def to_partners(array):
         return lax.all_to_all(array, AXES, split_axis=0, concat_axis=0, tiled=True)
 
-    product, *sides = opening(inverse, coupling, cotangent, well_mask, permeability)
-    home = to_partners(product)
+    *sides, field, mask, perm = opening(cotangent, well_mask, permeability)
     halos = exchange(*sides)
-    first, rounded = apply_transposed(cotangent, well_mask, permeability, halos, diag_block, flux_block, True)
-    rounded, home = lax.optimization_barrier((rounded, home))
-    picked, sent = gather(rounded, cells, helper_of, block_count, comps, rows, cols, width)
-    at_helper = to_partners(sent)
-    second, *sides = scatter(first, picked, home, helper_of, cells, well_mask, permeability)
+    first, rounded, *kept = apply_transposed(field, mask, perm, halos, diag_block, flux_block, True)
+    sent = gather(rounded, cells, helper_of, block_count, comps, rows, cols, width)
+    reply = at_helper(inverse, coupling, state, to_partners(sent))
+    devices = lax.axis_size("gx") * lax.axis_size("gy")
+    scale = -1.0 / math.sqrt(width * devices * devices)
+    second, *sides, interaction_grad = scatter(
+        first, to_partners(reply), helper_of, cells, mask, perm, scale
+    )
     halos = exchange(*sides)
-    at_helper, *halos = lax.optimization_barrier((at_helper, *halos))
-    devices = lax.axis_size("gx") * lax.axis_size("gy")
-    parts = to_partners(grad_part(inverse, state, at_helper, devices))
-    (adjoint,) = apply_transposed(second, well_mask, permeability, halos, diag_block, flux_block, False)
-    interaction_grad = grad_total(parts, -1.0 / math.sqrt(width * devices * devices))
+    (adjoint,) = apply_transposed(second, mask, perm, halos, *kept, False)
     return (adjoint, interaction_grad)
 
 

time: 85.3 us -> 70.1 us (0.82); the launches traced: 83.8 us -> 69.8 us
  blocking collectives: 0 us -> 21 us
  starting transfers between devices: 34.9 us -> 15 us
  local copies, waits for them, and re-layouts: 15.4 us -> 0.03 us
  waiting for transfers between devices: 3.76 us -> 5.09 us
    all_to_all x0 -> x2, blocking collectives: none -> 21 us  [to_partners(): return lax.all_to_all(array, AXES, split_axis=0, concat_axis=0, tiled=True)]
    all_to_all x3 -> x0, starting transfers between devices: 20.1 us -> none  [to_partners(): return lax.all_to_all(array, AXES, split_axis=0, concat_axis=0, tiled=True)]
    unnamed x32 -> x10, local copies, waits for them, and re-layouts: 15.4 us -> 0.03 us
    ppermute x8, waiting for transfers between devices: 3.75 us -> 5.09 us  [swaps(): lax.ppermute(array, axis, pairs + [(j, i) for i, j in pairs])]
    pallas_call x6 -> x5, Pallas kernels: 22.3 us -> 22 us  [the longest x2 12.5 us: apply_transposed(): pl.pallas_call(functools.partial(apply_kernel, is_first_apply), in_specs=...]
  transfers between devices with their start and end apart: 11 -> 8, of which waited for: 2 -> 2; matrix products, arithmetic and copies ran while one was open for 0% -> 0% of each run, Pallas kernels for 19% -> 0%
where the time goes in v5:
time: 70.1 us; the launch traced here: 69.8 us
  Pallas kernels  27.4 us (39%)
  blocking collectives  21 us (30%)
  starting transfers between devices  15 us (21%)
  waiting for transfers between devices  5.09 us (7%)
  between operations  1.43 us (2%)
    all_to_all x2, blocking collectives, to_partners(): return lax.all_to_all(array, AXES, split_axis=0, concat_axis=0, tiled=True)  21 us
    ppermute x8, starting transfers between devices, swaps(): lax.ppermute(array, axis, pairs + [(j, i) for i, j in pairs])  15 us
    pallas_call x2, Pallas kernels, apply_transposed(): pl.pallas_call(functools.partial(apply_kernel, is_first_apply), in_specs=...  12.5 us
    pallas_call x1, Pallas kernels, scatter(): pl.pallas_call(functools.partial(scatter_kernel, scale), in_specs=[smem]...  6.85 us
    pallas_call x1, Pallas kernels, gather(): pl.pallas_call(functools.partial(gather_kernel, rows, cols), in_specs=[sm...  5.35 us
    ppermute x8, waiting for transfers between devices, swaps(): lax.ppermute(array, axis, pairs + [(j, i) for i, j in pairs])  5.09 us
    pallas_call x1, Pallas kernels, opening(): pl.pallas_call(opening_kernel, in_specs=[hbm] * 3, out_specs=[vmem] * 6,...  1.76 us
  transfers between devices with their start and end apart: 8, of which 2 were waited for; matrix products, arithmetic and copies ran while one was open for 0% of the time, Pallas kernels for 0%

profile of v5, /device:TPU:9, one launch (start us, length us, event | category | flops | bytes accessed | tf_op | source)
XLA Modules:
  0.0 69.8 jit_solution(16304347976026793630)
XLA Ops:
  0.6 1.8 %shard_map.122 = (bf16[64,128]{1,0:T(8,128)(2,1)S(1)}, bf16[64,128]{1,0:T(8,128)(2,1)S(1)}, bf16[64,128]{1,0:T(8,128)(2,1)S(1)}, f32[6,8,64,128]{3,2,1,0:T(8,128...) custom-call(f32[6,8,64,128]{3,2,1,0:T(8,128)} %field_hbm.1, s32[64,128]{1,0:T(8,128)} %mask_hbm.1, ...), custom_call_target="tpu_custom_call" | custom-call | flops 1572864 | bytes 3145728 | tf_op jit(solution)/shard_map/pallas_call | solution.py:87
  2.4 0.7 %collective-permute-start.2 = (bf16[64,128]{1,0:T(8,128)(2,1)S(1)}, bf16[64,128]{1,0:T(8,128)(2,1)S(1)}, u32[]{:S(2)}, u32[]{:S(2)}) collective-permute-start(bf16[64,128]{1,0:T(8,128)(2,1)S(1)} %get-tuple-element.22), channel_id=1, source_target_pairs={{0,8},{16,24},{8,0},{24,16},{1,9},{17,25},{9,1},{25,17},{2,10},{18... | collective-permute-start | bytes 49160 | tf_op jit(solution)/shard_map/ppermute | solution.py:107
  3.1 3.0 %collective-permute-start.3 = (bf16[64,128]{1,0:T(8,128)(2,1)S(1)}, bf16[64,128]{1,0:T(8,128)(2,1)S(1)}, u32[]{:S(2)}, u32[]{:S(2)}) collective-permute-start(bf16[64,128]{1,0:T(8,128)(2,1)S(1)} %get-tuple-element.22), channel_id=1, source_target_pairs={{8,16},{16,8},{9,17},{17,9},{10,18},{18,10},{11,19},{19,11},{12,20... | collective-permute-start | bytes 49160 | tf_op jit(solution)/shard_map/ppermute | solution.py:107
  6.2 1.3 %collective-permute-start = (bf16[64,128]{1,0:T(8,128)(2,1)S(1)}, bf16[64,128]{1,0:T(8,128)(2,1)S(1)}, u32[]{:S(2)}, u32[]{:S(2)}) collective-permute-start(bf16[64,128]{1,0:T(8,128)(2,1)S(1)} %get-tuple-element.20), channel_id=1, source_target_pairs={{0,1},{2,3},{4,5},{6,7},{1,0},{3,2},{5,4},{7,6},{8,9},{10,11},{12,... | collective-permute-start | bytes 49160 | tf_op jit(solution)/shard_map/ppermute | solution.py:107
  7.5 2.0 %collective-permute-start.1 = (bf16[64,128]{1,0:T(8,128)(2,1)S(1)}, bf16[64,128]{1,0:T(8,128)(2,1)S(1)}, u32[]{:S(2)}, u32[]{:S(2)}) collective-permute-start(bf16[64,128]{1,0:T(8,128)(2,1)S(1)} %get-tuple-element.21), channel_id=1, source_target_pairs={{1,2},{3,4},{5,6},{2,1},{4,3},{6,5},{9,10},{11,12},{13,14},{10,9},... | collective-permute-start | bytes 49160 | tf_op jit(solution)/shard_map/ppermute | solution.py:107
  10.2 0.0 collective-permute-done.2.x_0
  10.2 0.0 collective-permute-done.3.x_1
  10.2 0.0 collective-permute-done.y_0
  10.2 2.6 %collective-permute-done.1.y_1 = bf16[64,128]{1,0:T(8,128)(2,1)S(1)} collective-permute-done((bf16[64,128]{1,0:T(8,128)(2,1)S(1)}, bf16[64,128]{1,0:T(8,128)(2,1)S(1)}, u32[]{:S(2)}, u32[]{:S(2)}) %collective-permute-start.1) | collective-permute-done | bytes 16416 | tf_op jit(solution)/shard_map/ppermute | solution.py:107
  12.8 6.9 %shard_map.123 = (f32[6,8,64,128]{3,2,1,0:T(8,128)S(1)}, bf16[512,768]{1,0:T(8,128)(2,1)S(1)}, bf16[6,8,8,64,128]{4,3,2,1,0:T(8,128)(2,1)S(1)}, bf16[6,8,8,64,128]{4,3,2,1,0:T(8,128)(2,1)S(1)}) custom-call(f32[6,8,64,128]{3,2,1,0:T(8,128)S(1)} %get-tuple-element.17.field_ref, s32[64,128]{1,0:T(8,128)S(1)} %get-tuple-element.18.mask_ref, ...), custom_call_target="tpu_custom_call" | custom-call | flops 25165824 | bytes 15728640 | tf_op jit(solution)/shard_map/pallas_call | solution.py:258
  19.7 0.0 copy-done.3
  19.7 0.0 copy-done.4
  19.7 0.0 copy-start
  19.7 0.0 copy-start.1
  19.8 0.0 copy-start.2
  19.8 5.4 %shard_map.124 = bf16[32,8,128]{2,1,0:T(8,128)(2,1)S(1)} custom-call(s32[1,1,32]{2,1,0:T(1,128)S(1)} %copy-done.4, s32[1,1]{1,0:T(1,128)S(6)} %copy.13.count_ref, s32[8,1,512]{2,1,0:T(1,128)S(1)} %bitcast.7, bf16[512,768]{1,0:T(8,128)(2,1)S(1)} %get-tuple-element.23.rounded_ref), custom_call_target="tpu_custom_call" | custom-call | flops 3221225472 | bytes 786432 | tf_op jit(solution)/shard_map/pallas_call | solution.py:318
  25.1 11.4 %all_to_all.10.picked_ref = bf16[32,8,128]{2,1,0:T(8,128)(2,1)S(1)} all-to-all(bf16[32,8,128]{2,1,0:T(8,128)(2,1)S(1)} %shard_map.124), channel_id=1, replica_groups=mesh['gx'=4,'gy'=8] {'gx','gy'}, dimensions={0} | all-to-all | bytes 131072 | tf_op jit(solution)/shard_map/all_to_all | solution.py:458
  36.5 0.0 copy-done
  36.5 0.0 copy-done.1
  36.5 0.0 copy-done.2
  36.5 0.9 %shard_map.125 = bf16[32,16,128]{2,1,0:T(8,128)(2,1)S(1)} custom-call(bf16[32,8,8,128]{3,2,1,0:T(8,128)(2,1)S(1)} %bitcast.4, bf16[32,8,8,128]{3,2,1,0:T(8,128)(2,1)S(1)} %bitcast.5, bf16[32,8,128]{2,1,0:T(8,128)(2,1)S(1)} %bitcast.6, bf16[32,8,128]{2,1,0:T(8,128)(2,1)S(1)} %all_to_all.10.picked_ref), custom_call_target="tpu_custom_call" | custom-call | flops 1048576 | bytes 1048576 | tf_op jit(solution)/shard_map/pallas_call | solution.py:368
  37.4 9.6 %all_to_all.11.back_ref = bf16[32,16,128]{2,1,0:T(8,128)(2,1)S(1)} all-to-all(bf16[32,16,128]{2,1,0:T(8,128)(2,1)S(1)} %shard_map.125), channel_id=1, replica_groups=mesh['gx'=4,'gy'=8] {'gx','gy'}, dimensions={0} | all-to-all | bytes 262144 | tf_op jit(solution)/shard_map/all_to_all | solution.py:458
  46.9 6.8 %shard_map.126 = (f32[6,8,64,128]{3,2,1,0:T(8,128)S(1)}, bf16[64,128]{1,0:T(8,128)(2,1)S(1)}, bf16[64,128]{1,0:T(8,128)(2,1)S(1)}, bf16[64,128]{1,0:T(8,128)(2,1)S(1)}, f32[8,8]{1,0:T(8,128)}) custom-call(s32[1,1,32]{2,1,0:T(1,128)S(1)} %copy-done.4, s32[8,1,512]{2,1,0:T(1,128)S(1)} %bitcast.8, bf16[32,16,128]{2,1,0:T(8,128)(2,1)S(1)} %all_to_all.11.back_ref, ...), custom_call_target="tpu_custom_call" | custom-call | flops 3221225472 | bytes 3145728 | tf_op jit(solution)/shard_map/pallas_call | solution.py:422
  53.8 1.1 %collective-permute-start.4 = (bf16[64,128]{1,0:T(8,128)(2,1)S(1)}, bf16[64,128]{1,0:T(8,128)(2,1)S(1)}, u32[]{:S(2)}, u32[]{:S(2)}) collective-permute-start(bf16[64,128]{1,0:T(8,128)(2,1)S(1)} %get-tuple-element.26), channel_id=1, source_target_pairs={{0,1},{2,3},{4,5},{6,7},{1,0},{3,2},{5,4},{7,6},{8,9},{10,11},{12,... | collective-permute-start | bytes 49160 | tf_op jit(solution)/shard_map/ppermute | solution.py:107
  54.8 3.2 %collective-permute-start.5 = (bf16[64,128]{1,0:T(8,128)(2,1)S(1)}, bf16[64,128]{1,0:T(8,128)(2,1)S(1)}, u32[]{:S(2)}, u32[]{:S(2)}) collective-permute-start(bf16[64,128]{1,0:T(8,128)(2,1)S(1)} %get-tuple-element.27), channel_id=1, source_target_pairs={{1,2},{3,4},{5,6},{2,1},{4,3},{6,5},{9,10},{11,12},{13,14},{10,9},... | collective-permute-start | bytes 49160 | tf_op jit(solution)/shard_map/ppermute | solution.py:107
  58.0 1.0 %collective-permute-start.6 = (bf16[64,128]{1,0:T(8,128)(2,1)S(1)}, bf16[64,128]{1,0:T(8,128)(2,1)S(1)}, u32[]{:S(2)}, u32[]{:S(2)}) collective-permute-start(bf16[64,128]{1,0:T(8,128)(2,1)S(1)} %get-tuple-element.28), channel_id=1, source_target_pairs={{0,8},{16,24},{8,0},{24,16},{1,9},{17,25},{9,1},{25,17},{2,10},{18... | collective-permute-start | bytes 49160 | tf_op jit(solution)/shard_map/ppermute | solution.py:107
  59.1 2.6 %collective-permute-start.7 = (bf16[64,128]{1,0:T(8,128)(2,1)S(1)}, bf16[64,128]{1,0:T(8,128)(2,1)S(1)}, u32[]{:S(2)}, u32[]{:S(2)}) collective-permute-start(bf16[64,128]{1,0:T(8,128)(2,1)S(1)} %get-tuple-element.28), channel_id=1, source_target_pairs={{8,16},{16,8},{9,17},{17,9},{10,18},{18,10},{11,19},{19,11},{12,20... | collective-permute-start | bytes 49160 | tf_op jit(solution)/shard_map/ppermute | solution.py:107
  61.7 0.0 collective-permute-done.4.y_0
  61.7 0.0 collective-permute-done.5.y_1
  61.7 0.0 collective-permute-done.6.x_0
  61.7 2.4 %collective-permute-done.7.x_1 = bf16[64,128]{1,0:T(8,128)(2,1)S(1)} collective-permute-done((bf16[64,128]{1,0:T(8,128)(2,1)S(1)}, bf16[64,128]{1,0:T(8,128)(2,1)S(1)}, u32[]{:S(2)}, u32[]{:S(2)}) %collective-permute-start.7) | collective-permute-done | bytes 16416 | tf_op jit(solution)/shard_map/ppermute | solution.py:107
  64.1 5.7 %shard_map.127 = f32[6,8,64,128]{3,2,1,0:T(8,128)} custom-call(f32[6,8,64,128]{3,2,1,0:T(8,128)S(1)} %get-tuple-element.25.field_ref, s32[64,128]{1,0:T(8,128)S(1)} %get-tuple-element.18.mask_ref, f32[6,64,128]{2,1,0:T(8,128)S(1)} %get-tuple-element.19.perm_ref, bf16[64,128]{1,0:T(8,128)(2,1)S(1)} %collective-permute-done.4.y_0, ...), custom_call_target="tpu_custom_call" | custom-call | flops 25165824 | bytes 15728640 | tf_op jit(solution)/shard_map/pallas_call | solution.py:258
  (2 shorter events, 0.0 us)
Async XLA Ops:
  2.4 7.8 %collective-permute-start.2 = (bf16[64,128]{1,0:T(8,128)(2,1)S(1)}, bf16[64,128]{1,0:T(8,128)(2,1)S(1)}, u32[]{:S(2)}, u32[]{:S(2)}) collective-permute-start(bf16[64,128]{1,0:T(8,128)(2,1)S(1)} %get-tuple-element.22), channel_id=1, source_target_pairs={{0,8},{16,24},{8,0},{24,16},{1,9},{17,25},{9,1},{25,17},{2,10},{18... | collective-permute-start | bytes 49160 | tf_op jit(solution)/shard_map/ppermute | solution.py:107
  3.1 7.0 %collective-permute-start.3 = (bf16[64,128]{1,0:T(8,128)(2,1)S(1)}, bf16[64,128]{1,0:T(8,128)(2,1)S(1)}, u32[]{:S(2)}, u32[]{:S(2)}) collective-permute-start(bf16[64,128]{1,0:T(8,128)(2,1)S(1)} %get-tuple-element.22), channel_id=1, source_target_pairs={{8,16},{16,8},{9,17},{17,9},{10,18},{18,10},{11,19},{19,11},{12,20... | collective-permute-start | bytes 49160 | tf_op jit(solution)/shard_map/ppermute | solution.py:107
  6.2 4.0 %collective-permute-start = (bf16[64,128]{1,0:T(8,128)(2,1)S(1)}, bf16[64,128]{1,0:T(8,128)(2,1)S(1)}, u32[]{:S(2)}, u32[]{:S(2)}) collective-permute-start(bf16[64,128]{1,0:T(8,128)(2,1)S(1)} %get-tuple-element.20), channel_id=1, source_target_pairs={{0,1},{2,3},{4,5},{6,7},{1,0},{3,2},{5,4},{7,6},{8,9},{10,11},{12,... | collective-permute-start | bytes 49160 | tf_op jit(solution)/shard_map/ppermute | solution.py:107
  7.5 5.4 %collective-permute-start.1 = (bf16[64,128]{1,0:T(8,128)(2,1)S(1)}, bf16[64,128]{1,0:T(8,128)(2,1)S(1)}, u32[]{:S(2)}, u32[]{:S(2)}) collective-permute-start(bf16[64,128]{1,0:T(8,128)(2,1)S(1)} %get-tuple-element.21), channel_id=1, source_target_pairs={{1,2},{3,4},{5,6},{2,1},{4,3},{6,5},{9,10},{11,12},{13,14},{10,9},... | collective-permute-start | bytes 49160 | tf_op jit(solution)/shard_map/ppermute | solution.py:107
  12.8 6.9 %copy-start.3 = (s32[1,1,4096]{2,1,0:T(1,128)S(1)}, s32[1,1,4096]{2,1,0:T(1,128)}, u32[]{:S(2)}) copy-start(s32[1,1,4096]{2,1,0:T(1,128)} %param.16) | copy-start | bytes 49156
  12.8 6.9 %copy-start.4 = (s32[1,1,32]{2,1,0:T(1,128)S(1)}, s32[1,1,32]{2,1,0:T(1,128)}, u32[]{:S(2)}) copy-start(s32[1,1,32]{2,1,0:T(1,128)} %helper_ref.3) | copy-start | bytes 388
  19.7 16.8 %copy-start = (bf16[1,1,32,8,8,128]{5,4,3,2,1,0:T(8,128)(2,1)S(1)}, bf16[1,1,32,8,8,128]{5,4,3,2,1,0:T(8,128)(2,1)}, u32[]{:S(2)}) copy-start(bf16[1,1,32,8,8,128]{5,4,3,2,1,0:T(8,128)(2,1)} %param.19) | copy-start | bytes 1572868
  19.7 16.8 %copy-start.1 = (bf16[1,1,32,8,8,128]{5,4,3,2,1,0:T(8,128)(2,1)S(1)}, bf16[1,1,32,8,8,128]{5,4,3,2,1,0:T(8,128)(2,1)}, u32[]{:S(2)}) copy-start(bf16[1,1,32,8,8,128]{5,4,3,2,1,0:T(8,128)(2,1)} %param.20) | copy-start | bytes 1572868
  19.8 16.8 %copy-start.2 = (bf16[1,1,32,8,128]{4,3,2,1,0:T(8,128)(2,1)S(1)}, bf16[1,1,32,8,128]{4,3,2,1,0:T(8,128)(2,1)}, u32[]{:S(2)}) copy-start(bf16[1,1,32,8,128]{4,3,2,1,0:T(8,128)(2,1)} %param.21) | copy-start | bytes 196612
  53.8 7.9 %collective-permute-start.4 = (bf16[64,128]{1,0:T(8,128)(2,1)S(1)}, bf16[64,128]{1,0:T(8,128)(2,1)S(1)}, u32[]{:S(2)}, u32[]{:S(2)}) collective-permute-start(bf16[64,128]{1,0:T(8,128)(2,1)S(1)} %get-tuple-element.26), channel_id=1, source_target_pairs={{0,1},{2,3},{4,5},{6,7},{1,0},{3,2},{5,4},{7,6},{8,9},{10,11},{12,... | collective-permute-start | bytes 49160 | tf_op jit(solution)/shard_map/ppermute | solution.py:107
  54.8 6.8 %collective-permute-start.5 = (bf16[64,128]{1,0:T(8,128)(2,1)S(1)}, bf16[64,128]{1,0:T(8,128)(2,1)S(1)}, u32[]{:S(2)}, u32[]{:S(2)}) collective-permute-start(bf16[64,128]{1,0:T(8,128)(2,1)S(1)} %get-tuple-element.27), channel_id=1, source_target_pairs={{1,2},{3,4},{5,6},{2,1},{4,3},{6,5},{9,10},{11,12},{13,14},{10,9},... | collective-permute-start | bytes 49160 | tf_op jit(solution)/shard_map/ppermute | solution.py:107
  58.0 3.6 %collective-permute-start.6 = (bf16[64,128]{1,0:T(8,128)(2,1)S(1)}, bf16[64,128]{1,0:T(8,128)(2,1)S(1)}, u32[]{:S(2)}, u32[]{:S(2)}) collective-permute-start(bf16[64,128]{1,0:T(8,128)(2,1)S(1)} %get-tuple-element.28), channel_id=1, source_target_pairs={{0,8},{16,24},{8,0},{24,16},{1,9},{17,25},{9,1},{25,17},{2,10},{18... | collective-permute-start | bytes 49160 | tf_op jit(solution)/shard_map/ppermute | solution.py:107
  59.1 5.0 %collective-permute-start.7 = (bf16[64,128]{1,0:T(8,128)(2,1)S(1)}, bf16[64,128]{1,0:T(8,128)(2,1)S(1)}, u32[]{:S(2)}, u32[]{:S(2)}) collective-permute-start(bf16[64,128]{1,0:T(8,128)(2,1)S(1)} %get-tuple-element.28), channel_id=1, source_target_pairs={{8,16},{16,8},{9,17},{17,9},{10,18},{18,10},{11,19},{19,11},{12,20... | collective-permute-start | bytes 49160 | tf_op jit(solution)/shard_map/ppermute | solution.py:107

commit v6 on v5

--- a/solution.py
+++ b/solution.py
@@ -12,7 +12,7 @@
 BF16 = jnp.bfloat16
 AXES = ("gx", "gy")
 MIB = 1024 * 1024
-CHUNK = 512
+GATHER_CHUNK, SCATTER_CHUNK = 512, 1024
 
 
 def params(mib):
@@ -27,15 +27,16 @@
     return -(-number // step) * step
 
 
-def write_edges(field, comps, clear, perm_ref, side_y, sends):
+def write_edges(field, shape, clear, perm_ref, side_y, sends):
     send_y_0, send_y_1, send_x = sends
-    layers, rows, cols = perm_ref.shape
+    layers, comps, rows, cols = shape
+    with_perm = perm_ref is not None
     lane = lax.broadcasted_iota(jnp.int32, (rows, cols), 1)
     pair = lane // 2
     along_x = jnp.zeros((rows, cols), F32)
     side_y[...] = jnp.zeros_like(side_y)
     for k in range(layers):
-        for c in range(comps + 1):
+        for c in range(comps + with_perm):
             if c < comps:
                 value, at = field(k, c) * clear, k * comps + c
             else:
@@ -51,19 +52,23 @@
 
 
 def opening_kernel(
-    field_hbm, mask_hbm, perm_hbm,
-    send_y_0, send_y_1, send_x, field_ref, mask_ref, perm_ref,
+    field_hbm, mask_hbm, perm_hbm, diag_hbm, flux_hbm,
+    send_y_0, send_y_1, send_x, field_ref, mask_ref, perm_ref, diag_ref, flux_ref,
     side_y, sems,
 ):
-    sources, targets = (field_hbm, mask_hbm, perm_hbm), (field_ref, mask_ref, perm_ref)
+    early = pl.ds(0, diag_ref.shape[0])
+    sources = (field_hbm, mask_hbm, perm_hbm, diag_hbm.at[early], flux_hbm.at[early])
+    targets = (field_ref, mask_ref, perm_ref, diag_ref, flux_ref)
     copies = [pltpu.make_async_copy(a, b, sems.at[i]) for i, (a, b) in enumerate(zip(sources, targets))]
     for copy in copies:
         copy.start()
-    for copy in copies:
+    for copy in copies[:3]:
         copy.wait()
     clear = 1.0 - mask_ref[...].astype(F32)
     sends = (send_y_0, send_y_1, send_x)
-    write_edges(lambda k, c: field_ref[k, c], field_ref.shape[1], clear, perm_ref, side_y, sends)
+    write_edges(lambda k, c: field_ref[k, c], field_ref.shape, clear, perm_ref, side_y, sends)
+    for copy in copies[3:]:
+        copy.wait()
 
 
 def edge_rows(layers, comps):
@@ -79,23 +84,25 @@
     return pltpu.VMEM((2, edge_rows(layers, comps), cols), F32)
 
 
-def opening(field, mask, perm):
+def in_hbm(*arrays):
+    return [pltpu.with_memory_space_constraint(array, pltpu.HBM) for array in arrays]
+
+
+def opening(field, mask, perm, diag, flux, early):
     layers, comps, rows, cols = field.shape
     hbm = pl.BlockSpec(memory_space=pltpu.HBM)
     vmem = pl.BlockSpec(memory_space=pltpu.VMEM)
-    arrays = (field, mask, perm)
+    kept = [(array.shape, array.dtype) for array in (field, mask, perm)]
+    kept += [((early, *block.shape[1:]), BF16) for block in (diag, flux)]
     return pl.pallas_call(
         opening_kernel,
-        in_specs=[hbm] * 3,
-        out_specs=[vmem] * 6,
-        out_shape=[*edge_shapes(*field.shape), *(pltpu.VMEM(array.shape, array.dtype) for array in arrays)],
-        scratch_shapes=[
-            edge_scratch(layers, comps, cols),
-            pltpu.SemaphoreType.DMA((3,)),
-        ],
+        in_specs=[hbm] * 5,
+        out_specs=[vmem] * 8,
+        out_shape=[*edge_shapes(*field.shape), *(pltpu.VMEM(*item) for item in kept)],
+        scratch_shapes=[edge_scratch(layers, comps, cols), pltpu.SemaphoreType.DMA((5,))],
         compiler_params=params(16),
         cost_estimate=cost(4 * field.size, 8 * field.size),
-    )(*(pltpu.with_memory_space_constraint(array, pltpu.HBM) for array in arrays))
+    )(*in_hbm(field, mask, perm, diag, flux))
 
 
 def exchange(send_y_0, send_y_1, send_x):
@@ -111,6 +118,8 @@
 
 
 TILE = 16
+EARLY = 2
+WEIGHTS = 7
 
 
 def reciprocal(value):
@@ -122,28 +131,59 @@
     return 2.0 * centre * beside * reciprocal(centre + beside)
 
 
-def apply_kernel(is_first_apply, field_ref, mask_ref, perm_ref, y_0, y_1, x_0, x_1, diag_in, flux_in, *rest):
+def write_weights(k, weights_ref, mask_ref, perm_ref, padded, edge_x, y_0, y_1, comps):
+    layers, rows, cols = perm_ref.shape
+    top = 8
+    lane = lax.broadcasted_iota(jnp.int32, (rows, cols), 1)
+    is_first, is_last = lane == 0, lane == cols - 1
+    even_y = lax.axis_index("gy") % 2 == 0
+    at_low = 2 * (layers * comps + k)
+    perm_low = pltpu.roll(edge_x[...], lax.rem(cols - at_low, cols), 1)
+    perm_high = pltpu.roll(edge_x[...], lax.rem(2 * cols - at_low - 2, cols), 1)
+    here = slice(layers * comps, layers * comps + 16)
+    mine = lax.broadcasted_iota(jnp.int32, (16, cols), 0) == k
+    perm_0 = jnp.sum(jnp.where(mine, y_0[here].astype(F32), 0.0), axis=0, keepdims=True)
+    perm_1 = jnp.sum(jnp.where(mine, y_1[here].astype(F32), 0.0), axis=0, keepdims=True)
+    centre = perm_ref[k]
+    padded[top : top + rows] = centre
+    padded[top - 1 : top] = jnp.where(even_y, perm_1, perm_0)
+    padded[top + rows : top + rows + 1] = jnp.where(even_y, perm_0, perm_1)
+    free = 1.0 - mask_ref[...].astype(F32)
+    above = perm_ref[jnp.minimum(k + 1, layers - 1)]
+    below = perm_ref[jnp.maximum(k - 1, 0)]
+    weights_ref[k, 0] = jnp.where(k < layers - 1, weight(centre, above), 0.0) * free
+    weights_ref[k, 1] = jnp.where(k > 0, weight(centre, below), 0.0) * free
+    weights_ref[k, 2] = weight(centre, padded[top + 1 : top + 1 + rows])
+    weights_ref[k, 3] = weight(centre, padded[top - 1 : top - 1 + rows])
+    to_left = weight(centre, jnp.where(is_first, perm_low, pltpu.roll(centre, 1, 1)))
+    to_right = weight(centre, jnp.where(is_last, perm_high, pltpu.roll(centre, cols - 1, 1)))
+    weights_ref[k, 4] = jnp.where(is_last, 0.0, to_right)
+    weights_ref[k, 5] = jnp.where(is_first, 0.0, to_left)
+    weights_ref[k, 6] = jnp.where(is_first, to_left, jnp.where(is_last, to_right, 0.0))
+
+
+def apply_kernel(is_first_apply, field_ref, mask_ref, y_0, y_1, x_0, x_1, early_diag, early_flux, *rest):
     if is_first_apply:
-        out_ref, rounded_ref, diag_ref, flux_ref, *rest, sems = rest
+        perm_ref, diag_hbm, flux_hbm, out_ref, rounded_ref, late_diag, late_flux, weights_ref, *rest, padded_perm, sems = rest
     else:
-        out_hbm, *rest, out_ref, out_sems = rest
-        diag_ref, flux_ref = diag_in, flux_in
-    padded, padded_perm, edge_x, place, beside_edge, perm_edge = rest
+        late_diag, late_flux, weights_ref, out_hbm, *rest, out_ref, out_sems = rest
+    padded, edge_x, place, beside_edge = rest
     layers, comps, rows, cols = field_ref.shape
+    early = early_diag.shape[0]
     top = 8
 
     def out_copy(k):
         return pltpu.make_async_copy(out_ref.at[k], out_hbm.at[k], out_sems.at[k])
 
-    def blocks(k):
+    def blocks(i):
         return (
-            pltpu.make_async_copy(diag_in.at[k], diag_ref.at[k], sems.at[0, k]),
-            pltpu.make_async_copy(flux_in.at[k], flux_ref.at[k], sems.at[1, k]),
+            pltpu.make_async_copy(diag_hbm.at[early + i], late_diag.at[i], sems.at[0, i]),
+            pltpu.make_async_copy(flux_hbm.at[early + i], late_flux.at[i], sems.at[1, i]),
         )
 
     if is_first_apply:
-        for k in range(layers):
-            for copy in blocks(k):
+        for i in range(layers - early):
+            for copy in blocks(i):
                 copy.start()
 
     lane = lax.broadcasted_iota(jnp.int32, (rows, cols), 1)
@@ -154,62 +194,36 @@
         place[:, r * cols : (r + 1) * cols] = jnp.where(taken, 1.0, 0.0).astype(BF16)
     even_x = lax.axis_index("gx") % 2 == 0
     even_y = lax.axis_index("gy") % 2 == 0
-    side_0, side_1 = x_0[...].astype(F32), x_1[...].astype(F32)
-    edge_x[...] = jnp.where((lane % 2 == 0) == even_x, side_1, side_0)
+    edge_x[...] = jnp.where((lane % 2 == 0) == even_x, x_1[...].astype(F32), x_0[...].astype(F32))
     clear = 1.0 - mask_ref[...].astype(F32)
 
-    def layer(k, carry):
+    def layer(diag_ref, flux_ref, start, i, carry):
+        k = i + start
         above = jnp.minimum(k + 1, layers - 1)
         below = jnp.maximum(k - 1, 0)
-
         turned = pltpu.roll(edge_x[...], lax.rem(cols - 2 * comps * k, cols), 1).astype(BF16)
         beside_edge[...] = jnp.dot(turned, place[...], preferred_element_type=F32)
-        at_low = 2 * (layers * comps + k)
-        perm_low = pltpu.roll(edge_x[...], lax.rem(cols - at_low, cols), 1)
-        perm_high = pltpu.roll(edge_x[...], lax.rem(2 * cols - at_low - 2, cols), 1)
-        perm_edge[...] = jnp.where(lane == 0, perm_low, perm_high)
-
         odd = k % 2 == 1
         here = pl.ds(pl.multiple_of(16 * (k // 2), 16), 16)
         side_0, side_1 = y_0[here].astype(F32), y_1[here].astype(F32)
         side_0 = jnp.where(odd, side_0[comps:], side_0[:comps])
         side_1 = jnp.where(odd, side_1[comps:], side_1[:comps])
         low_y, high_y = jnp.where(even_y, side_1, side_0), jnp.where(even_y, side_0, side_1)
-        here = slice(layers * comps, layers * comps + 16)
-        mine = lax.broadcasted_iota(jnp.int32, (16, cols), 0) == k
-        perm_0 = jnp.sum(jnp.where(mine, y_0[here].astype(F32), 0.0), axis=0, keepdims=True)
-        perm_1 = jnp.sum(jnp.where(mine, y_1[here].astype(F32), 0.0), axis=0, keepdims=True)
         for c in range(comps):
             padded[c, top : top + rows] = field_ref[k, c] * clear
             padded[c, top - 1 : top] = low_y[c : c + 1]
             padded[c, top + rows : top + rows + 1] = high_y[c : c + 1]
-        padded_perm[top : top + rows] = perm_ref[k]
-        padded_perm[top - 1 : top] = jnp.where(even_y, perm_1, perm_0)
-        padded_perm[top + rows : top + rows + 1] = jnp.where(even_y, perm_0, perm_1)
         if is_first_apply:
-            for copy in blocks(k):
-                copy.wait()
-        narrow = lax.broadcasted_iota(jnp.int32, (TILE, cols), 1)
-        is_first, is_last = narrow == 0, narrow == cols - 1
+            write_weights(k, weights_ref, mask_ref, perm_ref, padded_perm, edge_x, y_0, y_1, comps)
+            if start > 0:
+                for copy in blocks(i):
+                    copy.wait()
+
         for y in range(0, rows, TILE):
             here = slice(y, y + TILE)
             at = top + y
             well = mask_ref[here].astype(F32)
-            free = 1.0 - well
-            centre = perm_ref[k, here]
-            perm_beside = perm_edge[here]
-            perm_left = jnp.where(is_first, perm_beside, pltpu.roll(centre, 1, 1))
-            perm_right = jnp.where(is_last, perm_beside, pltpu.roll(centre, cols - 1, 1))
-            to_left, to_right = weight(centre, perm_left), weight(centre, perm_right)
-            weights = [
-                jnp.where(k < layers - 1, weight(centre, perm_ref[above, here]), 0.0) * free,
-                jnp.where(k > 0, weight(centre, perm_ref[below, here]), 0.0) * free,
-                weight(centre, padded_perm[at + 1 : at + 1 + TILE]),
-                weight(centre, padded_perm[at - 1 : at - 1 + TILE]),
-                jnp.where(is_last, 0.0, to_right),
-                jnp.where(is_first, 0.0, to_left),
-                jnp.where(is_first, to_left, jnp.where(is_last, to_right, 0.0)),
-            ]
+            weights = [weights_ref[k, j, here] for j in range(WEIGHTS)]
             total = [None] * comps
             for r in range(comps):
                 own = padded[r, at : at + TILE]
@@ -223,7 +237,7 @@
                     + weights[6] * beside_edge[here, r * cols : (r + 1) * cols]
                 )
                 for c in range(comps):
-                    term = diag_ref[k, r, c, here].astype(F32) * own - flux_ref[k, r, c, here].astype(F32) * summed
+                    term = diag_ref[i, r, c, here].astype(F32) * own - flux_ref[i, r, c, here].astype(F32) * summed
                     total[c] = term if r == 0 else total[c] + term
             for c in range(comps):
                 value = total[c] + well * field_ref[k, c, here]
@@ -235,49 +249,62 @@
             out_copy(k).start()
         return carry
 
-    lax.fori_loop(0, layers, layer, 0)
+    lax.fori_loop(0, early, functools.partial(layer, early_diag, early_flux, 0), 0)
+    lax.fori_loop(0, layers - early, functools.partial(layer, late_diag, late_flux, early), 0)
     if not is_first_apply:
         for k in range(layers):
             out_copy(k).wait()
 
 
-def apply_transposed(field, mask, perm, halos, diag, flux, is_first_apply):
+def apply_transposed(field, mask, halos, early_blocks, rest):
     layers, comps, rows, cols = field.shape
     vmem = pl.BlockSpec(memory_space=pltpu.VMEM)
     hbm = pl.BlockSpec(memory_space=pltpu.HBM)
+    is_first_apply = rest[0].ndim == 3
     out_shape = [jax.ShapeDtypeStruct(field.shape, F32)]
     if is_first_apply:
-        block_spec, out_specs = hbm, [vmem] * 4
+        perm, *blocks = rest
+        late = layers - early_blocks[0].shape[0]
+        rest, rest_specs, out_specs = [perm, *in_hbm(*blocks)], [vmem, hbm, hbm], [vmem] * 5
         out_shape.append(jax.ShapeDtypeStruct((comps * rows, layers * cols), BF16))
-        out_shape += [pltpu.VMEM(diag.shape, BF16), pltpu.VMEM(flux.shape, BF16)]
-        tail = [pltpu.SemaphoreType.DMA((2, layers))]
-        diag, flux = (pltpu.with_memory_space_constraint(block, pltpu.HBM) for block in (diag, flux))
+        out_shape += [pltpu.VMEM((late, *block.shape[1:]), BF16) for block in blocks]
+        out_shape.append(pltpu.VMEM((layers, WEIGHTS, rows, cols), F32))
+        tail = [pltpu.VMEM((rows + 16, cols), F32), pltpu.SemaphoreType.DMA((2, late))]
     else:
-        block_spec, out_specs = vmem, [hbm]
+        rest_specs, out_specs = [vmem] * 3, [hbm]
         tail = [pltpu.VMEM(field.shape, F32), pltpu.SemaphoreType.DMA((layers,))]
+    size = layers * comps * comps * rows * cols
     return pl.pallas_call(
         functools.partial(apply_kernel, is_first_apply),
-        in_specs=[vmem] * 7 + [block_spec] * 2,
+        in_specs=[vmem] * 8 + rest_specs,
         out_specs=out_specs,
         out_shape=out_shape,
         scratch_shapes=[
             pltpu.VMEM((comps, rows + 16, cols), F32),
-            pltpu.VMEM((rows + 16, cols), F32),
             pltpu.VMEM((rows, cols), F32),
             pltpu.VMEM((cols, comps * cols), BF16),
             pltpu.VMEM((rows, comps * cols), F32),
-            pltpu.VMEM((rows, cols), F32),
             *tail,
         ],
         compiler_params=params(24),
-        cost_estimate=cost(8 * diag.size, 4 * diag.size + 8 * field.size),
-    )(field, mask, perm, *halos, diag, flux)
+        cost_estimate=cost(8 * size, 4 * size + 8 * field.size),
+    )(field, mask, *halos, *early_blocks, *rest)
 
 
 def split_cells(cells, rows, cols):
     layer = cells // (rows * cols)
     y = (cells // cols) % rows
     return layer * cols + cells % cols, y
+
+
+def unrolled(count, together, body):
+    def group(i, carry):
+        for j in range(together):
+            body(i * together + j, None)
+        return carry
+
+    together = math.gcd(count, together)
+    lax.fori_loop(0, count // together, group, 0)
 
 
 def one_hot(column, count, slots):
@@ -307,7 +334,7 @@
             sent_ref[helper_ref[0, 0, b]] = (values[:, j * width : (j + 1) * width] * live).astype(BF16)
         return carry
 
-    lax.fori_loop(0, chunks, one, 0)
+    unrolled(chunks, 4, one)
 
 
 def gather(rounded, cells, helper, count, comps, rows, cols, width):
@@ -374,7 +401,7 @@
 
 
 def scatter_kernel(
-    scale, helper_ref, cells_ref, back_ref, first_ref, mask_ref, perm_ref,
+    scale, helper_ref, cells_ref, back_ref, first_ref, mask_ref,
     second_ref, send_y_0, send_y_1, send_x, grad_ref,
     added, side_y,
 ):
@@ -397,13 +424,13 @@
         added[...] += lax.dot_general(spread, chosen, (((1,), (1,)), ((), ())), preferred_element_type=F32)
         return carry
 
-    lax.fori_loop(0, chunks, one, 0)
+    unrolled(chunks, 2, one)
     for k in range(layers):
         for c in range(comps):
             second_ref[k, c] = first_ref[k, c] + added[c * rows : (c + 1) * rows, k * cols : (k + 1) * cols]
     clear = 1.0 - mask_ref[...].astype(F32)
     sends = (send_y_0, send_y_1, send_x)
-    write_edges(lambda k, c: second_ref[k, c], comps, clear, perm_ref, side_y, sends)
+    write_edges(lambda k, c: second_ref[k, c], second_ref.shape, clear, None, side_y, sends)
 
     def add_part(b, total):
         return total + back_ref[b].astype(F32)[comps:]
@@ -415,13 +442,13 @@
     grad_ref[...] = (whole * scale)[:, :comps]
 
 
-def scatter(first, back, helper, cells, mask, perm, scale):
+def scatter(first, back, helper, cells, mask, scale):
     layers, comps, rows, cols = first.shape
     smem = pl.BlockSpec(memory_space=pltpu.SMEM)
     vmem = pl.BlockSpec(memory_space=pltpu.VMEM)
     return pl.pallas_call(
         functools.partial(scatter_kernel, scale),
-        in_specs=[smem] + [vmem] * 5,
+        in_specs=[smem] + [vmem] * 4,
         out_specs=[vmem] * 5,
         out_shape=[
             jax.ShapeDtypeStruct(first.shape, F32),
@@ -431,7 +458,7 @@
         scratch_shapes=[pltpu.VMEM((comps * rows, layers * cols), F32), edge_scratch(layers, comps, cols)],
         compiler_params=params(24),
         cost_estimate=cost(2 * first.size * cells.size, 8 * first.size),
-    )(helper, cells, back, first, mask, perm)
+    )(helper, cells, back, first, mask)
 
 
 def shards(
@@ -452,23 +479,28 @@
     inverse = flash_inverse.reshape(blocks, comps, comps, width)
     coupling = flash_coupling.reshape(blocks, comps, comps, width)
     state = phase_state.reshape(blocks, comps, width)
-    cells = cell_list.reshape(-1, 1, min(CHUNK, cell_list.shape[-1]))
+
+    def cells(chunk):
+        return cell_list.reshape(-1, 1, min(chunk, cell_list.shape[-1]))
 
     def to_partners(array):
         return lax.all_to_all(array, AXES, split_axis=0, concat_axis=0, tiled=True)
 
-    *sides, field, mask, perm = opening(cotangent, well_mask, permeability)
+    *sides, field, mask, perm, early_diag, early_flux = opening(
+        cotangent, well_mask, permeability, diag_block, flux_block, min(EARLY, layers - 1)
+    )
+    early = (early_diag, early_flux)
     halos = exchange(*sides)
-    first, rounded, *kept = apply_transposed(field, mask, perm, halos, diag_block, flux_block, True)
-    sent = gather(rounded, cells, helper_of, block_count, comps, rows, cols, width)
+    first, rounded, *kept = apply_transposed(field, mask, halos, early, (perm, diag_block, flux_block))
+    sent = gather(rounded, cells(GATHER_CHUNK), helper_of, block_count, comps, rows, cols, width)
     reply = at_helper(inverse, coupling, state, to_partners(sent))
     devices = lax.axis_size("gx") * lax.axis_size("gy")
     scale = -1.0 / math.sqrt(width * devices * devices)
     second, *sides, interaction_grad = scatter(
-        first, to_partners(reply), helper_of, cells, mask, perm, scale
+        first, to_partners(reply), helper_of, cells(SCATTER_CHUNK), mask, scale
     )
     halos = exchange(*sides)
-    (adjoint,) = apply_transposed(second, mask, perm, halos, *kept, False)
+    (adjoint,) = apply_transposed(second, mask, halos, early, kept)
     return (adjoint, interaction_grad)
 
 

time: 70.1 us -> 66.8 us (0.953)
  Pallas kernels: 27.4 us -> 24.2 us
    pallas_call x2, Pallas kernels: 12.5 us -> 10.5 us  [apply_transposed(): pl.pallas_call(functools.partial(apply_kernel, is_first_apply), in_specs=...]
    pallas_call x1, Pallas kernels: 6.85 us -> 5.49 us  [scatter(): pl.pallas_call(functools.partial(scatter_kernel, scale), in_specs=[smem]...]
    pallas_call x1, Pallas kernels: 1.76 us -> 2.83 us  [opening(): pl.pallas_call(opening_kernel, in_specs=[hbm] * 5, out_specs=[vmem] * 8,...]
    pallas_call x1, Pallas kernels: 5.35 us -> 4.51 us  [gather(): pl.pallas_call(functools.partial(gather_kernel, rows, cols), in_specs=[sm...]
where the time goes in v6:
time: 66.8 us; the launch traced here: 66.6 us
  Pallas kernels  24.2 us (36%)
  blocking collectives  20.9 us (31%)
  starting transfers between devices  15 us (22%)
  waiting for transfers between devices  5.09 us (8%)
  between operations  1.43 us (2%)
    all_to_all x2, blocking collectives, to_partners(): return lax.all_to_all(array, AXES, split_axis=0, concat_axis=0, tiled=True)  20.9 us
    ppermute x8, starting transfers between devices, swaps(): lax.ppermute(array, axis, pairs + [(j, i) for i, j in pairs])  15 us
    pallas_call x2, Pallas kernels, apply_transposed(): pl.pallas_call(functools.partial(apply_kernel, is_first_apply), in_specs=...  10.5 us
    pallas_call x1, Pallas kernels, scatter(): pl.pallas_call(functools.partial(scatter_kernel, scale), in_specs=[smem]...  5.49 us
    ppermute x8, waiting for transfers between devices, swaps(): lax.ppermute(array, axis, pairs + [(j, i) for i, j in pairs])  5.09 us
    pallas_call x1, Pallas kernels, gather(): pl.pallas_call(functools.partial(gather_kernel, rows, cols), in_specs=[sm...  4.51 us
    pallas_call x1, Pallas kernels, opening(): pl.pallas_call(opening_kernel, in_specs=[hbm] * 5, out_specs=[vmem] * 8,...  2.83 us
  transfers between devices with their start and end apart: 8, of which 2 were waited for; matrix products, arithmetic and copies ran while one was open for 0% of the time, Pallas kernels for 0%

profile of v6, /device:TPU:9, one launch (start us, length us, event | category | flops | bytes accessed | tf_op | source)
XLA Modules:
  0.0 66.6 jit_solution(16281362935747226275)
XLA Ops:
  0.6 2.8 %shard_map.122 = (bf16[64,128]{1,0:T(8,128)(2,1)S(1)}, bf16[64,128]{1,0:T(8,128)(2,1)S(1)}, bf16[64,128]{1,0:T(8,128)(2,1)S(1)}, f32[6,8,64,128]{3,2,1,0:T(8,128...) custom-call(f32[6,8,64,128]{3,2,1,0:T(8,128)} %field_hbm.1, ...), custom_call_target="tpu_custom_call" | custom-call | flops 1572864 | bytes 3145728 | tf_op jit(solution)/shard_map/pallas_call | solution.py:97
  3.5 0.7 %collective-permute-start.2 = (bf16[64,128]{1,0:T(8,128)(2,1)S(1)}, bf16[64,128]{1,0:T(8,128)(2,1)S(1)}, u32[]{:S(2)}, u32[]{:S(2)}) collective-permute-start(bf16[64,128]{1,0:T(8,128)(2,1)S(1)} %get-tuple-element.24), channel_id=1, source_target_pairs={{0,8},{16,24},{8,0},{24,16},{1,9},{17,25},{9,1},{25,17},{2,10},{18... | collective-permute-start | bytes 49160 | tf_op jit(solution)/shard_map/ppermute | solution.py:114
  4.2 3.0 %collective-permute-start.3 = (bf16[64,128]{1,0:T(8,128)(2,1)S(1)}, bf16[64,128]{1,0:T(8,128)(2,1)S(1)}, u32[]{:S(2)}, u32[]{:S(2)}) collective-permute-start(bf16[64,128]{1,0:T(8,128)(2,1)S(1)} %get-tuple-element.24), channel_id=1, source_target_pairs={{8,16},{16,8},{9,17},{17,9},{10,18},{18,10},{11,19},{19,11},{12,20... | collective-permute-start | bytes 49160 | tf_op jit(solution)/shard_map/ppermute | solution.py:114
  7.3 1.3 %collective-permute-start = (bf16[64,128]{1,0:T(8,128)(2,1)S(1)}, bf16[64,128]{1,0:T(8,128)(2,1)S(1)}, u32[]{:S(2)}, u32[]{:S(2)}) collective-permute-start(bf16[64,128]{1,0:T(8,128)(2,1)S(1)} %get-tuple-element.22), channel_id=1, source_target_pairs={{0,1},{2,3},{4,5},{6,7},{1,0},{3,2},{5,4},{7,6},{8,9},{10,11},{12,... | collective-permute-start | bytes 49160 | tf_op jit(solution)/shard_map/ppermute | solution.py:114
  8.5 2.0 %collective-permute-start.1 = (bf16[64,128]{1,0:T(8,128)(2,1)S(1)}, bf16[64,128]{1,0:T(8,128)(2,1)S(1)}, u32[]{:S(2)}, u32[]{:S(2)}) collective-permute-start(bf16[64,128]{1,0:T(8,128)(2,1)S(1)} %get-tuple-element.23), channel_id=1, source_target_pairs={{1,2},{3,4},{5,6},{2,1},{4,3},{6,5},{9,10},{11,12},{13,14},{10,9},... | collective-permute-start | bytes 49160 | tf_op jit(solution)/shard_map/ppermute | solution.py:114
  11.2 0.0 collective-permute-done.2.x_0
  11.2 0.0 collective-permute-done.3.x_1
  11.3 0.0 collective-permute-done.y_0
  11.3 2.6 %collective-permute-done.1.y_1 = bf16[64,128]{1,0:T(8,128)(2,1)S(1)} collective-permute-done((bf16[64,128]{1,0:T(8,128)(2,1)S(1)}, bf16[64,128]{1,0:T(8,128)(2,1)S(1)}, u32[]{:S(2)}, u32[]{:S(2)}) %collective-permute-start.1) | collective-permute-done | bytes 16416 | tf_op jit(solution)/shard_map/ppermute | solution.py:114
  13.9 5.2 %shard_map.123 = (f32[6,8,64,128]{3,2,1,0:T(8,128)S(1)}, bf16[512,768]{1,0:T(8,128)(2,1)S(1)}, bf16[4,8,8,64,128]{4,3,2,1,0:T(8,128)(2,1)S(1)}, bf16[4,8,8,64,12...) custom-call(f32[6,8,64,128]{3,2,1,0:T(8,128)S(1)} %get-tuple-element.20.field_ref, s32[64,128]{1,0:T(8,128)S(1)} %get-tuple-element.21.mask_ref, ...), custom_call_target="tpu_custom_call" | custom-call | flops 25165824 | bytes 15728640 | tf_op jit(solution)/shard_map/pallas_call | solution.py:277
  19.1 0.0 copy-done.3
  19.1 0.0 copy-done.4
  19.1 0.0 copy-start
  19.1 0.0 copy-start.1
  19.1 0.0 copy-start.2
  19.2 4.5 %shard_map.124 = bf16[32,8,128]{2,1,0:T(8,128)(2,1)S(1)} custom-call(s32[1,1,32]{2,1,0:T(1,128)S(1)} %copy-done.4, s32[1,1]{1,0:T(1,128)S(6)} %copy.13.count_ref, s32[8,1,512]{2,1,0:T(1,128)S(1)} %bitcast.8, bf16[512,768]{1,0:T(8,128)(2,1)S(1)} %get-tuple-element.28.rounded_ref), custom_call_target="tpu_custom_call" | custom-call | flops 3221225472 | bytes 786432 | tf_op jit(solution)/shard_map/pallas_call | solution.py:345
  23.7 11.4 %all_to_all.10.picked_ref = bf16[32,8,128]{2,1,0:T(8,128)(2,1)S(1)} all-to-all(bf16[32,8,128]{2,1,0:T(8,128)(2,1)S(1)} %shard_map.124), channel_id=1, replica_groups=mesh['gx'=4,'gy'=8] {'gx','gy'}, dimensions={0} | all-to-all | bytes 131072 | tf_op jit(solution)/shard_map/all_to_all | solution.py:487
  35.0 0.0 copy-done
  35.0 0.0 copy-done.1
  35.1 0.0 copy-done.2
  35.1 0.9 %shard_map.125 = bf16[32,16,128]{2,1,0:T(8,128)(2,1)S(1)} custom-call(bf16[32,8,8,128]{3,2,1,0:T(8,128)(2,1)S(1)} %bitcast.5, bf16[32,8,8,128]{3,2,1,0:T(8,128)(2,1)S(1)} %bitcast.6, bf16[32,8,128]{2,1,0:T(8,128)(2,1)S(1)} %bitcast.7, bf16[32,8,128]{2,1,0:T(8,128)(2,1)S(1)} %all_to_all.10.picked_ref), custom_call_target="tpu_custom_call" | custom-call | flops 1048576 | bytes 1048576 | tf_op jit(solution)/shard_map/pallas_call | solution.py:395
  35.9 9.6 %all_to_all.11.back_ref = bf16[32,16,128]{2,1,0:T(8,128)(2,1)S(1)} all-to-all(bf16[32,16,128]{2,1,0:T(8,128)(2,1)S(1)} %shard_map.125), channel_id=1, replica_groups=mesh['gx'=4,'gy'=8] {'gx','gy'}, dimensions={0} | all-to-all | bytes 262144 | tf_op jit(solution)/shard_map/all_to_all | solution.py:487
  45.5 5.5 %shard_map.126 = (f32[6,8,64,128]{3,2,1,0:T(8,128)S(1)}, bf16[64,128]{1,0:T(8,128)(2,1)S(1)}, bf16[64,128]{1,0:T(8,128)(2,1)S(1)}, bf16[64,128]{1,0:T(8,128)(2,1)S(1)}, f32[8,8]{1,0:T(8,128)}) custom-call(s32[1,1,32]{2,1,0:T(1,128)S(1)} %copy-done.4, s32[4,1,1024]{2,1,0:T(1,128)S(1)} %bitcast.9, bf16[32,16,128]{2,1,0:T(8,128)(2,1)S(1)} %all_to_all.11.back_ref, ...), custom_call_target="tpu_custom_call" | custom-call | flops 3221225472 | bytes 3145728 | tf_op jit(solution)/shard_map/pallas_call | solution.py:449
  51.0 1.1 %collective-permute-start.4 = (bf16[64,128]{1,0:T(8,128)(2,1)S(1)}, bf16[64,128]{1,0:T(8,128)(2,1)S(1)}, u32[]{:S(2)}, u32[]{:S(2)}) collective-permute-start(bf16[64,128]{1,0:T(8,128)(2,1)S(1)} %get-tuple-element.31), channel_id=1, source_target_pairs={{0,1},{2,3},{4,5},{6,7},{1,0},{3,2},{5,4},{7,6},{8,9},{10,11},{12,... | collective-permute-start | bytes 49160 | tf_op jit(solution)/shard_map/ppermute | solution.py:114
  52.0 3.2 %collective-permute-start.5 = (bf16[64,128]{1,0:T(8,128)(2,1)S(1)}, bf16[64,128]{1,0:T(8,128)(2,1)S(1)}, u32[]{:S(2)}, u32[]{:S(2)}) collective-permute-start(bf16[64,128]{1,0:T(8,128)(2,1)S(1)} %get-tuple-element.32), channel_id=1, source_target_pairs={{1,2},{3,4},{5,6},{2,1},{4,3},{6,5},{9,10},{11,12},{13,14},{10,9},... | collective-permute-start | bytes 49160 | tf_op jit(solution)/shard_map/ppermute | solution.py:114
  55.2 1.0 %collective-permute-start.6 = (bf16[64,128]{1,0:T(8,128)(2,1)S(1)}, bf16[64,128]{1,0:T(8,128)(2,1)S(1)}, u32[]{:S(2)}, u32[]{:S(2)}) collective-permute-start(bf16[64,128]{1,0:T(8,128)(2,1)S(1)} %get-tuple-element.33), channel_id=1, source_target_pairs={{0,8},{16,24},{8,0},{24,16},{1,9},{17,25},{9,1},{25,17},{2,10},{18... | collective-permute-start | bytes 49160 | tf_op jit(solution)/shard_map/ppermute | solution.py:114
  56.3 2.6 %collective-permute-start.7 = (bf16[64,128]{1,0:T(8,128)(2,1)S(1)}, bf16[64,128]{1,0:T(8,128)(2,1)S(1)}, u32[]{:S(2)}, u32[]{:S(2)}) collective-permute-start(bf16[64,128]{1,0:T(8,128)(2,1)S(1)} %get-tuple-element.33), channel_id=1, source_target_pairs={{8,16},{16,8},{9,17},{17,9},{10,18},{18,10},{11,19},{19,11},{12,20... | collective-permute-start | bytes 49160 | tf_op jit(solution)/shard_map/ppermute | solution.py:114
  58.9 0.0 collective-permute-done.4.y_0
  58.9 0.0 collective-permute-done.5.y_1
  58.9 0.0 collective-permute-done.6.x_0
  58.9 2.4 %collective-permute-done.7.x_1 = bf16[64,128]{1,0:T(8,128)(2,1)S(1)} collective-permute-done((bf16[64,128]{1,0:T(8,128)(2,1)S(1)}, bf16[64,128]{1,0:T(8,128)(2,1)S(1)}, u32[]{:S(2)}, u32[]{:S(2)}) %collective-permute-start.7) | collective-permute-done | bytes 16416 | tf_op jit(solution)/shard_map/ppermute | solution.py:114
  61.3 5.3 %shard_map.127 = f32[6,8,64,128]{3,2,1,0:T(8,128)} custom-call(f32[6,8,64,128]{3,2,1,0:T(8,128)S(1)} %get-tuple-element.30.field_ref, s32[64,128]{1,0:T(8,128)S(1)} %get-tuple-element.21.mask_ref, bf16[64,128]{1,0:T(8,128)(2,1)S(1)} %collective-permute-done.4.y_0, bf16[64,128]{1,0:T(8,128)(2,1)S(1)} %collective-permute-done.5.y_1, ...), custom_call_target="tpu_custom_call" | custom-call | flops 25165824 | bytes 15728640 | tf_op jit(solution)/shard_map/pallas_call | solution.py:277
  (2 shorter events, 0.0 us)
Async XLA Ops:
  3.5 7.8 %collective-permute-start.2 = (bf16[64,128]{1,0:T(8,128)(2,1)S(1)}, bf16[64,128]{1,0:T(8,128)(2,1)S(1)}, u32[]{:S(2)}, u32[]{:S(2)}) collective-permute-start(bf16[64,128]{1,0:T(8,128)(2,1)S(1)} %get-tuple-element.24), channel_id=1, source_target_pairs={{0,8},{16,24},{8,0},{24,16},{1,9},{17,25},{9,1},{25,17},{2,10},{18... | collective-permute-start | bytes 49160 | tf_op jit(solution)/shard_map/ppermute | solution.py:114
  4.2 7.0 %collective-permute-start.3 = (bf16[64,128]{1,0:T(8,128)(2,1)S(1)}, bf16[64,128]{1,0:T(8,128)(2,1)S(1)}, u32[]{:S(2)}, u32[]{:S(2)}) collective-permute-start(bf16[64,128]{1,0:T(8,128)(2,1)S(1)} %get-tuple-element.24), channel_id=1, source_target_pairs={{8,16},{16,8},{9,17},{17,9},{10,18},{18,10},{11,19},{19,11},{12,20... | collective-permute-start | bytes 49160 | tf_op jit(solution)/shard_map/ppermute | solution.py:114
  7.3 4.0 %collective-permute-start = (bf16[64,128]{1,0:T(8,128)(2,1)S(1)}, bf16[64,128]{1,0:T(8,128)(2,1)S(1)}, u32[]{:S(2)}, u32[]{:S(2)}) collective-permute-start(bf16[64,128]{1,0:T(8,128)(2,1)S(1)} %get-tuple-element.22), channel_id=1, source_target_pairs={{0,1},{2,3},{4,5},{6,7},{1,0},{3,2},{5,4},{7,6},{8,9},{10,11},{12,... | collective-permute-start | bytes 49160 | tf_op jit(solution)/shard_map/ppermute | solution.py:114
  8.5 5.4 %collective-permute-start.1 = (bf16[64,128]{1,0:T(8,128)(2,1)S(1)}, bf16[64,128]{1,0:T(8,128)(2,1)S(1)}, u32[]{:S(2)}, u32[]{:S(2)}) collective-permute-start(bf16[64,128]{1,0:T(8,128)(2,1)S(1)} %get-tuple-element.23), channel_id=1, source_target_pairs={{1,2},{3,4},{5,6},{2,1},{4,3},{6,5},{9,10},{11,12},{13,14},{10,9},... | collective-permute-start | bytes 49160 | tf_op jit(solution)/shard_map/ppermute | solution.py:114
  13.9 5.2 %copy-start.3 = (s32[1,1,4096]{2,1,0:T(1,128)S(1)}, s32[1,1,4096]{2,1,0:T(1,128)}, u32[]{:S(2)}) copy-start(s32[1,1,4096]{2,1,0:T(1,128)} %param.16) | copy-start | bytes 49156
  13.9 5.2 %copy-start.4 = (s32[1,1,32]{2,1,0:T(1,128)S(1)}, s32[1,1,32]{2,1,0:T(1,128)}, u32[]{:S(2)}) copy-start(s32[1,1,32]{2,1,0:T(1,128)} %helper_ref.3) | copy-start | bytes 388
  19.1 15.9 %copy-start = (bf16[1,1,32,8,8,128]{5,4,3,2,1,0:T(8,128)(2,1)S(1)}, bf16[1,1,32,8,8,128]{5,4,3,2,1,0:T(8,128)(2,1)}, u32[]{:S(2)}) copy-start(bf16[1,1,32,8,8,128]{5,4,3,2,1,0:T(8,128)(2,1)} %param.19) | copy-start | bytes 1572868
  19.1 15.9 %copy-start.1 = (bf16[1,1,32,8,8,128]{5,4,3,2,1,0:T(8,128)(2,1)S(1)}, bf16[1,1,32,8,8,128]{5,4,3,2,1,0:T(8,128)(2,1)}, u32[]{:S(2)}) copy-start(bf16[1,1,32,8,8,128]{5,4,3,2,1,0:T(8,128)(2,1)} %param.20) | copy-start | bytes 1572868
  19.1 15.9 %copy-start.2 = (bf16[1,1,32,8,128]{4,3,2,1,0:T(8,128)(2,1)S(1)}, bf16[1,1,32,8,128]{4,3,2,1,0:T(8,128)(2,1)}, u32[]{:S(2)}) copy-start(bf16[1,1,32,8,128]{4,3,2,1,0:T(8,128)(2,1)} %param.21) | copy-start | bytes 196612
  51.0 7.9 %collective-permute-start.4 = (bf16[64,128]{1,0:T(8,128)(2,1)S(1)}, bf16[64,128]{1,0:T(8,128)(2,1)S(1)}, u32[]{:S(2)}, u32[]{:S(2)}) collective-permute-start(bf16[64,128]{1,0:T(8,128)(2,1)S(1)} %get-tuple-element.31), channel_id=1, source_target_pairs={{0,1},{2,3},{4,5},{6,7},{1,0},{3,2},{5,4},{7,6},{8,9},{10,11},{12,... | collective-permute-start | bytes 49160 | tf_op jit(solution)/shard_map/ppermute | solution.py:114
  52.0 6.8 %collective-permute-start.5 = (bf16[64,128]{1,0:T(8,128)(2,1)S(1)}, bf16[64,128]{1,0:T(8,128)(2,1)S(1)}, u32[]{:S(2)}, u32[]{:S(2)}) collective-permute-start(bf16[64,128]{1,0:T(8,128)(2,1)S(1)} %get-tuple-element.32), channel_id=1, source_target_pairs={{1,2},{3,4},{5,6},{2,1},{4,3},{6,5},{9,10},{11,12},{13,14},{10,9},... | collective-permute-start | bytes 49160 | tf_op jit(solution)/shard_map/ppermute | solution.py:114
  55.2 3.6 %collective-permute-start.6 = (bf16[64,128]{1,0:T(8,128)(2,1)S(1)}, bf16[64,128]{1,0:T(8,128)(2,1)S(1)}, u32[]{:S(2)}, u32[]{:S(2)}) collective-permute-start(bf16[64,128]{1,0:T(8,128)(2,1)S(1)} %get-tuple-element.33), channel_id=1, source_target_pairs={{0,8},{16,24},{8,0},{24,16},{1,9},{17,25},{9,1},{25,17},{2,10},{18... | collective-permute-start | bytes 49160 | tf_op jit(solution)/shard_map/ppermute | solution.py:114
  56.3 5.0 %collective-permute-start.7 = (bf16[64,128]{1,0:T(8,128)(2,1)S(1)}, bf16[64,128]{1,0:T(8,128)(2,1)S(1)}, u32[]{:S(2)}, u32[]{:S(2)}) collective-permute-start(bf16[64,128]{1,0:T(8,128)(2,1)S(1)} %get-tuple-element.33), channel_id=1, source_target_pairs={{8,16},{16,8},{9,17},{17,9},{10,18},{18,10},{11,19},{19,11},{12,20... | collective-permute-start | bytes 49160 | tf_op jit(solution)/shard_map/ppermute | solution.py:114

commit v7 on v6

--- a/solution.py
+++ b/solution.py
@@ -27,10 +27,11 @@
     return -(-number // step) * step
 
 
-def write_edges(field, shape, clear, perm_ref, side_y, sends):
+def write_edges(field_ref, mask_ref, perm_ref, masked_ref, side_y, sends):
     send_y_0, send_y_1, send_x = sends
-    layers, comps, rows, cols = shape
+    layers, comps, rows, cols = field_ref.shape
     with_perm = perm_ref is not None
+    clear = 1.0 - mask_ref[...].astype(F32)
     lane = lax.broadcasted_iota(jnp.int32, (rows, cols), 1)
     pair = lane // 2
     along_x = jnp.zeros((rows, cols), F32)
@@ -38,7 +39,8 @@
     for k in range(layers):
         for c in range(comps + with_perm):
             if c < comps:
-                value, at = field(k, c) * clear, k * comps + c
+                value, at = field_ref[k, c] * clear, k * comps + c
+                masked_ref[k, c] = value
             else:
                 value, at = perm_ref[k], layers * comps + k
             side_y[0, at : at + 1, :] = value[0:1]
@@ -53,7 +55,7 @@
 
 def opening_kernel(
     field_hbm, mask_hbm, perm_hbm, diag_hbm, flux_hbm,
-    send_y_0, send_y_1, send_x, field_ref, mask_ref, perm_ref, diag_ref, flux_ref,
+    send_y_0, send_y_1, send_x, masked_ref, field_ref, mask_ref, perm_ref, diag_ref, flux_ref,
     side_y, sems,
 ):
     early = pl.ds(0, diag_ref.shape[0])
@@ -64,9 +66,7 @@
         copy.start()
     for copy in copies[:3]:
         copy.wait()
-    clear = 1.0 - mask_ref[...].astype(F32)
-    sends = (send_y_0, send_y_1, send_x)
-    write_edges(lambda k, c: field_ref[k, c], field_ref.shape, clear, perm_ref, side_y, sends)
+    write_edges(field_ref, mask_ref, perm_ref, masked_ref, side_y, (send_y_0, send_y_1, send_x))
     for copy in copies[3:]:
         copy.wait()
 
@@ -92,12 +92,12 @@
     layers, comps, rows, cols = field.shape
     hbm = pl.BlockSpec(memory_space=pltpu.HBM)
     vmem = pl.BlockSpec(memory_space=pltpu.VMEM)
-    kept = [(array.shape, array.dtype) for array in (field, mask, perm)]
+    kept = [(array.shape, array.dtype) for array in (field, field, mask, perm)]
     kept += [((early, *block.shape[1:]), BF16) for block in (diag, flux)]
     return pl.pallas_call(
         opening_kernel,
         in_specs=[hbm] * 5,
-        out_specs=[vmem] * 8,
+        out_specs=[vmem] * 9,
         out_shape=[*edge_shapes(*field.shape), *(pltpu.VMEM(*item) for item in kept)],
         scratch_shapes=[edge_scratch(layers, comps, cols), pltpu.SemaphoreType.DMA((5,))],
         compiler_params=params(16),
@@ -114,7 +114,7 @@
             results.append(lax.ppermute(array, axis, pairs + [(j, i) for i, j in pairs]))
         return results
 
-    return (*swaps("gy", send_y_0, send_y_1), *swaps("gx", send_x, send_x))
+    return (*swaps("gx", send_x, send_x), *swaps("gy", send_y_0, send_y_1))
 
 
 TILE = 16
@@ -131,57 +131,78 @@
     return 2.0 * centre * beside * reciprocal(centre + beside)
 
 
-def write_weights(k, weights_ref, mask_ref, perm_ref, padded, edge_x, y_0, y_1, comps):
+def tile_weights(k, y, perm_ref, edge_x, y_rows, comps):
     layers, rows, cols = perm_ref.shape
-    top = 8
-    lane = lax.broadcasted_iota(jnp.int32, (rows, cols), 1)
+    here = slice(y, y + TILE)
+    lane = lax.broadcasted_iota(jnp.int32, (TILE, cols), 1)
     is_first, is_last = lane == 0, lane == cols - 1
-    even_y = lax.axis_index("gy") % 2 == 0
     at_low = 2 * (layers * comps + k)
-    perm_low = pltpu.roll(edge_x[...], lax.rem(cols - at_low, cols), 1)
-    perm_high = pltpu.roll(edge_x[...], lax.rem(2 * cols - at_low - 2, cols), 1)
-    here = slice(layers * comps, layers * comps + 16)
-    mine = lax.broadcasted_iota(jnp.int32, (16, cols), 0) == k
-    perm_0 = jnp.sum(jnp.where(mine, y_0[here].astype(F32), 0.0), axis=0, keepdims=True)
-    perm_1 = jnp.sum(jnp.where(mine, y_1[here].astype(F32), 0.0), axis=0, keepdims=True)
-    centre = perm_ref[k]
-    padded[top : top + rows] = centre
-    padded[top - 1 : top] = jnp.where(even_y, perm_1, perm_0)
-    padded[top + rows : top + rows + 1] = jnp.where(even_y, perm_0, perm_1)
-    free = 1.0 - mask_ref[...].astype(F32)
-    above = perm_ref[jnp.minimum(k + 1, layers - 1)]
-    below = perm_ref[jnp.maximum(k - 1, 0)]
-    weights_ref[k, 0] = jnp.where(k < layers - 1, weight(centre, above), 0.0) * free
-    weights_ref[k, 1] = jnp.where(k > 0, weight(centre, below), 0.0) * free
-    weights_ref[k, 2] = weight(centre, padded[top + 1 : top + 1 + rows])
-    weights_ref[k, 3] = weight(centre, padded[top - 1 : top - 1 + rows])
+    perm_low = pltpu.roll(edge_x[here], lax.rem(cols - at_low, cols), 1)
+    perm_high = pltpu.roll(edge_x[here], lax.rem(2 * cols - at_low - 2, cols), 1)
+    centre = perm_ref[k, here]
+    low_y, high_y = beside_y(perm_ref, (k,), y, y_rows)
     to_left = weight(centre, jnp.where(is_first, perm_low, pltpu.roll(centre, 1, 1)))
     to_right = weight(centre, jnp.where(is_last, perm_high, pltpu.roll(centre, cols - 1, 1)))
-    weights_ref[k, 4] = jnp.where(is_last, 0.0, to_right)
-    weights_ref[k, 5] = jnp.where(is_first, 0.0, to_left)
-    weights_ref[k, 6] = jnp.where(is_first, to_left, jnp.where(is_last, to_right, 0.0))
-
-
-def apply_kernel(is_first_apply, field_ref, mask_ref, y_0, y_1, x_0, x_1, early_diag, early_flux, *rest):
+    return [
+        jnp.where(k < layers - 1, weight(centre, perm_ref[jnp.minimum(k + 1, layers - 1), here]), 0.0),
+        jnp.where(k > 0, weight(centre, perm_ref[jnp.maximum(k - 1, 0), here]), 0.0),
+        weight(centre, high_y),
+        weight(centre, low_y),
+        jnp.where(is_last, 0.0, to_right),
+        jnp.where(is_first, 0.0, to_left),
+        jnp.where(is_first, to_left, jnp.where(is_last, to_right, 0.0)),
+    ]
+
+
+def beside_y(ref, index, y, y_rows):
+    rows, cols = ref.shape[-2:]
+    row = lax.broadcasted_iota(jnp.int32, (TILE, cols), 0)
+    if y > 0:
+        low = ref[(*index, slice(y - 1, y - 1 + TILE))]
+    else:
+        low = jnp.where(row == 0, y_rows[0], pltpu.roll(ref[(*index, slice(0, TILE))], 1, 0))
+    if y + TILE < rows:
+        high = ref[(*index, slice(y + 1, y + 1 + TILE))]
+    else:
+        high = jnp.where(row == TILE - 1, y_rows[1], pltpu.roll(ref[(*index, slice(y, y + TILE))], TILE - 1, 0))
+    return low, high
+
+
+def apply_kernel(is_first_apply, is_inner, *refs):
+    names = ["field", "masked", "mask", "x_0", "x_1", "early_diag", "early_flux"]
+    names += ["diag_hbm", "flux_hbm"] if is_first_apply and is_inner else ["late_diag", "late_flux"]
+    names += ["perm"] if is_first_apply else ["weights"]
+    names += [] if is_inner else ["y_0", "y_1", "inner"]
+    names += ["out"] if is_inner or is_first_apply else ["out_hbm"]
     if is_first_apply:
-        perm_ref, diag_hbm, flux_hbm, out_ref, rounded_ref, late_diag, late_flux, weights_ref, *rest, padded_perm, sems = rest
-    else:
-        late_diag, late_flux, weights_ref, out_hbm, *rest, out_ref, out_sems = rest
-    padded, edge_x, place, beside_edge = rest
+        names += ["late_diag", "late_flux"] if is_inner else ["rounded"]
+        names += ["weights"]
+    names += ["edge_x", "place", "turned", "beside_x"]
+    names += ["sems"] if is_first_apply and is_inner else []
+    names += [] if is_inner or is_first_apply else ["out", "sems"]
+    ref = dict(zip(names, refs, strict=True))
+    field_ref, masked_ref, edge_x, place = ref["field"], ref["masked"], ref["edge_x"], ref["place"]
     layers, comps, rows, cols = field_ref.shape
-    early = early_diag.shape[0]
-    top = 8
-
-    def out_copy(k):
-        return pltpu.make_async_copy(out_ref.at[k], out_hbm.at[k], out_sems.at[k])
+    early = ref["early_diag"].shape[0]
+    inner_rows = rows - 2 * TILE
+    tiles = list(range(TILE, rows - TILE, TILE)) if is_inner else [0, rows - TILE]
+    here_rows = len(tiles) * TILE
 
     def blocks(i):
-        return (
-            pltpu.make_async_copy(diag_hbm.at[early + i], late_diag.at[i], sems.at[0, i]),
-            pltpu.make_async_copy(flux_hbm.at[early + i], late_flux.at[i], sems.at[1, i]),
-        )
-
-    if is_first_apply:
+        return [
+            pltpu.make_async_copy(ref[f"{name}_hbm"].at[early + i], ref[f"late_{name}"].at[i], ref["sems"].at[j, i])
+            for j, name in enumerate(("diag", "flux"))
+        ]
+
+    def out_copies(k):
+        middle = slice(TILE, rows - TILE)
+        pairs = [(ref["inner"].at[k], ref["out_hbm"].at[k, :, middle])]
+        pairs += [
+            (ref["out"].at[k, :, j * TILE : (j + 1) * TILE], ref["out_hbm"].at[k, :, y : y + TILE]) for j, y in enumerate(tiles)
+        ]
+        return [pltpu.make_async_copy(a, b, ref["sems"].at[j, k]) for j, (a, b) in enumerate(pairs)]
+
+    if is_first_apply and is_inner:
         for i in range(layers - early):
             for copy in blocks(i):
                 copy.start()
@@ -194,101 +215,135 @@
         place[:, r * cols : (r + 1) * cols] = jnp.where(taken, 1.0, 0.0).astype(BF16)
     even_x = lax.axis_index("gx") % 2 == 0
     even_y = lax.axis_index("gy") % 2 == 0
-    edge_x[...] = jnp.where((lane % 2 == 0) == even_x, x_1[...].astype(F32), x_0[...].astype(F32))
-    clear = 1.0 - mask_ref[...].astype(F32)
+    edge_x[...] = jnp.where((lane % 2 == 0) == even_x, ref["x_1"][...].astype(F32), ref["x_0"][...].astype(F32))
+    for k in range(layers):
+        for j, y in enumerate(tiles):
+            start = k * here_rows + j * TILE
+            piece = pltpu.roll(edge_x[y : y + TILE], (cols - 2 * comps * k) % cols, 1)
+            ref["turned"][start : start + TILE] = piece.astype(BF16)
+    ref["beside_x"][...] = jnp.dot(ref["turned"][...], place[...], preferred_element_type=F32)
 
     def layer(diag_ref, flux_ref, start, i, carry):
         k = i + start
         above = jnp.minimum(k + 1, layers - 1)
         below = jnp.maximum(k - 1, 0)
-        turned = pltpu.roll(edge_x[...], lax.rem(cols - 2 * comps * k, cols), 1).astype(BF16)
-        beside_edge[...] = jnp.dot(turned, place[...], preferred_element_type=F32)
-        odd = k % 2 == 1
-        here = pl.ds(pl.multiple_of(16 * (k // 2), 16), 16)
-        side_0, side_1 = y_0[here].astype(F32), y_1[here].astype(F32)
-        side_0 = jnp.where(odd, side_0[comps:], side_0[:comps])
-        side_1 = jnp.where(odd, side_1[comps:], side_1[:comps])
-        low_y, high_y = jnp.where(even_y, side_1, side_0), jnp.where(even_y, side_0, side_1)
-        for c in range(comps):
-            padded[c, top : top + rows] = field_ref[k, c] * clear
-            padded[c, top - 1 : top] = low_y[c : c + 1]
-            padded[c, top + rows : top + rows + 1] = high_y[c : c + 1]
-        if is_first_apply:
-            write_weights(k, weights_ref, mask_ref, perm_ref, padded_perm, edge_x, y_0, y_1, comps)
-            if start > 0:
-                for copy in blocks(i):
-                    copy.wait()
-
-        for y in range(0, rows, TILE):
-            here = slice(y, y + TILE)
-            at = top + y
-            well = mask_ref[here].astype(F32)
-            weights = [weights_ref[k, j, here] for j in range(WEIGHTS)]
+        rows_y, perm_y = None, None
+        if not is_inner:
+            odd = k % 2 == 1
+            here = pl.ds(pl.multiple_of(16 * (k // 2), 16), 16)
+            sides = [ref[name][here].astype(F32) for name in ("y_0", "y_1")]
+            sides = [jnp.where(odd, side[comps:], side[:comps]) for side in sides]
+            rows_y = (jnp.where(even_y, sides[1], sides[0]), jnp.where(even_y, sides[0], sides[1]))
+        if is_first_apply and not is_inner:
+            here = slice(layers * comps, layers * comps + 16)
+            mine = lax.broadcasted_iota(jnp.int32, (16, cols), 0) == k
+            sides = [
+                jnp.sum(jnp.where(mine, ref[name][here].astype(F32), 0.0), axis=0, keepdims=True) for name in ("y_0", "y_1")
+            ]
+            perm_y = (jnp.where(even_y, sides[1], sides[0]), jnp.where(even_y, sides[0], sides[1]))
+        if is_first_apply and is_inner and start > 0:
+            for copy in blocks(i):
+                copy.wait()
+
+        for j, y in enumerate(tiles):
+            here, local = slice(y, y + TILE), slice(j * TILE, (j + 1) * TILE)
+            side_rows = pl.ds(pl.multiple_of(k * here_rows + j * TILE, TILE), TILE)
+            if is_first_apply:
+                weights = tile_weights(k, y, ref["perm"], edge_x, perm_y, comps)
+                for number, value in enumerate(weights):
+                    ref["weights"][k, number, local] = value
+            else:
+                weights = [ref["weights"][k, number, local] for number in range(WEIGHTS)]
             total = [None] * comps
             for r in range(comps):
-                own = padded[r, at : at + TILE]
+                own = masked_ref[k, r, here]
+                low, high = beside_y(masked_ref, (k, r), y, None if is_inner else [side[r : r + 1] for side in rows_y])
                 summed = (
-                    weights[0] * field_ref[above, r, here]
-                    + weights[1] * field_ref[below, r, here]
-                    + weights[2] * padded[r, at + 1 : at + 1 + TILE]
-                    + weights[3] * padded[r, at - 1 : at - 1 + TILE]
+                    weights[0] * masked_ref[above, r, here]
+                    + weights[1] * masked_ref[below, r, here]
+                    + weights[2] * high
+                    + weights[3] * low
                     + weights[4] * pltpu.roll(own, cols - 1, 1)
                     + weights[5] * pltpu.roll(own, 1, 1)
-                    + weights[6] * beside_edge[here, r * cols : (r + 1) * cols]
+                    + weights[6] * ref["beside_x"][side_rows, r * cols : (r + 1) * cols]
                 )
                 for c in range(comps):
                     term = diag_ref[i, r, c, here].astype(F32) * own - flux_ref[i, r, c, here].astype(F32) * summed
                     total[c] = term if r == 0 else total[c] + term
+            well = ref["mask"][here].astype(F32)
             for c in range(comps):
                 value = total[c] + well * field_ref[k, c, here]
-                out_ref[k, c, here] = value
-                if is_first_apply:
+                if is_first_apply and not is_inner:
+                    ref["out"][k, c, here] = value
                     columns = pl.ds(pl.multiple_of(k * cols, cols), cols)
-                    rounded_ref[c * rows + y : c * rows + y + TILE, columns] = value.astype(BF16)
-        if not is_first_apply:
-            out_copy(k).start()
+                    ref["rounded"][c * rows + y : c * rows + y + TILE, columns] = value.astype(BF16)
+                else:
+                    ref["out"][k, c, local] = value
+        if is_first_apply and not is_inner:
+            columns = pl.ds(pl.multiple_of(k * cols, cols), cols)
+            for c in range(comps):
+                value = ref["inner"][k, c]
+                ref["out"][k, c, TILE : rows - TILE] = value
+                ref["rounded"][c * rows + TILE : (c + 1) * rows - TILE, columns] = value.astype(BF16)
+        if not is_first_apply and not is_inner:
+            for copy in out_copies(k):
+                copy.start()
         return carry
 
-    lax.fori_loop(0, early, functools.partial(layer, early_diag, early_flux, 0), 0)
-    lax.fori_loop(0, layers - early, functools.partial(layer, late_diag, late_flux, early), 0)
-    if not is_first_apply:
+    lax.fori_loop(0, early, functools.partial(layer, ref["early_diag"], ref["early_flux"], 0), 0)
+    lax.fori_loop(0, layers - early, functools.partial(layer, ref["late_diag"], ref["late_flux"], early), 0)
+    if not is_first_apply and not is_inner:
         for k in range(layers):
-            out_copy(k).wait()
-
-
-def apply_transposed(field, mask, halos, early_blocks, rest):
+            for copy in out_copies(k):
+                copy.wait()
+
+
+def apply_rows(is_first_apply, is_inner, field, masked, mask, halos, early, late, third, inner=None):
     layers, comps, rows, cols = field.shape
     vmem = pl.BlockSpec(memory_space=pltpu.VMEM)
     hbm = pl.BlockSpec(memory_space=pltpu.HBM)
-    is_first_apply = rest[0].ndim == 3
-    out_shape = [jax.ShapeDtypeStruct(field.shape, F32)]
+    here_rows = rows - 2 * TILE if is_inner else 2 * TILE
+    late_count = layers - early[0].shape[0]
+    here = (layers, comps, here_rows, cols)
+    loads = is_first_apply and is_inner
+    late_spec = hbm if loads else vmem
+    arrays = [field, masked, mask, *halos[:2], *early, *(in_hbm(*late) if loads else late), third]
+    specs = [vmem] * 7 + [late_spec] * 2 + [vmem]
+    if not is_inner:
+        arrays += [*halos[2:], inner]
+        specs += [vmem] * 3
+    if is_inner:
+        out_shape, out_specs = [pltpu.VMEM(here, F32)], [vmem]
+    else:
+        out_shape = [jax.ShapeDtypeStruct(field.shape, F32)]
+        out_specs = [vmem if is_first_apply else hbm]
     if is_first_apply:
-        perm, *blocks = rest
-        late = layers - early_blocks[0].shape[0]
-        rest, rest_specs, out_specs = [perm, *in_hbm(*blocks)], [vmem, hbm, hbm], [vmem] * 5
-        out_shape.append(jax.ShapeDtypeStruct((comps * rows, layers * cols), BF16))
-        out_shape += [pltpu.VMEM((late, *block.shape[1:]), BF16) for block in blocks]
-        out_shape.append(pltpu.VMEM((layers, WEIGHTS, rows, cols), F32))
-        tail = [pltpu.VMEM((rows + 16, cols), F32), pltpu.SemaphoreType.DMA((2, late))]
-    else:
-        rest_specs, out_specs = [vmem] * 3, [hbm]
-        tail = [pltpu.VMEM(field.shape, F32), pltpu.SemaphoreType.DMA((layers,))]
-    size = layers * comps * comps * rows * cols
+        if is_inner:
+            out_shape += [pltpu.VMEM((late_count, *block.shape[1:]), BF16) for block in late]
+        else:
+            out_shape.append(jax.ShapeDtypeStruct((comps * rows, layers * cols), BF16))
+        out_shape.append(pltpu.VMEM((layers, WEIGHTS, here_rows, cols), F32))
+        out_specs = [vmem] * len(out_shape)
+    scratch = [
+        pltpu.VMEM((rows, cols), F32),
+        pltpu.VMEM((cols, comps * cols), BF16),
+        pltpu.VMEM((layers * here_rows, cols), BF16),
+        pltpu.VMEM((layers * here_rows, comps * cols), F32),
+    ]
+    if loads:
+        scratch.append(pltpu.SemaphoreType.DMA((2, late_count)))
+    if not is_first_apply and not is_inner:
+        scratch += [pltpu.VMEM(here, F32), pltpu.SemaphoreType.DMA((3, layers))]
+    size = layers * comps * comps * here_rows * cols
     return pl.pallas_call(
-        functools.partial(apply_kernel, is_first_apply),
-        in_specs=[vmem] * 8 + rest_specs,
+        functools.partial(apply_kernel, is_first_apply, is_inner),
+        in_specs=specs,
         out_specs=out_specs,
         out_shape=out_shape,
-        scratch_shapes=[
-            pltpu.VMEM((comps, rows + 16, cols), F32),
-            pltpu.VMEM((rows, cols), F32),
-            pltpu.VMEM((cols, comps * cols), BF16),
-            pltpu.VMEM((rows, comps * cols), F32),
-            *tail,
-        ],
-        compiler_params=params(24),
+        scratch_shapes=scratch,
+        compiler_params=params(16),
         cost_estimate=cost(8 * size, 4 * size + 8 * field.size),
-    )(field, mask, *halos, *early_blocks, *rest)
+    )(*arrays)
 
 
 def split_cells(cells, rows, cols):
@@ -402,7 +457,7 @@
 
 def scatter_kernel(
     scale, helper_ref, cells_ref, back_ref, first_ref, mask_ref,
-    second_ref, send_y_0, send_y_1, send_x, grad_ref,
+    second_ref, masked_ref, send_y_0, send_y_1, send_x, grad_ref,
     added, side_y,
 ):
     layers, comps, rows, cols = first_ref.shape
@@ -428,9 +483,7 @@
     for k in range(layers):
         for c in range(comps):
             second_ref[k, c] = first_ref[k, c] + added[c * rows : (c + 1) * rows, k * cols : (k + 1) * cols]
-    clear = 1.0 - mask_ref[...].astype(F32)
-    sends = (send_y_0, send_y_1, send_x)
-    write_edges(lambda k, c: second_ref[k, c], second_ref.shape, clear, None, side_y, sends)
+    write_edges(second_ref, mask_ref, None, masked_ref, side_y, (send_y_0, send_y_1, send_x))
 
     def add_part(b, total):
         return total + back_ref[b].astype(F32)[comps:]
@@ -449,9 +502,10 @@
     return pl.pallas_call(
         functools.partial(scatter_kernel, scale),
         in_specs=[smem] + [vmem] * 4,
-        out_specs=[vmem] * 5,
+        out_specs=[vmem] * 6,
         out_shape=[
-            jax.ShapeDtypeStruct(first.shape, F32),
+            pltpu.VMEM(first.shape, F32),
+            pltpu.VMEM(first.shape, F32),
             *edge_shapes(*first.shape),
             jax.ShapeDtypeStruct((comps, comps), F32),
         ],
@@ -486,21 +540,25 @@
     def to_partners(array):
         return lax.all_to_all(array, AXES, split_axis=0, concat_axis=0, tiled=True)
 
-    *sides, field, mask, perm, early_diag, early_flux = opening(
+    *sides, masked, field, mask, perm, early_diag, early_flux = opening(
         cotangent, well_mask, permeability, diag_block, flux_block, min(EARLY, layers - 1)
     )
     early = (early_diag, early_flux)
     halos = exchange(*sides)
-    first, rounded, *kept = apply_transposed(field, mask, halos, early, (perm, diag_block, flux_block))
+    inner, *late, inner_weights = apply_rows(
+        True, True, field, masked, mask, halos, early, (diag_block, flux_block), perm
+    )
+    first, rounded, outer_weights = apply_rows(True, False, field, masked, mask, halos, early, late, perm, inner)
     sent = gather(rounded, cells(GATHER_CHUNK), helper_of, block_count, comps, rows, cols, width)
     reply = at_helper(inverse, coupling, state, to_partners(sent))
     devices = lax.axis_size("gx") * lax.axis_size("gy")
     scale = -1.0 / math.sqrt(width * devices * devices)
-    second, *sides, interaction_grad = scatter(
+    second, masked, *sides, interaction_grad = scatter(
         first, to_partners(reply), helper_of, cells(SCATTER_CHUNK), mask, scale
     )
     halos = exchange(*sides)
-    (adjoint,) = apply_transposed(second, mask, halos, early, kept)
+    (inner,) = apply_rows(False, True, second, masked, mask, halos, early, late, inner_weights)
+    (adjoint,) = apply_rows(False, False, second, masked, mask, halos, early, late, outer_weights, inner)
     return (adjoint, interaction_grad)
 
 

time: 66.8 us -> 63.7 us (0.954); the launches traced: 66.6 us -> 62.8 us
  waiting for transfers between devices: 5.09 us -> 0.02 us
  Pallas kernels: 24.2 us -> 25.8 us
    ppermute x8, waiting for transfers between devices: 5.09 us -> 0.02 us  [swaps(): lax.ppermute(array, axis, pairs + [(j, i) for i, j in pairs])]
    pallas_call x3 -> x5, Pallas kernels: 13.3 us -> 14.9 us  [the longest x4 12.1 us: apply_rows(): pl.pallas_call(functools.partial(apply_kernel, is_first_apply, is_inner),...]
  transfers between devices with their start and end apart: 8 -> 8, of which waited for: 2 -> 0; matrix products, arithmetic and copies ran while one was open for 0% -> 0% of each run, Pallas kernels for 0% -> 10%
where the time goes in v7:
time: 63.7 us; the launch traced here: 62.8 us
  Pallas kernels  25.8 us (41%)
  blocking collectives  21.1 us (33%)
  starting transfers between devices  14.4 us (23%)
  between operations  1.48 us (2%)
    all_to_all x2, blocking collectives, to_partners(): return lax.all_to_all(array, AXES, split_axis=0, concat_axis=0, tiled=True)  21.1 us
    ppermute x8, starting transfers between devices, swaps(): lax.ppermute(array, axis, pairs + [(j, i) for i, j in pairs])  14.4 us
    pallas_call x4, Pallas kernels, apply_rows(): pl.pallas_call(functools.partial(apply_kernel, is_first_apply, is_inner),...  12.1 us
    pallas_call x1, Pallas kernels, scatter(): pl.pallas_call(functools.partial(scatter_kernel, scale), in_specs=[smem]...  5.53 us
    pallas_call x1, Pallas kernels, gather(): pl.pallas_call(functools.partial(gather_kernel, rows, cols), in_specs=[sm...  4.51 us
    pallas_call x1, Pallas kernels, opening(): pl.pallas_call(opening_kernel, in_specs=[hbm] * 5, out_specs=[vmem] * 9,...  2.83 us
  transfers between devices with their start and end apart: 8, of which 0 were waited for; matrix products, arithmetic and copies ran while one was open for 0% of the time, Pallas kernels for 10%

profile of v7, /device:TPU:9, one launch (start us, length us, event | category | flops | bytes accessed | tf_op | source)
XLA Modules:
  0.0 62.8 jit_solution(16558204366690525334)
XLA Ops:
  0.6 2.8 %shard_map.122 = (bf16[64,128]{1,0:T(8,128)(2,1)S(1)}, bf16[64,128]{1,0:T(8,128)(2,1)S(1)}, bf16[64,128]{1,0:T(8,128)(2,1)S(1)}, f32[6,8,64,128]{3,2,1,0:T(8,128...) custom-call(f32[6,8,64,128]{3,2,1,0:T(8,128)} %field_hbm.1, ...), custom_call_target="tpu_custom_call" | custom-call | flops 1572864 | bytes 3145728 | tf_op jit(solution)/shard_map/pallas_call | solution.py:97
  3.5 0.7 %collective-permute-start = (bf16[64,128]{1,0:T(8,128)(2,1)S(1)}, bf16[64,128]{1,0:T(8,128)(2,1)S(1)}, u32[]{:S(2)}, u32[]{:S(2)}) collective-permute-start(bf16[64,128]{1,0:T(8,128)(2,1)S(1)} %get-tuple-element.27), channel_id=1, source_target_pairs={{0,8},{16,24},{8,0},{24,16},{1,9},{17,25},{9,1},{25,17},{2,10},{18... | collective-permute-start | bytes 49160 | tf_op jit(solution)/shard_map/ppermute | solution.py:114
  4.2 3.0 %collective-permute-start.1 = (bf16[64,128]{1,0:T(8,128)(2,1)S(1)}, bf16[64,128]{1,0:T(8,128)(2,1)S(1)}, u32[]{:S(2)}, u32[]{:S(2)}) collective-permute-start(bf16[64,128]{1,0:T(8,128)(2,1)S(1)} %get-tuple-element.27), channel_id=1, source_target_pairs={{8,16},{16,8},{9,17},{17,9},{10,18},{18,10},{11,19},{19,11},{12,20... | collective-permute-start | bytes 49160 | tf_op jit(solution)/shard_map/ppermute | solution.py:114
  7.3 1.3 %collective-permute-start.2 = (bf16[64,128]{1,0:T(8,128)(2,1)S(1)}, bf16[64,128]{1,0:T(8,128)(2,1)S(1)}, u32[]{:S(2)}, u32[]{:S(2)}) collective-permute-start(bf16[64,128]{1,0:T(8,128)(2,1)S(1)} %get-tuple-element.33), channel_id=1, source_target_pairs={{0,1},{2,3},{4,5},{6,7},{1,0},{3,2},{5,4},{7,6},{8,9},{10,11},{12,... | collective-permute-start | bytes 49160 | tf_op jit(solution)/shard_map/ppermute | solution.py:114
  8.5 2.0 %collective-permute-start.3 = (bf16[64,128]{1,0:T(8,128)(2,1)S(1)}, bf16[64,128]{1,0:T(8,128)(2,1)S(1)}, u32[]{:S(2)}, u32[]{:S(2)}) collective-permute-start(bf16[64,128]{1,0:T(8,128)(2,1)S(1)} %get-tuple-element.34), channel_id=1, source_target_pairs={{1,2},{3,4},{5,6},{2,1},{4,3},{6,5},{9,10},{11,12},{13,14},{10,9},... | collective-permute-start | bytes 49160 | tf_op jit(solution)/shard_map/ppermute | solution.py:114
  11.2 0.0 collective-permute-done.refs_3_
  11.2 0.0 collective-permute-done.1.refs_4_
  11.3 3.9 %shard_map.123 = (f32[6,8,32,128]{3,2,1,0:T(8,128)S(1)}, bf16[4,8,8,64,128]{4,3,2,1,0:T(8,128)(2,1)S(1)}, bf16[4,8,8,64,128]{4,3,2,1,0:T(8,128)(2,1)S(1)}, f32[6,7,32,128]{3,2,1,0:T(8,128)S(1)}) custom-call(f32[6,8,64,128]{3,2,1,0:T(8,128)S(1)} %get-tuple-element.24.refs_0_, f32[6,8,64,128]{3,2,1,0:T(8,128)S(1)} %get-tuple-element.25.refs_1_, ...), custom_call_target="tpu_custom_call" | custom-call | flops 12582912 | bytes 9437184 | tf_op jit(solution)/shard_map/pallas_call | solution.py:338
  15.1 0.0 collective-permute-done.2.refs_10_
  15.1 0.0 collective-permute-done.3.refs_11_
  15.1 0.0 copy-start.3
  15.2 0.0 copy-start.4
  15.2 2.6 %shard_map.124 = (f32[6,8,64,128]{3,2,1,0:T(8,128)S(1)}, bf16[512,768]{1,0:T(8,128)(2,1)S(1)}, f32[6,7,32,128]{3,2,1,0:T(8,128)S(1)}) custom-call(f32[6,8,64,128]{3,2,1,0:T(8,128)S(1)} %get-tuple-element.24.refs_0_, f32[6,8,64,128]{3,2,1,0:T(8,128)S(1)} %get-tuple-element.25.refs_1_, s32[64,128]{1,0:T(8,128)S(1)} %get-tuple-element.26.refs_2_.mask_ref, ...), custom_call_target="tpu_custom_call" | custom-call | flops 12582912 | bytes 9437184 | tf_op jit(solution)/shard_map/pallas_call | solution.py:338
  17.8 0.0 copy-start
  17.8 0.0 copy-start.1
  17.9 0.0 copy-start.2
  17.9 4.5 %shard_map.125 = bf16[32,8,128]{2,1,0:T(8,128)(2,1)S(1)} custom-call(s32[1,1,32]{2,1,0:T(1,128)S(1)} %copy-done.4, s32[1,1]{1,0:T(1,128)S(6)} %copy.13.count_ref, s32[8,1,512]{2,1,0:T(1,128)S(1)} %bitcast.8, bf16[512,768]{1,0:T(8,128)(2,1)S(1)} %get-tuple-element.36.rounded_ref), custom_call_target="tpu_custom_call" | custom-call | flops 3221225472 | bytes 786432 | tf_op jit(solution)/shard_map/pallas_call | solution.py:400
  22.4 11.5 %all_to_all.10.picked_ref = bf16[32,8,128]{2,1,0:T(8,128)(2,1)S(1)} all-to-all(bf16[32,8,128]{2,1,0:T(8,128)(2,1)S(1)} %shard_map.125), channel_id=1, replica_groups=mesh['gx'=4,'gy'=8] {'gx','gy'}, dimensions={0} | all-to-all | bytes 131072 | tf_op jit(solution)/shard_map/all_to_all | solution.py:541
  33.9 0.0 copy-done.1
  33.9 0.9 %shard_map.126 = bf16[32,16,128]{2,1,0:T(8,128)(2,1)S(1)} custom-call(bf16[32,8,8,128]{3,2,1,0:T(8,128)(2,1)S(1)} %bitcast.5, bf16[32,8,8,128]{3,2,1,0:T(8,128)(2,1)S(1)} %bitcast.6, bf16[32,8,128]{2,1,0:T(8,128)(2,1)S(1)} %bitcast.7, bf16[32,8,128]{2,1,0:T(8,128)(2,1)S(1)} %all_to_all.10.picked_ref), custom_call_target="tpu_custom_call" | custom-call | flops 1048576 | bytes 1048576 | tf_op jit(solution)/shard_map/pallas_call | solution.py:450
  34.8 9.6 %all_to_all.11.back_ref = bf16[32,16,128]{2,1,0:T(8,128)(2,1)S(1)} all-to-all(bf16[32,16,128]{2,1,0:T(8,128)(2,1)S(1)} %shard_map.126), channel_id=1, replica_groups=mesh['gx'=4,'gy'=8] {'gx','gy'}, dimensions={0} | all-to-all | bytes 262144 | tf_op jit(solution)/shard_map/all_to_all | solution.py:541
  44.4 5.5 %shard_map.127 = (f32[6,8,64,128]{3,2,1,0:T(8,128)S(1)}, f32[6,8,64,128]{3,2,1,0:T(8,128)S(1)}, bf16[64,128]{1,0:T(8,128)(2,1)S(1)}, bf16[64,128]{1,0:T(8,128)(2...) custom-call(s32[1,1,32]{2,1,0:T(1,128)S(1)} %copy-done.4, s32[4,1,1024]{2,1,0:T(1,128)S(1)} %bitcast.9, ...), custom_call_target="tpu_custom_call" | custom-call | flops 3221225472 | bytes 3145728 | tf_op jit(solution)/shard_map/pallas_call | solution.py:502
  49.9 0.8 %collective-permute-start.4 = (bf16[64,128]{1,0:T(8,128)(2,1)S(1)}, bf16[64,128]{1,0:T(8,128)(2,1)S(1)}, u32[]{:S(2)}, u32[]{:S(2)}) collective-permute-start(bf16[64,128]{1,0:T(8,128)(2,1)S(1)} %get-tuple-element.40), channel_id=1, source_target_pairs={{0,8},{16,24},{8,0},{24,16},{1,9},{17,25},{9,1},{25,17},{2,10},{18... | collective-permute-start | bytes 49160 | tf_op jit(solution)/shard_map/ppermute | solution.py:114
  50.8 2.4 %collective-permute-start.5 = (bf16[64,128]{1,0:T(8,128)(2,1)S(1)}, bf16[64,128]{1,0:T(8,128)(2,1)S(1)}, u32[]{:S(2)}, u32[]{:S(2)}) collective-permute-start(bf16[64,128]{1,0:T(8,128)(2,1)S(1)} %get-tuple-element.40), channel_id=1, source_target_pairs={{8,16},{16,8},{9,17},{17,9},{10,18},{18,10},{11,19},{19,11},{12,20... | collective-permute-start | bytes 49160 | tf_op jit(solution)/shard_map/ppermute | solution.py:114
  53.1 0.5 collective-permute-start.6
  53.6 3.6 %collective-permute-start.7 = (bf16[64,128]{1,0:T(8,128)(2,1)S(1)}, bf16[64,128]{1,0:T(8,128)(2,1)S(1)}, u32[]{:S(2)}, u32[]{:S(2)}) collective-permute-start(bf16[64,128]{1,0:T(8,128)(2,1)S(1)} %get-tuple-element.43), channel_id=1, source_target_pairs={{1,2},{3,4},{5,6},{2,1},{4,3},{6,5},{9,10},{11,12},{13,14},{10,9},... | collective-permute-start | bytes 49160 | tf_op jit(solution)/shard_map/ppermute | solution.py:114
  57.2 0.0 collective-permute-done.4.refs_3_
  57.2 0.0 collective-permute-done.5.refs_4_
  57.2 2.4 %shard_map.128.refs_12_ = f32[6,8,32,128]{3,2,1,0:T(8,128)S(1)} custom-call(f32[6,8,64,128]{3,2,1,0:T(8,128)S(1)} %get-tuple-element.38.refs_0_, f32[6,8,64,128]{3,2,1,0:T(8,128)S(1)} %get-tuple-element.39.refs_1_, s32[64,128]{1,0:T(8,128)S(1)} %get-tuple-element.26.refs_2_.mask_ref, bf16[64,128]{1,0:T(8,128)(2,1)S(1)} %collective-permute-done.4.refs_3_, ...), custom_call_target="tpu_custom_call" | custom-call | flops 12582912 | bytes 9437184 | tf_op jit(solution)/shard_map/pallas_call | solution.py:338
  59.6 0.0 collective-permute-done.6.refs_10_
  59.6 0.0 collective-permute-done.7.refs_11_
  59.6 3.2 %shard_map.129 = f32[6,8,64,128]{3,2,1,0:T(8,128)} custom-call(f32[6,8,64,128]{3,2,1,0:T(8,128)S(1)} %get-tuple-element.38.refs_0_, f32[6,8,64,128]{3,2,1,0:T(8,128)S(1)} %get-tuple-element.39.refs_1_, s32[64,128]{1,0:T(8,128)S(1)} %get-tuple-element.26.refs_2_.mask_ref, bf16[64,128]{1,0:T(8,128)(2,1)S(1)} %collective-permute-done.4.refs_3_, ...), custom_call_target="tpu_custom_call" | custom-call | flops 12582912 | bytes 9437184 | tf_op jit(solution)/shard_map/pallas_call | solution.py:338
  (4 shorter events, 0.0 us)
Async XLA Ops:
  3.5 7.8 %collective-permute-start = (bf16[64,128]{1,0:T(8,128)(2,1)S(1)}, bf16[64,128]{1,0:T(8,128)(2,1)S(1)}, u32[]{:S(2)}, u32[]{:S(2)}) collective-permute-start(bf16[64,128]{1,0:T(8,128)(2,1)S(1)} %get-tuple-element.27), channel_id=1, source_target_pairs={{0,8},{16,24},{8,0},{24,16},{1,9},{17,25},{9,1},{25,17},{2,10},{18... | collective-permute-start | bytes 49160 | tf_op jit(solution)/shard_map/ppermute | solution.py:114
  4.2 7.0 %collective-permute-start.1 = (bf16[64,128]{1,0:T(8,128)(2,1)S(1)}, bf16[64,128]{1,0:T(8,128)(2,1)S(1)}, u32[]{:S(2)}, u32[]{:S(2)}) collective-permute-start(bf16[64,128]{1,0:T(8,128)(2,1)S(1)} %get-tuple-element.27), channel_id=1, source_target_pairs={{8,16},{16,8},{9,17},{17,9},{10,18},{18,10},{11,19},{19,11},{12,20... | collective-permute-start | bytes 49160 | tf_op jit(solution)/shard_map/ppermute | solution.py:114
  7.3 7.9 %collective-permute-start.2 = (bf16[64,128]{1,0:T(8,128)(2,1)S(1)}, bf16[64,128]{1,0:T(8,128)(2,1)S(1)}, u32[]{:S(2)}, u32[]{:S(2)}) collective-permute-start(bf16[64,128]{1,0:T(8,128)(2,1)S(1)} %get-tuple-element.33), channel_id=1, source_target_pairs={{0,1},{2,3},{4,5},{6,7},{1,0},{3,2},{5,4},{7,6},{8,9},{10,11},{12,... | collective-permute-start | bytes 49160 | tf_op jit(solution)/shard_map/ppermute | solution.py:114
  8.5 6.6 %collective-permute-start.3 = (bf16[64,128]{1,0:T(8,128)(2,1)S(1)}, bf16[64,128]{1,0:T(8,128)(2,1)S(1)}, u32[]{:S(2)}, u32[]{:S(2)}) collective-permute-start(bf16[64,128]{1,0:T(8,128)(2,1)S(1)} %get-tuple-element.34), channel_id=1, source_target_pairs={{1,2},{3,4},{5,6},{2,1},{4,3},{6,5},{9,10},{11,12},{13,14},{10,9},... | collective-permute-start | bytes 49160 | tf_op jit(solution)/shard_map/ppermute | solution.py:114
  15.1 2.7 %copy-start.3 = (s32[1,1,4096]{2,1,0:T(1,128)S(1)}, s32[1,1,4096]{2,1,0:T(1,128)}, u32[]{:S(2)}) copy-start(s32[1,1,4096]{2,1,0:T(1,128)} %param.16) | copy-start | bytes 49156
  15.2 2.7 %copy-start.4 = (s32[1,1,32]{2,1,0:T(1,128)S(1)}, s32[1,1,32]{2,1,0:T(1,128)}, u32[]{:S(2)}) copy-start(s32[1,1,32]{2,1,0:T(1,128)} %helper_ref.3) | copy-start | bytes 388
  17.8 16.1 %copy-start = (bf16[1,1,32,8,8,128]{5,4,3,2,1,0:T(8,128)(2,1)S(1)}, bf16[1,1,32,8,8,128]{5,4,3,2,1,0:T(8,128)(2,1)}, u32[]{:S(2)}) copy-start(bf16[1,1,32,8,8,128]{5,4,3,2,1,0:T(8,128)(2,1)} %param.19) | copy-start | bytes 1572868
  17.8 16.1 %copy-start.1 = (bf16[1,1,32,8,8,128]{5,4,3,2,1,0:T(8,128)(2,1)S(1)}, bf16[1,1,32,8,8,128]{5,4,3,2,1,0:T(8,128)(2,1)}, u32[]{:S(2)}) copy-start(bf16[1,1,32,8,8,128]{5,4,3,2,1,0:T(8,128)(2,1)} %param.20) | copy-start | bytes 1572868
  17.9 16.1 %copy-start.2 = (bf16[1,1,32,8,128]{4,3,2,1,0:T(8,128)(2,1)S(1)}, bf16[1,1,32,8,128]{4,3,2,1,0:T(8,128)(2,1)}, u32[]{:S(2)}) copy-start(bf16[1,1,32,8,128]{4,3,2,1,0:T(8,128)(2,1)} %param.21) | copy-start | bytes 196612
  49.9 7.3 %collective-permute-start.4 = (bf16[64,128]{1,0:T(8,128)(2,1)S(1)}, bf16[64,128]{1,0:T(8,128)(2,1)S(1)}, u32[]{:S(2)}, u32[]{:S(2)}) collective-permute-start(bf16[64,128]{1,0:T(8,128)(2,1)S(1)} %get-tuple-element.40), channel_id=1, source_target_pairs={{0,8},{16,24},{8,0},{24,16},{1,9},{17,25},{9,1},{25,17},{2,10},{18... | collective-permute-start | bytes 49160 | tf_op jit(solution)/shard_map/ppermute | solution.py:114
  50.8 6.5 %collective-permute-start.5 = (bf16[64,128]{1,0:T(8,128)(2,1)S(1)}, bf16[64,128]{1,0:T(8,128)(2,1)S(1)}, u32[]{:S(2)}, u32[]{:S(2)}) collective-permute-start(bf16[64,128]{1,0:T(8,128)(2,1)S(1)} %get-tuple-element.40), channel_id=1, source_target_pairs={{8,16},{16,8},{9,17},{17,9},{10,18},{18,10},{11,19},{19,11},{12,20... | collective-permute-start | bytes 49160 | tf_op jit(solution)/shard_map/ppermute | solution.py:114
  53.1 6.5 %collective-permute-start.6 = (bf16[64,128]{1,0:T(8,128)(2,1)S(1)}, bf16[64,128]{1,0:T(8,128)(2,1)S(1)}, u32[]{:S(2)}, u32[]{:S(2)}) collective-permute-start(bf16[64,128]{1,0:T(8,128)(2,1)S(1)} %get-tuple-element.42), channel_id=1, source_target_pairs={{0,1},{2,3},{4,5},{6,7},{1,0},{3,2},{5,4},{7,6},{8,9},{10,11},{12,... | collective-permute-start | bytes 49160 | tf_op jit(solution)/shard_map/ppermute | solution.py:114
  53.6 6.0 %collective-permute-start.7 = (bf16[64,128]{1,0:T(8,128)(2,1)S(1)}, bf16[64,128]{1,0:T(8,128)(2,1)S(1)}, u32[]{:S(2)}, u32[]{:S(2)}) collective-permute-start(bf16[64,128]{1,0:T(8,128)(2,1)S(1)} %get-tuple-element.43), channel_id=1, source_target_pairs={{1,2},{3,4},{5,6},{2,1},{4,3},{6,5},{9,10},{11,12},{13,14},{10,9},... | collective-permute-start | bytes 49160 | tf_op jit(solution)/shard_map/ppermute | solution.py:114

commit v8 on v7

--- a/solution.py
+++ b/solution.py
@@ -28,7 +28,7 @@
 
 
 def write_edges(field_ref, mask_ref, perm_ref, masked_ref, side_y, sends):
-    send_y_0, send_y_1, send_x = sends
+    send_y, send_x = sends
     layers, comps, rows, cols = field_ref.shape
     with_perm = perm_ref is not None
     clear = 1.0 - mask_ref[...].astype(F32)
@@ -49,13 +49,13 @@
     even = lax.axis_index("gy") % 2 == 0
     send_x[...] = along_x.astype(BF16)
     low, high = side_y[0].astype(BF16), side_y[1].astype(BF16)
-    send_y_0[...] = jnp.where(even, high, low)
-    send_y_1[...] = jnp.where(even, low, high)
+    send_y[0] = jnp.where(even, high, low)
+    send_y[1] = jnp.where(even, low, high)
 
 
 def opening_kernel(
     field_hbm, mask_hbm, perm_hbm, diag_hbm, flux_hbm,
-    send_y_0, send_y_1, send_x, masked_ref, field_ref, mask_ref, perm_ref, diag_ref, flux_ref,
+    send_y, send_x, masked_ref, field_ref, mask_ref, perm_ref, diag_ref, flux_ref,
     side_y, sems,
 ):
     early = pl.ds(0, diag_ref.shape[0])
@@ -66,7 +66,7 @@
         copy.start()
     for copy in copies[:3]:
         copy.wait()
-    write_edges(field_ref, mask_ref, perm_ref, masked_ref, side_y, (send_y_0, send_y_1, send_x))
+    write_edges(field_ref, mask_ref, perm_ref, masked_ref, side_y, (send_y, send_x))
     for copy in copies[3:]:
         copy.wait()
 
@@ -76,8 +76,8 @@
 
 
 def edge_shapes(layers, comps, rows, cols):
-    along_y = (edge_rows(layers, comps), cols)
-    return [jax.ShapeDtypeStruct(shape, BF16) for shape in (along_y, along_y, (rows, cols))]
+    along_y = (2, edge_rows(layers, comps), cols)
+    return [jax.ShapeDtypeStruct(shape, BF16) for shape in (along_y, (rows, cols))]
 
 
 def edge_scratch(layers, comps, cols):
@@ -97,7 +97,7 @@
     return pl.pallas_call(
         opening_kernel,
         in_specs=[hbm] * 5,
-        out_specs=[vmem] * 9,
+        out_specs=[vmem] * 8,
         out_shape=[*edge_shapes(*field.shape), *(pltpu.VMEM(*item) for item in kept)],
         scratch_shapes=[edge_scratch(layers, comps, cols), pltpu.SemaphoreType.DMA((5,))],
         compiler_params=params(16),
@@ -105,16 +105,18 @@
     )(*in_hbm(field, mask, perm, diag, flux))
 
 
-def exchange(send_y_0, send_y_1, send_x):
-    def swaps(axis, first, second):
+def exchange(send_y, send_x):
+    def swap(array, axis):
+        pairs = [(i, i + 1) for i in range(0, lax.axis_size(axis) - 1, 2)]
+        return lax.ppermute(array, axis, pairs + [(j, i) for i, j in pairs])
+
+    def pass_on(array, axis):
         count = lax.axis_size(axis)
-        results = []
-        for start, array in ((0, first), (1, second)):
-            pairs = [(i, i + 1) for i in range(start, count - 1, 2)]
-            results.append(lax.ppermute(array, axis, pairs + [(j, i) for i, j in pairs]))
-        return results
-
-    return (*swaps("gx", send_x, send_x), *swaps("gy", send_y_0, send_y_1))
+        pairs = [(i, i + 2 if i % 2 == 0 else i - 2) for i in range(count)]
+        return lax.ppermute(array, axis, [(i, j) for i, j in pairs if 0 <= j < count])
+
+    x, y = swap(send_x, "gx"), swap(send_y, "gy")
+    return x, pass_on(x, "gx"), y, pass_on(y, "gy")
 
 
 TILE = 16
@@ -231,14 +233,14 @@
         if not is_inner:
             odd = k % 2 == 1
             here = pl.ds(pl.multiple_of(16 * (k // 2), 16), 16)
-            sides = [ref[name][here].astype(F32) for name in ("y_0", "y_1")]
+            sides = [ref[f"y_{n}"][n, here].astype(F32) for n in range(2)]
             sides = [jnp.where(odd, side[comps:], side[:comps]) for side in sides]
             rows_y = (jnp.where(even_y, sides[1], sides[0]), jnp.where(even_y, sides[0], sides[1]))
         if is_first_apply and not is_inner:
             here = slice(layers * comps, layers * comps + 16)
             mine = lax.broadcasted_iota(jnp.int32, (16, cols), 0) == k
             sides = [
-                jnp.sum(jnp.where(mine, ref[name][here].astype(F32), 0.0), axis=0, keepdims=True) for name in ("y_0", "y_1")
+                jnp.sum(jnp.where(mine, ref[f"y_{n}"][n, here].astype(F32), 0.0), axis=0, keepdims=True) for n in range(2)
             ]
             perm_y = (jnp.where(even_y, sides[1], sides[0]), jnp.where(even_y, sides[0], sides[1]))
         if is_first_apply and is_inner and start > 0:
@@ -457,7 +459,7 @@
 
 def scatter_kernel(
     scale, helper_ref, cells_ref, back_ref, first_ref, mask_ref,
-    second_ref, masked_ref, send_y_0, send_y_1, send_x, grad_ref,
+    second_ref, masked_ref, send_y, send_x, grad_ref,
     added, side_y,
 ):
     layers, comps, rows, cols = first_ref.shape
@@ -483,7 +485,7 @@
     for k in range(layers):
         for c in range(comps):
             second_ref[k, c] = first_ref[k, c] + added[c * rows : (c + 1) * rows, k * cols : (k + 1) * cols]
-    write_edges(second_ref, mask_ref, None, masked_ref, side_y, (send_y_0, send_y_1, send_x))
+    write_edges(second_ref, mask_ref, None, masked_ref, side_y, (send_y, send_x))
 
     def add_part(b, total):
         return total + back_ref[b].astype(F32)[comps:]
@@ -502,7 +504,7 @@
     return pl.pallas_call(
         functools.partial(scatter_kernel, scale),
         in_specs=[smem] + [vmem] * 4,
-        out_specs=[vmem] * 6,
+        out_specs=[vmem] * 5,
         out_shape=[
             pltpu.VMEM(first.shape, F32),
             pltpu.VMEM(first.shape, F32),

time: 63.7 us -> 73.4 us (1.15)
  the two profiles are of different devices: /device:TPU:9 before, /device:TPU:0 now
where the time goes in v8:
time: 73.4 us; the launch traced here: 73.1 us
  Pallas kernels  25.8 us (35%)
  blocking collectives  22 us (30%)
  starting transfers between devices  17 us (23%)
  waiting for transfers between devices  6.79 us (9%)
  between operations  1.45 us (2%)
    all_to_all x2, blocking collectives, to_partners(): return lax.all_to_all(array, AXES, split_axis=0, concat_axis=0, tiled=True)  22 us
    ppermute x4, starting transfers between devices, pass_on(): lax.ppermute(array, axis, [(i, j) for i, j in pairs if 0 <= j < count])  12.8 us
    pallas_call x4, Pallas kernels, apply_rows(): pl.pallas_call(functools.partial(apply_kernel, is_first_apply, is_inner),...  12.1 us
    pallas_call x1, Pallas kernels, scatter(): pl.pallas_call(functools.partial(scatter_kernel, scale), in_specs=[smem]...  5.53 us
    ppermute x4, waiting for transfers between devices, swap(): return lax.ppermute(array, axis, pairs + [(j, i) for i, j in pairs])  4.58 us
    pallas_call x1, Pallas kernels, gather(): pl.pallas_call(functools.partial(gather_kernel, rows, cols), in_specs=[sm...  4.51 us
    ppermute x4, starting transfers between devices, swap(): return lax.ppermute(array, axis, pairs + [(j, i) for i, j in pairs])  4.24 us
    pallas_call x1, Pallas kernels, opening(): pl.pallas_call(opening_kernel, in_specs=[hbm] * 5, out_specs=[vmem] * 8,...  2.83 us
  transfers between devices with their start and end apart: 8, of which 4 were waited for; matrix products, arithmetic and copies ran while one was open for 0% of the time, Pallas kernels for 9%

profile of v8, /device:TPU:0, one launch (start us, length us, event | category | flops | bytes accessed | tf_op | source)
XLA Modules:
  0.0 73.1 jit_solution(17689758002628244831)
XLA Ops:
  0.6 2.8 %shard_map.122 = (bf16[2,64,128]{2,1,0:T(8,128)(2,1)S(1)}, bf16[64,128]{1,0:T(8,128)(2,1)S(1)}, f32[6,8,64,128]{3,2,1,0:T(8,128)S(1)}, f32[6,8,64,128]{3,2,1,0:T...) custom-call(f32[6,8,64,128]{3,2,1,0:T(8,128)} %field_hbm.1, ...), custom_call_target="tpu_custom_call" | custom-call | flops 1572864 | bytes 3145728 | tf_op jit(solution)/shard_map/pallas_call | solution.py:97
  3.5 3.0 %collective-permute-start.2 = (bf16[2,64,128]{2,1,0:T(8,128)(2,1)S(1)}, bf16[2,64,128]{2,1,0:T(8,128)(2,1)S(1)}, u32[]{:S(2)}, u32[]{:S(2)}) collective-permute-start(bf16[2,64,128]{2,1,0:T(8,128)(2,1)S(1)} %get-tuple-element.31), channel_id=1, source_target_pairs={{0,1},{2,3},{4,5},{6,7},{1,0},{3,2},{5,4},{7,6},{8,9},{10,11},{12,... | collective-permute-start | bytes 98312 | tf_op jit(solution)/shard_map/ppermute | solution.py:111
  6.5 0.0 collective-permute-start
  6.5 1.9 %collective-permute-done.2.refs_10_ = bf16[2,64,128]{2,1,0:T(8,128)(2,1)S(1)} collective-permute-done((bf16[2,64,128]{2,1,0:T(8,128)(2,1)S(1)}, bf16[2,64,128]{2,1,0:T(8,128)(2,1)S(1)}, u32[]{:S(2)}, u32[]{:S(2)}) %collective-permute-start.2) | collective-permute-done | bytes 32800 | tf_op jit(solution)/shard_map/ppermute | solution.py:111
  8.4 4.0 %collective-permute-start.3 = (bf16[2,64,128]{2,1,0:T(8,128)(2,1)S(1)}, bf16[2,64,128]{2,1,0:T(8,128)(2,1)S(1)}, u32[]{:S(2)}, u32[]{:S(2)}) collective-permute-start(bf16[2,64,128]{2,1,0:T(8,128)(2,1)S(1)} %collective-permute-done.2.refs_10_), channel_id=1, source_target_pairs={{0,2},{2,4},{3,1},{4,6},{5,3},{7,5},{8,10},{10,12},{11,9},{12,14},... | collective-permute-start | bytes 98312 | tf_op jit(solution)/shard_map/ppermute | solution.py:116
  12.4 0.0 collective-permute-done.refs_3_
  12.4 3.4 %collective-permute-start.1 = (bf16[64,128]{1,0:T(8,128)(2,1)S(1)}, bf16[64,128]{1,0:T(8,128)(2,1)S(1)}, u32[]{:S(2)}, u32[]{:S(2)}) collective-permute-start(bf16[64,128]{1,0:T(8,128)(2,1)S(1)} %collective-permute-done.refs_3_), channel_id=1, source_target_pairs={{0,16},{24,8},{1,17},{25,9},{2,18},{26,10},{3,19},{27,11},{4,20},{... | collective-permute-start | bytes 49160 | tf_op jit(solution)/shard_map/ppermute | solution.py:116
  16.5 0.8 %collective-permute-done.1.refs_4_ = bf16[64,128]{1,0:T(8,128)(2,1)S(1)} collective-permute-done((bf16[64,128]{1,0:T(8,128)(2,1)S(1)}, bf16[64,128]{1,0:T(8,128)(2,1)S(1)}, u32[]{:S(2)}, u32[]{:S(2)}) %collective-permute-start.1) | collective-permute-done | bytes 16416 | tf_op jit(solution)/shard_map/ppermute | solution.py:116
  17.2 3.9 %shard_map.123 = (f32[6,8,32,128]{3,2,1,0:T(8,128)S(1)}, bf16[4,8,8,64,128]{4,3,2,1,0:T(8,128)(2,1)S(1)}, bf16[4,8,8,64,128]{4,3,2,1,0:T(8,128)(2,1)S(1)}, f32[6,7,32,128]{3,2,1,0:T(8,128)S(1)}) custom-call(f32[6,8,64,128]{3,2,1,0:T(8,128)S(1)} %get-tuple-element.22.refs_0_, f32[6,8,64,128]{3,2,1,0:T(8,128)S(1)} %get-tuple-element.23.refs_1_, ...), custom_call_target="tpu_custom_call" | custom-call | flops 12582912 | bytes 9437184 | tf_op jit(solution)/shard_map/pallas_call | solution.py:340
  21.1 0.0 collective-permute-done.3.refs_11_
  21.1 0.0 copy-start.3
  21.1 0.0 copy-start.4
  21.1 2.6 %shard_map.124 = (f32[6,8,64,128]{3,2,1,0:T(8,128)S(1)}, bf16[512,768]{1,0:T(8,128)(2,1)S(1)}, f32[6,7,32,128]{3,2,1,0:T(8,128)S(1)}) custom-call(f32[6,8,64,128]{3,2,1,0:T(8,128)S(1)} %get-tuple-element.22.refs_0_, f32[6,8,64,128]{3,2,1,0:T(8,128)S(1)} %get-tuple-element.23.refs_1_, s32[64,128]{1,0:T(8,128)S(1)} %get-tuple-element.24.refs_2_.mask_ref, ...), custom_call_target="tpu_custom_call" | custom-call | flops 12582912 | bytes 9437184 | tf_op jit(solution)/shard_map/pallas_call | solution.py:340
  23.8 0.0 copy-done.3
  23.8 0.0 copy-start
  23.8 0.0 copy-start.1
  23.8 0.0 copy-start.2
  23.8 4.5 %shard_map.125 = bf16[32,8,128]{2,1,0:T(8,128)(2,1)S(1)} custom-call(s32[1,1,32]{2,1,0:T(1,128)S(1)} %copy-done.4, s32[1,1]{1,0:T(1,128)S(6)} %copy.13.count_ref, s32[8,1,512]{2,1,0:T(1,128)S(1)} %bitcast.8, bf16[512,768]{1,0:T(8,128)(2,1)S(1)} %get-tuple-element.33.rounded_ref), custom_call_target="tpu_custom_call" | custom-call | flops 3221225472 | bytes 786432 | tf_op jit(solution)/shard_map/pallas_call | solution.py:402
  28.4 12.6 %all_to_all.10.picked_ref = bf16[32,8,128]{2,1,0:T(8,128)(2,1)S(1)} all-to-all(bf16[32,8,128]{2,1,0:T(8,128)(2,1)S(1)} %shard_map.125), channel_id=1, replica_groups=mesh['gx'=4,'gy'=8] {'gx','gy'}, dimensions={0} | all-to-all | bytes 131072 | tf_op jit(solution)/shard_map/all_to_all | solution.py:543
  41.0 0.9 %shard_map.126 = bf16[32,16,128]{2,1,0:T(8,128)(2,1)S(1)} custom-call(bf16[32,8,8,128]{3,2,1,0:T(8,128)(2,1)S(1)} %bitcast.5, bf16[32,8,8,128]{3,2,1,0:T(8,128)(2,1)S(1)} %bitcast.6, bf16[32,8,128]{2,1,0:T(8,128)(2,1)S(1)} %bitcast.7, bf16[32,8,128]{2,1,0:T(8,128)(2,1)S(1)} %all_to_all.10.picked_ref), custom_call_target="tpu_custom_call" | custom-call | flops 1048576 | bytes 1048576 | tf_op jit(solution)/shard_map/pallas_call | solution.py:452
  41.8 9.4 %all_to_all.11.back_ref = bf16[32,16,128]{2,1,0:T(8,128)(2,1)S(1)} all-to-all(bf16[32,16,128]{2,1,0:T(8,128)(2,1)S(1)} %shard_map.126), channel_id=1, replica_groups=mesh['gx'=4,'gy'=8] {'gx','gy'}, dimensions={0} | all-to-all | bytes 262144 | tf_op jit(solution)/shard_map/all_to_all | solution.py:543
  51.3 5.5 %shard_map.127 = (f32[6,8,64,128]{3,2,1,0:T(8,128)S(1)}, f32[6,8,64,128]{3,2,1,0:T(8,128)S(1)}, bf16[2,64,128]{2,1,0:T(8,128)(2,1)S(1)}, bf16[64,128]{1,0:T(8,128)(2,1)S(1)}, f32[8,8]{1,0:T(8,128)}) custom-call(s32[1,1,32]{2,1,0:T(1,128)S(1)} %copy-done.4, s32[4,1,1024]{2,1,0:T(1,128)S(1)} %bitcast.9, bf16[32,16,128]{2,1,0:T(8,128)(2,1)S(1)} %all_to_all.11.back_ref, ...), custom_call_target="tpu_custom_call" | custom-call | flops 3221225472 | bytes 3145728 | tf_op jit(solution)/shard_map/pallas_call | solution.py:504
  56.8 1.2 %collective-permute-start.6 = (bf16[2,64,128]{2,1,0:T(8,128)(2,1)S(1)}, bf16[2,64,128]{2,1,0:T(8,128)(2,1)S(1)}, u32[]{:S(2)}, u32[]{:S(2)}) collective-permute-start(bf16[2,64,128]{2,1,0:T(8,128)(2,1)S(1)} %get-tuple-element.39), channel_id=1, source_target_pairs={{0,1},{2,3},{4,5},{6,7},{1,0},{3,2},{5,4},{7,6},{8,9},{10,11},{12,... | collective-permute-start | bytes 98312 | tf_op jit(solution)/shard_map/ppermute | solution.py:111
  58.0 0.0 collective-permute-start.4
  58.0 2.7 %collective-permute-done.6.refs_10_ = bf16[2,64,128]{2,1,0:T(8,128)(2,1)S(1)} collective-permute-done((bf16[2,64,128]{2,1,0:T(8,128)(2,1)S(1)}, bf16[2,64,128]{2,1,0:T(8,128)(2,1)S(1)}, u32[]{:S(2)}, u32[]{:S(2)}) %collective-permute-start.6) | collective-permute-done | bytes 32800 | tf_op jit(solution)/shard_map/ppermute | solution.py:111
  60.7 2.9 %collective-permute-start.7 = (bf16[2,64,128]{2,1,0:T(8,128)(2,1)S(1)}, bf16[2,64,128]{2,1,0:T(8,128)(2,1)S(1)}, u32[]{:S(2)}, u32[]{:S(2)}) collective-permute-start(bf16[2,64,128]{2,1,0:T(8,128)(2,1)S(1)} %collective-permute-done.6.refs_10_), channel_id=1, source_target_pairs={{0,2},{2,4},{3,1},{4,6},{5,3},{7,5},{8,10},{10,12},{11,9},{12,14},... | collective-permute-start | bytes 98312 | tf_op jit(solution)/shard_map/ppermute | solution.py:116
  63.6 0.0 collective-permute-done.4.refs_3_
  63.6 2.4 %collective-permute-start.5 = (bf16[64,128]{1,0:T(8,128)(2,1)S(1)}, bf16[64,128]{1,0:T(8,128)(2,1)S(1)}, u32[]{:S(2)}, u32[]{:S(2)}) collective-permute-start(bf16[64,128]{1,0:T(8,128)(2,1)S(1)} %collective-permute-done.4.refs_3_), channel_id=1, source_target_pairs={{0,16},{24,8},{1,17},{25,9},{2,18},{26,10},{3,19},{27,11},{4,20},{... | collective-permute-start | bytes 49160 | tf_op jit(solution)/shard_map/ppermute | solution.py:116
  66.1 1.4 %collective-permute-done.5.refs_4_ = bf16[64,128]{1,0:T(8,128)(2,1)S(1)} collective-permute-done((bf16[64,128]{1,0:T(8,128)(2,1)S(1)}, bf16[64,128]{1,0:T(8,128)(2,1)S(1)}, u32[]{:S(2)}, u32[]{:S(2)}) %collective-permute-start.5) | collective-permute-done | bytes 16416 | tf_op jit(solution)/shard_map/ppermute | solution.py:116
  67.5 2.4 %shard_map.128.refs_12_ = f32[6,8,32,128]{3,2,1,0:T(8,128)S(1)} custom-call(f32[6,8,64,128]{3,2,1,0:T(8,128)S(1)} %get-tuple-element.35.refs_0_, f32[6,8,64,128]{3,2,1,0:T(8,128)S(1)} %get-tuple-element.36.refs_1_, s32[64,128]{1,0:T(8,128)S(1)} %get-tuple-element.24.refs_2_.mask_ref, bf16[64,128]{1,0:T(8,128)(2,1)S(1)} %collective-permute-done.4.refs_3_, ...), custom_call_target="tpu_custom_call" | custom-call | flops 12582912 | bytes 9437184 | tf_op jit(solution)/shard_map/pallas_call | solution.py:340
  69.9 0.0 collective-permute-done.7.refs_11_
  69.9 3.2 %shard_map.129 = f32[6,8,64,128]{3,2,1,0:T(8,128)} custom-call(f32[6,8,64,128]{3,2,1,0:T(8,128)S(1)} %get-tuple-element.35.refs_0_, f32[6,8,64,128]{3,2,1,0:T(8,128)S(1)} %get-tuple-element.36.refs_1_, s32[64,128]{1,0:T(8,128)S(1)} %get-tuple-element.24.refs_2_.mask_ref, bf16[64,128]{1,0:T(8,128)(2,1)S(1)} %collective-permute-done.4.refs_3_, ...), custom_call_target="tpu_custom_call" | custom-call | flops 12582912 | bytes 9437184 | tf_op jit(solution)/shard_map/pallas_call | solution.py:340
  (4 shorter events, 0.0 us)
Async XLA Ops:
  3.5 4.9 %collective-permute-start.2 = (bf16[2,64,128]{2,1,0:T(8,128)(2,1)S(1)}, bf16[2,64,128]{2,1,0:T(8,128)(2,1)S(1)}, u32[]{:S(2)}, u32[]{:S(2)}) collective-permute-start(bf16[2,64,128]{2,1,0:T(8,128)(2,1)S(1)} %get-tuple-element.31), channel_id=1, source_target_pairs={{0,1},{2,3},{4,5},{6,7},{1,0},{3,2},{5,4},{7,6},{8,9},{10,11},{12,... | collective-permute-start | bytes 98312 | tf_op jit(solution)/shard_map/ppermute | solution.py:111
  6.5 5.9 %collective-permute-start = (bf16[64,128]{1,0:T(8,128)(2,1)S(1)}, bf16[64,128]{1,0:T(8,128)(2,1)S(1)}, u32[]{:S(2)}, u32[]{:S(2)}) collective-permute-start(bf16[64,128]{1,0:T(8,128)(2,1)S(1)} %get-tuple-element.25), channel_id=1, source_target_pairs={{0,8},{16,24},{8,0},{24,16},{1,9},{17,25},{9,1},{25,17},{2,10},{18... | collective-permute-start | bytes 49160 | tf_op jit(solution)/shard_map/ppermute | solution.py:111
  8.4 12.7 %collective-permute-start.3 = (bf16[2,64,128]{2,1,0:T(8,128)(2,1)S(1)}, bf16[2,64,128]{2,1,0:T(8,128)(2,1)S(1)}, u32[]{:S(2)}, u32[]{:S(2)}) collective-permute-start(bf16[2,64,128]{2,1,0:T(8,128)(2,1)S(1)} %collective-permute-done.2.refs_10_), channel_id=1, source_target_pairs={{0,2},{2,4},{3,1},{4,6},{5,3},{7,5},{8,10},{10,12},{11,9},{12,14},... | collective-permute-start | bytes 98312 | tf_op jit(solution)/shard_map/ppermute | solution.py:116
  12.4 4.9 %collective-permute-start.1 = (bf16[64,128]{1,0:T(8,128)(2,1)S(1)}, bf16[64,128]{1,0:T(8,128)(2,1)S(1)}, u32[]{:S(2)}, u32[]{:S(2)}) collective-permute-start(bf16[64,128]{1,0:T(8,128)(2,1)S(1)} %collective-permute-done.refs_3_), channel_id=1, source_target_pairs={{0,16},{24,8},{1,17},{25,9},{2,18},{26,10},{3,19},{27,11},{4,20},{... | collective-permute-start | bytes 49160 | tf_op jit(solution)/shard_map/ppermute | solution.py:116
  21.1 2.7 %copy-start.3 = (s32[1,1,4096]{2,1,0:T(1,128)S(1)}, s32[1,1,4096]{2,1,0:T(1,128)}, u32[]{:S(2)}) copy-start(s32[1,1,4096]{2,1,0:T(1,128)} %param.16) | copy-start | bytes 49156
  21.1 2.7 %copy-start.4 = (s32[1,1,32]{2,1,0:T(1,128)S(1)}, s32[1,1,32]{2,1,0:T(1,128)}, u32[]{:S(2)}) copy-start(s32[1,1,32]{2,1,0:T(1,128)} %helper_ref.3) | copy-start | bytes 388
  23.8 17.2 %copy-start = (bf16[1,1,32,8,8,128]{5,4,3,2,1,0:T(8,128)(2,1)S(1)}, bf16[1,1,32,8,8,128]{5,4,3,2,1,0:T(8,128)(2,1)}, u32[]{:S(2)}) copy-start(bf16[1,1,32,8,8,128]{5,4,3,2,1,0:T(8,128)(2,1)} %param.19) | copy-start | bytes 1572868
  23.8 17.1 %copy-start.1 = (bf16[1,1,32,8,8,128]{5,4,3,2,1,0:T(8,128)(2,1)S(1)}, bf16[1,1,32,8,8,128]{5,4,3,2,1,0:T(8,128)(2,1)}, u32[]{:S(2)}) copy-start(bf16[1,1,32,8,8,128]{5,4,3,2,1,0:T(8,128)(2,1)} %param.20) | copy-start | bytes 1572868
  23.8 17.1 %copy-start.2 = (bf16[1,1,32,8,128]{4,3,2,1,0:T(8,128)(2,1)S(1)}, bf16[1,1,32,8,128]{4,3,2,1,0:T(8,128)(2,1)}, u32[]{:S(2)}) copy-start(bf16[1,1,32,8,128]{4,3,2,1,0:T(8,128)(2,1)} %param.21) | copy-start | bytes 196612
  56.8 3.9 %collective-permute-start.6 = (bf16[2,64,128]{2,1,0:T(8,128)(2,1)S(1)}, bf16[2,64,128]{2,1,0:T(8,128)(2,1)S(1)}, u32[]{:S(2)}, u32[]{:S(2)}) collective-permute-start(bf16[2,64,128]{2,1,0:T(8,128)(2,1)S(1)} %get-tuple-element.39), channel_id=1, source_target_pairs={{0,1},{2,3},{4,5},{6,7},{1,0},{3,2},{5,4},{7,6},{8,9},{10,11},{12,... | collective-permute-start | bytes 98312 | tf_op jit(solution)/shard_map/ppermute | solution.py:111
  58.0 5.6 %collective-permute-start.4 = (bf16[64,128]{1,0:T(8,128)(2,1)S(1)}, bf16[64,128]{1,0:T(8,128)(2,1)S(1)}, u32[]{:S(2)}, u32[]{:S(2)}) collective-permute-start(bf16[64,128]{1,0:T(8,128)(2,1)S(1)} %get-tuple-element.37), channel_id=1, source_target_pairs={{0,8},{16,24},{8,0},{24,16},{1,9},{17,25},{9,1},{25,17},{2,10},{18... | collective-permute-start | bytes 49160 | tf_op jit(solution)/shard_map/ppermute | solution.py:111
  60.7 9.2 %collective-permute-start.7 = (bf16[2,64,128]{2,1,0:T(8,128)(2,1)S(1)}, bf16[2,64,128]{2,1,0:T(8,128)(2,1)S(1)}, u32[]{:S(2)}, u32[]{:S(2)}) collective-permute-start(bf16[2,64,128]{2,1,0:T(8,128)(2,1)S(1)} %collective-permute-done.6.refs_10_), channel_id=1, source_target_pairs={{0,2},{2,4},{3,1},{4,6},{5,3},{7,5},{8,10},{10,12},{11,9},{12,14},... | collective-permute-start | bytes 98312 | tf_op jit(solution)/shard_map/ppermute | solution.py:116
  63.6 3.9 %collective-permute-start.5 = (bf16[64,128]{1,0:T(8,128)(2,1)S(1)}, bf16[64,128]{1,0:T(8,128)(2,1)S(1)}, u32[]{:S(2)}, u32[]{:S(2)}) collective-permute-start(bf16[64,128]{1,0:T(8,128)(2,1)S(1)} %collective-permute-done.4.refs_3_), channel_id=1, source_target_pairs={{0,16},{24,8},{1,17},{25,9},{2,18},{26,10},{3,19},{27,11},{4,20},{... | collective-permute-start | bytes 49160 | tf_op jit(solution)/shard_map/ppermute | solution.py:116

commit v9 on v7

--- a/solution.py
+++ b/solution.py
@@ -12,7 +12,8 @@
 BF16 = jnp.bfloat16
 AXES = ("gx", "gy")
 MIB = 1024 * 1024
-GATHER_CHUNK, SCATTER_CHUNK = 512, 1024
+GATHER_CHUNK, SCATTER_CHUNK = 512, 2048
+KEPT_BYTES = 8 * MIB
 
 
 def params(mib):
@@ -53,9 +54,18 @@
     send_y_1[...] = jnp.where(even, low, high)
 
 
+def write_place(place_ref):
+    cols, width = place_ref.shape
+    number = lax.broadcasted_iota(jnp.int32, (cols, cols), 0)
+    spot = lax.broadcasted_iota(jnp.int32, (cols, cols), 1)
+    for r in range(width // cols):
+        taken = ((number == 2 * r) & (spot == 0)) | ((number == 2 * r + 1) & (spot == cols - 1))
+        place_ref[:, r * cols : (r + 1) * cols] = jnp.where(taken, 1.0, 0.0).astype(BF16)
+
+
 def opening_kernel(
     field_hbm, mask_hbm, perm_hbm, diag_hbm, flux_hbm,
-    send_y_0, send_y_1, send_x, masked_ref, field_ref, mask_ref, perm_ref, diag_ref, flux_ref,
+    send_y_0, send_y_1, send_x, masked_ref, field_ref, mask_ref, perm_ref, diag_ref, flux_ref, place_ref,
     side_y, sems,
 ):
     early = pl.ds(0, diag_ref.shape[0])
@@ -64,6 +74,7 @@
     copies = [pltpu.make_async_copy(a, b, sems.at[i]) for i, (a, b) in enumerate(zip(sources, targets))]
     for copy in copies:
         copy.start()
+    write_place(place_ref)
     for copy in copies[:3]:
         copy.wait()
     write_edges(field_ref, mask_ref, perm_ref, masked_ref, side_y, (send_y_0, send_y_1, send_x))
@@ -94,10 +105,11 @@
     vmem = pl.BlockSpec(memory_space=pltpu.VMEM)
     kept = [(array.shape, array.dtype) for array in (field, field, mask, perm)]
     kept += [((early, *block.shape[1:]), BF16) for block in (diag, flux)]
+    kept.append(((cols, comps * cols), BF16))
     return pl.pallas_call(
         opening_kernel,
         in_specs=[hbm] * 5,
-        out_specs=[vmem] * 9,
+        out_specs=[vmem] * 10,
         out_shape=[*edge_shapes(*field.shape), *(pltpu.VMEM(*item) for item in kept)],
         scratch_shapes=[edge_scratch(layers, comps, cols), pltpu.SemaphoreType.DMA((5,))],
         compiler_params=params(16),
@@ -169,7 +181,7 @@
 
 
 def apply_kernel(is_first_apply, is_inner, *refs):
-    names = ["field", "masked", "mask", "x_0", "x_1", "early_diag", "early_flux"]
+    names = ["field", "masked", "mask", "place", "x_0", "x_1", "early_diag", "early_flux"]
     names += ["diag_hbm", "flux_hbm"] if is_first_apply and is_inner else ["late_diag", "late_flux"]
     names += ["perm"] if is_first_apply else ["weights"]
     names += [] if is_inner else ["y_0", "y_1", "inner"]
@@ -177,7 +189,7 @@
     if is_first_apply:
         names += ["late_diag", "late_flux"] if is_inner else ["rounded"]
         names += ["weights"]
-    names += ["edge_x", "place", "turned", "beside_x"]
+    names += ["edge_x", "turned", "beside_x"]
     names += ["sems"] if is_first_apply and is_inner else []
     names += [] if is_inner or is_first_apply else ["out", "sems"]
     ref = dict(zip(names, refs, strict=True))
@@ -208,11 +220,6 @@
                 copy.start()
 
     lane = lax.broadcasted_iota(jnp.int32, (rows, cols), 1)
-    number = lax.broadcasted_iota(jnp.int32, (cols, cols), 0)
-    spot = lax.broadcasted_iota(jnp.int32, (cols, cols), 1)
-    for r in range(comps):
-        taken = ((number == 2 * r) & (spot == 0)) | ((number == 2 * r + 1) & (spot == cols - 1))
-        place[:, r * cols : (r + 1) * cols] = jnp.where(taken, 1.0, 0.0).astype(BF16)
     even_x = lax.axis_index("gx") % 2 == 0
     even_y = lax.axis_index("gy") % 2 == 0
     edge_x[...] = jnp.where((lane % 2 == 0) == even_x, ref["x_1"][...].astype(F32), ref["x_0"][...].astype(F32))
@@ -290,15 +297,15 @@
                 copy.start()
         return carry
 
-    lax.fori_loop(0, early, functools.partial(layer, ref["early_diag"], ref["early_flux"], 0), 0)
-    lax.fori_loop(0, layers - early, functools.partial(layer, ref["late_diag"], ref["late_flux"], early), 0)
+    unrolled(early, early, functools.partial(layer, ref["early_diag"], ref["early_flux"], 0))
+    unrolled(layers - early, 2, functools.partial(layer, ref["late_diag"], ref["late_flux"], early))
     if not is_first_apply and not is_inner:
         for k in range(layers):
             for copy in out_copies(k):
                 copy.wait()
 
 
-def apply_rows(is_first_apply, is_inner, field, masked, mask, halos, early, late, third, inner=None):
+def apply_rows(is_first_apply, is_inner, field, masked, mask, place, halos, early, late, third, inner=None):
     layers, comps, rows, cols = field.shape
     vmem = pl.BlockSpec(memory_space=pltpu.VMEM)
     hbm = pl.BlockSpec(memory_space=pltpu.HBM)
@@ -307,8 +314,8 @@
     here = (layers, comps, here_rows, cols)
     loads = is_first_apply and is_inner
     late_spec = hbm if loads else vmem
-    arrays = [field, masked, mask, *halos[:2], *early, *(in_hbm(*late) if loads else late), third]
-    specs = [vmem] * 7 + [late_spec] * 2 + [vmem]
+    arrays = [field, masked, mask, place, *halos[:2], *early, *(in_hbm(*late) if loads else late), third]
+    specs = [vmem] * 8 + [late_spec] * 2 + [vmem]
     if not is_inner:
         arrays += [*halos[2:], inner]
         specs += [vmem] * 3
@@ -326,7 +333,6 @@
         out_specs = [vmem] * len(out_shape)
     scratch = [
         pltpu.VMEM((rows, cols), F32),
-        pltpu.VMEM((cols, comps * cols), BF16),
         pltpu.VMEM((layers * here_rows, cols), BF16),
         pltpu.VMEM((layers * here_rows, comps * cols), F32),
     ]
@@ -367,7 +373,7 @@
     return jnp.where(number == column, 1.0, 0.0).astype(BF16)
 
 
-def gather_kernel(rows, cols, helper_ref, count_ref, cells_ref, rounded_ref, sent_ref):
+def gather_kernel(rows, cols, helper_ref, count_ref, cells_ref, rounded_ref, sent_ref, kept_ref=None):
     chunks, _, slots = cells_ref.shape
     comps, width = sent_ref.shape[1:]
     per_chunk = slots // width
@@ -376,6 +382,8 @@
     def one(i, carry):
         column, y = split_cells(cells_ref[i], rows, cols)
         chosen = one_hot(column, rounded_ref.shape[1], slots)
+        if kept_ref is not None:
+            kept_ref[:, pl.ds(pl.multiple_of(i * slots, slots), slots)] = chosen
         found = jnp.dot(rounded_ref[...], chosen, preferred_element_type=F32)
         at_row = row_number == y
         values = [
@@ -394,14 +402,16 @@
 
 def gather(rounded, cells, helper, count, comps, rows, cols, width):
     blocks = helper.shape[-1]
-    shape = jax.ShapeDtypeStruct((blocks, comps, width), BF16)
     smem = pl.BlockSpec(memory_space=pltpu.SMEM)
     vmem = pl.BlockSpec(memory_space=pltpu.VMEM)
+    out_shape = [jax.ShapeDtypeStruct((blocks, comps, width), BF16)]
+    if rounded.shape[1] * cells.size * 2 <= KEPT_BYTES:
+        out_shape.append(pltpu.VMEM((rounded.shape[1], cells.size), BF16))
     return pl.pallas_call(
         functools.partial(gather_kernel, rows, cols),
         in_specs=[smem, smem, vmem, vmem],
-        out_specs=vmem,
-        out_shape=shape,
+        out_specs=[vmem] * len(out_shape),
+        out_shape=out_shape,
         compiler_params=params(16),
         cost_estimate=cost(2 * rounded.size * cells.size, 2 * rounded.size),
     )(helper, count, cells, rounded)
@@ -455,21 +465,24 @@
     )(inverse, coupling, state, picked)
 
 
-def scatter_kernel(
-    scale, helper_ref, cells_ref, back_ref, first_ref, mask_ref,
-    second_ref, masked_ref, send_y_0, send_y_1, send_x, grad_ref,
-    added, side_y,
-):
+def scatter_kernel(scale, has_kept, helper_ref, cells_ref, back_ref, first_ref, mask_ref, *refs):
+    kept_ref = refs[0] if has_kept else None
+    second_ref, masked_ref, *sends, grad_ref, added, side_y = refs[has_kept:]
     layers, comps, rows, cols = first_ref.shape
     chunks, _, slots = cells_ref.shape
     width = back_ref.shape[-1]
     per_chunk = slots // width
     row_number = lax.broadcasted_iota(jnp.int32, (rows, slots), 0)
-    added[...] = jnp.zeros_like(added)
+    for k in range(layers):
+        for c in range(comps):
+            added[c * rows : (c + 1) * rows, k * cols : (k + 1) * cols] = first_ref[k, c]
 
     def one(i, carry):
         column, y = split_cells(cells_ref[i], rows, cols)
-        chosen = one_hot(column, added.shape[1], slots)
+        if has_kept:
+            chosen = kept_ref[:, pl.ds(pl.multiple_of(i * slots, slots), slots)]
+        else:
+            chosen = one_hot(column, added.shape[1], slots)
         parts = [back_ref[helper_ref[0, 0, i * per_chunk + j]].astype(F32)[:comps] for j in range(per_chunk)]
         correction = jnp.concatenate(parts, axis=1)
         at_row = row_number == y
@@ -482,37 +495,36 @@
     unrolled(chunks, 2, one)
     for k in range(layers):
         for c in range(comps):
-            second_ref[k, c] = first_ref[k, c] + added[c * rows : (c + 1) * rows, k * cols : (k + 1) * cols]
-    write_edges(second_ref, mask_ref, None, masked_ref, side_y, (send_y_0, send_y_1, send_x))
-
-    def add_part(b, total):
-        return total + back_ref[b].astype(F32)[comps:]
-
-    total = lax.fori_loop(0, back_ref.shape[0], add_part, jnp.zeros((comps, width), F32))
+            second_ref[k, c] = added[c * rows : (c + 1) * rows, k * cols : (k + 1) * cols]
+    write_edges(second_ref, mask_ref, None, masked_ref, side_y, sends)
+    total = back_ref[0].astype(F32)[comps:]
+    for b in range(1, back_ref.shape[0]):
+        total += back_ref[b].astype(F32)[comps:]
     whole = total
     for part in range(1, PARTS):
         whole += pltpu.roll(total, width - part * comps, 1)
     grad_ref[...] = (whole * scale)[:, :comps]
 
 
-def scatter(first, back, helper, cells, mask, scale):
+def scatter(first, back, helper, cells, mask, kept, scale):
     layers, comps, rows, cols = first.shape
     smem = pl.BlockSpec(memory_space=pltpu.SMEM)
     vmem = pl.BlockSpec(memory_space=pltpu.VMEM)
+    edges = edge_shapes(*first.shape)
     return pl.pallas_call(
-        functools.partial(scatter_kernel, scale),
-        in_specs=[smem] + [vmem] * 4,
-        out_specs=[vmem] * 6,
+        functools.partial(scatter_kernel, scale, len(kept)),
+        in_specs=[smem] + [vmem] * (4 + len(kept)),
+        out_specs=[vmem] * (3 + len(edges)),
         out_shape=[
             pltpu.VMEM(first.shape, F32),
             pltpu.VMEM(first.shape, F32),
-            *edge_shapes(*first.shape),
+            *edges,
             jax.ShapeDtypeStruct((comps, comps), F32),
         ],
         scratch_shapes=[pltpu.VMEM((comps * rows, layers * cols), F32), edge_scratch(layers, comps, cols)],
         compiler_params=params(24),
         cost_estimate=cost(2 * first.size * cells.size, 8 * first.size),
-    )(helper, cells, back, first, mask)
+    )(helper, cells, back, first, mask, *kept)
 
 
 def shards(
@@ -540,25 +552,25 @@
     def to_partners(array):
         return lax.all_to_all(array, AXES, split_axis=0, concat_axis=0, tiled=True)
 
-    *sides, masked, field, mask, perm, early_diag, early_flux = opening(
+    *sides, masked, field, mask, perm, early_diag, early_flux, place = opening(
         cotangent, well_mask, permeability, diag_block, flux_block, min(EARLY, layers - 1)
     )
     early = (early_diag, early_flux)
     halos = exchange(*sides)
     inner, *late, inner_weights = apply_rows(
-        True, True, field, masked, mask, halos, early, (diag_block, flux_block), perm
+        True, True, field, masked, mask, place, halos, early, (diag_block, flux_block), perm
     )
-    first, rounded, outer_weights = apply_rows(True, False, field, masked, mask, halos, early, late, perm, inner)
-    sent = gather(rounded, cells(GATHER_CHUNK), helper_of, block_count, comps, rows, cols, width)
+    first, rounded, outer_weights = apply_rows(True, False, field, masked, mask, place, halos, early, late, perm, inner)
+    sent, *chosen = gather(rounded, cells(GATHER_CHUNK), helper_of, block_count, comps, rows, cols, width)
     reply = at_helper(inverse, coupling, state, to_partners(sent))
     devices = lax.axis_size("gx") * lax.axis_size("gy")
     scale = -1.0 / math.sqrt(width * devices * devices)
     second, masked, *sides, interaction_grad = scatter(
-        first, to_partners(reply), helper_of, cells(SCATTER_CHUNK), mask, scale
+        first, to_partners(reply), helper_of, cells(SCATTER_CHUNK), mask, chosen, scale
     )
     halos = exchange(*sides)
-    (inner,) = apply_rows(False, True, second, masked, mask, halos, early, late, inner_weights)
-    (adjoint,) = apply_rows(False, False, second, masked, mask, halos, early, late, outer_weights, inner)
+    (inner,) = apply_rows(False, True, second, masked, mask, place, halos, early, late, inner_weights)
+    (adjoint,) = apply_rows(False, False, second, masked, mask, place, halos, early, late, outer_weights, inner)
     return (adjoint, interaction_grad)
 
 

time: 63.7 us -> 63.3 us (level)
  the two profiles are of different devices: /device:TPU:9 before, /device:TPU:2 now
where the time goes in v9:
time: 63.3 us; the launch traced here: 63.1 us
  Pallas kernels  24.1 us (38%)
  blocking collectives  20.1 us (32%)
  starting transfers between devices  15.4 us (24%)
  waiting for transfers between devices  1.75 us (3%)
  between operations  1.63 us (3%)
    all_to_all x2, blocking collectives, to_partners(): return lax.all_to_all(array, AXES, split_axis=0, concat_axis=0, tiled=True)  20.1 us
    ppermute x8, starting transfers between devices, swaps(): lax.ppermute(array, axis, pairs + [(j, i) for i, j in pairs])  15.4 us
    pallas_call x4, Pallas kernels, apply_rows(): pl.pallas_call(functools.partial(apply_kernel, is_first_apply, is_inner),...  11 us
    pallas_call x1, Pallas kernels, gather(): pl.pallas_call(functools.partial(gather_kernel, rows, cols), in_specs=[sm...  4.84 us
    pallas_call x1, Pallas kernels, scatter(): pl.pallas_call(functools.partial(scatter_kernel, scale, len(kept)), in_sp...  4.65 us
    pallas_call x1, Pallas kernels, opening(): pl.pallas_call(opening_kernel, in_specs=[hbm] * 5, out_specs=[vmem] * 10,...  2.83 us
    ppermute x8, waiting for transfers between devices, swaps(): lax.ppermute(array, axis, pairs + [(j, i) for i, j in pairs])  1.75 us
  transfers between devices with their start and end apart: 8, of which 1 were waited for; matrix products, arithmetic and copies ran while one was open for 0% of the time, Pallas kernels for 9%

profile of v9, /device:TPU:2, one launch (start us, length us, event | category | flops | bytes accessed | tf_op | source)
XLA Modules:
  0.0 63.1 jit_solution(13112231514812942957)
XLA Ops:
  0.6 2.8 %shard_map.122 = (bf16[64,128]{1,0:T(8,128)(2,1)S(1)}, bf16[64,128]{1,0:T(8,128)(2,1)S(1)}, bf16[64,128]{1,0:T(8,128)(2,1)S(1)}, f32[6,8,64,128]{3,2,1,0:T(8,128...) custom-call(f32[6,8,64,128]{3,2,1,0:T(8,128)} %field_hbm.1, ...), custom_call_target="tpu_custom_call" | custom-call | flops 1572864 | bytes 3145728 | tf_op jit(solution)/shard_map/pallas_call | solution.py:109
  3.5 0.7 %collective-permute-start.1 = (bf16[64,128]{1,0:T(8,128)(2,1)S(1)}, bf16[64,128]{1,0:T(8,128)(2,1)S(1)}, u32[]{:S(2)}, u32[]{:S(2)}) collective-permute-start(bf16[64,128]{1,0:T(8,128)(2,1)S(1)} %get-tuple-element.31), channel_id=1, source_target_pairs={{8,16},{16,8},{9,17},{17,9},{10,18},{18,10},{11,19},{19,11},{12,20... | collective-permute-start | bytes 49160 | tf_op jit(solution)/shard_map/ppermute | solution.py:126
  4.1 2.9 %collective-permute-start = (bf16[64,128]{1,0:T(8,128)(2,1)S(1)}, bf16[64,128]{1,0:T(8,128)(2,1)S(1)}, u32[]{:S(2)}, u32[]{:S(2)}) collective-permute-start(bf16[64,128]{1,0:T(8,128)(2,1)S(1)} %get-tuple-element.31), channel_id=1, source_target_pairs={{0,8},{16,24},{8,0},{24,16},{1,9},{17,25},{9,1},{25,17},{2,10},{18... | collective-permute-start | bytes 49160 | tf_op jit(solution)/shard_map/ppermute | solution.py:126
  7.1 0.5 collective-permute-start.2
  7.6 4.4 %collective-permute-start.3 = (bf16[64,128]{1,0:T(8,128)(2,1)S(1)}, bf16[64,128]{1,0:T(8,128)(2,1)S(1)}, u32[]{:S(2)}, u32[]{:S(2)}) collective-permute-start(bf16[64,128]{1,0:T(8,128)(2,1)S(1)} %get-tuple-element.38), channel_id=1, source_target_pairs={{1,2},{3,4},{5,6},{2,1},{4,3},{6,5},{9,10},{11,12},{13,14},{10,9},... | collective-permute-start | bytes 49160 | tf_op jit(solution)/shard_map/ppermute | solution.py:126
  12.7 0.0 collective-permute-done.1.refs_5_
  12.7 0.0 collective-permute-done.refs_4_
  12.7 4.0 %shard_map.123 = (f32[6,8,32,128]{3,2,1,0:T(8,128)S(1)}, bf16[4,8,8,64,128]{4,3,2,1,0:T(8,128)(2,1)S(1)}, bf16[4,8,8,64,128]{4,3,2,1,0:T(8,128)(2,1)S(1)}, f32[6,7,32,128]{3,2,1,0:T(8,128)S(1)}) custom-call(f32[6,8,64,128]{3,2,1,0:T(8,128)S(1)} %get-tuple-element.27.refs_0_, f32[6,8,64,128]{3,2,1,0:T(8,128)S(1)} %get-tuple-element.28.refs_1_, ...), custom_call_target="tpu_custom_call" | custom-call | flops 12582912 | bytes 9437184 | tf_op jit(solution)/shard_map/pallas_call | solution.py:344
  16.7 0.0 collective-permute-done.2.refs_11_
  16.7 0.0 collective-permute-done.3.refs_12_
  16.7 0.0 copy-start.3
  16.7 0.0 copy-start.4
  16.7 2.3 %shard_map.124 = (f32[6,8,64,128]{3,2,1,0:T(8,128)S(1)}, bf16[512,768]{1,0:T(8,128)(2,1)S(1)}, f32[6,7,32,128]{3,2,1,0:T(8,128)S(1)}) custom-call(f32[6,8,64,128]{3,2,1,0:T(8,128)S(1)} %get-tuple-element.27.refs_0_, f32[6,8,64,128]{3,2,1,0:T(8,128)S(1)} %get-tuple-element.28.refs_1_, s32[64,128]{1,0:T(8,128)S(1)} %get-tuple-element.29.refs_2_.mask_ref, ...), custom_call_target="tpu_custom_call" | custom-call | flops 12582912 | bytes 9437184 | tf_op jit(solution)/shard_map/pallas_call | solution.py:344
  19.0 0.0 copy-done.3
  19.0 0.0 copy-start
  19.1 0.0 copy-start.1
  19.1 0.0 copy-start.2
  19.1 4.8 %shard_map.125 = (bf16[32,8,128]{2,1,0:T(8,128)(2,1)S(1)}, bf16[768,4096]{1,0:T(8,128)(2,1)S(1)}) custom-call(s32[1,1,32]{2,1,0:T(1,128)S(1)} %copy-done.4, s32[1,1]{1,0:T(1,128)S(6)} %copy.13.count_ref, s32[8,1,512]{2,1,0:T(1,128)S(1)} %bitcast.8, bf16[512,768]{1,0:T(8,128)(2,1)S(1)} %get-tuple-element.40.rounded_ref), custom_call_target="tpu_custom_call" | custom-call | flops 3221225472 | bytes 786432 | tf_op jit(solution)/shard_map/pallas_call | solution.py:410
  23.9 10.3 %all_to_all.10.picked_ref = bf16[32,8,128]{2,1,0:T(8,128)(2,1)S(1)} all-to-all(bf16[32,8,128]{2,1,0:T(8,128)(2,1)S(1)} %get-tuple-element.41), channel_id=1, replica_groups=mesh['gx'=4,'gy'=8] {'gx','gy'}, dimensions={0} | all-to-all | bytes 131072 | tf_op jit(solution)/shard_map/all_to_all | solution.py:553
  34.2 0.9 %shard_map.126 = bf16[32,16,128]{2,1,0:T(8,128)(2,1)S(1)} custom-call(bf16[32,8,8,128]{3,2,1,0:T(8,128)(2,1)S(1)} %bitcast.5, bf16[32,8,8,128]{3,2,1,0:T(8,128)(2,1)S(1)} %bitcast.6, bf16[32,8,128]{2,1,0:T(8,128)(2,1)S(1)} %bitcast.7, bf16[32,8,128]{2,1,0:T(8,128)(2,1)S(1)} %all_to_all.10.picked_ref), custom_call_target="tpu_custom_call" | custom-call | flops 1048576 | bytes 1048576 | tf_op jit(solution)/shard_map/pallas_call | solution.py:460
  35.1 9.9 %all_to_all.11.back_ref = bf16[32,16,128]{2,1,0:T(8,128)(2,1)S(1)} all-to-all(bf16[32,16,128]{2,1,0:T(8,128)(2,1)S(1)} %shard_map.126), channel_id=1, replica_groups=mesh['gx'=4,'gy'=8] {'gx','gy'}, dimensions={0} | all-to-all | bytes 262144 | tf_op jit(solution)/shard_map/all_to_all | solution.py:553
  44.9 4.7 %shard_map.127 = (f32[6,8,64,128]{3,2,1,0:T(8,128)S(1)}, f32[6,8,64,128]{3,2,1,0:T(8,128)S(1)}, bf16[64,128]{1,0:T(8,128)(2,1)S(1)}, bf16[64,128]{1,0:T(8,128)(2...) custom-call(s32[1,1,32]{2,1,0:T(1,128)S(1)} %copy-done.4, s32[2,1,2048]{2,1,0:T(1,128)S(1)} %bitcast.9, ...), custom_call_target="tpu_custom_call" | custom-call | flops 3221225472 | bytes 3145728 | tf_op jit(solution)/shard_map/pallas_call | solution.py:514
  49.6 0.7 %collective-permute-start.5 = (bf16[64,128]{1,0:T(8,128)(2,1)S(1)}, bf16[64,128]{1,0:T(8,128)(2,1)S(1)}, u32[]{:S(2)}, u32[]{:S(2)}) collective-permute-start(bf16[64,128]{1,0:T(8,128)(2,1)S(1)} %get-tuple-element.46), channel_id=1, source_target_pairs={{8,16},{16,8},{9,17},{17,9},{10,18},{18,10},{11,19},{19,11},{12,20... | collective-permute-start | bytes 49160 | tf_op jit(solution)/shard_map/ppermute | solution.py:126
  50.3 2.2 %collective-permute-start.4 = (bf16[64,128]{1,0:T(8,128)(2,1)S(1)}, bf16[64,128]{1,0:T(8,128)(2,1)S(1)}, u32[]{:S(2)}, u32[]{:S(2)}) collective-permute-start(bf16[64,128]{1,0:T(8,128)(2,1)S(1)} %get-tuple-element.46), channel_id=1, source_target_pairs={{0,8},{16,24},{8,0},{24,16},{1,9},{17,25},{9,1},{25,17},{2,10},{18... | collective-permute-start | bytes 49160 | tf_op jit(solution)/shard_map/ppermute | solution.py:126
  52.4 1.1 %collective-permute-start.6 = (bf16[64,128]{1,0:T(8,128)(2,1)S(1)}, bf16[64,128]{1,0:T(8,128)(2,1)S(1)}, u32[]{:S(2)}, u32[]{:S(2)}) collective-permute-start(bf16[64,128]{1,0:T(8,128)(2,1)S(1)} %get-tuple-element.48), channel_id=1, source_target_pairs={{0,1},{2,3},{4,5},{6,7},{1,0},{3,2},{5,4},{7,6},{8,9},{10,11},{12,... | collective-permute-start | bytes 49160 | tf_op jit(solution)/shard_map/ppermute | solution.py:126
  53.5 2.9 %collective-permute-start.7 = (bf16[64,128]{1,0:T(8,128)(2,1)S(1)}, bf16[64,128]{1,0:T(8,128)(2,1)S(1)}, u32[]{:S(2)}, u32[]{:S(2)}) collective-permute-start(bf16[64,128]{1,0:T(8,128)(2,1)S(1)} %get-tuple-element.49), channel_id=1, source_target_pairs={{1,2},{3,4},{5,6},{2,1},{4,3},{6,5},{9,10},{11,12},{13,14},{10,9},... | collective-permute-start | bytes 49160 | tf_op jit(solution)/shard_map/ppermute | solution.py:126
  56.4 0.0 collective-permute-done.5.refs_5_
  56.4 0.0 collective-permute-done.4.refs_4_
  56.5 1.8 %shard_map.128.refs_13_ = f32[6,8,32,128]{3,2,1,0:T(8,128)S(1)} custom-call(f32[6,8,64,128]{3,2,1,0:T(8,128)S(1)} %get-tuple-element.44.refs_0_, f32[6,8,64,128]{3,2,1,0:T(8,128)S(1)} %get-tuple-element.45.refs_1_, s32[64,128]{1,0:T(8,128)S(1)} %get-tuple-element.29.refs_2_.mask_ref, bf16[128,1024]{1,0:T(8,128)(2,1)S(1)} %get-tuple-element.30.refs_3_, ...), custom_call_target="tpu_custom_call" | custom-call | flops 12582912 | bytes 9437184 | tf_op jit(solution)/shard_map/pallas_call | solution.py:344
  58.3 0.0 collective-permute-done.6.refs_11_
  58.3 1.7 %collective-permute-done.7.refs_12_ = bf16[64,128]{1,0:T(8,128)(2,1)S(1)} collective-permute-done((bf16[64,128]{1,0:T(8,128)(2,1)S(1)}, bf16[64,128]{1,0:T(8,128)(2,1)S(1)}, u32[]{:S(2)}, u32[]{:S(2)}) %collective-permute-start.7) | collective-permute-done | bytes 16416 | tf_op jit(solution)/shard_map/ppermute | solution.py:126
  60.1 2.9 %shard_map.129 = f32[6,8,64,128]{3,2,1,0:T(8,128)} custom-call(f32[6,8,64,128]{3,2,1,0:T(8,128)S(1)} %get-tuple-element.44.refs_0_, f32[6,8,64,128]{3,2,1,0:T(8,128)S(1)} %get-tuple-element.45.refs_1_, s32[64,128]{1,0:T(8,128)S(1)} %get-tuple-element.29.refs_2_.mask_ref, bf16[128,1024]{1,0:T(8,128)(2,1)S(1)} %get-tuple-element.30.refs_3_, ...), custom_call_target="tpu_custom_call" | custom-call | flops 12582912 | bytes 9437184 | tf_op jit(solution)/shard_map/pallas_call | solution.py:344
  (4 shorter events, 0.0 us)
Async XLA Ops:
  3.5 9.2 %collective-permute-start.1 = (bf16[64,128]{1,0:T(8,128)(2,1)S(1)}, bf16[64,128]{1,0:T(8,128)(2,1)S(1)}, u32[]{:S(2)}, u32[]{:S(2)}) collective-permute-start(bf16[64,128]{1,0:T(8,128)(2,1)S(1)} %get-tuple-element.31), channel_id=1, source_target_pairs={{8,16},{16,8},{9,17},{17,9},{10,18},{18,10},{11,19},{19,11},{12,20... | collective-permute-start | bytes 49160 | tf_op jit(solution)/shard_map/ppermute | solution.py:126
  4.1 8.6 %collective-permute-start = (bf16[64,128]{1,0:T(8,128)(2,1)S(1)}, bf16[64,128]{1,0:T(8,128)(2,1)S(1)}, u32[]{:S(2)}, u32[]{:S(2)}) collective-permute-start(bf16[64,128]{1,0:T(8,128)(2,1)S(1)} %get-tuple-element.31), channel_id=1, source_target_pairs={{0,8},{16,24},{8,0},{24,16},{1,9},{17,25},{9,1},{25,17},{2,10},{18... | collective-permute-start | bytes 49160 | tf_op jit(solution)/shard_map/ppermute | solution.py:126
  7.1 9.6 %collective-permute-start.2 = (bf16[64,128]{1,0:T(8,128)(2,1)S(1)}, bf16[64,128]{1,0:T(8,128)(2,1)S(1)}, u32[]{:S(2)}, u32[]{:S(2)}) collective-permute-start(bf16[64,128]{1,0:T(8,128)(2,1)S(1)} %get-tuple-element.37), channel_id=1, source_target_pairs={{0,1},{2,3},{4,5},{6,7},{1,0},{3,2},{5,4},{7,6},{8,9},{10,11},{12,... | collective-permute-start | bytes 49160 | tf_op jit(solution)/shard_map/ppermute | solution.py:126
  7.6 9.1 %collective-permute-start.3 = (bf16[64,128]{1,0:T(8,128)(2,1)S(1)}, bf16[64,128]{1,0:T(8,128)(2,1)S(1)}, u32[]{:S(2)}, u32[]{:S(2)}) collective-permute-start(bf16[64,128]{1,0:T(8,128)(2,1)S(1)} %get-tuple-element.38), channel_id=1, source_target_pairs={{1,2},{3,4},{5,6},{2,1},{4,3},{6,5},{9,10},{11,12},{13,14},{10,9},... | collective-permute-start | bytes 49160 | tf_op jit(solution)/shard_map/ppermute | solution.py:126
  16.7 2.3 %copy-start.3 = (s32[1,1,4096]{2,1,0:T(1,128)S(1)}, s32[1,1,4096]{2,1,0:T(1,128)}, u32[]{:S(2)}) copy-start(s32[1,1,4096]{2,1,0:T(1,128)} %param.16) | copy-start | bytes 49156
  16.7 2.3 %copy-start.4 = (s32[1,1,32]{2,1,0:T(1,128)S(1)}, s32[1,1,32]{2,1,0:T(1,128)}, u32[]{:S(2)}) copy-start(s32[1,1,32]{2,1,0:T(1,128)} %helper_ref.3) | copy-start | bytes 388
  19.0 15.2 %copy-start = (bf16[1,1,32,8,8,128]{5,4,3,2,1,0:T(8,128)(2,1)S(1)}, bf16[1,1,32,8,8,128]{5,4,3,2,1,0:T(8,128)(2,1)}, u32[]{:S(2)}) copy-start(bf16[1,1,32,8,8,128]{5,4,3,2,1,0:T(8,128)(2,1)} %param.19) | copy-start | bytes 1572868
  19.1 15.1 %copy-start.1 = (bf16[1,1,32,8,8,128]{5,4,3,2,1,0:T(8,128)(2,1)S(1)}, bf16[1,1,32,8,8,128]{5,4,3,2,1,0:T(8,128)(2,1)}, u32[]{:S(2)}) copy-start(bf16[1,1,32,8,8,128]{5,4,3,2,1,0:T(8,128)(2,1)} %param.20) | copy-start | bytes 1572868
  19.1 15.1 %copy-start.2 = (bf16[1,1,32,8,128]{4,3,2,1,0:T(8,128)(2,1)S(1)}, bf16[1,1,32,8,128]{4,3,2,1,0:T(8,128)(2,1)}, u32[]{:S(2)}) copy-start(bf16[1,1,32,8,128]{4,3,2,1,0:T(8,128)(2,1)} %param.21) | copy-start | bytes 196612
  49.6 6.8 %collective-permute-start.5 = (bf16[64,128]{1,0:T(8,128)(2,1)S(1)}, bf16[64,128]{1,0:T(8,128)(2,1)S(1)}, u32[]{:S(2)}, u32[]{:S(2)}) collective-permute-start(bf16[64,128]{1,0:T(8,128)(2,1)S(1)} %get-tuple-element.46), channel_id=1, source_target_pairs={{8,16},{16,8},{9,17},{17,9},{10,18},{18,10},{11,19},{19,11},{12,20... | collective-permute-start | bytes 49160 | tf_op jit(solution)/shard_map/ppermute | solution.py:126
  50.3 6.2 %collective-permute-start.4 = (bf16[64,128]{1,0:T(8,128)(2,1)S(1)}, bf16[64,128]{1,0:T(8,128)(2,1)S(1)}, u32[]{:S(2)}, u32[]{:S(2)}) collective-permute-start(bf16[64,128]{1,0:T(8,128)(2,1)S(1)} %get-tuple-element.46), channel_id=1, source_target_pairs={{0,8},{16,24},{8,0},{24,16},{1,9},{17,25},{9,1},{25,17},{2,10},{18... | collective-permute-start | bytes 49160 | tf_op jit(solution)/shard_map/ppermute | solution.py:126
  52.4 5.9 %collective-permute-start.6 = (bf16[64,128]{1,0:T(8,128)(2,1)S(1)}, bf16[64,128]{1,0:T(8,128)(2,1)S(1)}, u32[]{:S(2)}, u32[]{:S(2)}) collective-permute-start(bf16[64,128]{1,0:T(8,128)(2,1)S(1)} %get-tuple-element.48), channel_id=1, source_target_pairs={{0,1},{2,3},{4,5},{6,7},{1,0},{3,2},{5,4},{7,6},{8,9},{10,11},{12,... | collective-permute-start | bytes 49160 | tf_op jit(solution)/shard_map/ppermute | solution.py:126
  53.5 6.5 %collective-permute-start.7 = (bf16[64,128]{1,0:T(8,128)(2,1)S(1)}, bf16[64,128]{1,0:T(8,128)(2,1)S(1)}, u32[]{:S(2)}, u32[]{:S(2)}) collective-permute-start(bf16[64,128]{1,0:T(8,128)(2,1)S(1)} %get-tuple-element.49), channel_id=1, source_target_pairs={{1,2},{3,4},{5,6},{2,1},{4,3},{6,5},{9,10},{11,12},{13,14},{10,9},... | collective-permute-start | bytes 49160 | tf_op jit(solution)/shard_map/ppermute | solution.py:126

commit v10 on v9

--- a/solution.py
+++ b/solution.py
@@ -65,21 +65,17 @@
 
 def opening_kernel(
     field_hbm, mask_hbm, perm_hbm, diag_hbm, flux_hbm,
-    send_y_0, send_y_1, send_x, masked_ref, field_ref, mask_ref, perm_ref, diag_ref, flux_ref, place_ref,
+    send_y_0, send_y_1, send_x, masked_ref, field_ref, mask_ref, perm_ref, place_ref,
     side_y, sems,
 ):
-    early = pl.ds(0, diag_ref.shape[0])
-    sources = (field_hbm, mask_hbm, perm_hbm, diag_hbm.at[early], flux_hbm.at[early])
-    targets = (field_ref, mask_ref, perm_ref, diag_ref, flux_ref)
+    sources, targets = (field_hbm, mask_hbm, perm_hbm), (field_ref, mask_ref, perm_ref)
     copies = [pltpu.make_async_copy(a, b, sems.at[i]) for i, (a, b) in enumerate(zip(sources, targets))]
     for copy in copies:
         copy.start()
     write_place(place_ref)
-    for copy in copies[:3]:
+    for copy in copies:
         copy.wait()
     write_edges(field_ref, mask_ref, perm_ref, masked_ref, side_y, (send_y_0, send_y_1, send_x))
-    for copy in copies[3:]:
-        copy.wait()
 
 
 def edge_rows(layers, comps):
@@ -95,26 +91,21 @@
     return pltpu.VMEM((2, edge_rows(layers, comps), cols), F32)
 
 
-def in_hbm(*arrays):
-    return [pltpu.with_memory_space_constraint(array, pltpu.HBM) for array in arrays]
-
-
-def opening(field, mask, perm, diag, flux, early):
+def opening(field, mask, perm, diag, flux):
     layers, comps, rows, cols = field.shape
     hbm = pl.BlockSpec(memory_space=pltpu.HBM)
     vmem = pl.BlockSpec(memory_space=pltpu.VMEM)
     kept = [(array.shape, array.dtype) for array in (field, field, mask, perm)]
-    kept += [((early, *block.shape[1:]), BF16) for block in (diag, flux)]
     kept.append(((cols, comps * cols), BF16))
     return pl.pallas_call(
         opening_kernel,
         in_specs=[hbm] * 5,
-        out_specs=[vmem] * 10,
+        out_specs=[vmem] * 8,
         out_shape=[*edge_shapes(*field.shape), *(pltpu.VMEM(*item) for item in kept)],
-        scratch_shapes=[edge_scratch(layers, comps, cols), pltpu.SemaphoreType.DMA((5,))],
+        scratch_shapes=[edge_scratch(layers, comps, cols), pltpu.SemaphoreType.DMA((3,))],
         compiler_params=params(16),
         cost_estimate=cost(4 * field.size, 8 * field.size),
-    )(*in_hbm(field, mask, perm, diag, flux))
+    )(*(pltpu.with_memory_space_constraint(array, pltpu.HBM) for array in (field, mask, perm, diag, flux)))
 
 
 def exchange(send_y_0, send_y_1, send_x):
@@ -130,7 +121,6 @@
 
 
 TILE = 16
-EARLY = 2
 WEIGHTS = 7
 
 
@@ -181,30 +171,22 @@
 
 
 def apply_kernel(is_first_apply, is_inner, *refs):
-    names = ["field", "masked", "mask", "place", "x_0", "x_1", "early_diag", "early_flux"]
-    names += ["diag_hbm", "flux_hbm"] if is_first_apply and is_inner else ["late_diag", "late_flux"]
+    names = ["field", "masked", "mask", "place", "x_0", "x_1", "diag", "flux"]
     names += ["perm"] if is_first_apply else ["weights"]
-    names += [] if is_inner else ["y_0", "y_1", "inner"]
+    names += [] if is_inner else ["y_0", "y_1", "inner", "begun"]
     names += ["out"] if is_inner or is_first_apply else ["out_hbm"]
+    names += ["begun"] if is_inner else []
     if is_first_apply:
-        names += ["late_diag", "late_flux"] if is_inner else ["rounded"]
+        names += [] if is_inner else ["rounded"]
         names += ["weights"]
     names += ["edge_x", "turned", "beside_x"]
-    names += ["sems"] if is_first_apply and is_inner else []
     names += [] if is_inner or is_first_apply else ["out", "sems"]
     ref = dict(zip(names, refs, strict=True))
     field_ref, masked_ref, edge_x, place = ref["field"], ref["masked"], ref["edge_x"], ref["place"]
     layers, comps, rows, cols = field_ref.shape
-    early = ref["early_diag"].shape[0]
-    inner_rows = rows - 2 * TILE
+    diag_ref, flux_ref = ref["diag"], ref["flux"]
     tiles = list(range(TILE, rows - TILE, TILE)) if is_inner else [0, rows - TILE]
     here_rows = len(tiles) * TILE
-
-    def blocks(i):
-        return [
-            pltpu.make_async_copy(ref[f"{name}_hbm"].at[early + i], ref[f"late_{name}"].at[i], ref["sems"].at[j, i])
-            for j, name in enumerate(("diag", "flux"))
-        ]
 
     def out_copies(k):
         middle = slice(TILE, rows - TILE)
@@ -213,11 +195,6 @@
             (ref["out"].at[k, :, j * TILE : (j + 1) * TILE], ref["out_hbm"].at[k, :, y : y + TILE]) for j, y in enumerate(tiles)
         ]
         return [pltpu.make_async_copy(a, b, ref["sems"].at[j, k]) for j, (a, b) in enumerate(pairs)]
-
-    if is_first_apply and is_inner:
-        for i in range(layers - early):
-            for copy in blocks(i):
-                copy.start()
 
     lane = lax.broadcasted_iota(jnp.int32, (rows, cols), 1)
     even_x = lax.axis_index("gx") % 2 == 0
@@ -230,8 +207,7 @@
             ref["turned"][start : start + TILE] = piece.astype(BF16)
     ref["beside_x"][...] = jnp.dot(ref["turned"][...], place[...], preferred_element_type=F32)
 
-    def layer(diag_ref, flux_ref, start, i, carry):
-        k = i + start
+    def layer(k, carry):
         above = jnp.minimum(k + 1, layers - 1)
         below = jnp.maximum(k - 1, 0)
         rows_y, perm_y = None, None
@@ -248,10 +224,6 @@
                 jnp.sum(jnp.where(mine, ref[name][here].astype(F32), 0.0), axis=0, keepdims=True) for name in ("y_0", "y_1")
             ]
             perm_y = (jnp.where(even_y, sides[1], sides[0]), jnp.where(even_y, sides[0], sides[1]))
-        if is_first_apply and is_inner and start > 0:
-            for copy in blocks(i):
-                copy.wait()
-
         for j, y in enumerate(tiles):
             here, local = slice(y, y + TILE), slice(j * TILE, (j + 1) * TILE)
             side_rows = pl.ds(pl.multiple_of(k * here_rows + j * TILE, TILE), TILE)
@@ -275,17 +247,29 @@
                     + weights[6] * ref["beside_x"][side_rows, r * cols : (r + 1) * cols]
                 )
                 for c in range(comps):
-                    term = diag_ref[i, r, c, here].astype(F32) * own - flux_ref[i, r, c, here].astype(F32) * summed
+                    term = -flux_ref[k, r, c, here].astype(F32) * summed
+                    if is_inner:
+                        term = diag_ref[k, r, c, here].astype(F32) * own + term
                     total[c] = term if r == 0 else total[c] + term
-            well = ref["mask"][here].astype(F32)
+            well = ref["mask"][here].astype(F32) if is_inner else None
             for c in range(comps):
-                value = total[c] + well * field_ref[k, c, here]
+                value = total[c] + (well * field_ref[k, c, here] if is_inner else ref["begun"][k, c, local])
                 if is_first_apply and not is_inner:
                     ref["out"][k, c, here] = value
                     columns = pl.ds(pl.multiple_of(k * cols, cols), cols)
                     ref["rounded"][c * rows + y : c * rows + y + TILE, columns] = value.astype(BF16)
                 else:
                     ref["out"][k, c, local] = value
+        for j, y in enumerate([0, rows - TILE] if is_inner else []):
+            here, local = slice(y, y + TILE), slice(j * TILE, (j + 1) * TILE)
+            well = ref["mask"][here].astype(F32)
+            total = [well * field_ref[k, c, here] for c in range(comps)]
+            for r in range(comps):
+                own = masked_ref[k, r, here]
+                for c in range(comps):
+                    total[c] += diag_ref[k, r, c, here].astype(F32) * own
+            for c in range(comps):
+                ref["begun"][k, c, local] = total[c]
         if is_first_apply and not is_inner:
             columns = pl.ds(pl.multiple_of(k * cols, cols), cols)
             for c in range(comps):
@@ -297,37 +281,32 @@
                 copy.start()
         return carry
 
-    unrolled(early, early, functools.partial(layer, ref["early_diag"], ref["early_flux"], 0))
-    unrolled(layers - early, 2, functools.partial(layer, ref["late_diag"], ref["late_flux"], early))
+    unrolled(layers, 2, layer)
     if not is_first_apply and not is_inner:
         for k in range(layers):
             for copy in out_copies(k):
                 copy.wait()
 
 
-def apply_rows(is_first_apply, is_inner, field, masked, mask, place, halos, early, late, third, inner=None):
+def apply_rows(is_first_apply, is_inner, field, masked, mask, place, halos, blocks, third, *inner):
     layers, comps, rows, cols = field.shape
     vmem = pl.BlockSpec(memory_space=pltpu.VMEM)
     hbm = pl.BlockSpec(memory_space=pltpu.HBM)
     here_rows = rows - 2 * TILE if is_inner else 2 * TILE
-    late_count = layers - early[0].shape[0]
     here = (layers, comps, here_rows, cols)
-    loads = is_first_apply and is_inner
-    late_spec = hbm if loads else vmem
-    arrays = [field, masked, mask, place, *halos[:2], *early, *(in_hbm(*late) if loads else late), third]
-    specs = [vmem] * 8 + [late_spec] * 2 + [vmem]
+    arrays = [field, masked, mask, place, *halos[:2], *blocks, third]
+    specs = [vmem] * 9
     if not is_inner:
-        arrays += [*halos[2:], inner]
-        specs += [vmem] * 3
+        arrays += [*halos[2:], *inner]
+        specs += [vmem] * 4
     if is_inner:
-        out_shape, out_specs = [pltpu.VMEM(here, F32)], [vmem]
+        begun = (layers, comps, 2 * TILE, cols)
+        out_shape, out_specs = [pltpu.VMEM(here, F32), pltpu.VMEM(begun, F32)], [vmem] * 2
     else:
         out_shape = [jax.ShapeDtypeStruct(field.shape, F32)]
         out_specs = [vmem if is_first_apply else hbm]
     if is_first_apply:
-        if is_inner:
-            out_shape += [pltpu.VMEM((late_count, *block.shape[1:]), BF16) for block in late]
-        else:
+        if not is_inner:
             out_shape.append(jax.ShapeDtypeStruct((comps * rows, layers * cols), BF16))
         out_shape.append(pltpu.VMEM((layers, WEIGHTS, here_rows, cols), F32))
         out_specs = [vmem] * len(out_shape)
@@ -336,8 +315,6 @@
         pltpu.VMEM((layers * here_rows, cols), BF16),
         pltpu.VMEM((layers * here_rows, comps * cols), F32),
     ]
-    if loads:
-        scratch.append(pltpu.SemaphoreType.DMA((2, late_count)))
     if not is_first_apply and not is_inner:
         scratch += [pltpu.VMEM(here, F32), pltpu.SemaphoreType.DMA((3, layers))]
     size = layers * comps * comps * here_rows * cols
@@ -541,10 +518,10 @@
     phase_state,
 ):
     layers, comps, rows, cols = cotangent.shape
-    blocks, width = helper_of.shape[-1], flash_inverse.shape[-1]
-    inverse = flash_inverse.reshape(blocks, comps, comps, width)
-    coupling = flash_coupling.reshape(blocks, comps, comps, width)
-    state = phase_state.reshape(blocks, comps, width)
+    slots, width = helper_of.shape[-1], flash_inverse.shape[-1]
+    inverse = flash_inverse.reshape(slots, comps, comps, width)
+    coupling = flash_coupling.reshape(slots, comps, comps, width)
+    state = phase_state.reshape(slots, comps, width)
 
     def cells(chunk):
         return cell_list.reshape(-1, 1, min(chunk, cell_list.shape[-1]))
@@ -552,15 +529,13 @@
     def to_partners(array):
         return lax.all_to_all(array, AXES, split_axis=0, concat_axis=0, tiled=True)
 
-    *sides, masked, field, mask, perm, early_diag, early_flux, place = opening(
-        cotangent, well_mask, permeability, diag_block, flux_block, min(EARLY, layers - 1)
+    *sides, masked, field, mask, perm, place = opening(cotangent, well_mask, permeability, diag_block, flux_block)
+    halos = exchange(*sides)
+    blocks = [pltpu.with_memory_space_constraint(block, pltpu.VMEM) for block in (diag_block, flux_block)]
+    inner, begun, inner_weights = apply_rows(True, True, field, masked, mask, place, halos, blocks, perm)
+    first, rounded, outer_weights = apply_rows(
+        True, False, field, masked, mask, place, halos, blocks, perm, inner, begun
     )
-    early = (early_diag, early_flux)
-    halos = exchange(*sides)
-    inner, *late, inner_weights = apply_rows(
-        True, True, field, masked, mask, place, halos, early, (diag_block, flux_block), perm
-    )
-    first, rounded, outer_weights = apply_rows(True, False, field, masked, mask, place, halos, early, late, perm, inner)
     sent, *chosen = gather(rounded, cells(GATHER_CHUNK), helper_of, block_count, comps, rows, cols, width)
     reply = at_helper(inverse, coupling, state, to_partners(sent))
     devices = lax.axis_size("gx") * lax.axis_size("gy")
@@ -569,8 +544,8 @@
         first, to_partners(reply), helper_of, cells(SCATTER_CHUNK), mask, chosen, scale
     )
     halos = exchange(*sides)
-    (inner,) = apply_rows(False, True, second, masked, mask, place, halos, early, late, inner_weights)
-    (adjoint,) = apply_rows(False, False, second, masked, mask, place, halos, early, late, outer_weights, inner)
+    inner, begun = apply_rows(False, True, second, masked, mask, place, halos, blocks, inner_weights)
+    (adjoint,) = apply_rows(False, False, second, masked, mask, place, halos, blocks, outer_weights, inner, begun)
     return (adjoint, interaction_grad)
 
 

time: 63.3 us -> 60.9 us (0.962)
  the two profiles are of different devices: /device:TPU:2 before, /device:TPU:9 now
where the time goes in v10:
time: 60.9 us; the launch traced here: 59.9 us
  Pallas kernels  22.5 us (37%)
  blocking collectives  21.1 us (35%)
  starting transfers between devices  14.7 us (24%)
  between operations  1.53 us (3%)
    all_to_all x2, blocking collectives, to_partners(): return lax.all_to_all(array, AXES, split_axis=0, concat_axis=0, tiled=True)  21.1 us
    ppermute x8, starting transfers between devices, swaps(): lax.ppermute(array, axis, pairs + [(j, i) for i, j in pairs])  14.7 us
    pallas_call x4, Pallas kernels, apply_rows(): pl.pallas_call(functools.partial(apply_kernel, is_first_apply, is_inner),...  10.2 us
    pallas_call x1, Pallas kernels, gather(): pl.pallas_call(functools.partial(gather_kernel, rows, cols), in_specs=[sm...  4.87 us
    pallas_call x1, Pallas kernels, scatter(): pl.pallas_call(functools.partial(scatter_kernel, scale, len(kept)), in_sp...  4.65 us
    pallas_call x1, Pallas kernels, opening(): pl.pallas_call(opening_kernel, in_specs=[hbm] * 5, out_specs=[vmem] * 8,...  1.97 us
  transfers between devices with their start and end apart: 8, of which 0 were waited for; matrix products, arithmetic and copies ran while one was open for 0% of the time, Pallas kernels for 10%

profile of v10, /device:TPU:9, one launch (start us, length us, event | category | flops | bytes accessed | tf_op | source)
XLA Modules:
  0.0 59.9 jit_solution(17008145561887724925)
XLA Ops:
  0.7 2.0 %shard_map.122 = (bf16[64,128]{1,0:T(8,128)(2,1)S(1)}, bf16[64,128]{1,0:T(8,128)(2,1)S(1)}, bf16[64,128]{1,0:T(8,128)(2,1)S(1)}, f32[6,8,64,128]{3,2,1,0:T(8,128...) custom-call(f32[6,8,64,128]{3,2,1,0:T(8,128)} %field_hbm.1, ...), custom_call_target="tpu_custom_call" | custom-call | flops 1572864 | bytes 3145728 | tf_op jit(solution)/shard_map/pallas_call | solution.py:100
  2.6 4.0 %collective-permute-start.1 = (bf16[64,128]{1,0:T(8,128)(2,1)S(1)}, bf16[64,128]{1,0:T(8,128)(2,1)S(1)}, u32[]{:S(2)}, u32[]{:S(2)}) collective-permute-start(bf16[64,128]{1,0:T(8,128)(2,1)S(1)} %get-tuple-element.30), channel_id=1, source_target_pairs={{8,16},{16,8},{9,17},{17,9},{10,18},{18,10},{11,19},{19,11},{12,20... | collective-permute-start | bytes 49160 | tf_op jit(solution)/shard_map/ppermute | solution.py:117
  6.6 0.1 collective-permute-start
  6.7 1.3 %collective-permute-start.2 = (bf16[64,128]{1,0:T(8,128)(2,1)S(1)}, bf16[64,128]{1,0:T(8,128)(2,1)S(1)}, u32[]{:S(2)}, u32[]{:S(2)}) collective-permute-start(bf16[64,128]{1,0:T(8,128)(2,1)S(1)} %get-tuple-element.32), channel_id=1, source_target_pairs={{0,1},{2,3},{4,5},{6,7},{1,0},{3,2},{5,4},{7,6},{8,9},{10,11},{12,... | collective-permute-start | bytes 49160 | tf_op jit(solution)/shard_map/ppermute | solution.py:117
  8.0 2.0 %collective-permute-start.3 = (bf16[64,128]{1,0:T(8,128)(2,1)S(1)}, bf16[64,128]{1,0:T(8,128)(2,1)S(1)}, u32[]{:S(2)}, u32[]{:S(2)}) collective-permute-start(bf16[64,128]{1,0:T(8,128)(2,1)S(1)} %get-tuple-element.33), channel_id=1, source_target_pairs={{1,2},{3,4},{5,6},{2,1},{4,3},{6,5},{9,10},{11,12},{13,14},{10,9},... | collective-permute-start | bytes 49160 | tf_op jit(solution)/shard_map/ppermute | solution.py:117
  10.7 0.0 collective-permute-done.1.refs_5_
  10.7 0.0 collective-permute-done.refs_4_
  10.7 3.0 %shard_map.123 = (f32[6,8,32,128]{3,2,1,0:T(8,128)S(1)}, f32[6,8,32,128]{3,2,1,0:T(8,128)S(1)}, f32[6,7,32,128]{3,2,1,0:T(8,128)S(1)}) custom-call(f32[6,8,64,128]{3,2,1,0:T(8,128)S(1)} %get-tuple-element.26.refs_0_, f32[6,8,64,128]{3,2,1,0:T(8,128)S(1)} %get-tuple-element.27.refs_1_, s32[64,128]{1,0:T(8,128)S(1)} %get-tuple-element.28.refs_2_.mask_ref, ...), custom_call_target="tpu_custom_call" | custom-call | flops 12582912 | bytes 9437184 | tf_op jit(solution)/shard_map/pallas_call | solution.py:321
  13.7 0.0 collective-permute-done.2.refs_9_
  13.7 0.0 collective-permute-done.3.refs_10_
  13.7 0.0 copy-start.5
  13.8 0.0 copy-start.6
  13.8 1.9 %shard_map.124 = (f32[6,8,64,128]{3,2,1,0:T(8,128)S(1)}, bf16[512,768]{1,0:T(8,128)(2,1)S(1)}, f32[6,7,32,128]{3,2,1,0:T(8,128)S(1)}) custom-call(f32[6,8,64,128]{3,2,1,0:T(8,128)S(1)} %get-tuple-element.26.refs_0_, f32[6,8,64,128]{3,2,1,0:T(8,128)S(1)} %get-tuple-element.27.refs_1_, s32[64,128]{1,0:T(8,128)S(1)} %get-tuple-element.28.refs_2_.mask_ref, ...), custom_call_target="tpu_custom_call" | custom-call | flops 12582912 | bytes 9437184 | tf_op jit(solution)/shard_map/pallas_call | solution.py:321
  15.7 0.0 copy-done.5
  15.7 0.0 copy-start.2
  15.8 0.0 copy-start.3
  15.8 0.0 copy-start.4
  15.8 4.9 %shard_map.125 = (bf16[32,8,128]{2,1,0:T(8,128)(2,1)S(1)}, bf16[768,4096]{1,0:T(8,128)(2,1)S(1)}) custom-call(s32[1,1,32]{2,1,0:T(1,128)S(1)} %copy-done.6, s32[1,1]{1,0:T(1,128)S(6)} %copy.13.count_ref, s32[8,1,512]{2,1,0:T(1,128)S(1)} %bitcast.8, bf16[512,768]{1,0:T(8,128)(2,1)S(1)} %get-tuple-element.36.rounded_ref), custom_call_target="tpu_custom_call" | custom-call | flops 3221225472 | bytes 786432 | tf_op jit(solution)/shard_map/pallas_call | solution.py:387
  20.7 11.5 %all_to_all.10.picked_ref = bf16[32,8,128]{2,1,0:T(8,128)(2,1)S(1)} all-to-all(bf16[32,8,128]{2,1,0:T(8,128)(2,1)S(1)} %get-tuple-element.37), channel_id=1, replica_groups=mesh['gx'=4,'gy'=8] {'gx','gy'}, dimensions={0} | all-to-all | bytes 131072 | tf_op jit(solution)/shard_map/all_to_all | solution.py:530
  32.2 0.9 %shard_map.126 = bf16[32,16,128]{2,1,0:T(8,128)(2,1)S(1)} custom-call(bf16[32,8,8,128]{3,2,1,0:T(8,128)(2,1)S(1)} %bitcast.5, bf16[32,8,8,128]{3,2,1,0:T(8,128)(2,1)S(1)} %bitcast.6, bf16[32,8,128]{2,1,0:T(8,128)(2,1)S(1)} %bitcast.7, bf16[32,8,128]{2,1,0:T(8,128)(2,1)S(1)} %all_to_all.10.picked_ref), custom_call_target="tpu_custom_call" | custom-call | flops 1048576 | bytes 1048576 | tf_op jit(solution)/shard_map/pallas_call | solution.py:437
  33.1 9.6 %all_to_all.11.back_ref = bf16[32,16,128]{2,1,0:T(8,128)(2,1)S(1)} all-to-all(bf16[32,16,128]{2,1,0:T(8,128)(2,1)S(1)} %shard_map.126), channel_id=1, replica_groups=mesh['gx'=4,'gy'=8] {'gx','gy'}, dimensions={0} | all-to-all | bytes 262144 | tf_op jit(solution)/shard_map/all_to_all | solution.py:530
  42.6 4.7 %shard_map.127 = (f32[6,8,64,128]{3,2,1,0:T(8,128)S(1)}, f32[6,8,64,128]{3,2,1,0:T(8,128)S(1)}, bf16[64,128]{1,0:T(8,128)(2,1)S(1)}, bf16[64,128]{1,0:T(8,128)(2...) custom-call(s32[1,1,32]{2,1,0:T(1,128)S(1)} %copy-done.6, s32[2,1,2048]{2,1,0:T(1,128)S(1)} %bitcast.9, ...), custom_call_target="tpu_custom_call" | custom-call | flops 3221225472 | bytes 3145728 | tf_op jit(solution)/shard_map/pallas_call | solution.py:491
  47.3 2.9 %collective-permute-start.5 = (bf16[64,128]{1,0:T(8,128)(2,1)S(1)}, bf16[64,128]{1,0:T(8,128)(2,1)S(1)}, u32[]{:S(2)}, u32[]{:S(2)}) collective-permute-start(bf16[64,128]{1,0:T(8,128)(2,1)S(1)} %get-tuple-element.42), channel_id=1, source_target_pairs={{8,16},{16,8},{9,17},{17,9},{10,18},{18,10},{11,19},{19,11},{12,20... | collective-permute-start | bytes 49160 | tf_op jit(solution)/shard_map/ppermute | solution.py:117
  50.2 0.1 collective-permute-start.4
  50.3 0.7 %collective-permute-start.6 = (bf16[64,128]{1,0:T(8,128)(2,1)S(1)}, bf16[64,128]{1,0:T(8,128)(2,1)S(1)}, u32[]{:S(2)}, u32[]{:S(2)}) collective-permute-start(bf16[64,128]{1,0:T(8,128)(2,1)S(1)} %get-tuple-element.44), channel_id=1, source_target_pairs={{0,1},{2,3},{4,5},{6,7},{1,0},{3,2},{5,4},{7,6},{8,9},{10,11},{12,... | collective-permute-start | bytes 49160 | tf_op jit(solution)/shard_map/ppermute | solution.py:117
  50.9 3.7 %collective-permute-start.7 = (bf16[64,128]{1,0:T(8,128)(2,1)S(1)}, bf16[64,128]{1,0:T(8,128)(2,1)S(1)}, u32[]{:S(2)}, u32[]{:S(2)}) collective-permute-start(bf16[64,128]{1,0:T(8,128)(2,1)S(1)} %get-tuple-element.45), channel_id=1, source_target_pairs={{1,2},{3,4},{5,6},{2,1},{4,3},{6,5},{9,10},{11,12},{13,14},{10,9},... | collective-permute-start | bytes 49160 | tf_op jit(solution)/shard_map/ppermute | solution.py:117
  54.7 0.0 collective-permute-done.5.refs_5_
  54.7 0.0 collective-permute-done.4.refs_4_
  54.7 2.8 %shard_map.128 = (f32[6,8,32,128]{3,2,1,0:T(8,128)S(1)}, f32[6,8,32,128]{3,2,1,0:T(8,128)S(1)}) custom-call(f32[6,8,64,128]{3,2,1,0:T(8,128)S(1)} %get-tuple-element.40.refs_0_, f32[6,8,64,128]{3,2,1,0:T(8,128)S(1)} %get-tuple-element.41.refs_1_, s32[64,128]{1,0:T(8,128)S(1)} %get-tuple-element.28.refs_2_.mask_ref, ...), custom_call_target="tpu_custom_call" | custom-call | flops 12582912 | bytes 9437184 | tf_op jit(solution)/shard_map/pallas_call | solution.py:321
  57.5 0.0 collective-permute-done.6.refs_9_
  57.5 0.0 collective-permute-done.7.refs_10_
  57.5 2.4 %shard_map.129 = f32[6,8,64,128]{3,2,1,0:T(8,128)} custom-call(f32[6,8,64,128]{3,2,1,0:T(8,128)S(1)} %get-tuple-element.40.refs_0_, f32[6,8,64,128]{3,2,1,0:T(8,128)S(1)} %get-tuple-element.41.refs_1_, s32[64,128]{1,0:T(8,128)S(1)} %get-tuple-element.28.refs_2_.mask_ref, bf16[128,1024]{1,0:T(8,128)(2,1)S(1)} %get-tuple-element.29.refs_3_, ...), custom_call_target="tpu_custom_call" | custom-call | flops 12582912 | bytes 9437184 | tf_op jit(solution)/shard_map/pallas_call | solution.py:321
  (8 shorter events, 0.0 us)
Async XLA Ops:
  0.6 10.1 %copy-start = (bf16[6,8,8,64,128]{4,3,2,1,0:T(8,128)(2,1)S(1)}, bf16[6,8,8,64,128]{4,3,2,1,0:T(8,128)(2,1)}, u32[]{:S(2)}) copy-start(bf16[6,8,8,64,128]{4,3,2,1,0:T(8,128)(2,1)} %refs_6_.7) | copy-start | bytes 18874372
  0.6 10.1 %copy-start.1 = (bf16[6,8,8,64,128]{4,3,2,1,0:T(8,128)(2,1)S(1)}, bf16[6,8,8,64,128]{4,3,2,1,0:T(8,128)(2,1)}, u32[]{:S(2)}) copy-start(bf16[6,8,8,64,128]{4,3,2,1,0:T(8,128)(2,1)} %refs_7_.7) | copy-start | bytes 18874372
  2.6 8.0 %collective-permute-start.1 = (bf16[64,128]{1,0:T(8,128)(2,1)S(1)}, bf16[64,128]{1,0:T(8,128)(2,1)S(1)}, u32[]{:S(2)}, u32[]{:S(2)}) collective-permute-start(bf16[64,128]{1,0:T(8,128)(2,1)S(1)} %get-tuple-element.30), channel_id=1, source_target_pairs={{8,16},{16,8},{9,17},{17,9},{10,18},{18,10},{11,19},{19,11},{12,20... | collective-permute-start | bytes 49160 | tf_op jit(solution)/shard_map/ppermute | solution.py:117
  6.6 4.1 %collective-permute-start = (bf16[64,128]{1,0:T(8,128)(2,1)S(1)}, bf16[64,128]{1,0:T(8,128)(2,1)S(1)}, u32[]{:S(2)}, u32[]{:S(2)}) collective-permute-start(bf16[64,128]{1,0:T(8,128)(2,1)S(1)} %get-tuple-element.30), channel_id=1, source_target_pairs={{0,8},{16,24},{8,0},{24,16},{1,9},{17,25},{9,1},{25,17},{2,10},{18... | collective-permute-start | bytes 49160 | tf_op jit(solution)/shard_map/ppermute | solution.py:117
  6.7 7.0 %collective-permute-start.2 = (bf16[64,128]{1,0:T(8,128)(2,1)S(1)}, bf16[64,128]{1,0:T(8,128)(2,1)S(1)}, u32[]{:S(2)}, u32[]{:S(2)}) collective-permute-start(bf16[64,128]{1,0:T(8,128)(2,1)S(1)} %get-tuple-element.32), channel_id=1, source_target_pairs={{0,1},{2,3},{4,5},{6,7},{1,0},{3,2},{5,4},{7,6},{8,9},{10,11},{12,... | collective-permute-start | bytes 49160 | tf_op jit(solution)/shard_map/ppermute | solution.py:117
  8.0 5.8 %collective-permute-start.3 = (bf16[64,128]{1,0:T(8,128)(2,1)S(1)}, bf16[64,128]{1,0:T(8,128)(2,1)S(1)}, u32[]{:S(2)}, u32[]{:S(2)}) collective-permute-start(bf16[64,128]{1,0:T(8,128)(2,1)S(1)} %get-tuple-element.33), channel_id=1, source_target_pairs={{1,2},{3,4},{5,6},{2,1},{4,3},{6,5},{9,10},{11,12},{13,14},{10,9},... | collective-permute-start | bytes 49160 | tf_op jit(solution)/shard_map/ppermute | solution.py:117
  13.7 2.0 %copy-start.5 = (s32[1,1,4096]{2,1,0:T(1,128)S(1)}, s32[1,1,4096]{2,1,0:T(1,128)}, u32[]{:S(2)}) copy-start(s32[1,1,4096]{2,1,0:T(1,128)} %param.16) | copy-start | bytes 49156
  13.8 2.0 %copy-start.6 = (s32[1,1,32]{2,1,0:T(1,128)S(1)}, s32[1,1,32]{2,1,0:T(1,128)}, u32[]{:S(2)}) copy-start(s32[1,1,32]{2,1,0:T(1,128)} %helper_ref.3) | copy-start | bytes 388
  15.7 16.5 %copy-start.2 = (bf16[1,1,32,8,8,128]{5,4,3,2,1,0:T(8,128)(2,1)S(1)}, bf16[1,1,32,8,8,128]{5,4,3,2,1,0:T(8,128)(2,1)}, u32[]{:S(2)}) copy-start(bf16[1,1,32,8,8,128]{5,4,3,2,1,0:T(8,128)(2,1)} %param.19) | copy-start | bytes 1572868
  15.8 16.5 %copy-start.3 = (bf16[1,1,32,8,8,128]{5,4,3,2,1,0:T(8,128)(2,1)S(1)}, bf16[1,1,32,8,8,128]{5,4,3,2,1,0:T(8,128)(2,1)}, u32[]{:S(2)}) copy-start(bf16[1,1,32,8,8,128]{5,4,3,2,1,0:T(8,128)(2,1)} %param.20) | copy-start | bytes 1572868
  15.8 16.4 %copy-start.4 = (bf16[1,1,32,8,128]{4,3,2,1,0:T(8,128)(2,1)S(1)}, bf16[1,1,32,8,128]{4,3,2,1,0:T(8,128)(2,1)}, u32[]{:S(2)}) copy-start(bf16[1,1,32,8,128]{4,3,2,1,0:T(8,128)(2,1)} %param.21) | copy-start | bytes 196612
  47.3 7.4 %collective-permute-start.5 = (bf16[64,128]{1,0:T(8,128)(2,1)S(1)}, bf16[64,128]{1,0:T(8,128)(2,1)S(1)}, u32[]{:S(2)}, u32[]{:S(2)}) collective-permute-start(bf16[64,128]{1,0:T(8,128)(2,1)S(1)} %get-tuple-element.42), channel_id=1, source_target_pairs={{8,16},{16,8},{9,17},{17,9},{10,18},{18,10},{11,19},{19,11},{12,20... | collective-permute-start | bytes 49160 | tf_op jit(solution)/shard_map/ppermute | solution.py:117
  50.2 4.5 %collective-permute-start.4 = (bf16[64,128]{1,0:T(8,128)(2,1)S(1)}, bf16[64,128]{1,0:T(8,128)(2,1)S(1)}, u32[]{:S(2)}, u32[]{:S(2)}) collective-permute-start(bf16[64,128]{1,0:T(8,128)(2,1)S(1)} %get-tuple-element.42), channel_id=1, source_target_pairs={{0,8},{16,24},{8,0},{24,16},{1,9},{17,25},{9,1},{25,17},{2,10},{18... | collective-permute-start | bytes 49160 | tf_op jit(solution)/shard_map/ppermute | solution.py:117
  50.3 7.2 %collective-permute-start.6 = (bf16[64,128]{1,0:T(8,128)(2,1)S(1)}, bf16[64,128]{1,0:T(8,128)(2,1)S(1)}, u32[]{:S(2)}, u32[]{:S(2)}) collective-permute-start(bf16[64,128]{1,0:T(8,128)(2,1)S(1)} %get-tuple-element.44), channel_id=1, source_target_pairs={{0,1},{2,3},{4,5},{6,7},{1,0},{3,2},{5,4},{7,6},{8,9},{10,11},{12,... | collective-permute-start | bytes 49160 | tf_op jit(solution)/shard_map/ppermute | solution.py:117
  50.9 6.6 %collective-permute-start.7 = (bf16[64,128]{1,0:T(8,128)(2,1)S(1)}, bf16[64,128]{1,0:T(8,128)(2,1)S(1)}, u32[]{:S(2)}, u32[]{:S(2)}) collective-permute-start(bf16[64,128]{1,0:T(8,128)(2,1)S(1)} %get-tuple-element.45), channel_id=1, source_target_pairs={{1,2},{3,4},{5,6},{2,1},{4,3},{6,5},{9,10},{11,12},{13,14},{10,9},... | collective-permute-start | bytes 49160 | tf_op jit(solution)/shard_map/ppermute | solution.py:117

commit v11 on v10

--- a/solution.py
+++ b/solution.py
@@ -28,7 +28,7 @@
     return -(-number // step) * step
 
 
-def write_edges(field_ref, mask_ref, perm_ref, masked_ref, side_y, sends):
+def write_edges(field_ref, mask_ref, perm_ref, masked_ref, side_y, sends, ready=lambda k: None):
     send_y_0, send_y_1, send_x = sends
     layers, comps, rows, cols = field_ref.shape
     with_perm = perm_ref is not None
@@ -38,6 +38,7 @@
     along_x = jnp.zeros((rows, cols), F32)
     side_y[...] = jnp.zeros_like(side_y)
     for k in range(layers):
+        ready(k)
         for c in range(comps + with_perm):
             if c < comps:
                 value, at = field_ref[k, c] * clear, k * comps + c
@@ -68,14 +69,17 @@
     send_y_0, send_y_1, send_x, masked_ref, field_ref, mask_ref, perm_ref, place_ref,
     side_y, sems,
 ):
-    sources, targets = (field_hbm, mask_hbm, perm_hbm), (field_ref, mask_ref, perm_ref)
-    copies = [pltpu.make_async_copy(a, b, sems.at[i]) for i, (a, b) in enumerate(zip(sources, targets))]
+    layers = field_ref.shape[0]
+    pairs = [(mask_hbm, mask_ref), (perm_hbm, perm_ref)]
+    pairs += [(field_hbm.at[k], field_ref.at[k]) for k in range(layers)]
+    copies = [pltpu.make_async_copy(a, b, sems.at[i]) for i, (a, b) in enumerate(pairs)]
     for copy in copies:
         copy.start()
     write_place(place_ref)
-    for copy in copies:
+    for copy in copies[:2]:
         copy.wait()
-    write_edges(field_ref, mask_ref, perm_ref, masked_ref, side_y, (send_y_0, send_y_1, send_x))
+    sends = (send_y_0, send_y_1, send_x)
+    write_edges(field_ref, mask_ref, perm_ref, masked_ref, side_y, sends, lambda k: copies[2 + k].wait())
 
 
 def edge_rows(layers, comps):
@@ -102,7 +106,7 @@
         in_specs=[hbm] * 5,
         out_specs=[vmem] * 8,
         out_shape=[*edge_shapes(*field.shape), *(pltpu.VMEM(*item) for item in kept)],
-        scratch_shapes=[edge_scratch(layers, comps, cols), pltpu.SemaphoreType.DMA((3,))],
+        scratch_shapes=[edge_scratch(layers, comps, cols), pltpu.SemaphoreType.DMA((2 + layers,))],
         compiler_params=params(16),
         cost_estimate=cost(4 * field.size, 8 * field.size),
     )(*(pltpu.with_memory_space_constraint(array, pltpu.HBM) for array in (field, mask, perm, diag, flux)))
@@ -171,7 +175,7 @@
 
 
 def apply_kernel(is_first_apply, is_inner, *refs):
-    names = ["field", "masked", "mask", "place", "x_0", "x_1", "diag", "flux"]
+    names = ["field", "masked", "mask", "place", "x_1", "x_0", "diag", "flux"]
     names += ["perm"] if is_first_apply else ["weights"]
     names += [] if is_inner else ["y_0", "y_1", "inner", "begun"]
     names += ["out"] if is_inner or is_first_apply else ["out_hbm"]
@@ -294,7 +298,7 @@
     hbm = pl.BlockSpec(memory_space=pltpu.HBM)
     here_rows = rows - 2 * TILE if is_inner else 2 * TILE
     here = (layers, comps, here_rows, cols)
-    arrays = [field, masked, mask, place, *halos[:2], *blocks, third]
+    arrays = [field, masked, mask, place, halos[1], halos[0], *blocks, third]
     specs = [vmem] * 9
     if not is_inner:
         arrays += [*halos[2:], *inner]

time: 60.9 us -> 60.5 us (level)
  no operation moved by 1% of the time
where the time goes in v11:
time: 60.5 us; the launch traced here: 60 us
  Pallas kernels  22.7 us (38%)
  blocking collectives  21.1 us (35%)
  starting transfers between devices  14.6 us (24%)
  between operations  1.51 us (2%)
    all_to_all x2, blocking collectives, to_partners(): return lax.all_to_all(array, AXES, split_axis=0, concat_axis=0, tiled=True)  21.1 us
    ppermute x8, starting transfers between devices, swaps(): lax.ppermute(array, axis, pairs + [(j, i) for i, j in pairs])  14.6 us
    pallas_call x4, Pallas kernels, apply_rows(): pl.pallas_call(functools.partial(apply_kernel, is_first_apply, is_inner),...  10.2 us
    pallas_call x1, Pallas kernels, gather(): pl.pallas_call(functools.partial(gather_kernel, rows, cols), in_specs=[sm...  4.87 us
    pallas_call x1, Pallas kernels, scatter(): pl.pallas_call(functools.partial(scatter_kernel, scale, len(kept)), in_sp...  4.66 us
    pallas_call x1, Pallas kernels, opening(): pl.pallas_call(opening_kernel, in_specs=[hbm] * 5, out_specs=[vmem] * 8,...  2.14 us
  transfers between devices with their start and end apart: 8, of which 0 were waited for; matrix products, arithmetic and copies ran while one was open for 0% of the time, Pallas kernels for 10%

profile of v11, /device:TPU:9, one launch (start us, length us, event | category | flops | bytes accessed | tf_op | source)
XLA Modules:
  0.0 60.0 jit_solution(5152619755806378214)
XLA Ops:
  0.7 2.1 %shard_map.122 = (bf16[64,128]{1,0:T(8,128)(2,1)S(1)}, bf16[64,128]{1,0:T(8,128)(2,1)S(1)}, bf16[64,128]{1,0:T(8,128)(2,1)S(1)}, f32[6,8,64,128]{3,2,1,0:T(8,128...) custom-call(f32[6,8,64,128]{3,2,1,0:T(8,128)} %field_hbm.1, ...), custom_call_target="tpu_custom_call" | custom-call | flops 1572864 | bytes 3145728 | tf_op jit(solution)/shard_map/pallas_call | solution.py:104
  2.8 0.7 %collective-permute-start.1 = (bf16[64,128]{1,0:T(8,128)(2,1)S(1)}, bf16[64,128]{1,0:T(8,128)(2,1)S(1)}, u32[]{:S(2)}, u32[]{:S(2)}) collective-permute-start(bf16[64,128]{1,0:T(8,128)(2,1)S(1)} %get-tuple-element.30), channel_id=1, source_target_pairs={{0,8},{16,24},{8,0},{24,16},{1,9},{17,25},{9,1},{25,17},{2,10},{18... | collective-permute-start | bytes 49160 | tf_op jit(solution)/shard_map/ppermute | solution.py:121
  3.5 3.3 %collective-permute-start = (bf16[64,128]{1,0:T(8,128)(2,1)S(1)}, bf16[64,128]{1,0:T(8,128)(2,1)S(1)}, u32[]{:S(2)}, u32[]{:S(2)}) collective-permute-start(bf16[64,128]{1,0:T(8,128)(2,1)S(1)} %get-tuple-element.30), channel_id=1, source_target_pairs={{8,16},{16,8},{9,17},{17,9},{10,18},{18,10},{11,19},{19,11},{12,20... | collective-permute-start | bytes 49160 | tf_op jit(solution)/shard_map/ppermute | solution.py:121
  6.9 1.3 %collective-permute-start.2 = (bf16[64,128]{1,0:T(8,128)(2,1)S(1)}, bf16[64,128]{1,0:T(8,128)(2,1)S(1)}, u32[]{:S(2)}, u32[]{:S(2)}) collective-permute-start(bf16[64,128]{1,0:T(8,128)(2,1)S(1)} %get-tuple-element.32), channel_id=1, source_target_pairs={{0,1},{2,3},{4,5},{6,7},{1,0},{3,2},{5,4},{7,6},{8,9},{10,11},{12,... | collective-permute-start | bytes 49160 | tf_op jit(solution)/shard_map/ppermute | solution.py:121
  8.1 2.0 %collective-permute-start.3 = (bf16[64,128]{1,0:T(8,128)(2,1)S(1)}, bf16[64,128]{1,0:T(8,128)(2,1)S(1)}, u32[]{:S(2)}, u32[]{:S(2)}) collective-permute-start(bf16[64,128]{1,0:T(8,128)(2,1)S(1)} %get-tuple-element.33), channel_id=1, source_target_pairs={{1,2},{3,4},{5,6},{2,1},{4,3},{6,5},{9,10},{11,12},{13,14},{10,9},... | collective-permute-start | bytes 49160 | tf_op jit(solution)/shard_map/ppermute | solution.py:121
  10.8 0.0 collective-permute-done.1.refs_5_
  10.8 0.0 collective-permute-done.refs_4_
  10.9 3.0 %shard_map.123 = (f32[6,8,32,128]{3,2,1,0:T(8,128)S(1)}, f32[6,8,32,128]{3,2,1,0:T(8,128)S(1)}, f32[6,7,32,128]{3,2,1,0:T(8,128)S(1)}) custom-call(f32[6,8,64,128]{3,2,1,0:T(8,128)S(1)} %get-tuple-element.26.refs_0_, f32[6,8,64,128]{3,2,1,0:T(8,128)S(1)} %get-tuple-element.27.refs_1_, s32[64,128]{1,0:T(8,128)S(1)} %get-tuple-element.28.refs_2_.mask_ref, ...), custom_call_target="tpu_custom_call" | custom-call | flops 12582912 | bytes 9437184 | tf_op jit(solution)/shard_map/pallas_call | solution.py:325
  13.9 0.0 collective-permute-done.2.refs_9_
  13.9 0.0 collective-permute-done.3.refs_10_
  13.9 0.0 copy-start.5
  13.9 0.0 copy-start.6
  13.9 1.9 %shard_map.124 = (f32[6,8,64,128]{3,2,1,0:T(8,128)S(1)}, bf16[512,768]{1,0:T(8,128)(2,1)S(1)}, f32[6,7,32,128]{3,2,1,0:T(8,128)S(1)}) custom-call(f32[6,8,64,128]{3,2,1,0:T(8,128)S(1)} %get-tuple-element.26.refs_0_, f32[6,8,64,128]{3,2,1,0:T(8,128)S(1)} %get-tuple-element.27.refs_1_, s32[64,128]{1,0:T(8,128)S(1)} %get-tuple-element.28.refs_2_.mask_ref, ...), custom_call_target="tpu_custom_call" | custom-call | flops 12582912 | bytes 9437184 | tf_op jit(solution)/shard_map/pallas_call | solution.py:325
  15.9 0.0 copy-done.5
  15.9 0.0 copy-start.2
  15.9 0.0 copy-start.3
  15.9 0.0 copy-start.4
  15.9 4.9 %shard_map.125 = (bf16[32,8,128]{2,1,0:T(8,128)(2,1)S(1)}, bf16[768,4096]{1,0:T(8,128)(2,1)S(1)}) custom-call(s32[1,1,32]{2,1,0:T(1,128)S(1)} %copy-done.6, s32[1,1]{1,0:T(1,128)S(6)} %copy.13.count_ref, s32[8,1,512]{2,1,0:T(1,128)S(1)} %bitcast.8, bf16[512,768]{1,0:T(8,128)(2,1)S(1)} %get-tuple-element.36.rounded_ref), custom_call_target="tpu_custom_call" | custom-call | flops 3221225472 | bytes 786432 | tf_op jit(solution)/shard_map/pallas_call | solution.py:391
  20.8 11.5 %all_to_all.10.picked_ref = bf16[32,8,128]{2,1,0:T(8,128)(2,1)S(1)} all-to-all(bf16[32,8,128]{2,1,0:T(8,128)(2,1)S(1)} %get-tuple-element.37), channel_id=1, replica_groups=mesh['gx'=4,'gy'=8] {'gx','gy'}, dimensions={0} | all-to-all | bytes 131072 | tf_op jit(solution)/shard_map/all_to_all | solution.py:534
  32.4 0.9 %shard_map.126 = bf16[32,16,128]{2,1,0:T(8,128)(2,1)S(1)} custom-call(bf16[32,8,8,128]{3,2,1,0:T(8,128)(2,1)S(1)} %bitcast.5, bf16[32,8,8,128]{3,2,1,0:T(8,128)(2,1)S(1)} %bitcast.6, bf16[32,8,128]{2,1,0:T(8,128)(2,1)S(1)} %bitcast.7, bf16[32,8,128]{2,1,0:T(8,128)(2,1)S(1)} %all_to_all.10.picked_ref), custom_call_target="tpu_custom_call" | custom-call | flops 1048576 | bytes 1048576 | tf_op jit(solution)/shard_map/pallas_call | solution.py:441
  33.2 9.6 %all_to_all.11.back_ref = bf16[32,16,128]{2,1,0:T(8,128)(2,1)S(1)} all-to-all(bf16[32,16,128]{2,1,0:T(8,128)(2,1)S(1)} %shard_map.126), channel_id=1, replica_groups=mesh['gx'=4,'gy'=8] {'gx','gy'}, dimensions={0} | all-to-all | bytes 262144 | tf_op jit(solution)/shard_map/all_to_all | solution.py:534
  42.8 4.7 %shard_map.127 = (f32[6,8,64,128]{3,2,1,0:T(8,128)S(1)}, f32[6,8,64,128]{3,2,1,0:T(8,128)S(1)}, bf16[64,128]{1,0:T(8,128)(2,1)S(1)}, bf16[64,128]{1,0:T(8,128)(2...) custom-call(s32[1,1,32]{2,1,0:T(1,128)S(1)} %copy-done.6, s32[2,1,2048]{2,1,0:T(1,128)S(1)} %bitcast.9, ...), custom_call_target="tpu_custom_call" | custom-call | flops 3221225472 | bytes 3145728 | tf_op jit(solution)/shard_map/pallas_call | solution.py:495
  47.5 0.8 %collective-permute-start.5 = (bf16[64,128]{1,0:T(8,128)(2,1)S(1)}, bf16[64,128]{1,0:T(8,128)(2,1)S(1)}, u32[]{:S(2)}, u32[]{:S(2)}) collective-permute-start(bf16[64,128]{1,0:T(8,128)(2,1)S(1)} %get-tuple-element.42), channel_id=1, source_target_pairs={{0,8},{16,24},{8,0},{24,16},{1,9},{17,25},{9,1},{25,17},{2,10},{18... | collective-permute-start | bytes 49160 | tf_op jit(solution)/shard_map/ppermute | solution.py:121
  48.3 2.4 %collective-permute-start.4 = (bf16[64,128]{1,0:T(8,128)(2,1)S(1)}, bf16[64,128]{1,0:T(8,128)(2,1)S(1)}, u32[]{:S(2)}, u32[]{:S(2)}) collective-permute-start(bf16[64,128]{1,0:T(8,128)(2,1)S(1)} %get-tuple-element.42), channel_id=1, source_target_pairs={{8,16},{16,8},{9,17},{17,9},{10,18},{18,10},{11,19},{19,11},{12,20... | collective-permute-start | bytes 49160 | tf_op jit(solution)/shard_map/ppermute | solution.py:121
  50.7 0.5 collective-permute-start.6
  51.1 3.6 %collective-permute-start.7 = (bf16[64,128]{1,0:T(8,128)(2,1)S(1)}, bf16[64,128]{1,0:T(8,128)(2,1)S(1)}, u32[]{:S(2)}, u32[]{:S(2)}) collective-permute-start(bf16[64,128]{1,0:T(8,128)(2,1)S(1)} %get-tuple-element.45), channel_id=1, source_target_pairs={{1,2},{3,4},{5,6},{2,1},{4,3},{6,5},{9,10},{11,12},{13,14},{10,9},... | collective-permute-start | bytes 49160 | tf_op jit(solution)/shard_map/ppermute | solution.py:121
  54.7 0.0 collective-permute-done.5.refs_5_
  54.8 0.0 collective-permute-done.4.refs_4_
  54.8 2.8 %shard_map.128 = (f32[6,8,32,128]{3,2,1,0:T(8,128)S(1)}, f32[6,8,32,128]{3,2,1,0:T(8,128)S(1)}) custom-call(f32[6,8,64,128]{3,2,1,0:T(8,128)S(1)} %get-tuple-element.40.refs_0_, f32[6,8,64,128]{3,2,1,0:T(8,128)S(1)} %get-tuple-element.41.refs_1_, s32[64,128]{1,0:T(8,128)S(1)} %get-tuple-element.28.refs_2_.mask_ref, ...), custom_call_target="tpu_custom_call" | custom-call | flops 12582912 | bytes 9437184 | tf_op jit(solution)/shard_map/pallas_call | solution.py:325
  57.6 0.0 collective-permute-done.6.refs_9_
  57.6 0.0 collective-permute-done.7.refs_10_
  57.6 2.4 %shard_map.129 = f32[6,8,64,128]{3,2,1,0:T(8,128)} custom-call(f32[6,8,64,128]{3,2,1,0:T(8,128)S(1)} %get-tuple-element.40.refs_0_, f32[6,8,64,128]{3,2,1,0:T(8,128)S(1)} %get-tuple-element.41.refs_1_, s32[64,128]{1,0:T(8,128)S(1)} %get-tuple-element.28.refs_2_.mask_ref, bf16[128,1024]{1,0:T(8,128)(2,1)S(1)} %get-tuple-element.29.refs_3_, ...), custom_call_target="tpu_custom_call" | custom-call | flops 12582912 | bytes 9437184 | tf_op jit(solution)/shard_map/pallas_call | solution.py:325
  (8 shorter events, 0.0 us)
Async XLA Ops:
  0.6 10.2 %copy-start = (bf16[6,8,8,64,128]{4,3,2,1,0:T(8,128)(2,1)S(1)}, bf16[6,8,8,64,128]{4,3,2,1,0:T(8,128)(2,1)}, u32[]{:S(2)}) copy-start(bf16[6,8,8,64,128]{4,3,2,1,0:T(8,128)(2,1)} %refs_6_.7) | copy-start | bytes 18874372
  0.6 10.2 %copy-start.1 = (bf16[6,8,8,64,128]{4,3,2,1,0:T(8,128)(2,1)S(1)}, bf16[6,8,8,64,128]{4,3,2,1,0:T(8,128)(2,1)}, u32[]{:S(2)}) copy-start(bf16[6,8,8,64,128]{4,3,2,1,0:T(8,128)(2,1)} %refs_7_.7) | copy-start | bytes 18874372
  2.8 8.0 %collective-permute-start.1 = (bf16[64,128]{1,0:T(8,128)(2,1)S(1)}, bf16[64,128]{1,0:T(8,128)(2,1)S(1)}, u32[]{:S(2)}, u32[]{:S(2)}) collective-permute-start(bf16[64,128]{1,0:T(8,128)(2,1)S(1)} %get-tuple-element.30), channel_id=1, source_target_pairs={{0,8},{16,24},{8,0},{24,16},{1,9},{17,25},{9,1},{25,17},{2,10},{18... | collective-permute-start | bytes 49160 | tf_op jit(solution)/shard_map/ppermute | solution.py:121
  3.5 7.3 %collective-permute-start = (bf16[64,128]{1,0:T(8,128)(2,1)S(1)}, bf16[64,128]{1,0:T(8,128)(2,1)S(1)}, u32[]{:S(2)}, u32[]{:S(2)}) collective-permute-start(bf16[64,128]{1,0:T(8,128)(2,1)S(1)} %get-tuple-element.30), channel_id=1, source_target_pairs={{8,16},{16,8},{9,17},{17,9},{10,18},{18,10},{11,19},{19,11},{12,20... | collective-permute-start | bytes 49160 | tf_op jit(solution)/shard_map/ppermute | solution.py:121
  6.9 7.0 %collective-permute-start.2 = (bf16[64,128]{1,0:T(8,128)(2,1)S(1)}, bf16[64,128]{1,0:T(8,128)(2,1)S(1)}, u32[]{:S(2)}, u32[]{:S(2)}) collective-permute-start(bf16[64,128]{1,0:T(8,128)(2,1)S(1)} %get-tuple-element.32), channel_id=1, source_target_pairs={{0,1},{2,3},{4,5},{6,7},{1,0},{3,2},{5,4},{7,6},{8,9},{10,11},{12,... | collective-permute-start | bytes 49160 | tf_op jit(solution)/shard_map/ppermute | solution.py:121
  8.1 5.8 %collective-permute-start.3 = (bf16[64,128]{1,0:T(8,128)(2,1)S(1)}, bf16[64,128]{1,0:T(8,128)(2,1)S(1)}, u32[]{:S(2)}, u32[]{:S(2)}) collective-permute-start(bf16[64,128]{1,0:T(8,128)(2,1)S(1)} %get-tuple-element.33), channel_id=1, source_target_pairs={{1,2},{3,4},{5,6},{2,1},{4,3},{6,5},{9,10},{11,12},{13,14},{10,9},... | collective-permute-start | bytes 49160 | tf_op jit(solution)/shard_map/ppermute | solution.py:121
  13.9 2.0 %copy-start.5 = (s32[1,1,4096]{2,1,0:T(1,128)S(1)}, s32[1,1,4096]{2,1,0:T(1,128)}, u32[]{:S(2)}) copy-start(s32[1,1,4096]{2,1,0:T(1,128)} %param.16) | copy-start | bytes 49156
  13.9 2.0 %copy-start.6 = (s32[1,1,32]{2,1,0:T(1,128)S(1)}, s32[1,1,32]{2,1,0:T(1,128)}, u32[]{:S(2)}) copy-start(s32[1,1,32]{2,1,0:T(1,128)} %helper_ref.3) | copy-start | bytes 388
  15.9 16.5 %copy-start.2 = (bf16[1,1,32,8,8,128]{5,4,3,2,1,0:T(8,128)(2,1)S(1)}, bf16[1,1,32,8,8,128]{5,4,3,2,1,0:T(8,128)(2,1)}, u32[]{:S(2)}) copy-start(bf16[1,1,32,8,8,128]{5,4,3,2,1,0:T(8,128)(2,1)} %param.19) | copy-start | bytes 1572868
  15.9 16.4 %copy-start.3 = (bf16[1,1,32,8,8,128]{5,4,3,2,1,0:T(8,128)(2,1)S(1)}, bf16[1,1,32,8,8,128]{5,4,3,2,1,0:T(8,128)(2,1)}, u32[]{:S(2)}) copy-start(bf16[1,1,32,8,8,128]{5,4,3,2,1,0:T(8,128)(2,1)} %param.20) | copy-start | bytes 1572868
  15.9 16.4 %copy-start.4 = (bf16[1,1,32,8,128]{4,3,2,1,0:T(8,128)(2,1)S(1)}, bf16[1,1,32,8,128]{4,3,2,1,0:T(8,128)(2,1)}, u32[]{:S(2)}) copy-start(bf16[1,1,32,8,128]{4,3,2,1,0:T(8,128)(2,1)} %param.21) | copy-start | bytes 196612
  47.5 7.3 %collective-permute-start.5 = (bf16[64,128]{1,0:T(8,128)(2,1)S(1)}, bf16[64,128]{1,0:T(8,128)(2,1)S(1)}, u32[]{:S(2)}, u32[]{:S(2)}) collective-permute-start(bf16[64,128]{1,0:T(8,128)(2,1)S(1)} %get-tuple-element.42), channel_id=1, source_target_pairs={{0,8},{16,24},{8,0},{24,16},{1,9},{17,25},{9,1},{25,17},{2,10},{18... | collective-permute-start | bytes 49160 | tf_op jit(solution)/shard_map/ppermute | solution.py:121
  48.3 6.5 %collective-permute-start.4 = (bf16[64,128]{1,0:T(8,128)(2,1)S(1)}, bf16[64,128]{1,0:T(8,128)(2,1)S(1)}, u32[]{:S(2)}, u32[]{:S(2)}) collective-permute-start(bf16[64,128]{1,0:T(8,128)(2,1)S(1)} %get-tuple-element.42), channel_id=1, source_target_pairs={{8,16},{16,8},{9,17},{17,9},{10,18},{18,10},{11,19},{19,11},{12,20... | collective-permute-start | bytes 49160 | tf_op jit(solution)/shard_map/ppermute | solution.py:121
  50.7 6.9 %collective-permute-start.6 = (bf16[64,128]{1,0:T(8,128)(2,1)S(1)}, bf16[64,128]{1,0:T(8,128)(2,1)S(1)}, u32[]{:S(2)}, u32[]{:S(2)}) collective-permute-start(bf16[64,128]{1,0:T(8,128)(2,1)S(1)} %get-tuple-element.44), channel_id=1, source_target_pairs={{0,1},{2,3},{4,5},{6,7},{1,0},{3,2},{5,4},{7,6},{8,9},{10,11},{12,... | collective-permute-start | bytes 49160 | tf_op jit(solution)/shard_map/ppermute | solution.py:121
  51.1 6.5 %collective-permute-start.7 = (bf16[64,128]{1,0:T(8,128)(2,1)S(1)}, bf16[64,128]{1,0:T(8,128)(2,1)S(1)}, u32[]{:S(2)}, u32[]{:S(2)}) collective-permute-start(bf16[64,128]{1,0:T(8,128)(2,1)S(1)} %get-tuple-element.45), channel_id=1, source_target_pairs={{1,2},{3,4},{5,6},{2,1},{4,3},{6,5},{9,10},{11,12},{13,14},{10,9},... | collective-permute-start | bytes 49160 | tf_op jit(solution)/shard_map/ppermute | solution.py:121

commit v12 on v10

--- a/solution.py
+++ b/solution.py
@@ -68,8 +68,9 @@
     send_y_0, send_y_1, send_x, masked_ref, field_ref, mask_ref, perm_ref, place_ref,
     side_y, sems,
 ):
-    sources, targets = (field_hbm, mask_hbm, perm_hbm), (field_ref, mask_ref, perm_ref)
-    copies = [pltpu.make_async_copy(a, b, sems.at[i]) for i, (a, b) in enumerate(zip(sources, targets))]
+    pairs = [(mask_hbm, mask_ref), (perm_hbm, perm_ref)]
+    pairs.append((field_hbm, field_ref))
+    copies = [pltpu.make_async_copy(a, b, sems.at[i]) for i, (a, b) in enumerate(pairs)]
     for copy in copies:
         copy.start()
     write_place(place_ref)
@@ -171,7 +172,7 @@
 
 
 def apply_kernel(is_first_apply, is_inner, *refs):
-    names = ["field", "masked", "mask", "place", "x_0", "x_1", "diag", "flux"]
+    names = ["field", "masked", "mask", "place", "x_1", "x_0", "diag", "flux"]
     names += ["perm"] if is_first_apply else ["weights"]
     names += [] if is_inner else ["y_0", "y_1", "inner", "begun"]
     names += ["out"] if is_inner or is_first_apply else ["out_hbm"]
@@ -281,7 +282,7 @@
                 copy.start()
         return carry
 
-    unrolled(layers, 2, layer)
+    unrolled(layers, 3, layer)
     if not is_first_apply and not is_inner:
         for k in range(layers):
             for copy in out_copies(k):
@@ -294,7 +295,7 @@
     hbm = pl.BlockSpec(memory_space=pltpu.HBM)
     here_rows = rows - 2 * TILE if is_inner else 2 * TILE
     here = (layers, comps, here_rows, cols)
-    arrays = [field, masked, mask, place, *halos[:2], *blocks, third]
+    arrays = [field, masked, mask, place, halos[1], halos[0], *blocks, third]
     specs = [vmem] * 9
     if not is_inner:
         arrays += [*halos[2:], *inner]
@@ -342,7 +343,14 @@
         return carry
 
     together = math.gcd(count, together)
-    lax.fori_loop(0, count // together, group, 0)
+    if together == count:
+        group(0, None)
+    else:
+        lax.fori_loop(0, count // together, group, 0)
+
+
+def stretch(i, size):
+    return pl.ds(i * size if isinstance(i, int) else pl.multiple_of(i * size, size), size)
 
 
 def one_hot(column, count, slots):
@@ -360,7 +368,7 @@
         column, y = split_cells(cells_ref[i], rows, cols)
         chosen = one_hot(column, rounded_ref.shape[1], slots)
         if kept_ref is not None:
-            kept_ref[:, pl.ds(pl.multiple_of(i * slots, slots), slots)] = chosen
+            kept_ref[:, stretch(i, slots)] = chosen
         found = jnp.dot(rounded_ref[...], chosen, preferred_element_type=F32)
         at_row = row_number == y
         values = [
@@ -374,7 +382,7 @@
             sent_ref[helper_ref[0, 0, b]] = (values[:, j * width : (j + 1) * width] * live).astype(BF16)
         return carry
 
-    unrolled(chunks, 4, one)
+    unrolled(chunks, 8, one)
 
 
 def gather(rounded, cells, helper, count, comps, rows, cols, width):
@@ -457,7 +465,7 @@
     def one(i, carry):
         column, y = split_cells(cells_ref[i], rows, cols)
         if has_kept:
-            chosen = kept_ref[:, pl.ds(pl.multiple_of(i * slots, slots), slots)]
+            chosen = kept_ref[:, stretch(i, slots)]
         else:
             chosen = one_hot(column, added.shape[1], slots)
         parts = [back_ref[helper_ref[0, 0, i * per_chunk + j]].astype(F32)[:comps] for j in range(per_chunk)]

time: 60.9 us -> 60.2 us (0.989)
  no operation moved by 1% of the time
where the time goes in v12:
time: 60.2 us; the launch traced here: 59.7 us
  Pallas kernels  22.4 us (37%)
  blocking collectives  21.1 us (35%)
  starting transfers between devices  14.6 us (24%)
  between operations  1.51 us (3%)
    all_to_all x2, blocking collectives, to_partners(): return lax.all_to_all(array, AXES, split_axis=0, concat_axis=0, tiled=True)  21.1 us
    ppermute x8, starting transfers between devices, swaps(): lax.ppermute(array, axis, pairs + [(j, i) for i, j in pairs])  14.6 us
    pallas_call x4, Pallas kernels, apply_rows(): pl.pallas_call(functools.partial(apply_kernel, is_first_apply, is_inner),...  10.1 us
    pallas_call x1, Pallas kernels, gather(): pl.pallas_call(functools.partial(gather_kernel, rows, cols), in_specs=[sm...  4.71 us
    pallas_call x1, Pallas kernels, scatter(): pl.pallas_call(functools.partial(scatter_kernel, scale, len(kept)), in_sp...  4.65 us
    pallas_call x1, Pallas kernels, opening(): pl.pallas_call(opening_kernel, in_specs=[hbm] * 5, out_specs=[vmem] * 8,...  2.08 us
  transfers between devices with their start and end apart: 8, of which 0 were waited for; matrix products, arithmetic and copies ran while one was open for 0% of the time, Pallas kernels for 10%

profile of v12, /device:TPU:9, one launch (start us, length us, event | category | flops | bytes accessed | tf_op | source)
XLA Modules:
  0.0 59.7 jit_solution(16199161831594415571)
XLA Ops:
  0.6 0.0 copy-start
  0.7 2.1 %shard_map.122 = (bf16[64,128]{1,0:T(8,128)(2,1)S(1)}, bf16[64,128]{1,0:T(8,128)(2,1)S(1)}, bf16[64,128]{1,0:T(8,128)(2,1)S(1)}, f32[6,8,64,128]{3,2,1,0:T(8,128...) custom-call(f32[6,8,64,128]{3,2,1,0:T(8,128)} %field_hbm.1, ...), custom_call_target="tpu_custom_call" | custom-call | flops 1572864 | bytes 3145728 | tf_op jit(solution)/shard_map/pallas_call | solution.py:101
  2.7 0.7 %collective-permute-start.1 = (bf16[64,128]{1,0:T(8,128)(2,1)S(1)}, bf16[64,128]{1,0:T(8,128)(2,1)S(1)}, u32[]{:S(2)}, u32[]{:S(2)}) collective-permute-start(bf16[64,128]{1,0:T(8,128)(2,1)S(1)} %get-tuple-element.30), channel_id=1, source_target_pairs={{0,8},{16,24},{8,0},{24,16},{1,9},{17,25},{9,1},{25,17},{2,10},{18... | collective-permute-start | bytes 49160 | tf_op jit(solution)/shard_map/ppermute | solution.py:118
  3.5 3.3 %collective-permute-start = (bf16[64,128]{1,0:T(8,128)(2,1)S(1)}, bf16[64,128]{1,0:T(8,128)(2,1)S(1)}, u32[]{:S(2)}, u32[]{:S(2)}) collective-permute-start(bf16[64,128]{1,0:T(8,128)(2,1)S(1)} %get-tuple-element.30), channel_id=1, source_target_pairs={{8,16},{16,8},{9,17},{17,9},{10,18},{18,10},{11,19},{19,11},{12,20... | collective-permute-start | bytes 49160 | tf_op jit(solution)/shard_map/ppermute | solution.py:118
  6.8 1.3 %collective-permute-start.2 = (bf16[64,128]{1,0:T(8,128)(2,1)S(1)}, bf16[64,128]{1,0:T(8,128)(2,1)S(1)}, u32[]{:S(2)}, u32[]{:S(2)}) collective-permute-start(bf16[64,128]{1,0:T(8,128)(2,1)S(1)} %get-tuple-element.32), channel_id=1, source_target_pairs={{0,1},{2,3},{4,5},{6,7},{1,0},{3,2},{5,4},{7,6},{8,9},{10,11},{12,... | collective-permute-start | bytes 49160 | tf_op jit(solution)/shard_map/ppermute | solution.py:118
  8.1 2.0 %collective-permute-start.3 = (bf16[64,128]{1,0:T(8,128)(2,1)S(1)}, bf16[64,128]{1,0:T(8,128)(2,1)S(1)}, u32[]{:S(2)}, u32[]{:S(2)}) collective-permute-start(bf16[64,128]{1,0:T(8,128)(2,1)S(1)} %get-tuple-element.33), channel_id=1, source_target_pairs={{1,2},{3,4},{5,6},{2,1},{4,3},{6,5},{9,10},{11,12},{13,14},{10,9},... | collective-permute-start | bytes 49160 | tf_op jit(solution)/shard_map/ppermute | solution.py:118
  10.8 0.0 collective-permute-done.1.refs_5_
  10.8 0.0 collective-permute-done.refs_4_
  10.8 3.0 %shard_map.123 = (f32[6,8,32,128]{3,2,1,0:T(8,128)S(1)}, f32[6,8,32,128]{3,2,1,0:T(8,128)S(1)}, f32[6,7,32,128]{3,2,1,0:T(8,128)S(1)}) custom-call(f32[6,8,64,128]{3,2,1,0:T(8,128)S(1)} %get-tuple-element.26.refs_0_, f32[6,8,64,128]{3,2,1,0:T(8,128)S(1)} %get-tuple-element.27.refs_1_, s32[64,128]{1,0:T(8,128)S(1)} %get-tuple-element.28.refs_2_.mask_ref, ...), custom_call_target="tpu_custom_call" | custom-call | flops 12582912 | bytes 9437184 | tf_op jit(solution)/shard_map/pallas_call | solution.py:322
  13.8 0.0 collective-permute-done.2.refs_9_
  13.8 0.0 collective-permute-done.3.refs_10_
  13.8 0.0 copy-start.5
  13.8 0.0 copy-start.6
  13.9 1.9 %shard_map.124 = (f32[6,8,64,128]{3,2,1,0:T(8,128)S(1)}, bf16[512,768]{1,0:T(8,128)(2,1)S(1)}, f32[6,7,32,128]{3,2,1,0:T(8,128)S(1)}) custom-call(f32[6,8,64,128]{3,2,1,0:T(8,128)S(1)} %get-tuple-element.26.refs_0_, f32[6,8,64,128]{3,2,1,0:T(8,128)S(1)} %get-tuple-element.27.refs_1_, s32[64,128]{1,0:T(8,128)S(1)} %get-tuple-element.28.refs_2_.mask_ref, ...), custom_call_target="tpu_custom_call" | custom-call | flops 12582912 | bytes 9437184 | tf_op jit(solution)/shard_map/pallas_call | solution.py:322
  15.8 0.0 copy-start.2
  15.8 0.0 copy-start.3
  15.8 0.0 copy-start.4
  15.8 4.7 %shard_map.125 = (bf16[32,8,128]{2,1,0:T(8,128)(2,1)S(1)}, bf16[768,4096]{1,0:T(8,128)(2,1)S(1)}) custom-call(s32[1,1,32]{2,1,0:T(1,128)S(1)} %copy-done.6, s32[1,1]{1,0:T(1,128)S(6)} %copy.13.count_ref, s32[8,1,512]{2,1,0:T(1,128)S(1)} %bitcast.8, bf16[512,768]{1,0:T(8,128)(2,1)S(1)} %get-tuple-element.36.rounded_ref), custom_call_target="tpu_custom_call" | custom-call | flops 3221225472 | bytes 786432 | tf_op jit(solution)/shard_map/pallas_call | solution.py:395
  20.6 11.5 %all_to_all.10.picked_ref = bf16[32,8,128]{2,1,0:T(8,128)(2,1)S(1)} all-to-all(bf16[32,8,128]{2,1,0:T(8,128)(2,1)S(1)} %get-tuple-element.37), channel_id=1, replica_groups=mesh['gx'=4,'gy'=8] {'gx','gy'}, dimensions={0} | all-to-all | bytes 131072 | tf_op jit(solution)/shard_map/all_to_all | solution.py:538
  32.1 0.9 %shard_map.126 = bf16[32,16,128]{2,1,0:T(8,128)(2,1)S(1)} custom-call(bf16[32,8,8,128]{3,2,1,0:T(8,128)(2,1)S(1)} %bitcast.5, bf16[32,8,8,128]{3,2,1,0:T(8,128)(2,1)S(1)} %bitcast.6, bf16[32,8,128]{2,1,0:T(8,128)(2,1)S(1)} %bitcast.7, bf16[32,8,128]{2,1,0:T(8,128)(2,1)S(1)} %all_to_all.10.picked_ref), custom_call_target="tpu_custom_call" | custom-call | flops 1048576 | bytes 1048576 | tf_op jit(solution)/shard_map/pallas_call | solution.py:445
  33.0 9.6 %all_to_all.11.back_ref = bf16[32,16,128]{2,1,0:T(8,128)(2,1)S(1)} all-to-all(bf16[32,16,128]{2,1,0:T(8,128)(2,1)S(1)} %shard_map.126), channel_id=1, replica_groups=mesh['gx'=4,'gy'=8] {'gx','gy'}, dimensions={0} | all-to-all | bytes 262144 | tf_op jit(solution)/shard_map/all_to_all | solution.py:538
  42.5 4.7 %shard_map.127 = (f32[6,8,64,128]{3,2,1,0:T(8,128)S(1)}, f32[6,8,64,128]{3,2,1,0:T(8,128)S(1)}, bf16[64,128]{1,0:T(8,128)(2,1)S(1)}, bf16[64,128]{1,0:T(8,128)(2...) custom-call(s32[1,1,32]{2,1,0:T(1,128)S(1)} %copy-done.6, s32[2,1,2048]{2,1,0:T(1,128)S(1)} %bitcast.9, ...), custom_call_target="tpu_custom_call" | custom-call | flops 3221225472 | bytes 3145728 | tf_op jit(solution)/shard_map/pallas_call | solution.py:499
  47.2 0.8 %collective-permute-start.5 = (bf16[64,128]{1,0:T(8,128)(2,1)S(1)}, bf16[64,128]{1,0:T(8,128)(2,1)S(1)}, u32[]{:S(2)}, u32[]{:S(2)}) collective-permute-start(bf16[64,128]{1,0:T(8,128)(2,1)S(1)} %get-tuple-element.42), channel_id=1, source_target_pairs={{0,8},{16,24},{8,0},{24,16},{1,9},{17,25},{9,1},{25,17},{2,10},{18... | collective-permute-start | bytes 49160 | tf_op jit(solution)/shard_map/ppermute | solution.py:118
  48.0 2.4 %collective-permute-start.4 = (bf16[64,128]{1,0:T(8,128)(2,1)S(1)}, bf16[64,128]{1,0:T(8,128)(2,1)S(1)}, u32[]{:S(2)}, u32[]{:S(2)}) collective-permute-start(bf16[64,128]{1,0:T(8,128)(2,1)S(1)} %get-tuple-element.42), channel_id=1, source_target_pairs={{8,16},{16,8},{9,17},{17,9},{10,18},{18,10},{11,19},{19,11},{12,20... | collective-permute-start | bytes 49160 | tf_op jit(solution)/shard_map/ppermute | solution.py:118
  50.4 0.5 collective-permute-start.6
  50.9 3.6 %collective-permute-start.7 = (bf16[64,128]{1,0:T(8,128)(2,1)S(1)}, bf16[64,128]{1,0:T(8,128)(2,1)S(1)}, u32[]{:S(2)}, u32[]{:S(2)}) collective-permute-start(bf16[64,128]{1,0:T(8,128)(2,1)S(1)} %get-tuple-element.45), channel_id=1, source_target_pairs={{1,2},{3,4},{5,6},{2,1},{4,3},{6,5},{9,10},{11,12},{13,14},{10,9},... | collective-permute-start | bytes 49160 | tf_op jit(solution)/shard_map/ppermute | solution.py:118
  54.5 0.0 collective-permute-done.5.refs_5_
  54.5 0.0 collective-permute-done.4.refs_4_
  54.5 2.8 %shard_map.128 = (f32[6,8,32,128]{3,2,1,0:T(8,128)S(1)}, f32[6,8,32,128]{3,2,1,0:T(8,128)S(1)}) custom-call(f32[6,8,64,128]{3,2,1,0:T(8,128)S(1)} %get-tuple-element.40.refs_0_, f32[6,8,64,128]{3,2,1,0:T(8,128)S(1)} %get-tuple-element.41.refs_1_, s32[64,128]{1,0:T(8,128)S(1)} %get-tuple-element.28.refs_2_.mask_ref, ...), custom_call_target="tpu_custom_call" | custom-call | flops 12582912 | bytes 9437184 | tf_op jit(solution)/shard_map/pallas_call | solution.py:322
  57.3 0.0 collective-permute-done.6.refs_9_
  57.3 0.0 collective-permute-done.7.refs_10_
  57.4 2.4 %shard_map.129 = f32[6,8,64,128]{3,2,1,0:T(8,128)} custom-call(f32[6,8,64,128]{3,2,1,0:T(8,128)S(1)} %get-tuple-element.40.refs_0_, f32[6,8,64,128]{3,2,1,0:T(8,128)S(1)} %get-tuple-element.41.refs_1_, s32[64,128]{1,0:T(8,128)S(1)} %get-tuple-element.28.refs_2_.mask_ref, bf16[128,1024]{1,0:T(8,128)(2,1)S(1)} %get-tuple-element.29.refs_3_, ...), custom_call_target="tpu_custom_call" | custom-call | flops 12582912 | bytes 9437184 | tf_op jit(solution)/shard_map/pallas_call | solution.py:322
  (8 shorter events, 0.0 us)
Async XLA Ops:
  0.6 10.2 %copy-start = (bf16[6,8,8,64,128]{4,3,2,1,0:T(8,128)(2,1)S(1)}, bf16[6,8,8,64,128]{4,3,2,1,0:T(8,128)(2,1)}, u32[]{:S(2)}) copy-start(bf16[6,8,8,64,128]{4,3,2,1,0:T(8,128)(2,1)} %refs_6_.7) | copy-start | bytes 18874372
  0.6 10.2 %copy-start.1 = (bf16[6,8,8,64,128]{4,3,2,1,0:T(8,128)(2,1)S(1)}, bf16[6,8,8,64,128]{4,3,2,1,0:T(8,128)(2,1)}, u32[]{:S(2)}) copy-start(bf16[6,8,8,64,128]{4,3,2,1,0:T(8,128)(2,1)} %refs_7_.7) | copy-start | bytes 18874372
  2.7 8.0 %collective-permute-start.1 = (bf16[64,128]{1,0:T(8,128)(2,1)S(1)}, bf16[64,128]{1,0:T(8,128)(2,1)S(1)}, u32[]{:S(2)}, u32[]{:S(2)}) collective-permute-start(bf16[64,128]{1,0:T(8,128)(2,1)S(1)} %get-tuple-element.30), channel_id=1, source_target_pairs={{0,8},{16,24},{8,0},{24,16},{1,9},{17,25},{9,1},{25,17},{2,10},{18... | collective-permute-start | bytes 49160 | tf_op jit(solution)/shard_map/ppermute | solution.py:118
  3.5 7.3 %collective-permute-start = (bf16[64,128]{1,0:T(8,128)(2,1)S(1)}, bf16[64,128]{1,0:T(8,128)(2,1)S(1)}, u32[]{:S(2)}, u32[]{:S(2)}) collective-permute-start(bf16[64,128]{1,0:T(8,128)(2,1)S(1)} %get-tuple-element.30), channel_id=1, source_target_pairs={{8,16},{16,8},{9,17},{17,9},{10,18},{18,10},{11,19},{19,11},{12,20... | collective-permute-start | bytes 49160 | tf_op jit(solution)/shard_map/ppermute | solution.py:118
  6.8 7.0 %collective-permute-start.2 = (bf16[64,128]{1,0:T(8,128)(2,1)S(1)}, bf16[64,128]{1,0:T(8,128)(2,1)S(1)}, u32[]{:S(2)}, u32[]{:S(2)}) collective-permute-start(bf16[64,128]{1,0:T(8,128)(2,1)S(1)} %get-tuple-element.32), channel_id=1, source_target_pairs={{0,1},{2,3},{4,5},{6,7},{1,0},{3,2},{5,4},{7,6},{8,9},{10,11},{12,... | collective-permute-start | bytes 49160 | tf_op jit(solution)/shard_map/ppermute | solution.py:118
  8.1 5.7 %collective-permute-start.3 = (bf16[64,128]{1,0:T(8,128)(2,1)S(1)}, bf16[64,128]{1,0:T(8,128)(2,1)S(1)}, u32[]{:S(2)}, u32[]{:S(2)}) collective-permute-start(bf16[64,128]{1,0:T(8,128)(2,1)S(1)} %get-tuple-element.33), channel_id=1, source_target_pairs={{1,2},{3,4},{5,6},{2,1},{4,3},{6,5},{9,10},{11,12},{13,14},{10,9},... | collective-permute-start | bytes 49160 | tf_op jit(solution)/shard_map/ppermute | solution.py:118
  13.8 2.0 %copy-start.5 = (s32[1,1,4096]{2,1,0:T(1,128)S(1)}, s32[1,1,4096]{2,1,0:T(1,128)}, u32[]{:S(2)}) copy-start(s32[1,1,4096]{2,1,0:T(1,128)} %param.16) | copy-start | bytes 49156
  13.8 2.0 %copy-start.6 = (s32[1,1,32]{2,1,0:T(1,128)S(1)}, s32[1,1,32]{2,1,0:T(1,128)}, u32[]{:S(2)}) copy-start(s32[1,1,32]{2,1,0:T(1,128)} %helper_ref.3) | copy-start | bytes 388
  15.8 16.3 %copy-start.2 = (bf16[1,1,32,8,8,128]{5,4,3,2,1,0:T(8,128)(2,1)S(1)}, bf16[1,1,32,8,8,128]{5,4,3,2,1,0:T(8,128)(2,1)}, u32[]{:S(2)}) copy-start(bf16[1,1,32,8,8,128]{5,4,3,2,1,0:T(8,128)(2,1)} %param.19) | copy-start | bytes 1572868
  15.8 16.3 %copy-start.3 = (bf16[1,1,32,8,8,128]{5,4,3,2,1,0:T(8,128)(2,1)S(1)}, bf16[1,1,32,8,8,128]{5,4,3,2,1,0:T(8,128)(2,1)}, u32[]{:S(2)}) copy-start(bf16[1,1,32,8,8,128]{5,4,3,2,1,0:T(8,128)(2,1)} %param.20) | copy-start | bytes 1572868
  15.8 16.3 %copy-start.4 = (bf16[1,1,32,8,128]{4,3,2,1,0:T(8,128)(2,1)S(1)}, bf16[1,1,32,8,128]{4,3,2,1,0:T(8,128)(2,1)}, u32[]{:S(2)}) copy-start(bf16[1,1,32,8,128]{4,3,2,1,0:T(8,128)(2,1)} %param.21) | copy-start | bytes 196612
  47.2 7.3 %collective-permute-start.5 = (bf16[64,128]{1,0:T(8,128)(2,1)S(1)}, bf16[64,128]{1,0:T(8,128)(2,1)S(1)}, u32[]{:S(2)}, u32[]{:S(2)}) collective-permute-start(bf16[64,128]{1,0:T(8,128)(2,1)S(1)} %get-tuple-element.42), channel_id=1, source_target_pairs={{0,8},{16,24},{8,0},{24,16},{1,9},{17,25},{9,1},{25,17},{2,10},{18... | collective-permute-start | bytes 49160 | tf_op jit(solution)/shard_map/ppermute | solution.py:118
  48.0 6.5 %collective-permute-start.4 = (bf16[64,128]{1,0:T(8,128)(2,1)S(1)}, bf16[64,128]{1,0:T(8,128)(2,1)S(1)}, u32[]{:S(2)}, u32[]{:S(2)}) collective-permute-start(bf16[64,128]{1,0:T(8,128)(2,1)S(1)} %get-tuple-element.42), channel_id=1, source_target_pairs={{8,16},{16,8},{9,17},{17,9},{10,18},{18,10},{11,19},{19,11},{12,20... | collective-permute-start | bytes 49160 | tf_op jit(solution)/shard_map/ppermute | solution.py:118
  50.4 6.9 %collective-permute-start.6 = (bf16[64,128]{1,0:T(8,128)(2,1)S(1)}, bf16[64,128]{1,0:T(8,128)(2,1)S(1)}, u32[]{:S(2)}, u32[]{:S(2)}) collective-permute-start(bf16[64,128]{1,0:T(8,128)(2,1)S(1)} %get-tuple-element.44), channel_id=1, source_target_pairs={{0,1},{2,3},{4,5},{6,7},{1,0},{3,2},{5,4},{7,6},{8,9},{10,11},{12,... | collective-permute-start | bytes 49160 | tf_op jit(solution)/shard_map/ppermute | solution.py:118
  50.9 6.5 %collective-permute-start.7 = (bf16[64,128]{1,0:T(8,128)(2,1)S(1)}, bf16[64,128]{1,0:T(8,128)(2,1)S(1)}, u32[]{:S(2)}, u32[]{:S(2)}) collective-permute-start(bf16[64,128]{1,0:T(8,128)(2,1)S(1)} %get-tuple-element.45), channel_id=1, source_target_pairs={{1,2},{3,4},{5,6},{2,1},{4,3},{6,5},{9,10},{11,12},{13,14},{10,9},... | collective-permute-start | bytes 49160 | tf_op jit(solution)/shard_map/ppermute | solution.py:118

commit v13 on v12

--- a/solution.py
+++ b/solution.py
@@ -12,7 +12,7 @@
 BF16 = jnp.bfloat16
 AXES = ("gx", "gy")
 MIB = 1024 * 1024
-GATHER_CHUNK, SCATTER_CHUNK = 512, 2048
+GATHER_CHUNK, SCATTER_CHUNK = 512, 4096
 KEPT_BYTES = 8 * MIB
 
 
@@ -278,10 +278,13 @@
                 ref["out"][k, c, TILE : rows - TILE] = value
                 ref["rounded"][c * rows + TILE : (c + 1) * rows - TILE, columns] = value.astype(BF16)
         if not is_first_apply and not is_inner:
-            for copy in out_copies(k):
+            for copy in out_copies(k)[1:]:
                 copy.start()
         return carry
 
+    if not is_first_apply and not is_inner:
+        for k in range(layers):
+            out_copies(k)[0].start()
     unrolled(layers, 3, layer)
     if not is_first_apply and not is_inner:
         for k in range(layers):
@@ -458,9 +461,8 @@
     width = back_ref.shape[-1]
     per_chunk = slots // width
     row_number = lax.broadcasted_iota(jnp.int32, (rows, slots), 0)
-    for k in range(layers):
-        for c in range(comps):
-            added[c * rows : (c + 1) * rows, k * cols : (k + 1) * cols] = first_ref[k, c]
+    if chunks > 1:
+        added[...] = jnp.zeros_like(added)
 
     def one(i, carry):
         column, y = split_cells(cells_ref[i], rows, cols)
@@ -474,13 +476,14 @@
         spread = jnp.concatenate(
             [jnp.where(at_row, correction[c : c + 1], 0.0).astype(BF16) for c in range(comps)], axis=0
         )
-        added[...] += lax.dot_general(spread, chosen, (((1,), (1,)), ((), ())), preferred_element_type=F32)
+        product = lax.dot_general(spread, chosen, (((1,), (1,)), ((), ())), preferred_element_type=F32)
+        added[...] = product if chunks == 1 else added[...] + product
         return carry
 
-    unrolled(chunks, 2, one)
+    unrolled(chunks, 1, one)
     for k in range(layers):
         for c in range(comps):
-            second_ref[k, c] = added[c * rows : (c + 1) * rows, k * cols : (k + 1) * cols]
+            second_ref[k, c] = first_ref[k, c] + added[c * rows : (c + 1) * rows, k * cols : (k + 1) * cols]
     write_edges(second_ref, mask_ref, None, masked_ref, side_y, sends)
     total = back_ref[0].astype(F32)[comps:]
     for b in range(1, back_ref.shape[0]):

time: 60.2 us -> 60.2 us (level)
  no operation moved by 1% of the time
where the time goes in v13:
time: 60.2 us; the launch traced here: 59.8 us
  Pallas kernels  22.4 us (37%)
  blocking collectives  21.1 us (35%)
  starting transfers between devices  14.6 us (24%)
  between operations  1.51 us (3%)
    all_to_all x2, blocking collectives, to_partners(): return lax.all_to_all(array, AXES, split_axis=0, concat_axis=0, tiled=True)  21.1 us
    ppermute x8, starting transfers between devices, swaps(): lax.ppermute(array, axis, pairs + [(j, i) for i, j in pairs])  14.6 us
    pallas_call x4, Pallas kernels, apply_rows(): pl.pallas_call(functools.partial(apply_kernel, is_first_apply, is_inner),...  10.1 us
    pallas_call x1, Pallas kernels, gather(): pl.pallas_call(functools.partial(gather_kernel, rows, cols), in_specs=[sm...  4.71 us
    pallas_call x1, Pallas kernels, scatter(): pl.pallas_call(functools.partial(scatter_kernel, scale, len(kept)), in_sp...  4.65 us
    pallas_call x1, Pallas kernels, opening(): pl.pallas_call(opening_kernel, in_specs=[hbm] * 5, out_specs=[vmem] * 8,...  2.08 us
  transfers between devices with their start and end apart: 8, of which 0 were waited for; matrix products, arithmetic and copies ran while one was open for 0% of the time, Pallas kernels for 10%

profile of v13, /device:TPU:9, one launch (start us, length us, event | category | flops | bytes accessed | tf_op | source)
XLA Modules:
  0.0 59.8 jit_solution(7152812720507562574)
XLA Ops:
  0.6 0.0 copy-start
  0.7 2.1 %shard_map.122 = (bf16[64,128]{1,0:T(8,128)(2,1)S(1)}, bf16[64,128]{1,0:T(8,128)(2,1)S(1)}, bf16[64,128]{1,0:T(8,128)(2,1)S(1)}, f32[6,8,64,128]{3,2,1,0:T(8,128...) custom-call(f32[6,8,64,128]{3,2,1,0:T(8,128)} %field_hbm.1, ...), custom_call_target="tpu_custom_call" | custom-call | flops 1572864 | bytes 3145728 | tf_op jit(solution)/shard_map/pallas_call | solution.py:101
  2.7 0.7 %collective-permute-start.1 = (bf16[64,128]{1,0:T(8,128)(2,1)S(1)}, bf16[64,128]{1,0:T(8,128)(2,1)S(1)}, u32[]{:S(2)}, u32[]{:S(2)}) collective-permute-start(bf16[64,128]{1,0:T(8,128)(2,1)S(1)} %get-tuple-element.30), channel_id=1, source_target_pairs={{0,8},{16,24},{8,0},{24,16},{1,9},{17,25},{9,1},{25,17},{2,10},{18... | collective-permute-start | bytes 49160 | tf_op jit(solution)/shard_map/ppermute | solution.py:118
  3.5 3.3 %collective-permute-start = (bf16[64,128]{1,0:T(8,128)(2,1)S(1)}, bf16[64,128]{1,0:T(8,128)(2,1)S(1)}, u32[]{:S(2)}, u32[]{:S(2)}) collective-permute-start(bf16[64,128]{1,0:T(8,128)(2,1)S(1)} %get-tuple-element.30), channel_id=1, source_target_pairs={{8,16},{16,8},{9,17},{17,9},{10,18},{18,10},{11,19},{19,11},{12,20... | collective-permute-start | bytes 49160 | tf_op jit(solution)/shard_map/ppermute | solution.py:118
  6.8 1.3 %collective-permute-start.2 = (bf16[64,128]{1,0:T(8,128)(2,1)S(1)}, bf16[64,128]{1,0:T(8,128)(2,1)S(1)}, u32[]{:S(2)}, u32[]{:S(2)}) collective-permute-start(bf16[64,128]{1,0:T(8,128)(2,1)S(1)} %get-tuple-element.32), channel_id=1, source_target_pairs={{0,1},{2,3},{4,5},{6,7},{1,0},{3,2},{5,4},{7,6},{8,9},{10,11},{12,... | collective-permute-start | bytes 49160 | tf_op jit(solution)/shard_map/ppermute | solution.py:118
  8.1 2.0 %collective-permute-start.3 = (bf16[64,128]{1,0:T(8,128)(2,1)S(1)}, bf16[64,128]{1,0:T(8,128)(2,1)S(1)}, u32[]{:S(2)}, u32[]{:S(2)}) collective-permute-start(bf16[64,128]{1,0:T(8,128)(2,1)S(1)} %get-tuple-element.33), channel_id=1, source_target_pairs={{1,2},{3,4},{5,6},{2,1},{4,3},{6,5},{9,10},{11,12},{13,14},{10,9},... | collective-permute-start | bytes 49160 | tf_op jit(solution)/shard_map/ppermute | solution.py:118
  10.8 0.0 collective-permute-done.1.refs_5_
  10.8 0.0 collective-permute-done.refs_4_
  10.8 3.0 %shard_map.123 = (f32[6,8,32,128]{3,2,1,0:T(8,128)S(1)}, f32[6,8,32,128]{3,2,1,0:T(8,128)S(1)}, f32[6,7,32,128]{3,2,1,0:T(8,128)S(1)}) custom-call(f32[6,8,64,128]{3,2,1,0:T(8,128)S(1)} %get-tuple-element.26.refs_0_, f32[6,8,64,128]{3,2,1,0:T(8,128)S(1)} %get-tuple-element.27.refs_1_, s32[64,128]{1,0:T(8,128)S(1)} %get-tuple-element.28.refs_2_.mask_ref, ...), custom_call_target="tpu_custom_call" | custom-call | flops 12582912 | bytes 9437184 | tf_op jit(solution)/shard_map/pallas_call | solution.py:325
  13.8 0.0 collective-permute-done.2.refs_9_
  13.8 0.0 collective-permute-done.3.refs_10_
  13.8 0.0 copy-start.5
  13.8 0.0 copy-start.6
  13.9 1.9 %shard_map.124 = (f32[6,8,64,128]{3,2,1,0:T(8,128)S(1)}, bf16[512,768]{1,0:T(8,128)(2,1)S(1)}, f32[6,7,32,128]{3,2,1,0:T(8,128)S(1)}) custom-call(f32[6,8,64,128]{3,2,1,0:T(8,128)S(1)} %get-tuple-element.26.refs_0_, f32[6,8,64,128]{3,2,1,0:T(8,128)S(1)} %get-tuple-element.27.refs_1_, s32[64,128]{1,0:T(8,128)S(1)} %get-tuple-element.28.refs_2_.mask_ref, ...), custom_call_target="tpu_custom_call" | custom-call | flops 12582912 | bytes 9437184 | tf_op jit(solution)/shard_map/pallas_call | solution.py:325
  15.8 0.0 copy-start.2
  15.8 0.0 copy-start.3
  15.8 0.0 copy-start.4
  15.8 4.7 %shard_map.125 = (bf16[32,8,128]{2,1,0:T(8,128)(2,1)S(1)}, bf16[768,4096]{1,0:T(8,128)(2,1)S(1)}) custom-call(s32[1,1,32]{2,1,0:T(1,128)S(1)} %copy-done.6, s32[1,1]{1,0:T(1,128)S(6)} %copy.13.count_ref, s32[8,1,512]{2,1,0:T(1,128)S(1)} %bitcast.7, bf16[512,768]{1,0:T(8,128)(2,1)S(1)} %get-tuple-element.36.rounded_ref), custom_call_target="tpu_custom_call" | custom-call | flops 3221225472 | bytes 786432 | tf_op jit(solution)/shard_map/pallas_call | solution.py:398
  20.6 11.5 %all_to_all.10.picked_ref = bf16[32,8,128]{2,1,0:T(8,128)(2,1)S(1)} all-to-all(bf16[32,8,128]{2,1,0:T(8,128)(2,1)S(1)} %get-tuple-element.37), channel_id=1, replica_groups=mesh['gx'=4,'gy'=8] {'gx','gy'}, dimensions={0} | all-to-all | bytes 131072 | tf_op jit(solution)/shard_map/all_to_all | solution.py:541
  32.1 0.9 %shard_map.126 = bf16[32,16,128]{2,1,0:T(8,128)(2,1)S(1)} custom-call(bf16[32,8,8,128]{3,2,1,0:T(8,128)(2,1)S(1)} %bitcast.4, bf16[32,8,8,128]{3,2,1,0:T(8,128)(2,1)S(1)} %bitcast.5, bf16[32,8,128]{2,1,0:T(8,128)(2,1)S(1)} %bitcast.6, bf16[32,8,128]{2,1,0:T(8,128)(2,1)S(1)} %all_to_all.10.picked_ref), custom_call_target="tpu_custom_call" | custom-call | flops 1048576 | bytes 1048576 | tf_op jit(solution)/shard_map/pallas_call | solution.py:448
  33.0 9.6 %all_to_all.11.back_ref = bf16[32,16,128]{2,1,0:T(8,128)(2,1)S(1)} all-to-all(bf16[32,16,128]{2,1,0:T(8,128)(2,1)S(1)} %shard_map.126), channel_id=1, replica_groups=mesh['gx'=4,'gy'=8] {'gx','gy'}, dimensions={0} | all-to-all | bytes 262144 | tf_op jit(solution)/shard_map/all_to_all | solution.py:541
  42.5 4.7 %shard_map.127 = (f32[6,8,64,128]{3,2,1,0:T(8,128)S(1)}, f32[6,8,64,128]{3,2,1,0:T(8,128)S(1)}, bf16[64,128]{1,0:T(8,128)(2,1)S(1)}, bf16[64,128]{1,0:T(8,128)(2...) custom-call(s32[1,1,32]{2,1,0:T(1,128)S(1)} %copy-done.6, s32[1,1,4096]{2,1,0:T(1,128)S(1)} %copy-done.5, ...), custom_call_target="tpu_custom_call" | custom-call | flops 3221225472 | bytes 3145728 | tf_op jit(solution)/shard_map/pallas_call | solution.py:502
  47.2 0.8 %collective-permute-start.5 = (bf16[64,128]{1,0:T(8,128)(2,1)S(1)}, bf16[64,128]{1,0:T(8,128)(2,1)S(1)}, u32[]{:S(2)}, u32[]{:S(2)}) collective-permute-start(bf16[64,128]{1,0:T(8,128)(2,1)S(1)} %get-tuple-element.42), channel_id=1, source_target_pairs={{0,8},{16,24},{8,0},{24,16},{1,9},{17,25},{9,1},{25,17},{2,10},{18... | collective-permute-start | bytes 49160 | tf_op jit(solution)/shard_map/ppermute | solution.py:118
  48.0 2.4 %collective-permute-start.4 = (bf16[64,128]{1,0:T(8,128)(2,1)S(1)}, bf16[64,128]{1,0:T(8,128)(2,1)S(1)}, u32[]{:S(2)}, u32[]{:S(2)}) collective-permute-start(bf16[64,128]{1,0:T(8,128)(2,1)S(1)} %get-tuple-element.42), channel_id=1, source_target_pairs={{8,16},{16,8},{9,17},{17,9},{10,18},{18,10},{11,19},{19,11},{12,20... | collective-permute-start | bytes 49160 | tf_op jit(solution)/shard_map/ppermute | solution.py:118
  50.4 0.5 collective-permute-start.6
  50.9 3.6 %collective-permute-start.7 = (bf16[64,128]{1,0:T(8,128)(2,1)S(1)}, bf16[64,128]{1,0:T(8,128)(2,1)S(1)}, u32[]{:S(2)}, u32[]{:S(2)}) collective-permute-start(bf16[64,128]{1,0:T(8,128)(2,1)S(1)} %get-tuple-element.45), channel_id=1, source_target_pairs={{1,2},{3,4},{5,6},{2,1},{4,3},{6,5},{9,10},{11,12},{13,14},{10,9},... | collective-permute-start | bytes 49160 | tf_op jit(solution)/shard_map/ppermute | solution.py:118
  54.5 0.0 collective-permute-done.5.refs_5_
  54.5 0.0 collective-permute-done.4.refs_4_
  54.5 2.8 %shard_map.128 = (f32[6,8,32,128]{3,2,1,0:T(8,128)S(1)}, f32[6,8,32,128]{3,2,1,0:T(8,128)S(1)}) custom-call(f32[6,8,64,128]{3,2,1,0:T(8,128)S(1)} %get-tuple-element.40.refs_0_, f32[6,8,64,128]{3,2,1,0:T(8,128)S(1)} %get-tuple-element.41.refs_1_, s32[64,128]{1,0:T(8,128)S(1)} %get-tuple-element.28.refs_2_.mask_ref, ...), custom_call_target="tpu_custom_call" | custom-call | flops 12582912 | bytes 9437184 | tf_op jit(solution)/shard_map/pallas_call | solution.py:325
  57.3 0.0 collective-permute-done.6.refs_9_
  57.3 0.0 collective-permute-done.7.refs_10_
  57.4 2.4 %shard_map.129 = f32[6,8,64,128]{3,2,1,0:T(8,128)} custom-call(f32[6,8,64,128]{3,2,1,0:T(8,128)S(1)} %get-tuple-element.40.refs_0_, f32[6,8,64,128]{3,2,1,0:T(8,128)S(1)} %get-tuple-element.41.refs_1_, s32[64,128]{1,0:T(8,128)S(1)} %get-tuple-element.28.refs_2_.mask_ref, bf16[128,1024]{1,0:T(8,128)(2,1)S(1)} %get-tuple-element.29.refs_3_, ...), custom_call_target="tpu_custom_call" | custom-call | flops 12582912 | bytes 9437184 | tf_op jit(solution)/shard_map/pallas_call | solution.py:325
  (8 shorter events, 0.0 us)
Async XLA Ops:
  0.6 10.2 %copy-start = (bf16[6,8,8,64,128]{4,3,2,1,0:T(8,128)(2,1)S(1)}, bf16[6,8,8,64,128]{4,3,2,1,0:T(8,128)(2,1)}, u32[]{:S(2)}) copy-start(bf16[6,8,8,64,128]{4,3,2,1,0:T(8,128)(2,1)} %refs_6_.7) | copy-start | bytes 18874372
  0.6 10.2 %copy-start.1 = (bf16[6,8,8,64,128]{4,3,2,1,0:T(8,128)(2,1)S(1)}, bf16[6,8,8,64,128]{4,3,2,1,0:T(8,128)(2,1)}, u32[]{:S(2)}) copy-start(bf16[6,8,8,64,128]{4,3,2,1,0:T(8,128)(2,1)} %refs_7_.7) | copy-start | bytes 18874372
  2.7 8.0 %collective-permute-start.1 = (bf16[64,128]{1,0:T(8,128)(2,1)S(1)}, bf16[64,128]{1,0:T(8,128)(2,1)S(1)}, u32[]{:S(2)}, u32[]{:S(2)}) collective-permute-start(bf16[64,128]{1,0:T(8,128)(2,1)S(1)} %get-tuple-element.30), channel_id=1, source_target_pairs={{0,8},{16,24},{8,0},{24,16},{1,9},{17,25},{9,1},{25,17},{2,10},{18... | collective-permute-start | bytes 49160 | tf_op jit(solution)/shard_map/ppermute | solution.py:118
  3.5 7.3 %collective-permute-start = (bf16[64,128]{1,0:T(8,128)(2,1)S(1)}, bf16[64,128]{1,0:T(8,128)(2,1)S(1)}, u32[]{:S(2)}, u32[]{:S(2)}) collective-permute-start(bf16[64,128]{1,0:T(8,128)(2,1)S(1)} %get-tuple-element.30), channel_id=1, source_target_pairs={{8,16},{16,8},{9,17},{17,9},{10,18},{18,10},{11,19},{19,11},{12,20... | collective-permute-start | bytes 49160 | tf_op jit(solution)/shard_map/ppermute | solution.py:118
  6.8 7.0 %collective-permute-start.2 = (bf16[64,128]{1,0:T(8,128)(2,1)S(1)}, bf16[64,128]{1,0:T(8,128)(2,1)S(1)}, u32[]{:S(2)}, u32[]{:S(2)}) collective-permute-start(bf16[64,128]{1,0:T(8,128)(2,1)S(1)} %get-tuple-element.32), channel_id=1, source_target_pairs={{0,1},{2,3},{4,5},{6,7},{1,0},{3,2},{5,4},{7,6},{8,9},{10,11},{12,... | collective-permute-start | bytes 49160 | tf_op jit(solution)/shard_map/ppermute | solution.py:118
  8.1 5.7 %collective-permute-start.3 = (bf16[64,128]{1,0:T(8,128)(2,1)S(1)}, bf16[64,128]{1,0:T(8,128)(2,1)S(1)}, u32[]{:S(2)}, u32[]{:S(2)}) collective-permute-start(bf16[64,128]{1,0:T(8,128)(2,1)S(1)} %get-tuple-element.33), channel_id=1, source_target_pairs={{1,2},{3,4},{5,6},{2,1},{4,3},{6,5},{9,10},{11,12},{13,14},{10,9},... | collective-permute-start | bytes 49160 | tf_op jit(solution)/shard_map/ppermute | solution.py:118
  13.8 2.0 %copy-start.5 = (s32[1,1,4096]{2,1,0:T(1,128)S(1)}, s32[1,1,4096]{2,1,0:T(1,128)}, u32[]{:S(2)}) copy-start(s32[1,1,4096]{2,1,0:T(1,128)} %cells_ref.1) | copy-start | bytes 49156
  13.8 2.0 %copy-start.6 = (s32[1,1,32]{2,1,0:T(1,128)S(1)}, s32[1,1,32]{2,1,0:T(1,128)}, u32[]{:S(2)}) copy-start(s32[1,1,32]{2,1,0:T(1,128)} %helper_ref.3) | copy-start | bytes 388
  15.8 16.3 %copy-start.2 = (bf16[1,1,32,8,8,128]{5,4,3,2,1,0:T(8,128)(2,1)S(1)}, bf16[1,1,32,8,8,128]{5,4,3,2,1,0:T(8,128)(2,1)}, u32[]{:S(2)}) copy-start(bf16[1,1,32,8,8,128]{5,4,3,2,1,0:T(8,128)(2,1)} %param.19) | copy-start | bytes 1572868
  15.8 16.3 %copy-start.3 = (bf16[1,1,32,8,8,128]{5,4,3,2,1,0:T(8,128)(2,1)S(1)}, bf16[1,1,32,8,8,128]{5,4,3,2,1,0:T(8,128)(2,1)}, u32[]{:S(2)}) copy-start(bf16[1,1,32,8,8,128]{5,4,3,2,1,0:T(8,128)(2,1)} %param.20) | copy-start | bytes 1572868
  15.8 16.3 %copy-start.4 = (bf16[1,1,32,8,128]{4,3,2,1,0:T(8,128)(2,1)S(1)}, bf16[1,1,32,8,128]{4,3,2,1,0:T(8,128)(2,1)}, u32[]{:S(2)}) copy-start(bf16[1,1,32,8,128]{4,3,2,1,0:T(8,128)(2,1)} %param.21) | copy-start | bytes 196612
  47.2 7.3 %collective-permute-start.5 = (bf16[64,128]{1,0:T(8,128)(2,1)S(1)}, bf16[64,128]{1,0:T(8,128)(2,1)S(1)}, u32[]{:S(2)}, u32[]{:S(2)}) collective-permute-start(bf16[64,128]{1,0:T(8,128)(2,1)S(1)} %get-tuple-element.42), channel_id=1, source_target_pairs={{0,8},{16,24},{8,0},{24,16},{1,9},{17,25},{9,1},{25,17},{2,10},{18... | collective-permute-start | bytes 49160 | tf_op jit(solution)/shard_map/ppermute | solution.py:118
  48.0 6.5 %collective-permute-start.4 = (bf16[64,128]{1,0:T(8,128)(2,1)S(1)}, bf16[64,128]{1,0:T(8,128)(2,1)S(1)}, u32[]{:S(2)}, u32[]{:S(2)}) collective-permute-start(bf16[64,128]{1,0:T(8,128)(2,1)S(1)} %get-tuple-element.42), channel_id=1, source_target_pairs={{8,16},{16,8},{9,17},{17,9},{10,18},{18,10},{11,19},{19,11},{12,20... | collective-permute-start | bytes 49160 | tf_op jit(solution)/shard_map/ppermute | solution.py:118
  50.4 6.9 %collective-permute-start.6 = (bf16[64,128]{1,0:T(8,128)(2,1)S(1)}, bf16[64,128]{1,0:T(8,128)(2,1)S(1)}, u32[]{:S(2)}, u32[]{:S(2)}) collective-permute-start(bf16[64,128]{1,0:T(8,128)(2,1)S(1)} %get-tuple-element.44), channel_id=1, source_target_pairs={{0,1},{2,3},{4,5},{6,7},{1,0},{3,2},{5,4},{7,6},{8,9},{10,11},{12,... | collective-permute-start | bytes 49160 | tf_op jit(solution)/shard_map/ppermute | solution.py:118
  50.9 6.5 %collective-permute-start.7 = (bf16[64,128]{1,0:T(8,128)(2,1)S(1)}, bf16[64,128]{1,0:T(8,128)(2,1)S(1)}, u32[]{:S(2)}, u32[]{:S(2)}) collective-permute-start(bf16[64,128]{1,0:T(8,128)(2,1)S(1)} %get-tuple-element.45), channel_id=1, source_target_pairs={{1,2},{3,4},{5,6},{2,1},{4,3},{6,5},{9,10},{11,12},{13,14},{10,9},... | collective-permute-start | bytes 49160 | tf_op jit(solution)/shard_map/ppermute | solution.py:118

commit v14 on v13

--- a/solution.py
+++ b/solution.py
@@ -12,7 +12,7 @@
 BF16 = jnp.bfloat16
 AXES = ("gx", "gy")
 MIB = 1024 * 1024
-GATHER_CHUNK, SCATTER_CHUNK = 512, 4096
+GATHER_CHUNK, SCATTER_CHUNK = 1024, 4096
 KEPT_BYTES = 8 * MIB
 
 

time: 60.2 us -> 60.1 us (level)
  no operation moved by 1% of the time
where the time goes in v14:
time: 60.1 us; the launch traced here: 59.7 us
  Pallas kernels  22.4 us (37%)
  blocking collectives  21.1 us (35%)
  starting transfers between devices  14.6 us (24%)
  between operations  1.51 us (3%)
    all_to_all x2, blocking collectives, to_partners(): return lax.all_to_all(array, AXES, split_axis=0, concat_axis=0, tiled=True)  21.1 us
    ppermute x8, starting transfers between devices, swaps(): lax.ppermute(array, axis, pairs + [(j, i) for i, j in pairs])  14.6 us
    pallas_call x4, Pallas kernels, apply_rows(): pl.pallas_call(functools.partial(apply_kernel, is_first_apply, is_inner),...  10.1 us
    pallas_call x1, Pallas kernels, gather(): pl.pallas_call(functools.partial(gather_kernel, rows, cols), in_specs=[sm...  4.67 us
    pallas_call x1, Pallas kernels, scatter(): pl.pallas_call(functools.partial(scatter_kernel, scale, len(kept)), in_sp...  4.65 us
    pallas_call x1, Pallas kernels, opening(): pl.pallas_call(opening_kernel, in_specs=[hbm] * 5, out_specs=[vmem] * 8,...  2.08 us
  transfers between devices with their start and end apart: 8, of which 0 were waited for; matrix products, arithmetic and copies ran while one was open for 0% of the time, Pallas kernels for 10%

profile of v14, /device:TPU:9, one launch (start us, length us, event | category | flops | bytes accessed | tf_op | source)
XLA Modules:
  0.0 59.7 jit_solution(12590234560361339451)
XLA Ops:
  0.7 2.1 %shard_map.122 = (bf16[64,128]{1,0:T(8,128)(2,1)S(1)}, bf16[64,128]{1,0:T(8,128)(2,1)S(1)}, bf16[64,128]{1,0:T(8,128)(2,1)S(1)}, f32[6,8,64,128]{3,2,1,0:T(8,128...) custom-call(f32[6,8,64,128]{3,2,1,0:T(8,128)} %field_hbm.1, ...), custom_call_target="tpu_custom_call" | custom-call | flops 1572864 | bytes 3145728 | tf_op jit(solution)/shard_map/pallas_call | solution.py:101
  2.7 0.7 %collective-permute-start.1 = (bf16[64,128]{1,0:T(8,128)(2,1)S(1)}, bf16[64,128]{1,0:T(8,128)(2,1)S(1)}, u32[]{:S(2)}, u32[]{:S(2)}) collective-permute-start(bf16[64,128]{1,0:T(8,128)(2,1)S(1)} %get-tuple-element.30), channel_id=1, source_target_pairs={{0,8},{16,24},{8,0},{24,16},{1,9},{17,25},{9,1},{25,17},{2,10},{18... | collective-permute-start | bytes 49160 | tf_op jit(solution)/shard_map/ppermute | solution.py:118
  3.5 3.3 %collective-permute-start = (bf16[64,128]{1,0:T(8,128)(2,1)S(1)}, bf16[64,128]{1,0:T(8,128)(2,1)S(1)}, u32[]{:S(2)}, u32[]{:S(2)}) collective-permute-start(bf16[64,128]{1,0:T(8,128)(2,1)S(1)} %get-tuple-element.30), channel_id=1, source_target_pairs={{8,16},{16,8},{9,17},{17,9},{10,18},{18,10},{11,19},{19,11},{12,20... | collective-permute-start | bytes 49160 | tf_op jit(solution)/shard_map/ppermute | solution.py:118
  6.8 1.3 %collective-permute-start.2 = (bf16[64,128]{1,0:T(8,128)(2,1)S(1)}, bf16[64,128]{1,0:T(8,128)(2,1)S(1)}, u32[]{:S(2)}, u32[]{:S(2)}) collective-permute-start(bf16[64,128]{1,0:T(8,128)(2,1)S(1)} %get-tuple-element.32), channel_id=1, source_target_pairs={{0,1},{2,3},{4,5},{6,7},{1,0},{3,2},{5,4},{7,6},{8,9},{10,11},{12,... | collective-permute-start | bytes 49160 | tf_op jit(solution)/shard_map/ppermute | solution.py:118
  8.1 2.0 %collective-permute-start.3 = (bf16[64,128]{1,0:T(8,128)(2,1)S(1)}, bf16[64,128]{1,0:T(8,128)(2,1)S(1)}, u32[]{:S(2)}, u32[]{:S(2)}) collective-permute-start(bf16[64,128]{1,0:T(8,128)(2,1)S(1)} %get-tuple-element.33), channel_id=1, source_target_pairs={{1,2},{3,4},{5,6},{2,1},{4,3},{6,5},{9,10},{11,12},{13,14},{10,9},... | collective-permute-start | bytes 49160 | tf_op jit(solution)/shard_map/ppermute | solution.py:118
  10.8 0.0 collective-permute-done.1.refs_5_
  10.8 0.0 collective-permute-done.refs_4_
  10.8 3.0 %shard_map.123 = (f32[6,8,32,128]{3,2,1,0:T(8,128)S(1)}, f32[6,8,32,128]{3,2,1,0:T(8,128)S(1)}, f32[6,7,32,128]{3,2,1,0:T(8,128)S(1)}) custom-call(f32[6,8,64,128]{3,2,1,0:T(8,128)S(1)} %get-tuple-element.26.refs_0_, f32[6,8,64,128]{3,2,1,0:T(8,128)S(1)} %get-tuple-element.27.refs_1_, s32[64,128]{1,0:T(8,128)S(1)} %get-tuple-element.28.refs_2_.mask_ref, ...), custom_call_target="tpu_custom_call" | custom-call | flops 12582912 | bytes 9437184 | tf_op jit(solution)/shard_map/pallas_call | solution.py:325
  13.8 0.0 collective-permute-done.2.refs_9_
  13.8 0.0 collective-permute-done.3.refs_10_
  13.8 0.0 copy-start.5
  13.8 0.0 copy-start.6
  13.9 1.9 %shard_map.124 = (f32[6,8,64,128]{3,2,1,0:T(8,128)S(1)}, bf16[512,768]{1,0:T(8,128)(2,1)S(1)}, f32[6,7,32,128]{3,2,1,0:T(8,128)S(1)}) custom-call(f32[6,8,64,128]{3,2,1,0:T(8,128)S(1)} %get-tuple-element.26.refs_0_, f32[6,8,64,128]{3,2,1,0:T(8,128)S(1)} %get-tuple-element.27.refs_1_, s32[64,128]{1,0:T(8,128)S(1)} %get-tuple-element.28.refs_2_.mask_ref, ...), custom_call_target="tpu_custom_call" | custom-call | flops 12582912 | bytes 9437184 | tf_op jit(solution)/shard_map/pallas_call | solution.py:325
  15.8 0.0 copy-start.2
  15.8 0.0 copy-start.3
  15.8 0.0 copy-start.4
  15.8 4.7 %shard_map.125 = (bf16[32,8,128]{2,1,0:T(8,128)(2,1)S(1)}, bf16[768,4096]{1,0:T(8,128)(2,1)S(1)}) custom-call(s32[1,1,32]{2,1,0:T(1,128)S(1)} %copy-done.6, s32[1,1]{1,0:T(1,128)S(6)} %copy.13.count_ref, s32[4,1,1024]{2,1,0:T(1,128)S(1)} %bitcast.7, bf16[512,768]{1,0:T(8,128)(2,1)S(1)} %get-tuple-element.36.rounded_ref), custom_call_target="tpu_custom_call" | custom-call | flops 3221225472 | bytes 786432 | tf_op jit(solution)/shard_map/pallas_call | solution.py:398
  20.5 11.5 %all_to_all.10.picked_ref = bf16[32,8,128]{2,1,0:T(8,128)(2,1)S(1)} all-to-all(bf16[32,8,128]{2,1,0:T(8,128)(2,1)S(1)} %get-tuple-element.37), channel_id=1, replica_groups=mesh['gx'=4,'gy'=8] {'gx','gy'}, dimensions={0} | all-to-all | bytes 131072 | tf_op jit(solution)/shard_map/all_to_all | solution.py:541
  32.1 0.0 copy-done.2
  32.1 0.9 %shard_map.126 = bf16[32,16,128]{2,1,0:T(8,128)(2,1)S(1)} custom-call(bf16[32,8,8,128]{3,2,1,0:T(8,128)(2,1)S(1)} %bitcast.4, bf16[32,8,8,128]{3,2,1,0:T(8,128)(2,1)S(1)} %bitcast.5, bf16[32,8,128]{2,1,0:T(8,128)(2,1)S(1)} %bitcast.6, bf16[32,8,128]{2,1,0:T(8,128)(2,1)S(1)} %all_to_all.10.picked_ref), custom_call_target="tpu_custom_call" | custom-call | flops 1048576 | bytes 1048576 | tf_op jit(solution)/shard_map/pallas_call | solution.py:448
  32.9 9.6 %all_to_all.11.back_ref = bf16[32,16,128]{2,1,0:T(8,128)(2,1)S(1)} all-to-all(bf16[32,16,128]{2,1,0:T(8,128)(2,1)S(1)} %shard_map.126), channel_id=1, replica_groups=mesh['gx'=4,'gy'=8] {'gx','gy'}, dimensions={0} | all-to-all | bytes 262144 | tf_op jit(solution)/shard_map/all_to_all | solution.py:541
  42.5 4.7 %shard_map.127 = (f32[6,8,64,128]{3,2,1,0:T(8,128)S(1)}, f32[6,8,64,128]{3,2,1,0:T(8,128)S(1)}, bf16[64,128]{1,0:T(8,128)(2,1)S(1)}, bf16[64,128]{1,0:T(8,128)(2...) custom-call(s32[1,1,32]{2,1,0:T(1,128)S(1)} %copy-done.6, s32[1,1,4096]{2,1,0:T(1,128)S(1)} %copy-done.5, ...), custom_call_target="tpu_custom_call" | custom-call | flops 3221225472 | bytes 3145728 | tf_op jit(solution)/shard_map/pallas_call | solution.py:502
  47.1 0.8 %collective-permute-start.5 = (bf16[64,128]{1,0:T(8,128)(2,1)S(1)}, bf16[64,128]{1,0:T(8,128)(2,1)S(1)}, u32[]{:S(2)}, u32[]{:S(2)}) collective-permute-start(bf16[64,128]{1,0:T(8,128)(2,1)S(1)} %get-tuple-element.42), channel_id=1, source_target_pairs={{0,8},{16,24},{8,0},{24,16},{1,9},{17,25},{9,1},{25,17},{2,10},{18... | collective-permute-start | bytes 49160 | tf_op jit(solution)/shard_map/ppermute | solution.py:118
  48.0 2.4 %collective-permute-start.4 = (bf16[64,128]{1,0:T(8,128)(2,1)S(1)}, bf16[64,128]{1,0:T(8,128)(2,1)S(1)}, u32[]{:S(2)}, u32[]{:S(2)}) collective-permute-start(bf16[64,128]{1,0:T(8,128)(2,1)S(1)} %get-tuple-element.42), channel_id=1, source_target_pairs={{8,16},{16,8},{9,17},{17,9},{10,18},{18,10},{11,19},{19,11},{12,20... | collective-permute-start | bytes 49160 | tf_op jit(solution)/shard_map/ppermute | solution.py:118
  50.4 0.5 collective-permute-start.6
  50.8 3.6 %collective-permute-start.7 = (bf16[64,128]{1,0:T(8,128)(2,1)S(1)}, bf16[64,128]{1,0:T(8,128)(2,1)S(1)}, u32[]{:S(2)}, u32[]{:S(2)}) collective-permute-start(bf16[64,128]{1,0:T(8,128)(2,1)S(1)} %get-tuple-element.45), channel_id=1, source_target_pairs={{1,2},{3,4},{5,6},{2,1},{4,3},{6,5},{9,10},{11,12},{13,14},{10,9},... | collective-permute-start | bytes 49160 | tf_op jit(solution)/shard_map/ppermute | solution.py:118
  54.4 0.0 collective-permute-done.5.refs_5_
  54.5 0.0 collective-permute-done.4.refs_4_
  54.5 2.8 %shard_map.128 = (f32[6,8,32,128]{3,2,1,0:T(8,128)S(1)}, f32[6,8,32,128]{3,2,1,0:T(8,128)S(1)}) custom-call(f32[6,8,64,128]{3,2,1,0:T(8,128)S(1)} %get-tuple-element.40.refs_0_, f32[6,8,64,128]{3,2,1,0:T(8,128)S(1)} %get-tuple-element.41.refs_1_, s32[64,128]{1,0:T(8,128)S(1)} %get-tuple-element.28.refs_2_.mask_ref, ...), custom_call_target="tpu_custom_call" | custom-call | flops 12582912 | bytes 9437184 | tf_op jit(solution)/shard_map/pallas_call | solution.py:325
  57.3 0.0 collective-permute-done.6.refs_9_
  57.3 0.0 collective-permute-done.7.refs_10_
  57.3 2.4 %shard_map.129 = f32[6,8,64,128]{3,2,1,0:T(8,128)} custom-call(f32[6,8,64,128]{3,2,1,0:T(8,128)S(1)} %get-tuple-element.40.refs_0_, f32[6,8,64,128]{3,2,1,0:T(8,128)S(1)} %get-tuple-element.41.refs_1_, s32[64,128]{1,0:T(8,128)S(1)} %get-tuple-element.28.refs_2_.mask_ref, bf16[128,1024]{1,0:T(8,128)(2,1)S(1)} %get-tuple-element.29.refs_3_, ...), custom_call_target="tpu_custom_call" | custom-call | flops 12582912 | bytes 9437184 | tf_op jit(solution)/shard_map/pallas_call | solution.py:325
  (8 shorter events, 0.0 us)
Async XLA Ops:
  0.6 10.2 %copy-start = (bf16[6,8,8,64,128]{4,3,2,1,0:T(8,128)(2,1)S(1)}, bf16[6,8,8,64,128]{4,3,2,1,0:T(8,128)(2,1)}, u32[]{:S(2)}) copy-start(bf16[6,8,8,64,128]{4,3,2,1,0:T(8,128)(2,1)} %refs_6_.7) | copy-start | bytes 18874372
  0.6 10.2 %copy-start.1 = (bf16[6,8,8,64,128]{4,3,2,1,0:T(8,128)(2,1)S(1)}, bf16[6,8,8,64,128]{4,3,2,1,0:T(8,128)(2,1)}, u32[]{:S(2)}) copy-start(bf16[6,8,8,64,128]{4,3,2,1,0:T(8,128)(2,1)} %refs_7_.7) | copy-start | bytes 18874372
  2.7 8.0 %collective-permute-start.1 = (bf16[64,128]{1,0:T(8,128)(2,1)S(1)}, bf16[64,128]{1,0:T(8,128)(2,1)S(1)}, u32[]{:S(2)}, u32[]{:S(2)}) collective-permute-start(bf16[64,128]{1,0:T(8,128)(2,1)S(1)} %get-tuple-element.30), channel_id=1, source_target_pairs={{0,8},{16,24},{8,0},{24,16},{1,9},{17,25},{9,1},{25,17},{2,10},{18... | collective-permute-start | bytes 49160 | tf_op jit(solution)/shard_map/ppermute | solution.py:118
  3.5 7.3 %collective-permute-start = (bf16[64,128]{1,0:T(8,128)(2,1)S(1)}, bf16[64,128]{1,0:T(8,128)(2,1)S(1)}, u32[]{:S(2)}, u32[]{:S(2)}) collective-permute-start(bf16[64,128]{1,0:T(8,128)(2,1)S(1)} %get-tuple-element.30), channel_id=1, source_target_pairs={{8,16},{16,8},{9,17},{17,9},{10,18},{18,10},{11,19},{19,11},{12,20... | collective-permute-start | bytes 49160 | tf_op jit(solution)/shard_map/ppermute | solution.py:118
  6.8 7.0 %collective-permute-start.2 = (bf16[64,128]{1,0:T(8,128)(2,1)S(1)}, bf16[64,128]{1,0:T(8,128)(2,1)S(1)}, u32[]{:S(2)}, u32[]{:S(2)}) collective-permute-start(bf16[64,128]{1,0:T(8,128)(2,1)S(1)} %get-tuple-element.32), channel_id=1, source_target_pairs={{0,1},{2,3},{4,5},{6,7},{1,0},{3,2},{5,4},{7,6},{8,9},{10,11},{12,... | collective-permute-start | bytes 49160 | tf_op jit(solution)/shard_map/ppermute | solution.py:118
  8.1 5.7 %collective-permute-start.3 = (bf16[64,128]{1,0:T(8,128)(2,1)S(1)}, bf16[64,128]{1,0:T(8,128)(2,1)S(1)}, u32[]{:S(2)}, u32[]{:S(2)}) collective-permute-start(bf16[64,128]{1,0:T(8,128)(2,1)S(1)} %get-tuple-element.33), channel_id=1, source_target_pairs={{1,2},{3,4},{5,6},{2,1},{4,3},{6,5},{9,10},{11,12},{13,14},{10,9},... | collective-permute-start | bytes 49160 | tf_op jit(solution)/shard_map/ppermute | solution.py:118
  13.8 2.0 %copy-start.5 = (s32[1,1,4096]{2,1,0:T(1,128)S(1)}, s32[1,1,4096]{2,1,0:T(1,128)}, u32[]{:S(2)}) copy-start(s32[1,1,4096]{2,1,0:T(1,128)} %cells_ref.1) | copy-start | bytes 49156
  13.8 2.0 %copy-start.6 = (s32[1,1,32]{2,1,0:T(1,128)S(1)}, s32[1,1,32]{2,1,0:T(1,128)}, u32[]{:S(2)}) copy-start(s32[1,1,32]{2,1,0:T(1,128)} %helper_ref.3) | copy-start | bytes 388
  15.8 16.3 %copy-start.2 = (bf16[1,1,32,8,8,128]{5,4,3,2,1,0:T(8,128)(2,1)S(1)}, bf16[1,1,32,8,8,128]{5,4,3,2,1,0:T(8,128)(2,1)}, u32[]{:S(2)}) copy-start(bf16[1,1,32,8,8,128]{5,4,3,2,1,0:T(8,128)(2,1)} %param.19) | copy-start | bytes 1572868
  15.8 16.2 %copy-start.3 = (bf16[1,1,32,8,8,128]{5,4,3,2,1,0:T(8,128)(2,1)S(1)}, bf16[1,1,32,8,8,128]{5,4,3,2,1,0:T(8,128)(2,1)}, u32[]{:S(2)}) copy-start(bf16[1,1,32,8,8,128]{5,4,3,2,1,0:T(8,128)(2,1)} %param.20) | copy-start | bytes 1572868
  15.8 16.2 %copy-start.4 = (bf16[1,1,32,8,128]{4,3,2,1,0:T(8,128)(2,1)S(1)}, bf16[1,1,32,8,128]{4,3,2,1,0:T(8,128)(2,1)}, u32[]{:S(2)}) copy-start(bf16[1,1,32,8,128]{4,3,2,1,0:T(8,128)(2,1)} %param.21) | copy-start | bytes 196612
  47.1 7.3 %collective-permute-start.5 = (bf16[64,128]{1,0:T(8,128)(2,1)S(1)}, bf16[64,128]{1,0:T(8,128)(2,1)S(1)}, u32[]{:S(2)}, u32[]{:S(2)}) collective-permute-start(bf16[64,128]{1,0:T(8,128)(2,1)S(1)} %get-tuple-element.42), channel_id=1, source_target_pairs={{0,8},{16,24},{8,0},{24,16},{1,9},{17,25},{9,1},{25,17},{2,10},{18... | collective-permute-start | bytes 49160 | tf_op jit(solution)/shard_map/ppermute | solution.py:118
  48.0 6.5 %collective-permute-start.4 = (bf16[64,128]{1,0:T(8,128)(2,1)S(1)}, bf16[64,128]{1,0:T(8,128)(2,1)S(1)}, u32[]{:S(2)}, u32[]{:S(2)}) collective-permute-start(bf16[64,128]{1,0:T(8,128)(2,1)S(1)} %get-tuple-element.42), channel_id=1, source_target_pairs={{8,16},{16,8},{9,17},{17,9},{10,18},{18,10},{11,19},{19,11},{12,20... | collective-permute-start | bytes 49160 | tf_op jit(solution)/shard_map/ppermute | solution.py:118
  50.4 6.9 %collective-permute-start.6 = (bf16[64,128]{1,0:T(8,128)(2,1)S(1)}, bf16[64,128]{1,0:T(8,128)(2,1)S(1)}, u32[]{:S(2)}, u32[]{:S(2)}) collective-permute-start(bf16[64,128]{1,0:T(8,128)(2,1)S(1)} %get-tuple-element.44), channel_id=1, source_target_pairs={{0,1},{2,3},{4,5},{6,7},{1,0},{3,2},{5,4},{7,6},{8,9},{10,11},{12,... | collective-permute-start | bytes 49160 | tf_op jit(solution)/shard_map/ppermute | solution.py:118
  50.8 6.5 %collective-permute-start.7 = (bf16[64,128]{1,0:T(8,128)(2,1)S(1)}, bf16[64,128]{1,0:T(8,128)(2,1)S(1)}, u32[]{:S(2)}, u32[]{:S(2)}) collective-permute-start(bf16[64,128]{1,0:T(8,128)(2,1)S(1)} %get-tuple-element.45), channel_id=1, source_target_pairs={{1,2},{3,4},{5,6},{2,1},{4,3},{6,5},{9,10},{11,12},{13,14},{10,9},... | collective-permute-start | bytes 49160 | tf_op jit(solution)/shard_map/ppermute | solution.py:118
